TPU v7x, 32 devices: a whole 2x2x4 slice. The times are simulated.
32 devices in a mesh: shot: 2 (over core), tx: 2 (over y), ty: 8 (over z, x).
Axes of the slice: x: 2, y: 2, z: 4, core: 2. Of those that a mesh axis runs over, the one named last changes fastest.
Arguments:
- forward_fields: float32 [2, 9, 32, 128, 128], P('shot', None, 'tx', 'ty'), may hold values from -6 to 6
- adjoint_fields: float32 [2, 9, 32, 128, 128], P('shot', None, 'tx', 'ty'), may hold values from -6 to 6
- lame_lambda: float32 [32, 128, 128], P('tx', 'ty'), may hold values from 1 to 4
- shear_modulus: float32 [32, 128, 128], P('tx', 'ty'), may hold values from 0.5 to 2
- density: float32 [32, 128, 128], P('tx', 'ty'), may hold values from 1 to 3
- source_cell: int32 [2], P('shot'), may hold values from 0 to 524287
- source_amp: float32 [2], P('shot'), may hold values from 4 to 12
- receiver_cell: int32 [2, 256], P('shot'), may hold values from 0 to 524287
- residual_amp: float32 [2, 256], P('shot'), may hold values from -16 to 16
Outputs:
- forward_next: float32 [2, 9, 32, 128, 128], P('shot', None, 'tx', 'ty')
- adjoint_next: float32 [2, 9, 32, 128, 128], P('shot', None, 'tx', 'ty')
- gradient: float32 [3, 32, 128, 128], P(None, 'tx', 'ty')
Inputs may be any that keep to these rules, and one draw needn't show every extreme that they name: `source_cell`: each value is a flat index x * 128 * 128 + y * 128 + z of a grid cell. `receiver_cell`: each value is a flat index x * 128 * 128 + y * 128 + z of a grid cell; receivers may share cells.
All inputs are finite; a program needn't handle non-finite values.
Results may differ from a plain program's by a relative error of at most 0.0001.
Values sent between devices are 32-bit elements; how exact they have to be, the bound alone decides.
No kernel may reach another device: no remote copies, remote signals or barrier semaphores. Data moves between devices by JAX's collectives and lax.ppermute only.
A program may use at most 64 MiB of HBM per device.

v0:
```python
import jax
import jax.numpy as jnp
from jax import lax
from jax.sharding import PartitionSpec as P

near_coef = 9.0 / 8.0
far_coef = -1.0 / 24.0
time_step = 0.15


def extended(value, sides, width):
    for axis, dim in sides:
        peers, length = (lax.axis_size(axis), value.shape[dim])
        up = [(i, (i + 1) % peers) for i in range(peers - 1)]
        down = [(j, i) for i, j in up]
        last = lax.slice_in_dim(value, length - width, length, axis=dim)
        initial = lax.slice_in_dim(value, 0, width, axis=dim)
        before = lax.ppermute(last, axis, up)
        after = lax.ppermute(initial, axis, down)
        value = jnp.concatenate([before, value, after], axis=dim)
    return value


def shifted(padded, margin, rim_width, direction, offset):
    rank_count = padded.ndim
    sliced = padded
    for which in range(3):
        length = padded.shape[rank_count - 3 + which] - 2 * margin[which] + 2 * rim_width[which]
        begin_at = margin[which] - rim_width[which] + (offset if which == direction else 0)
        sliced = lax.slice_in_dim(sliced, begin_at, begin_at + length, axis=rank_count - 3 + which)
    return sliced


def depth_table(depth_cells, upward):
    source_row = lax.broadcasted_iota(jnp.int32, (depth_cells, depth_cells), 0)
    target_col = lax.broadcasted_iota(jnp.int32, (depth_cells, depth_cells), 1)
    gap = source_row - target_col
    if upward:
        table = near_coef * (
            (gap == 1).astype(jnp.float32) - (gap == 0).astype(jnp.float32)
        ) + far_coef * ((gap == 2).astype(jnp.float32) - (gap == -1).astype(jnp.float32))
    else:
        table = near_coef * (
            (gap == 0).astype(jnp.float32) - (gap == -1).astype(jnp.float32)
        ) + far_coef * ((gap == 1).astype(jnp.float32) - (gap == -2).astype(jnp.float32))
    return table


def derive(padded, margin, rim_width, direction, upward):
    if direction == 2:
        core = shifted(padded, margin, rim_width, 2, 0)
        return jnp.einsum(
            "...k,ki->...i",
            core,
            depth_table(core.shape[-1], upward),
            precision=lax.Precision.HIGHEST,
        )
    if upward:
        return near_coef * (
            shifted(padded, margin, rim_width, direction, 1)
            - shifted(padded, margin, rim_width, direction, 0)
        ) + far_coef * (
            shifted(padded, margin, rim_width, direction, 2)
            - shifted(padded, margin, rim_width, direction, -1)
        )
    return near_coef * (
        shifted(padded, margin, rim_width, direction, 0)
        - shifted(padded, margin, rim_width, direction, -1)
    ) + far_coef * (
        shifted(padded, margin, rim_width, direction, 1)
        - shifted(padded, margin, rim_width, direction, -2)
    )


def accelerate(stress_ext, buoyancy, margin, rim_width):
    comps = [stress_ext[..., which, :, :, :] for which in range(6)]
    accel_x = (
        derive(comps[0], margin, rim_width, 0, True)
        + derive(comps[3], margin, rim_width, 1, False)
        + derive(comps[4], margin, rim_width, 2, False)
    )
    accel_y = (
        derive(comps[3], margin, rim_width, 0, False)
        + derive(comps[1], margin, rim_width, 1, True)
        + derive(comps[5], margin, rim_width, 2, False)
    )
    accel_z = (
        derive(comps[4], margin, rim_width, 0, False)
        + derive(comps[5], margin, rim_width, 1, False)
        + derive(comps[2], margin, rim_width, 2, True)
    )
    return jnp.stack([accel_x, accel_y, accel_z], axis=-4) * buoyancy


def strain_rates(velocity_ext, margin):
    flat_rim = (0, 0, 0)
    comps = [velocity_ext[..., which, :, :, :] for which in range(3)]
    return jnp.stack(
        [
            derive(comps[0], margin, flat_rim, 0, False),
            derive(comps[1], margin, flat_rim, 1, False),
            derive(comps[2], margin, flat_rim, 2, False),
            derive(comps[0], margin, flat_rim, 1, True)
            + derive(comps[1], margin, flat_rim, 0, True),
            derive(comps[0], margin, flat_rim, 2, True)
            + derive(comps[2], margin, flat_rim, 0, True),
            derive(comps[1], margin, flat_rim, 2, True)
            + derive(comps[2], margin, flat_rim, 1, True),
        ],
        axis=-4,
    )


def new_stress(stress_now, strain, lame_lambda, shear_modulus):
    trace = strain[..., 0, :, :, :] + strain[..., 1, :, :, :] + strain[..., 2, :, :, :]
    normal = stress_now[..., :3, :, :, :] + time_step * (
        lame_lambda * trace[..., None, :, :, :] + 2.0 * shear_modulus * strain[..., :3, :, :, :]
    )
    shear = stress_now[..., 3:, :, :, :] + time_step * shear_modulus * strain[..., 3:, :, :, :]
    return jnp.concatenate([normal, shear], axis=-4)


def image_terms(strain_fwd, stress_adj, accel_fwd, velocity_adj):
    trace_fwd = (
        strain_fwd[..., 0, :, :, :] + strain_fwd[..., 1, :, :, :] + strain_fwd[..., 2, :, :, :]
    )
    trace_adj = (
        stress_adj[..., 0, :, :, :] + stress_adj[..., 1, :, :, :] + stress_adj[..., 2, :, :, :]
    )
    grad_lambda = -time_step * trace_fwd * trace_adj
    grad_shear = -time_step * jnp.sum(strain_fwd * stress_adj, axis=-4)
    grad_density = -time_step * jnp.sum(accel_fwd * velocity_adj, axis=-4)
    return jnp.stack([grad_lambda, grad_shear, grad_density], axis=-4)


def localize(cell_index, x_start, y_start, tile_x, tile_y, width_y, depth_cells):
    plane_size = width_y * depth_cells
    global_x = cell_index // plane_size
    remainder = cell_index % plane_size
    global_y = remainder // depth_cells
    global_z = remainder % depth_cells
    local_x = global_x - x_start
    local_y = global_y - y_start
    inside = (local_x >= 0) & (local_x < tile_x) & (local_y >= 0) & (local_y < tile_y)
    return jnp.where(
        inside, (local_x * tile_y + local_y) * depth_cells + global_z, tile_x * tile_y * depth_cells
    )


def inject(fields, where_cells, amounts):
    field_count, tile_x, tile_y, depth_cells = fields.shape
    column_count = tile_x * tile_y
    column = where_cells // depth_cells
    depth = where_cells % depth_cells
    column_hot = (column[:, None] == lax.broadcasted_iota(jnp.int32, (1, column_count), 1)).astype(
        jnp.float32
    )
    depth_hot = (depth[:, None] == lax.broadcasted_iota(jnp.int32, (1, depth_cells), 1)).astype(
        jnp.float32
    ) * amounts[:, None]
    added = jnp.dot(
        column_hot.T, depth_hot, precision=lax.Precision.HIGHEST, preferred_element_type=jnp.float32
    )
    added = added.reshape(1, tile_x, tile_y, depth_cells)
    return jnp.concatenate([fields[:3], fields[3:6] + added, fields[6:]], axis=0)


def body(
    forward_fields,
    adjoint_fields,
    lame_lambda,
    shear_modulus,
    density,
    source_cell,
    source_amp,
    receiver_cell,
    residual_amp,
):
    shot_count, field_count, tile_x, tile_y, depth_cells = forward_fields.shape
    width_y = tile_y * lax.axis_size("ty")
    x_start = lax.axis_index("tx") * tile_x
    y_start = lax.axis_index("ty") * tile_y
    source_local = localize(source_cell, x_start, y_start, tile_x, tile_y, width_y, depth_cells)
    receiver_local = localize(receiver_cell, x_start, y_start, tile_x, tile_y, width_y, depth_cells)
    forward = jax.vmap(inject)(forward_fields, source_local[:, None], source_amp[:, None])
    adjoint = jax.vmap(inject)(adjoint_fields, receiver_local, residual_amp)
    wavefields = jnp.concatenate([forward, adjoint], axis=0)
    buoyancy = 1.0 / density
    margin = (2, 2, 0)
    stress_ext = extended(wavefields[:, 3:], (("tx", 2), ("ty", 3)), 2)
    acceleration = accelerate(stress_ext, buoyancy, margin, (0, 0, 0))
    velocity = wavefields[:, :3] + time_step * acceleration
    velocity_ext = extended(velocity, (("tx", 2), ("ty", 3)), 2)
    strain = strain_rates(velocity_ext, margin)
    stress = new_stress(wavefields[:, 3:], strain, lame_lambda, shear_modulus)
    local_terms = jnp.sum(
        image_terms(
            strain[:shot_count],
            stress[shot_count:],
            acceleration[:shot_count],
            velocity[shot_count:],
        ),
        axis=0,
    )
    gradient = lax.psum(local_terms, "shot")
    stepped = jnp.concatenate([velocity, stress], axis=1)
    return (stepped[:shot_count], stepped[shot_count:], gradient)


def solution(mesh):
    return jax.shard_map(
        body,
        mesh=mesh,
        in_specs=(
            P("shot", None, "tx", "ty", None),
            P("shot", None, "tx", "ty", None),
            P("tx", "ty", None),
            P("tx", "ty", None),
            P("tx", "ty", None),
            P("shot"),
            P("shot"),
            P("shot", None),
            P("shot", None),
        ),
        out_specs=(
            P("shot", None, "tx", "ty", None),
            P("shot", None, "tx", "ty", None),
            P(None, "tx", "ty", None),
        ),
        check_vma=False,
    )
```

profile of v0, /device:TPU:9, one launch (start us, length us, event | category | flops | bytes accessed | tf_op | source)
XLA Modules:
  0.0 91.3 jit_solution(17876590053302734075)
XLA Ops:
  8.6 0.7 and_select_fusion
  9.4 0.1 reshape.277
  9.5 0.1 broadcast_multiply_fusion.2
  9.6 1.1 %fusion.53 = f32[16,16,128]{2,1,0:T(8,128)S(1)} fusion(s32[16,16]{1,0:T(8,128)S(1)} %multiply_add_fusion, s32[256]{0:T(256)S(1)} %bitcast.100, f32[256]{0:T(256)} %bitcast.101, s32[256]{0:T(256)S(1)} %bitcast.99), kind=kOutput, calls=%fused_computation.112 | convolution fusion | flops 100794368 | bytes 135168 | tf_op jit(solution)/shard_map/vmap()/dot_general | solution.py:161
  10.6 1.8 %fusion.168 = (f32[1,3,16,16,128]{4,3,2,1,0:T(8,128)S(1)}, f32[1,3,16,16,128]{4,3,2,1,0:T(8,128)S(1)}, f32[1,3,16,16,128]{4,3,2,1,0:T(8,128)S(1)}, f32[1,3,16,16...) fusion(f32[1,9,16,16,128]{4,3,2,1,0:T(8,128)} %param.9, ...), kind=kLoop, calls=%fused_computation.264 | loop fusion | flops 196608 | bytes 4980736 | tf_op jit(solution)/shard_map/vmap()/slice | solution.py:165
  12.5 3.2 %collective-permute-start = (f32[2,6,2,16,128]{4,3,2,1,0:T(8,128)S(1)}, f32[2,6,2,16,128]{4,3,2,1,0:T(8,128)S(1)}, u32[]{:S(2)}, u32[]{:S(2)}) collective-permute-start(f32[2,6,2,16,128]{4,3,2,1,0:T(8,128)S(1)} %get-tuple-element.25), channel_id=1, source_target_pairs={{0,8},{1,9},{2,10},{3,11},{4,12},{5,13},{6,14},{7,15},{16,24},{17,... | collective-permute-start | bytes 589832 | tf_op jit(solution)/shard_map/ppermute | solution.py:18
  15.6 1.3 %collective-permute-start.1 = (f32[2,6,2,16,128]{4,3,2,1,0:T(8,128)S(1)}, f32[2,6,2,16,128]{4,3,2,1,0:T(8,128)S(1)}, u32[]{:S(2)}, u32[]{:S(2)}) collective-permute-start(f32[2,6,2,16,128]{4,3,2,1,0:T(8,128)S(1)} %get-tuple-element.26), channel_id=1, source_target_pairs={{8,0},{9,1},{10,2},{11,3},{12,4},{13,5},{14,6},{15,7},{24,16},{25,... | collective-permute-start | bytes 589832 | tf_op jit(solution)/shard_map/ppermute | solution.py:19
  16.9 0.2 maximum_maximum_fusion
  17.1 0.1 slice.469
  17.2 1.9 %collective-permute-done = f32[2,6,2,16,128]{4,3,2,1,0:T(8,128)S(1)} collective-permute-done((f32[2,6,2,16,128]{4,3,2,1,0:T(8,128)S(1)}, f32[2,6,2,16,128]{4,3,2,1,0:T(8,128)S(1)}, u32[]{:S(2)}, u32[]{:S(2)}) %collective-permute-start) | collective-permute-done | bytes 196640 | tf_op jit(solution)/shard_map/ppermute | solution.py:18
  19.2 3.8 %collective-permute-done.1 = f32[2,6,2,16,128]{4,3,2,1,0:T(8,128)S(1)} collective-permute-done((f32[2,6,2,16,128]{4,3,2,1,0:T(8,128)S(1)}, f32[2,6,2,16,128]{4,3,2,1,0:T(8,128)S(1)}, u32[]{:S(2)}, u32[]{:S(2)}) %collective-permute-start.1) | collective-permute-done | bytes 196640 | tf_op jit(solution)/shard_map/ppermute | solution.py:19
  23.0 0.2 pad_maximum_fusion.6
  23.1 3.1 %collective-permute-start.2 = (f32[2,6,20,2,128]{4,3,2,1,0:T(2,128)S(1)}, f32[2,6,20,2,128]{4,3,2,1,0:T(2,128)S(1)}, u32[]{:S(2)}, u32[]{:S(2)}) collective-permute-start(f32[2,6,20,2,128]{4,3,2,1,0:T(2,128)S(1)} %get-tuple-element.27), channel_id=1, source_target_pairs={{0,1},{1,2},{2,3},{3,4},{4,5},{5,6},{6,7},{8,9},{9,10},{10,11},{11... | collective-permute-start | bytes 737288 | tf_op jit(solution)/shard_map/ppermute | solution.py:18
  26.3 3.1 %collective-permute-start.3 = (f32[2,6,20,2,128]{4,3,2,1,0:T(2,128)S(1)}, f32[2,6,20,2,128]{4,3,2,1,0:T(2,128)S(1)}, u32[]{:S(2)}, u32[]{:S(2)}) collective-permute-start(f32[2,6,20,2,128]{4,3,2,1,0:T(2,128)S(1)} %get-tuple-element.28), channel_id=1, source_target_pairs={{1,0},{2,1},{3,2},{4,3},{5,4},{6,5},{7,6},{9,8},{10,9},{11,10},{12... | collective-permute-start | bytes 737288 | tf_op jit(solution)/shard_map/ppermute | solution.py:19
  29.4 2.1 %collective-permute-done.2 = f32[2,6,20,2,128]{4,3,2,1,0:T(2,128)S(1)} collective-permute-done((f32[2,6,20,2,128]{4,3,2,1,0:T(2,128)S(1)}, f32[2,6,20,2,128]{4,3,2,1,0:T(2,128)S(1)}, u32[]{:S(2)}, u32[]{:S(2)}) %collective-permute-start.2) | collective-permute-done | bytes 245792 | tf_op jit(solution)/shard_map/ppermute | solution.py:18
  31.5 7.6 %collective-permute-done.3 = f32[2,6,20,2,128]{4,3,2,1,0:T(2,128)S(1)} collective-permute-done((f32[2,6,20,2,128]{4,3,2,1,0:T(2,128)S(1)}, f32[2,6,20,2,128]{4,3,2,1,0:T(2,128)S(1)}, u32[]{:S(2)}, u32[]{:S(2)}) %collective-permute-start.3) | collective-permute-done | bytes 245792 | tf_op jit(solution)/shard_map/ppermute | solution.py:19
  39.1 0.4 pad_maximum_fusion
  39.5 0.2 slice_bitcast_fusion.10
  39.7 0.5 fusion.4
  40.2 0.5 fusion.2
  40.7 0.5 fusion.3
  41.1 0.1 copy_add_fusion
  41.3 0.1 maximum_multiply_fusion
  41.4 1.3 %collective-permute-start.4 = (f32[2,3,2,16,128]{4,3,2,0,1:T(8,128)S(1)}, f32[2,3,2,16,128]{4,3,2,0,1:T(8,128)S(1)}, u32[]{:S(2)}, u32[]{:S(2)}) collective-permute-start(f32[2,3,2,16,128]{4,3,2,0,1:T(8,128)S(1)} %get-tuple-element.40), channel_id=1, source_target_pairs={{0,8},{1,9},{2,10},{3,11},{4,12},{5,13},{6,14},{7,15},{16,24},{17,... | collective-permute-start | bytes 294920 | tf_op jit(solution)/shard_map/ppermute | solution.py:18
  42.7 1.3 %collective-permute-start.5 = (f32[2,3,2,16,128]{4,3,2,0,1:T(8,128)S(1)}, f32[2,3,2,16,128]{4,3,2,0,1:T(8,128)S(1)}, u32[]{:S(2)}, u32[]{:S(2)}) collective-permute-start(f32[2,3,2,16,128]{4,3,2,0,1:T(8,128)S(1)} %get-tuple-element.41), channel_id=1, source_target_pairs={{8,0},{9,1},{10,2},{11,3},{12,4},{13,5},{14,6},{15,7},{24,16},{25,... | collective-permute-start | bytes 294920 | tf_op jit(solution)/shard_map/ppermute | solution.py:19
  44.1 0.4 collective-permute-done.4
  44.5 3.6 %collective-permute-done.5 = f32[2,3,2,16,128]{4,3,2,0,1:T(8,128)S(1)} collective-permute-done((f32[2,3,2,16,128]{4,3,2,0,1:T(8,128)S(1)}, f32[2,3,2,16,128]{4,3,2,0,1:T(8,128)S(1)}, u32[]{:S(2)}, u32[]{:S(2)}) %collective-permute-start.5) | collective-permute-done | bytes 98336 | tf_op jit(solution)/shard_map/ppermute | solution.py:19
  48.1 0.1 pad_maximum_fusion.9
  48.1 1.9 %collective-permute-start.6 = (f32[2,3,20,2,128]{4,3,2,0,1:T(2,128)S(1)}, f32[2,3,20,2,128]{4,3,2,0,1:T(2,128)S(1)}, u32[]{:S(2)}, u32[]{:S(2)}) collective-permute-start(f32[2,3,20,2,128]{4,3,2,0,1:T(2,128)S(1)} %get-tuple-element.38), channel_id=1, source_target_pairs={{0,1},{1,2},{2,3},{3,4},{4,5},{5,6},{6,7},{8,9},{9,10},{10,11},{11... | collective-permute-start | bytes 368648 | tf_op jit(solution)/shard_map/ppermute | solution.py:18
  50.1 4.3 %collective-permute-start.7 = (f32[2,3,20,2,128]{4,3,2,0,1:T(2,128)S(1)}, f32[2,3,20,2,128]{4,3,2,0,1:T(2,128)S(1)}, u32[]{:S(2)}, u32[]{:S(2)}) collective-permute-start(f32[2,3,20,2,128]{4,3,2,0,1:T(2,128)S(1)} %get-tuple-element.39), channel_id=1, source_target_pairs={{1,0},{2,1},{3,2},{4,3},{5,4},{6,5},{7,6},{9,8},{10,9},{11,10},{12... | collective-permute-start | bytes 368648 | tf_op jit(solution)/shard_map/ppermute | solution.py:19
  54.4 0.3 collective-permute-done.6
  54.7 4.0 %collective-permute-done.7 = f32[2,3,20,2,128]{4,3,2,0,1:T(2,128)S(1)} collective-permute-done((f32[2,3,20,2,128]{4,3,2,0,1:T(2,128)S(1)}, f32[2,3,20,2,128]{4,3,2,0,1:T(2,128)S(1)}, u32[]{:S(2)}, u32[]{:S(2)}) %collective-permute-start.7) | collective-permute-done | bytes 122912 | tf_op jit(solution)/shard_map/ppermute | solution.py:19
  58.6 0.2 pad_maximum_fusion.2
  58.9 0.1 slice_bitcast_fusion.4
  59.1 0.1 bitcast_dynamic-update-slice_fusion.1
  59.2 0.4 bitcast_dynamic-update-slice_fusion
  59.6 0.4 copy-done.1
  60.0 0.2 slice_add_fusion
  60.3 0.2 constant_dynamic-update-slice_fusion.2
  60.5 0.4 constant_dynamic-update-slice_fusion.1
  60.9 0.4 constant_dynamic-update-slice_fusion
  61.3 0.1 fusion.9
  61.4 0.1 fusion.6
  61.5 0.8 maximum_bitcast_fusion
  62.3 0.2 pad_maximum_fusion.1
  62.5 1.6 %slice_bitcast_fusion = (f32[1,9,16,16,128]{4,3,2,1,0:T(8,128)}, f32[1,9,16,16,128]{4,3,2,1,0:T(8,128)}) fusion(f32[2,9,16,16,128]{4,3,2,0,1:T(8,128)S(1)} %pad_maximum_fusion.1), kind=kLoop, calls=%fused_computation.4 | loop fusion | bytes 4718592
  64.0 18.6 %all-reduce.2.cloned.1.call-done = f32[3,16,16,128]{3,2,1,0:T(8,128)} async-done(((f32[3,16,16,128]{3,2,1,0:T(8,128)}), f32[3,16,16,128]{3,2,1,0:T(8,128)}) %all-reduce.2.cloned.1.call-update) | async-done | bytes 393232 | tf_op jit(solution)/shard_map/psum | solution.py:205
  82.7 1.8 %copy.46 = f32[3,16,16,128]{3,2,1,0:T(8,128)} copy(f32[3,16,16,128]{3,2,1,0:T(8,128)} %all-reduce.2.cloned.1.call-done) | data formatting | bytes 786432
  (21 shorter events, 0.4 us)
Async XLA Ops:
  7.2 75.5 %all-reduce.2.cloned.1.call-start = ((), (), s32[]{:S(2)}) async-start(), calls=%async_computation | async-start | bytes 786432 | tf_op jit(solution)/shard_map/psum | solution.py:205
  12.5 6.7 %collective-permute-start = (f32[2,6,2,16,128]{4,3,2,1,0:T(8,128)S(1)}, f32[2,6,2,16,128]{4,3,2,1,0:T(8,128)S(1)}, u32[]{:S(2)}, u32[]{:S(2)}) collective-permute-start(f32[2,6,2,16,128]{4,3,2,1,0:T(8,128)S(1)} %get-tuple-element.25), channel_id=1, source_target_pairs={{0,8},{1,9},{2,10},{3,11},{4,12},{5,13},{6,14},{7,15},{16,24},{17,... | collective-permute-start | bytes 589832 | tf_op jit(solution)/shard_map/ppermute | solution.py:18
  15.6 7.3 %collective-permute-start.1 = (f32[2,6,2,16,128]{4,3,2,1,0:T(8,128)S(1)}, f32[2,6,2,16,128]{4,3,2,1,0:T(8,128)S(1)}, u32[]{:S(2)}, u32[]{:S(2)}) collective-permute-start(f32[2,6,2,16,128]{4,3,2,1,0:T(8,128)S(1)} %get-tuple-element.26), channel_id=1, source_target_pairs={{8,0},{9,1},{10,2},{11,3},{12,4},{13,5},{14,6},{15,7},{24,16},{25,... | collective-permute-start | bytes 589832 | tf_op jit(solution)/shard_map/ppermute | solution.py:19
  17.2 12.1 %copy-start.2 = (f32[16,16,128]{2,1,0:T(8,128)S(1)}, f32[16,16,128]{2,1,0:T(8,128)}, u32[]{:S(2)}) copy-start(f32[16,16,128]{2,1,0:T(8,128)} %param.13) | copy-start | bytes 393220
  17.2 12.2 %copy-start = (f32[16,16,128]{2,1,0:T(8,128)S(1)}, f32[16,16,128]{2,1,0:T(8,128)}, u32[]{:S(2)}) copy-start(f32[16,16,128]{2,1,0:T(8,128)} %param.12) | copy-start | bytes 393220
  23.1 8.4 %collective-permute-start.2 = (f32[2,6,20,2,128]{4,3,2,1,0:T(2,128)S(1)}, f32[2,6,20,2,128]{4,3,2,1,0:T(2,128)S(1)}, u32[]{:S(2)}, u32[]{:S(2)}) collective-permute-start(f32[2,6,20,2,128]{4,3,2,1,0:T(2,128)S(1)} %get-tuple-element.27), channel_id=1, source_target_pairs={{0,1},{1,2},{2,3},{3,4},{4,5},{5,6},{6,7},{8,9},{9,10},{10,11},{11... | collective-permute-start | bytes 737288 | tf_op jit(solution)/shard_map/ppermute | solution.py:18
  26.3 12.8 %collective-permute-start.3 = (f32[2,6,20,2,128]{4,3,2,1,0:T(2,128)S(1)}, f32[2,6,20,2,128]{4,3,2,1,0:T(2,128)S(1)}, u32[]{:S(2)}, u32[]{:S(2)}) collective-permute-start(f32[2,6,20,2,128]{4,3,2,1,0:T(2,128)S(1)} %get-tuple-element.28), channel_id=1, source_target_pairs={{1,0},{2,1},{3,2},{4,3},{5,4},{6,5},{7,6},{9,8},{10,9},{11,10},{12... | collective-permute-start | bytes 737288 | tf_op jit(solution)/shard_map/ppermute | solution.py:19
  41.4 3.1 %collective-permute-start.4 = (f32[2,3,2,16,128]{4,3,2,0,1:T(8,128)S(1)}, f32[2,3,2,16,128]{4,3,2,0,1:T(8,128)S(1)}, u32[]{:S(2)}, u32[]{:S(2)}) collective-permute-start(f32[2,3,2,16,128]{4,3,2,0,1:T(8,128)S(1)} %get-tuple-element.40), channel_id=1, source_target_pairs={{0,8},{1,9},{2,10},{3,11},{4,12},{5,13},{6,14},{7,15},{16,24},{17,... | collective-permute-start | bytes 294920 | tf_op jit(solution)/shard_map/ppermute | solution.py:18
  42.7 5.4 %collective-permute-start.5 = (f32[2,3,2,16,128]{4,3,2,0,1:T(8,128)S(1)}, f32[2,3,2,16,128]{4,3,2,0,1:T(8,128)S(1)}, u32[]{:S(2)}, u32[]{:S(2)}) collective-permute-start(f32[2,3,2,16,128]{4,3,2,0,1:T(8,128)S(1)} %get-tuple-element.41), channel_id=1, source_target_pairs={{8,0},{9,1},{10,2},{11,3},{12,4},{13,5},{14,6},{15,7},{24,16},{25,... | collective-permute-start | bytes 294920 | tf_op jit(solution)/shard_map/ppermute | solution.py:19
  48.1 6.5 %collective-permute-start.6 = (f32[2,3,20,2,128]{4,3,2,0,1:T(2,128)S(1)}, f32[2,3,20,2,128]{4,3,2,0,1:T(2,128)S(1)}, u32[]{:S(2)}, u32[]{:S(2)}) collective-permute-start(f32[2,3,20,2,128]{4,3,2,0,1:T(2,128)S(1)} %get-tuple-element.38), channel_id=1, source_target_pairs={{0,1},{1,2},{2,3},{3,4},{4,5},{5,6},{6,7},{8,9},{9,10},{10,11},{11... | collective-permute-start | bytes 368648 | tf_op jit(solution)/shard_map/ppermute | solution.py:18
  50.1 8.6 %collective-permute-start.7 = (f32[2,3,20,2,128]{4,3,2,0,1:T(2,128)S(1)}, f32[2,3,20,2,128]{4,3,2,0,1:T(2,128)S(1)}, u32[]{:S(2)}, u32[]{:S(2)}) collective-permute-start(f32[2,3,20,2,128]{4,3,2,0,1:T(2,128)S(1)} %get-tuple-element.39), channel_id=1, source_target_pairs={{1,0},{2,1},{3,2},{4,3},{5,4},{6,5},{7,6},{9,8},{10,9},{11,10},{12... | collective-permute-start | bytes 368648 | tf_op jit(solution)/shard_map/ppermute | solution.py:19
  59.0 0.9 copy-start.1
Sparse Core Ops, SparseCore 0:
  62.4 20.1 all-reduce.1
where the time goes:
time: 92.5 us; the launch traced here: 91.3 us
  waiting for transfers between devices  42.3 us (46%)
  starting transfers between devices  19.4 us (21%)
  between operations  15.8 us (17%)
  other arithmetic  5.89 us (6%)
  local copies, waits for them, and re-layouts  4.22 us (5%)
  matrix products  3.62 us (4%)
    ppermute x4, waiting for transfers between devices, extended(): after = lax.ppermute(initial, axis, down)  18.9 us
    psum x1, waiting for transfers between devices, body(): gradient = lax.psum(local_terms, 'shot')  18.6 us
    ppermute x4, starting transfers between devices, extended(): after = lax.ppermute(initial, axis, down)  9.91 us
    ppermute x4, starting transfers between devices, extended(): before = lax.ppermute(last, axis, up)  9.49 us
    ppermute x4, waiting for transfers between devices, extended(): before = lax.ppermute(last, axis, up)  4.76 us
    unnamed x8, local copies, waits for them, and re-layouts  3.74 us
    dot_general x6, matrix products, derive(): jnp.einsum('...k,ki->...i', core, depth_table(core.shape[-1], upward), pr...  2.57 us
  transfers between devices with their start and end apart: 9, of which 9 were waited for; matrix products, arithmetic and copies ran while one was open for 2% of the time, Pallas kernels for 0%

commit v1 on v0

v1 whole, which is shorter than its diff:
```python
import functools

import jax
import jax.numpy as jnp
from jax import lax
from jax.experimental import pallas as pl
from jax.experimental.pallas import tpu as pltpu
from jax.sharding import PartitionSpec as P

near = 9.0 / 8.0
far = -1.0 / 24.0
time_step = 0.15

LAYERS = 2
ROWS = 8
SLOTS = 5

STRESS_ALONG = ((0, 3, 4), (1, 3, 5))
ACCEL_OF = ((0, 1, 2), (1, 0, 2))
VELOCITY_ALONG = ((0, 1, 2), (1, 0, 2))
STRAIN_OF = ((0, 3, 4), (1, 3, 5))

vmem = pl.BlockSpec(memory_space=pltpu.VMEM)
smem = pl.BlockSpec(memory_space=pltpu.SMEM)
anywhere = pl.BlockSpec(memory_space=pl.ANY)
params = pltpu.CompilerParams(vmem_limit_bytes=24 * 1024 * 1024)


def links_of(sizes):
    return [
        (name, dim, first)
        for dim, name in enumerate(("tx", "ty"))
        for first in (0, 1)
        if first + 1 < sizes[name]
    ]


def swap(value, axis, first):
    pairs = [(i, i + 1) for i in range(first, lax.axis_size(axis) - 1, 2)]
    return lax.ppermute(value, axis, pairs + [(j, i) for i, j in pairs])


def is_lower(axis, first):
    return lax.axis_index(axis) % 2 == first


def has_peer(axis, first):
    index = lax.axis_index(axis)
    partner = jnp.where(is_lower(axis, first), index + 1, index - 1)
    return (partner >= 0) & (partner < lax.axis_size(axis))


def pack_kernel(links, *refs):
    fields = refs[:2]
    sends = refs[2 : 2 + len(links)]
    edge, sems = refs[2 + len(links) :]
    _, tile_x, tile_y, _ = fields[0].shape
    copies = []

    def copy(source, target):
        started = pltpu.make_async_copy(source, target, sems.at[len(copies)])
        started.start()
        copies.append(started)

    for wave in range(2):
        for slot, part in enumerate(STRESS_ALONG[1]):
            for side, row in enumerate((0, tile_y - 8)):
                copy(fields[wave].at[3 + part, :, pl.ds(row, 8), :], edge.at[wave, slot, side])
    for (axis, dim, first), send in zip(links, sends):
        if dim == 1:
            continue
        lower = is_lower(axis, first)
        normal, one, two = (3 + part for part in STRESS_ALONG[0])
        last = tile_x - 1
        for wave in range(2):
            for slot, (upper_part, upper_layer, lower_part, lower_layer) in enumerate((
                (normal, 0, normal, last),
                (normal, 1, one, last - 1),
                (one, 0, one, last),
                (two, 0, two, last - 1),
                (two, 1, two, last),
            )):
                part = jnp.where(lower, lower_part, upper_part)
                layer = jnp.where(lower, lower_layer, upper_layer)
                copy(fields[wave].at[part, layer], send.at[wave, slot])
    for started in copies:
        started.wait()
    rows = edge.reshape(2, 3, 2, tile_x * 8, edge.shape[-1])

    def row_of(wave, part, row):
        side, at = (0, row) if row < 8 else (1, row - (tile_y - 8))
        return rows[wave, part, side, pl.ds(at, tile_x, stride=8), :]

    last = tile_y - 1
    for (axis, dim, first), send in zip(links, sends):
        if dim == 0:
            continue
        lower = is_lower(axis, first)
        for wave in range(2):
            for slot, (upper_part, upper_row, lower_part, lower_row) in enumerate((
                (0, 0, 0, last),
                (0, 1, 1, last - 1),
                (1, 0, 1, last),
                (2, 0, 2, last - 1),
                (2, 1, 2, last),
            )):
                send[wave, slot] = jnp.where(
                    lower, row_of(wave, lower_part, lower_row), row_of(wave, upper_part, upper_row)
                )


def column_ids(tile_x, tile_y, width_y, lanes):
    x_start = lax.axis_index("tx") * tile_x
    y_start = lax.axis_index("ty") * tile_y

    def column(x, y):
        inside = (y >= 0) & (y < width_y)
        return jnp.where(inside, x * width_y + y, -1)

    def iota(shape, dim):
        return lax.broadcasted_iota(jnp.int32, shape, dim)

    shape = (tile_x, tile_y, lanes)
    tile = column(x_start + iota(shape, 0), y_start + iota(shape, 1))
    shape = (3, tile_y, lanes)
    layer = iota(shape, 0)
    along_x = column(
        x_start + jnp.where(layer == 0, -1, tile_x - 1 + layer), y_start + iota(shape, 1)
    )
    shape = (3, tile_x, lanes)
    layer = iota(shape, 0)
    along_y = column(
        x_start + iota(shape, 1), y_start + jnp.where(layer == 0, -1, tile_y - 1 + layer)
    )
    return jnp.concatenate([part.reshape(-1, lanes) for part in (tile, along_x, along_y)], axis=0)


def differ(zero, one, two, minus):
    return near * (one - zero) + far * (two - minus)


def along_x(ref, part, x, tile_y, upward):
    def at(offset):
        return ref[part, x + (LAYERS + offset), pl.ds(ROWS, tile_y), :]

    return differ(at(0), at(1), at(2), at(-1)) if upward else differ(at(-1), at(0), at(1), at(-2))


def along_y(ref, part, x, tile_y, upward):
    def at(offset):
        return ref[part, x + LAYERS, pl.ds(ROWS + offset, tile_y), :]

    return differ(at(0), at(1), at(2), at(-1)) if upward else differ(at(-1), at(0), at(1), at(-2))


def along_z(ref, part, x, tile_y, upward):
    value = ref[part, x + LAYERS, pl.ds(ROWS, tile_y), :]
    depth = value.shape[-1]
    lane = lax.broadcasted_iota(jnp.int32, value.shape, 1)

    def at(offset):
        if offset == 0:
            return value
        moved = pltpu.roll(value, (-offset) % depth, 1)
        inside = lane < depth - offset if offset > 0 else lane >= -offset
        return jnp.where(inside, moved, 0.0)

    return differ(at(0), at(1), at(2), at(-1)) if upward else differ(at(-1), at(0), at(1), at(-2))


def clear_rim(ref, tile_x, tile_y):
    parts, layers, rows, depth = ref.shape
    for part in range(parts):
        for layer in (*range(LAYERS), *range(LAYERS + tile_x, layers)):
            ref[part, layer] = jnp.zeros((rows, depth), jnp.float32)
        for row in (0, ROWS + tile_y):
            ref[part, pl.ds(LAYERS, tile_x), pl.ds(row, ROWS), :] = jnp.zeros(
                (tile_x, ROWS, depth), jnp.float32
            )


def velocity_kernel(
    width_y,
    source_cell,
    source_amp,
    receiver_cell,
    residual_amp,
    forward,
    adjoint,
    lame,
    shear,
    density,
    stress,
    velocity,
    accel,
    rim_added,
    buoyancy,
    scaled_lame,
    scaled_shear,
    added,
):
    _, tile_x, tile_y, depth = forward.shape
    receivers = receiver_cell.shape[-1]
    cells = tile_x * tile_y
    columns = column_ids(tile_x, tile_y, width_y, depth)
    lane = lax.broadcasted_iota(jnp.int32, columns.shape, 1)
    added[0] = jnp.where(columns * depth + lane == source_cell[0], source_amp[0], 0.0)
    where = receiver_cell[...]
    column = lax.div(where, depth)
    depth_of = where - column * depth
    columns = column_ids(tile_x, tile_y, width_y, receivers)
    column_hot = (columns == column).astype(jnp.float32)
    level = lax.broadcasted_iota(jnp.int32, (depth, receivers), 0)
    depth_hot = jnp.where(level == depth_of, residual_amp[...], 0.0)
    added[1] = lax.dot_general(
        column_hot,
        depth_hot,
        (((1,), (1,)), ((), ())),
        precision=lax.Precision.HIGHEST,
        preferred_element_type=jnp.float32,
    )
    for wave in range(2):
        for layer in range(3):
            rim_added[wave, 0, layer] = added[wave, pl.ds(cells + layer * tile_y, tile_y), :]
            rim_added[wave, 1, layer] = added[
                wave, pl.ds(cells + 3 * tile_y + layer * tile_x, tile_x), :
            ]
    clear_rim(stress, tile_x, tile_y)
    clear_rim(velocity, tile_x, tile_y)
    middle = pl.ds(ROWS, tile_y)

    def fill(x, carry):
        for wave, fields in enumerate((forward, adjoint)):
            extra = added[wave, pl.ds(pl.multiple_of(x * tile_y, 8), tile_y), :]
            for part in range(6):
                value = fields[3 + part, x]
                stress[6 * wave + part, x + LAYERS, middle, :] = (
                    value + extra if part < 3 else value
                )
        buoyancy[x] = 1.0 / density[x]
        scaled_lame[x] = time_step * lame[x]
        scaled_shear[x] = time_step * shear[x]
        return carry

    lax.fori_loop(0, tile_x, fill, 0)

    def layer(x, carry):
        light = buoyancy[x]
        for wave, fields in enumerate((forward, adjoint)):
            xx, yy, zz, xy, xz, yz = range(6 * wave, 6 * wave + 6)
            values = (
                along_x(stress, xx, x, tile_y, True)
                + along_y(stress, xy, x, tile_y, False)
                + along_z(stress, xz, x, tile_y, False),
                along_x(stress, xy, x, tile_y, False)
                + along_y(stress, yy, x, tile_y, True)
                + along_z(stress, yz, x, tile_y, False),
                along_x(stress, xz, x, tile_y, False)
                + along_y(stress, yz, x, tile_y, False)
                + along_z(stress, zz, x, tile_y, True),
            )
            for part, value in enumerate(values):
                value = light * value
                if wave == 0:
                    accel[part, x] = value
                velocity[3 * wave + part, x + LAYERS, middle, :] = (
                    fields[part, x] + time_step * value
                )
        return carry

    lax.fori_loop(0, tile_x, layer, 0)


def stress_halo_terms(links, received, rim_added, waves, add):
    for (axis, dim, first), halo in zip(links, received):
        part_n, part_a, part_b = ACCEL_OF[dim]
        lower = is_lower(axis, first)
        real = has_peer(axis, first)

        @pl.when(real & lower)
        def after():
            for wave in waves:
                n0 = halo[wave, 0] + rim_added[wave, dim, 1]
                n1 = halo[wave, 1] + rim_added[wave, dim, 2]
                add(wave, part_n, dim, -1, near * n0 + far * n1)
                add(wave, part_n, dim, -2, far * n0)
                add(wave, part_a, dim, -1, far * halo[wave, 2])
                add(wave, part_b, dim, -1, far * halo[wave, 3])

        @pl.when(real & jnp.logical_not(lower))
        def before():
            for wave in waves:
                n0 = halo[wave, 0] + rim_added[wave, dim, 0]
                add(wave, part_n, dim, 0, -far * n0)
                for part, slot in ((part_a, 1), (part_b, 3)):
                    outer, inner = halo[wave, slot], halo[wave, slot + 1]
                    add(wave, part, dim, 0, -near * inner - far * outer)
                    add(wave, part, dim, 1, -far * inner)


def velocity_halo_terms(links, received, add):
    for (axis, dim, first), halo in zip(links, received):
        part_n, part_a, part_b = STRAIN_OF[dim]
        lower = is_lower(axis, first)
        real = has_peer(axis, first)

        @pl.when(real & lower)
        def after():
            for wave in range(2):
                add(wave, part_n, dim, -1, far * halo[wave, 0])
                for part, slot in ((part_a, 1), (part_b, 3)):
                    inner, outer = halo[wave, slot], halo[wave, slot + 1]
                    add(wave, part, dim, -1, near * inner + far * outer)
                    add(wave, part, dim, -2, far * inner)

        @pl.when(real & jnp.logical_not(lower))
        def before():
            for wave in range(2):
                outer, inner = halo[wave, 0], halo[wave, 1]
                add(wave, part_n, dim, 0, -near * inner - far * outer)
                add(wave, part_n, dim, 1, -far * inner)
                add(wave, part_a, dim, 0, -far * halo[wave, 2])
                add(wave, part_b, dim, 0, -far * halo[wave, 3])


def face(ref, part, dim, index, padded):
    layers, rows, depth = ref.shape[1:]
    tile_x = layers - 2 * LAYERS if padded else layers
    tile_y = rows - 2 * ROWS if padded else rows
    if dim == 0:
        at = index % tile_x
        if padded:
            return ref.at[part, at + LAYERS, pl.ds(ROWS, tile_y), :]
        return ref.at[part, at]
    at = index % tile_y
    flat = ref.reshape(ref.shape[0], layers * rows, depth)
    begin = LAYERS * rows + ROWS + at if padded else at
    return flat.at[part, pl.ds(begin, tile_x, stride=rows), :]


def light_face(buoyancy, dim, index):
    layers, rows, depth = buoyancy.shape
    if dim == 0:
        return buoyancy[index % layers]
    return buoyancy.reshape(layers * rows, depth)[pl.ds(index % rows, layers, stride=rows), :]


def boundary_kernel(links, *refs):
    count = len(links)
    received = refs[:count]
    rim_added, buoyancy, _ = refs[count : count + 3]
    velocity = refs[count + 3]
    sends = refs[count + 4 :]

    def add(wave, part, dim, index, term):
        target = face(velocity, 3 * wave + part, dim, index, True)
        target[...] += time_step * light_face(buoyancy, dim, index) * term

    stress_halo_terms(links, received, rim_added, (0, 1), add)
    for (axis, dim, first), send in zip(links, sends):
        lower = is_lower(axis, first)
        n, a, b = VELOCITY_ALONG[dim]

        def put(plan):
            for wave in range(2):
                for slot, (part, index) in enumerate(plan):
                    send[wave, slot] = face(velocity, 3 * wave + part, dim, index, True)[...]

        @pl.when(lower)
        def up():
            put(((n, -2), (n, -1), (a, -1), (b, -1), (b, -1)))

        @pl.when(jnp.logical_not(lower))
        def down():
            put(((n, 0), (a, 0), (a, 1), (b, 0), (b, 1)))


def strain_kernel(links, *refs):
    count = len(links)
    received = refs[:count]
    rim_added, buoyancy, velocity, accel, strain, gradient, accel_now = refs[count:]
    tile_x, tile_y, _ = buoyancy.shape
    middle = pl.ds(ROWS, tile_y)
    accel_now[...] = accel[...]

    def add(wave, part, dim, index, term):
        target = face(accel_now, part, dim, index, False)
        target[...] += light_face(buoyancy, dim, index) * term

    stress_halo_terms(links, received, rim_added, (0,), add)

    def layer(x, carry):
        for wave in range(2):
            vx, vy, vz = range(3 * wave, 3 * wave + 3)
            values = (
                along_x(velocity, vx, x, tile_y, False),
                along_y(velocity, vy, x, tile_y, False),
                along_z(velocity, vz, x, tile_y, False),
                along_y(velocity, vx, x, tile_y, True) + along_x(velocity, vy, x, tile_y, True),
                along_z(velocity, vx, x, tile_y, True) + along_x(velocity, vz, x, tile_y, True),
                along_z(velocity, vy, x, tile_y, True) + along_y(velocity, vz, x, tile_y, True),
            )
            for part, value in enumerate(values):
                strain[6 * wave + part, x] = value
        total = sum(
            accel_now[part, x] * velocity[3 + part, x + LAYERS, middle, :] for part in range(3)
        )
        gradient[2, x] = -time_step * total
        return carry

    lax.fori_loop(0, tile_x, layer, 0)


def new_stress(strain, stress, scaled_lame, scaled_shear, wave, x, tile_y):
    lame, shear = scaled_lame[x], scaled_shear[x]
    strains = [strain[6 * wave + part, x] for part in range(6)]
    volume = lame * (strains[0] + strains[1] + strains[2])
    values = []
    for part in range(6):
        old = stress[6 * wave + part, x + LAYERS, pl.ds(ROWS, tile_y), :]
        if part < 3:
            values.append(old + (volume + 2.0 * shear * strains[part]))
        else:
            values.append(old + shear * strains[part])
    return strains, values


def gradient_kernel(links, *refs):
    count = len(links)
    received = refs[:count]
    stress, scaled_lame, scaled_shear, _, _, strain, gradient = refs[count:]
    tile_x, tile_y, _ = scaled_lame.shape

    def add(wave, part, dim, index, term):
        target = face(strain, 6 * wave + part, dim, index, False)
        target[...] += term

    velocity_halo_terms(links, received, add)

    def layer(x, carry):
        strains = [strain[part, x] for part in range(6)]
        _, values = new_stress(strain, stress, scaled_lame, scaled_shear, 1, x, tile_y)
        trace = strains[0] + strains[1] + strains[2]
        gradient[0, x] = -time_step * trace * (values[0] + values[1] + values[2])
        total = sum(left * right for left, right in zip(strains, values))
        gradient[1, x] = -time_step * total
        return carry

    lax.fori_loop(0, tile_x, layer, 0)


def output_kernel(velocity, strain, stress, scaled_lame, scaled_shear, forward, adjoint):
    layers, tile_y = forward.shape[1:3]
    begin = pl.program_id(0) * layers
    for at in range(layers):
        x = begin + at
        for wave, out in enumerate((forward, adjoint)):
            for part in range(3):
                out[part, at] = velocity[3 * wave + part, x + LAYERS, pl.ds(ROWS, tile_y), :]
            _, values = new_stress(strain, stress, scaled_lame, scaled_shear, wave, x, tile_y)
            for part in range(6):
                out[3 + part, at] = values[part]


def cost(flops, size):
    return pl.CostEstimate(flops=flops, bytes_accessed=size, transcendentals=0)


def body(
    forward_fields,
    adjoint_fields,
    lame_lambda,
    shear_modulus,
    density,
    source_cell,
    source_amp,
    receiver_cell,
    residual_amp,
):
    _, _, tile_x, tile_y, depth = forward_fields.shape
    forward = forward_fields.reshape(forward_fields.shape[1:])
    adjoint = adjoint_fields.reshape(adjoint_fields.shape[1:])
    sizes = {name: lax.axis_size(name) for name in ("tx", "ty")}
    width_y = tile_y * sizes["ty"]
    links = links_of(sizes)
    cells = tile_x * tile_y * depth
    rims = 3 * tile_x + 3 * tile_y

    def buffers(dim):
        return pltpu.VMEM((2, SLOTS, tile_y if dim == 0 else tile_x, depth), jnp.float32)

    def tile(*lead):
        return pltpu.VMEM((*lead, tile_x, tile_y, depth), jnp.float32)

    def padded(parts):
        return pltpu.VMEM(
            (parts, tile_x + 2 * LAYERS, tile_y + 2 * ROWS, depth), jnp.float32
        )

    def exchange(sends):
        return [swap(send, axis, first) for (axis, _, first), send in zip(links, sends)]

    send_shapes = [buffers(dim) for _, dim, _ in links]
    sends = pl.pallas_call(
        functools.partial(pack_kernel, links),
        out_shape=send_shapes,
        in_specs=[anywhere] * 2,
        out_specs=[vmem] * len(links),
        scratch_shapes=[
            pltpu.VMEM((2, 3, 2, tile_x, 8, depth), jnp.float32),
            pltpu.SemaphoreType.DMA((12 + 10 * len(links),)),
        ],
        compiler_params=params,
        cost_estimate=cost(0, 10 * 2 * tile_x * depth * 4),
        name="pack",
    )(forward, adjoint)
    halos = exchange(sends)

    stress, velocity, accel, rim_added, buoyancy, scaled_lame, scaled_shear = pl.pallas_call(
        functools.partial(velocity_kernel, width_y),
        out_shape=[
            padded(12),
            padded(6),
            tile(3),
            pltpu.VMEM((2, 2, 3, max(tile_x, tile_y), depth), jnp.float32),
            tile(),
            tile(),
            tile(),
        ],
        in_specs=[smem] * 2 + [vmem] * 7,
        out_specs=[vmem] * 7,
        scratch_shapes=[pltpu.VMEM((2, tile_x * tile_y + rims, depth), jnp.float32)],
        compiler_params=params,
        cost_estimate=cost(200 * cells, 18 * 4 * cells),
        name="velocity",
    )(
        source_cell,
        source_amp,
        receiver_cell,
        residual_amp,
        forward,
        adjoint,
        lame_lambda,
        shear_modulus,
        density,
    )

    count = len(links)
    velocity, *sends = pl.pallas_call(
        functools.partial(boundary_kernel, links),
        out_shape=[padded(6)] + send_shapes,
        in_specs=[vmem] * (count + 3),
        out_specs=[vmem] * (count + 1),
        input_output_aliases={count + 2: 0},
        compiler_params=params,
        cost_estimate=cost(cells, 10 * 2 * tile_x * depth * 4),
        name="boundary",
    )(*halos, rim_added, buoyancy, velocity)
    velocity_halos = exchange(sends)

    strain, gradient = pl.pallas_call(
        functools.partial(strain_kernel, links),
        out_shape=[tile(12), tile(3)],
        in_specs=[vmem] * (count + 4),
        out_specs=[vmem] * 2,
        scratch_shapes=[tile(3)],
        compiler_params=params,
        cost_estimate=cost(200 * cells, 18 * 4 * cells),
        name="strain",
    )(*halos, rim_added, buoyancy, velocity, accel)

    strain, gradient = pl.pallas_call(
        functools.partial(gradient_kernel, links),
        out_shape=[tile(12), tile(3)],
        in_specs=[vmem] * (count + 5),
        out_specs=[vmem] * 2,
        input_output_aliases={count + 3: 0, count + 4: 1},
        compiler_params=params,
        cost_estimate=cost(30 * cells, 2 * 4 * cells),
        name="gradient",
    )(*velocity_halos, stress, scaled_lame, scaled_shear, strain, gradient)
    other = lax.ppermute(gradient, "shot", [(0, 1), (1, 0)])

    step = 4 if tile_x % 4 == 0 else 1
    out_block = pl.BlockSpec((9, step, tile_y, depth), lambda i: (0, i, 0, 0))
    forward_next, adjoint_next = pl.pallas_call(
        output_kernel,
        grid=(tile_x // step,),
        out_shape=[jax.ShapeDtypeStruct(forward.shape, jnp.float32)] * 2,
        in_specs=[vmem] * 5,
        out_specs=[out_block] * 2,
        compiler_params=params,
        cost_estimate=cost(60 * cells, 18 * 4 * cells),
        name="outputs",
    )(velocity, strain, stress, scaled_lame, scaled_shear)
    return forward_next[None], adjoint_next[None], gradient + other


def solution(mesh):
    return jax.shard_map(
        body,
        mesh=mesh,
        in_specs=(
            P("shot", None, "tx", "ty", None),
            P("shot", None, "tx", "ty", None),
            P("tx", "ty", None),
            P("tx", "ty", None),
            P("tx", "ty", None),
            P("shot"),
            P("shot"),
            P("shot", None),
            P("shot", None),
        ),
        out_specs=(
            P("shot", None, "tx", "ty", None),
            P("shot", None, "tx", "ty", None),
            P(None, "tx", "ty", None),
        ),
        check_vma=False,
    )
```

time: 92.5 us -> 28.5 us (0.31); the launches traced: 91.3 us -> 28.3 us
  waiting for transfers between devices: 42.3 us -> 2.25 us
  between operations: 15.8 us -> 2.09 us
  Pallas kernels: 0 us -> 8.19 us
  starting transfers between devices: 19.4 us -> 12.4 us
  other arithmetic: 5.89 us -> 0.8 us
  matrix products: 3.62 us -> 0 us
  local copies, waits for them, and re-layouts: 4.22 us -> 2.56 us
    ppermute x8 -> x7, waiting for transfers between devices: 23.7 us -> 2.25 us  [the longest x6 2.24 us: swap(): return lax.ppermute(value, axis, pairs + [(j, i) for i, j in pairs])]
    psum x1 -> x0, waiting for transfers between devices: 18.6 us -> none  [body(): gradient = lax.psum(local_terms, 'shot')]
    pallas_call x0 -> x6, Pallas kernels: none -> 8.19 us  [the longest x1 2.86 us: body(): pl.pallas_call(functools.partial(velocity_kernel, width_y), out_shape=[pa...]
    ppermute x8 -> x7, starting transfers between devices: 19.4 us -> 12.4 us  [the longest x6 9.09 us: swap(): return lax.ppermute(value, axis, pairs + [(j, i) for i, j in pairs])]
    dot_general x7 -> x0, matrix products: 3.62 us -> none  [the longest x6 2.57 us: derive(): jnp.einsum('...k,ki->...i', core, depth_table(core.shape[-1], upward), pr...]
    slice x4 -> x0, other arithmetic: 2.08 us -> none  [the longest x1 1.79 us: inject(): fields[:3]]
    unnamed x8 -> x14, local copies, waits for them, and re-layouts: 3.74 us -> 2.56 us
    concatenate x4 -> x0, other arithmetic: 0.99 us -> none  [the longest x2 0.68 us: extended(): value = jnp.concatenate([before, value, after], axis=dim)]
  transfers between devices with their start and end apart: 9 -> 7, of which waited for: 9 -> 1; matrix products, arithmetic and copies ran while one was open for 2% -> 0% of each run, Pallas kernels for 0% -> 24%
where the time goes in v1:
time: 28.5 us; the launch traced here: 28.3 us
  starting transfers between devices  12.4 us (44%)
  Pallas kernels  8.19 us (29%)
  local copies, waits for them, and re-layouts  2.56 us (9%)
  waiting for transfers between devices  2.25 us (8%)
  between operations  2.09 us (7%)
  other arithmetic  0.8 us (3%)
    ppermute x6, starting transfers between devices, swap(): return lax.ppermute(value, axis, pairs + [(j, i) for i, j in pairs])  9.09 us
    ppermute x1, starting transfers between devices, body(): other = lax.ppermute(gradient, 'shot', [(0, 1), (1, 0)])  3.29 us
    pallas_call x1, Pallas kernels, body(): pl.pallas_call(functools.partial(velocity_kernel, width_y), out_shape=[pa...  2.86 us
    unnamed x14, local copies, waits for them, and re-layouts  2.56 us
    ppermute x6, waiting for transfers between devices, swap(): return lax.ppermute(value, axis, pairs + [(j, i) for i, j in pairs])  2.24 us
    pallas_call x1, Pallas kernels, body(): pl.pallas_call(output_kernel, grid=(tile_x // step,), out_shape=[jax.Shap...  1.98 us
    pallas_call x1, Pallas kernels, body(): pl.pallas_call(functools.partial(strain_kernel, links), out_shape=[tile(1...  1.9 us
    add x1, other arithmetic, body(): return (forward_next[None], adjoint_next[None], gradient + other)  0.8 us
  transfers between devices with their start and end apart: 7, of which 1 were waited for; matrix products, arithmetic and copies ran while one was open for 0% of the time, Pallas kernels for 24%

profile of v1, /device:TPU:9, one launch (start us, length us, event | category | flops | bytes accessed | tf_op | source)
XLA Modules:
  0.0 28.3 jit_solution(18128804890523121754)
XLA Ops:
  0.6 0.0 copy-start.6
  0.6 0.0 copy-start.5
  0.7 0.0 copy-start
  0.7 1.3 %copy-done = f32[1,9,16,16,128]{4,3,2,1,0:T(8,128)S(1)} copy-done((f32[1,9,16,16,128]{4,3,2,1,0:T(8,128)S(1)}, f32[1,9,16,16,128]{4,3,2,1,0:T(8,128)}, u32[]{:S(2)}) %copy-start) | copy-done | bytes 1179672
  1.9 0.0 copy-start.1
  1.9 1.3 %copy-done.1 = f32[1,9,16,16,128]{4,3,2,1,0:T(8,128)S(1)} copy-done((f32[1,9,16,16,128]{4,3,2,1,0:T(8,128)S(1)}, f32[1,9,16,16,128]{4,3,2,1,0:T(8,128)}, u32[]{:S(2)}) %copy-start.1) | copy-done | bytes 1179672
  3.2 0.0 copy-start.2
  3.2 0.0 copy-start.3
  3.2 0.0 copy-start.4
  3.2 0.6 %pack.1 = (f32[2,5,16,128]{3,2,1,0:T(8,128)S(1)}, f32[2,5,16,128]{3,2,1,0:T(8,128)S(1)}, f32[2,5,16,128]{3,2,1,0:T(8,128)S(1)}) custom-call(f32[9,16,16,128]{3,2,1,0:T(8,128)S(1)} %bitcast.4, f32[9,16,16,128]{3,2,1,0:T(8,128)S(1)} %bitcast.6), custom_call_target="tpu_custom_call" | custom-call | bytes 163840 | tf_op jit(solution)/shard_map/pack/pallas_call | solution.py:504
  3.9 1.3 %collective-permute-start = (f32[2,5,16,128]{3,2,1,0:T(8,128)S(1)}, f32[2,5,16,128]{3,2,1,0:T(8,128)S(1)}, u32[]{:S(2)}, u32[]{:S(2)}) collective-permute-start(f32[2,5,16,128]{3,2,1,0:T(8,128)S(1)} %get-tuple-element.23), channel_id=1, source_target_pairs={{0,8},{8,0},{1,9},{9,1},{2,10},{10,2},{3,11},{11,3},{4,12},{12,4},... | collective-permute-start | bytes 245768 | tf_op jit(solution)/shard_map/ppermute | solution.py:40
  5.2 1.2 %collective-permute-start.1 = (f32[2,5,16,128]{3,2,1,0:T(8,128)S(1)}, f32[2,5,16,128]{3,2,1,0:T(8,128)S(1)}, u32[]{:S(2)}, u32[]{:S(2)}) collective-permute-start(f32[2,5,16,128]{3,2,1,0:T(8,128)S(1)} %get-tuple-element.24), channel_id=1, source_target_pairs={{0,1},{2,3},{4,5},{6,7},{1,0},{3,2},{5,4},{7,6},{8,9},{10,11},{12,... | collective-permute-start | bytes 245768 | tf_op jit(solution)/shard_map/ppermute | solution.py:40
  6.4 2.0 %collective-permute-start.2 = (f32[2,5,16,128]{3,2,1,0:T(8,128)S(1)}, f32[2,5,16,128]{3,2,1,0:T(8,128)S(1)}, u32[]{:S(2)}, u32[]{:S(2)}) collective-permute-start(f32[2,5,16,128]{3,2,1,0:T(8,128)S(1)} %get-tuple-element.25), channel_id=1, source_target_pairs={{1,2},{3,4},{5,6},{2,1},{4,3},{6,5},{9,10},{11,12},{13,14},{10,9},... | collective-permute-start | bytes 245768 | tf_op jit(solution)/shard_map/ppermute | solution.py:40
  9.7 0.0 copy-done.6
  9.7 0.0 copy-done.5
  9.7 0.0 copy-done.2
  9.8 0.0 copy-done.3
  9.8 0.0 copy-done.4
  9.8 2.9 %velocity.1 = (f32[12,20,32,128]{3,2,1,0:T(8,128)S(1)}, f32[6,20,32,128]{3,2,1,0:T(8,128)S(1)}, f32[3,16,16,128]{3,2,1,0:T(8,128)S(1)}, f32[2,2,3,16,128]{4,3,2,...) custom-call(s32[1]{0:T(128)S(6)} %copy.18.source_cell, ...), custom_call_target="tpu_custom_call" | custom-call | flops 6553600 | bytes 2359296 | tf_op jit(solution)/shard_map/velocity/pallas_call | solution.py:519
  12.6 0.0 collective-permute-done.refs_0_
  12.6 0.0 collective-permute-done.1.refs_1_
  12.7 0.0 collective-permute-done.2.refs_2_
  12.7 0.4 %boundary.1 = (f32[6,20,32,128]{3,2,1,0:T(8,128)S(1)}, f32[2,5,16,128]{3,2,1,0:T(8,128)S(1)}, f32[2,5,16,128]{3,2,1,0:T(8,128)S(1)}, f32[2,5,16,128]{3,2,1,0:T(8,128)S(1)}) custom-call(f32[2,5,16,128]{3,2,1,0:T(8,128)S(1)} %collective-permute-done.refs_0_, f32[2,5,16,128]{3,2,1,0:T(8,128)S(1)} %collective-permute-done.1.refs_1_, ...), custom_call_target="tpu_custom_call", output_to_operand_aliasing={{0}: (5, {})} | custom-call | flops 32768 | bytes 163840 | tf_op jit(solution)/shard_map/boundary/pallas_call | solution.py:549
  13.1 0.2 collective-permute-start.3
  13.2 2.5 %collective-permute-start.4 = (f32[2,5,16,128]{3,2,1,0:T(8,128)S(1)}, f32[2,5,16,128]{3,2,1,0:T(8,128)S(1)}, u32[]{:S(2)}, u32[]{:S(2)}) collective-permute-start(f32[2,5,16,128]{3,2,1,0:T(8,128)S(1)} %get-tuple-element.31), channel_id=1, source_target_pairs={{0,1},{2,3},{4,5},{6,7},{1,0},{3,2},{5,4},{7,6},{8,9},{10,11},{12,... | collective-permute-start | bytes 245768 | tf_op jit(solution)/shard_map/ppermute | solution.py:40
  15.7 1.9 %collective-permute-start.5 = (f32[2,5,16,128]{3,2,1,0:T(8,128)S(1)}, f32[2,5,16,128]{3,2,1,0:T(8,128)S(1)}, u32[]{:S(2)}, u32[]{:S(2)}) collective-permute-start(f32[2,5,16,128]{3,2,1,0:T(8,128)S(1)} %get-tuple-element.32), channel_id=1, source_target_pairs={{1,2},{3,4},{5,6},{2,1},{4,3},{6,5},{9,10},{11,12},{13,14},{10,9},... | collective-permute-start | bytes 245768 | tf_op jit(solution)/shard_map/ppermute | solution.py:40
  17.6 1.9 %strain.1 = (f32[12,16,16,128]{3,2,1,0:T(8,128)S(1)}, f32[3,16,16,128]{3,2,1,0:T(8,128)S(1)}) custom-call(f32[2,5,16,128]{3,2,1,0:T(8,128)S(1)} %collective-permute-done.refs_0_, f32[2,5,16,128]{3,2,1,0:T(8,128)S(1)} %collective-permute-done.1.refs_1_, f32[2,5,16,128]{3,2,1,0:T(8,128)S(1)} %collective-permute-done.2.refs_2_, ...), custom_call_target="tpu_custom_call" | custom-call | flops 6553600 | bytes 2359296 | tf_op jit(solution)/shard_map/strain/pallas_call | solution.py:561
  19.5 0.0 collective-permute-done.3.refs_0_
  19.5 0.0 collective-permute-done.4.refs_1_
  19.5 2.2 %collective-permute-done.5.refs_2_ = f32[2,5,16,128]{3,2,1,0:T(8,128)S(1)} collective-permute-done((f32[2,5,16,128]{3,2,1,0:T(8,128)S(1)}, f32[2,5,16,128]{3,2,1,0:T(8,128)S(1)}, u32[]{:S(2)}, u32[]{:S(2)}) %collective-permute-start.5) | collective-permute-done | bytes 81952 | tf_op jit(solution)/shard_map/ppermute | solution.py:40
  21.8 0.4 %gradient.1 = (f32[12,16,16,128]{3,2,1,0:T(8,128)S(1)}, f32[3,16,16,128]{3,2,1,0:T(8,128)S(1)}) custom-call(f32[2,5,16,128]{3,2,1,0:T(8,128)S(1)} %collective-permute-done.3.refs_0_, f32[2,5,16,128]{3,2,1,0:T(8,128)S(1)} %collective-permute-done.4.refs_1_, ...), custom_call_target="tpu_custom_call", output_to_operand_aliasing={{0}: (6, {}), {1}: (7, {})} | custom-call | flops 983040 | bytes 262144 | tf_op jit(solution)/shard_map/gradient/pallas_call | solution.py:572
  22.2 3.3 %collective-permute-start.6 = (f32[3,16,16,128]{3,2,1,0:T(8,128)S(1)}, f32[3,16,16,128]{3,2,1,0:T(8,128)S(1)}, u32[]{:S(2)}, u32[]{:S(2)}) collective-permute-start(f32[3,16,16,128]{3,2,1,0:T(8,128)S(1)} %get-tuple-element.42), channel_id=1, source_target_pairs={{0,16},{16,0},{1,17},{17,1},{2,18},{18,2},{3,19},{19,3},{4,20},{20... | collective-permute-start | bytes 1179656 | tf_op jit(solution)/shard_map/ppermute | solution.py:582
  25.5 2.0 %outputs.1 = (f32[9,16,16,128]{3,2,1,0:T(8,128)}, f32[9,16,16,128]{3,2,1,0:T(8,128)}) custom-call(f32[6,20,32,128]{3,2,1,0:T(8,128)S(1)} %get-tuple-element.29.refs_5_.velocity, f32[12,16,16,128]{3,2,1,0:T(8,128)S(1)} %get-tuple-element.39.strain, f32[12,20,32,128]{3,2,1,0:T(8,128)S(1)} %get-tuple-element.33.refs_3_.stress, ...), custom_call_target="tpu_custom_call" | custom-call | flops 1966080 | bytes 2359296 | tf_op jit(solution)/shard_map/outputs/pallas_call | solution.py:586
  27.5 0.0 collective-permute-done.6
  27.5 0.8 %add.3 = f32[3,16,16,128]{3,2,1,0:T(8,128)} add(f32[3,16,16,128]{3,2,1,0:T(8,128)S(1)} %get-tuple-element.42, f32[3,16,16,128]{3,2,1,0:T(8,128)S(1)} %collective-permute-done.6) | non-fusion elementwise | flops 98304 | bytes 1179648 | tf_op jit(solution)/shard_map/add | solution.py:596
Async XLA Ops:
  0.6 9.1 %copy-start.6 = (f32[1,256]{1,0:T(1,128)S(1)}, f32[1,256]{1,0:T(1,128)}, u32[]{:S(2)}) copy-start(f32[1,256]{1,0:T(1,128)} %residual_amp.1) | copy-start | bytes 3076
  0.6 9.1 %copy-start.5 = (s32[1,256]{1,0:T(1,128)S(1)}, s32[1,256]{1,0:T(1,128)}, u32[]{:S(2)}) copy-start(s32[1,256]{1,0:T(1,128)} %receiver_cell.1) | copy-start | bytes 3076
  0.7 1.3 %copy-start = (f32[1,9,16,16,128]{4,3,2,1,0:T(8,128)S(1)}, f32[1,9,16,16,128]{4,3,2,1,0:T(8,128)}, u32[]{:S(2)}) copy-start(f32[1,9,16,16,128]{4,3,2,1,0:T(8,128)} %param.9) | copy-start | bytes 3538948
  1.9 1.3 %copy-start.1 = (f32[1,9,16,16,128]{4,3,2,1,0:T(8,128)S(1)}, f32[1,9,16,16,128]{4,3,2,1,0:T(8,128)}, u32[]{:S(2)}) copy-start(f32[1,9,16,16,128]{4,3,2,1,0:T(8,128)} %param.10) | copy-start | bytes 3538948
  3.2 6.5 %copy-start.2 = (f32[16,16,128]{2,1,0:T(8,128)S(1)}, f32[16,16,128]{2,1,0:T(8,128)}, u32[]{:S(2)}) copy-start(f32[16,16,128]{2,1,0:T(8,128)} %lame.1) | copy-start | bytes 393220
  3.2 6.5 %copy-start.3 = (f32[16,16,128]{2,1,0:T(8,128)S(1)}, f32[16,16,128]{2,1,0:T(8,128)}, u32[]{:S(2)}) copy-start(f32[16,16,128]{2,1,0:T(8,128)} %shear.1) | copy-start | bytes 393220
  3.2 6.6 %copy-start.4 = (f32[16,16,128]{2,1,0:T(8,128)S(1)}, f32[16,16,128]{2,1,0:T(8,128)}, u32[]{:S(2)}) copy-start(f32[16,16,128]{2,1,0:T(8,128)} %density.1) | copy-start | bytes 393220
  3.9 8.8 %collective-permute-start = (f32[2,5,16,128]{3,2,1,0:T(8,128)S(1)}, f32[2,5,16,128]{3,2,1,0:T(8,128)S(1)}, u32[]{:S(2)}, u32[]{:S(2)}) collective-permute-start(f32[2,5,16,128]{3,2,1,0:T(8,128)S(1)} %get-tuple-element.23), channel_id=1, source_target_pairs={{0,8},{8,0},{1,9},{9,1},{2,10},{10,2},{3,11},{11,3},{4,12},{12,4},... | collective-permute-start | bytes 245768 | tf_op jit(solution)/shard_map/ppermute | solution.py:40
  5.2 7.5 %collective-permute-start.1 = (f32[2,5,16,128]{3,2,1,0:T(8,128)S(1)}, f32[2,5,16,128]{3,2,1,0:T(8,128)S(1)}, u32[]{:S(2)}, u32[]{:S(2)}) collective-permute-start(f32[2,5,16,128]{3,2,1,0:T(8,128)S(1)} %get-tuple-element.24), channel_id=1, source_target_pairs={{0,1},{2,3},{4,5},{6,7},{1,0},{3,2},{5,4},{7,6},{8,9},{10,11},{12,... | collective-permute-start | bytes 245768 | tf_op jit(solution)/shard_map/ppermute | solution.py:40
  6.4 6.3 %collective-permute-start.2 = (f32[2,5,16,128]{3,2,1,0:T(8,128)S(1)}, f32[2,5,16,128]{3,2,1,0:T(8,128)S(1)}, u32[]{:S(2)}, u32[]{:S(2)}) collective-permute-start(f32[2,5,16,128]{3,2,1,0:T(8,128)S(1)} %get-tuple-element.25), channel_id=1, source_target_pairs={{1,2},{3,4},{5,6},{2,1},{4,3},{6,5},{9,10},{11,12},{13,14},{10,9},... | collective-permute-start | bytes 245768 | tf_op jit(solution)/shard_map/ppermute | solution.py:40
  13.1 6.5 %collective-permute-start.3 = (f32[2,5,16,128]{3,2,1,0:T(8,128)S(1)}, f32[2,5,16,128]{3,2,1,0:T(8,128)S(1)}, u32[]{:S(2)}, u32[]{:S(2)}) collective-permute-start(f32[2,5,16,128]{3,2,1,0:T(8,128)S(1)} %get-tuple-element.30), channel_id=1, source_target_pairs={{0,8},{8,0},{1,9},{9,1},{2,10},{10,2},{3,11},{11,3},{4,12},{12,4},... | collective-permute-start | bytes 245768 | tf_op jit(solution)/shard_map/ppermute | solution.py:40
  13.2 6.3 %collective-permute-start.4 = (f32[2,5,16,128]{3,2,1,0:T(8,128)S(1)}, f32[2,5,16,128]{3,2,1,0:T(8,128)S(1)}, u32[]{:S(2)}, u32[]{:S(2)}) collective-permute-start(f32[2,5,16,128]{3,2,1,0:T(8,128)S(1)} %get-tuple-element.31), channel_id=1, source_target_pairs={{0,1},{2,3},{4,5},{6,7},{1,0},{3,2},{5,4},{7,6},{8,9},{10,11},{12,... | collective-permute-start | bytes 245768 | tf_op jit(solution)/shard_map/ppermute | solution.py:40
  15.7 6.1 %collective-permute-start.5 = (f32[2,5,16,128]{3,2,1,0:T(8,128)S(1)}, f32[2,5,16,128]{3,2,1,0:T(8,128)S(1)}, u32[]{:S(2)}, u32[]{:S(2)}) collective-permute-start(f32[2,5,16,128]{3,2,1,0:T(8,128)S(1)} %get-tuple-element.32), channel_id=1, source_target_pairs={{1,2},{3,4},{5,6},{2,1},{4,3},{6,5},{9,10},{11,12},{13,14},{10,9},... | collective-permute-start | bytes 245768 | tf_op jit(solution)/shard_map/ppermute | solution.py:40
  22.2 5.3 %collective-permute-start.6 = (f32[3,16,16,128]{3,2,1,0:T(8,128)S(1)}, f32[3,16,16,128]{3,2,1,0:T(8,128)S(1)}, u32[]{:S(2)}, u32[]{:S(2)}) collective-permute-start(f32[3,16,16,128]{3,2,1,0:T(8,128)S(1)} %get-tuple-element.42), channel_id=1, source_target_pairs={{0,16},{16,0},{1,17},{17,1},{2,18},{18,2},{3,19},{19,3},{4,20},{20... | collective-permute-start | bytes 1179656 | tf_op jit(solution)/shard_map/ppermute | solution.py:582

commit v2 on v1

--- a/solution.py
+++ b/solution.py
@@ -22,17 +22,13 @@
 
 vmem = pl.BlockSpec(memory_space=pltpu.VMEM)
 smem = pl.BlockSpec(memory_space=pltpu.SMEM)
-anywhere = pl.BlockSpec(memory_space=pl.ANY)
+hbm = pl.BlockSpec(memory_space=pltpu.HBM)
 params = pltpu.CompilerParams(vmem_limit_bytes=24 * 1024 * 1024)
 
 
 def links_of(sizes):
-    return [
-        (name, dim, first)
-        for dim, name in enumerate(("tx", "ty"))
-        for first in (0, 1)
-        if first + 1 < sizes[name]
-    ]
+    order = (("ty", 1, 1), ("tx", 0, 1), ("tx", 0, 0), ("ty", 1, 0))
+    return [(name, dim, first) for name, dim, first in order if first + 1 < sizes[name]]
 
 
 def swap(value, axis, first):
@@ -181,15 +177,15 @@
 
 def velocity_kernel(
     width_y,
+    lame,
+    shear,
+    density,
     source_cell,
     source_amp,
     receiver_cell,
     residual_amp,
     forward,
     adjoint,
-    lame,
-    shear,
-    density,
     stress,
     velocity,
     accel,
@@ -198,27 +194,52 @@
     scaled_lame,
     scaled_shear,
     added,
+    lame_now,
+    shear_now,
+    density_now,
+    sems,
 ):
     _, tile_x, tile_y, depth = forward.shape
     receivers = receiver_cell.shape[-1]
     cells = tile_x * tile_y
-    columns = column_ids(tile_x, tile_y, width_y, depth)
-    lane = lax.broadcasted_iota(jnp.int32, columns.shape, 1)
-    added[0] = jnp.where(columns * depth + lane == source_cell[0], source_amp[0], 0.0)
+    copies = [
+        pltpu.make_async_copy(source, target, sems.at[at])
+        for at, (source, target) in enumerate((
+            (density, density_now),
+            (lame, lame_now),
+            (shear, shear_now),
+        ))
+    ]
+    for copy in copies:
+        copy.start()
     where = receiver_cell[...]
     column = lax.div(where, depth)
     depth_of = where - column * depth
-    columns = column_ids(tile_x, tile_y, width_y, receivers)
-    column_hot = (columns == column).astype(jnp.float32)
+    columns = column_ids(tile_x, tile_y, width_y, depth)
+    column_hot = jnp.concatenate(
+        [
+            (columns == column[:, begin : begin + depth]).astype(jnp.bfloat16)
+            for begin in range(0, receivers, depth)
+        ],
+        axis=1,
+    )
     level = lax.broadcasted_iota(jnp.int32, (depth, receivers), 0)
-    depth_hot = jnp.where(level == depth_of, residual_amp[...], 0.0)
-    added[1] = lax.dot_general(
-        column_hot,
-        depth_hot,
-        (((1,), (1,)), ((), ())),
-        precision=lax.Precision.HIGHEST,
-        preferred_element_type=jnp.float32,
-    )
+    rest = jnp.where(level == depth_of, residual_amp[...], 0.0)
+    total = jnp.zeros(columns.shape, jnp.float32)
+    for _ in range(3):
+        part = rest.astype(jnp.bfloat16)
+        rest = rest - part.astype(jnp.float32)
+        total = total + lax.dot_general(
+            column_hot,
+            part,
+            (((1,), (1,)), ((), ())),
+            preferred_element_type=jnp.float32,
+        )
+    added[1] = total
+    lane = lax.broadcasted_iota(jnp.int32, columns.shape, 1)
+    added[0] = jnp.where(columns * depth + lane == source_cell[0], source_amp[0], 0.0)
+    for copy in copies:
+        copy.wait()
     for wave in range(2):
         for layer in range(3):
             rim_added[wave, 0, layer] = added[wave, pl.ds(cells + layer * tile_y, tile_y), :]
@@ -237,12 +258,12 @@
                 stress[6 * wave + part, x + LAYERS, middle, :] = (
                     value + extra if part < 3 else value
                 )
-        buoyancy[x] = 1.0 / density[x]
-        scaled_lame[x] = time_step * lame[x]
-        scaled_shear[x] = time_step * shear[x]
+        buoyancy[x] = 1.0 / density_now[x]
+        scaled_lame[x] = time_step * lame_now[x]
+        scaled_shear[x] = time_step * shear_now[x]
         return carry
 
-    lax.fori_loop(0, tile_x, fill, 0)
+    lax.fori_loop(0, tile_x, fill, 0, unroll=4)
 
     def layer(x, carry):
         light = buoyancy[x]
@@ -268,7 +289,7 @@
                 )
         return carry
 
-    lax.fori_loop(0, tile_x, layer, 0)
+    lax.fori_loop(0, tile_x, layer, 0, unroll=4)
 
 
 def stress_halo_terms(links, received, rim_added, waves, add):
@@ -408,7 +429,7 @@
         gradient[2, x] = -time_step * total
         return carry
 
-    lax.fori_loop(0, tile_x, layer, 0)
+    lax.fori_loop(0, tile_x, layer, 0, unroll=4)
 
 
 def new_stress(strain, stress, scaled_lame, scaled_shear, wave, x, tile_y):
@@ -446,7 +467,7 @@
         gradient[1, x] = -time_step * total
         return carry
 
-    lax.fori_loop(0, tile_x, layer, 0)
+    lax.fori_loop(0, tile_x, layer, 0, unroll=4)
 
 
 def output_kernel(velocity, strain, stress, scaled_lame, scaled_shear, forward, adjoint):
@@ -460,6 +481,10 @@
             _, values = new_stress(strain, stress, scaled_lame, scaled_shear, wave, x, tile_y)
             for part in range(6):
                 out[3 + part, at] = values[part]
+
+
+def in_hbm(value):
+    return pltpu.with_memory_space_constraint(value, pltpu.HBM)
 
 
 def cost(flops, size):
@@ -504,7 +529,7 @@
     sends = pl.pallas_call(
         functools.partial(pack_kernel, links),
         out_shape=send_shapes,
-        in_specs=[anywhere] * 2,
+        in_specs=[hbm] * 2,
         out_specs=[vmem] * len(links),
         scratch_shapes=[
             pltpu.VMEM((2, 3, 2, tile_x, 8, depth), jnp.float32),
@@ -513,7 +538,7 @@
         compiler_params=params,
         cost_estimate=cost(0, 10 * 2 * tile_x * depth * 4),
         name="pack",
-    )(forward, adjoint)
+    )(in_hbm(forward), in_hbm(adjoint))
     halos = exchange(sends)
 
     stress, velocity, accel, rim_added, buoyancy, scaled_lame, scaled_shear = pl.pallas_call(
@@ -527,22 +552,26 @@
             tile(),
             tile(),
         ],
-        in_specs=[smem] * 2 + [vmem] * 7,
+        in_specs=[hbm] * 3 + [smem] * 2 + [vmem] * 4,
         out_specs=[vmem] * 7,
-        scratch_shapes=[pltpu.VMEM((2, tile_x * tile_y + rims, depth), jnp.float32)],
+        scratch_shapes=[
+            pltpu.VMEM((2, tile_x * tile_y + rims, depth), jnp.float32),
+            tile(),
+            tile(),
+            tile(),
+            pltpu.SemaphoreType.DMA((3,)),
+        ],
         compiler_params=params,
         cost_estimate=cost(200 * cells, 18 * 4 * cells),
         name="velocity",
     )(
+        *(in_hbm(x) for x in (lame_lambda, shear_modulus, density)),
         source_cell,
         source_amp,
         receiver_cell,
         residual_amp,
         forward,
         adjoint,
-        lame_lambda,
-        shear_modulus,
-        density,
     )
 
     count = len(links)

time: 28.5 us -> 26 us (0.912)
  the two profiles are of different devices: /device:TPU:9 before, /device:TPU:1 now
where the time goes in v2:
time: 26 us; the launch traced here: 25.8 us
  starting transfers between devices  13.9 us (53%)
  Pallas kernels  7.77 us (30%)
  between operations  2.09 us (8%)
  waiting for transfers between devices  1.25 us (5%)
  other arithmetic  0.8 us (3%)
    ppermute x6, starting transfers between devices, swap(): return lax.ppermute(value, axis, pairs + [(j, i) for i, j in pairs])  11.3 us
    ppermute x1, starting transfers between devices, body(): other = lax.ppermute(gradient, 'shot', [(0, 1), (1, 0)])  2.57 us
    pallas_call x1, Pallas kernels, body(): pl.pallas_call(functools.partial(velocity_kernel, width_y), out_shape=[pa...  2.5 us
    pallas_call x1, Pallas kernels, body(): pl.pallas_call(output_kernel, grid=(tile_x // step,), out_shape=[jax.Shap...  1.97 us
    pallas_call x1, Pallas kernels, body(): pl.pallas_call(functools.partial(pack_kernel, links), out_shape=send_shap...  1.72 us
    ppermute x6, waiting for transfers between devices, swap(): return lax.ppermute(value, axis, pairs + [(j, i) for i, j in pairs])  1.25 us
    pallas_call x1, Pallas kernels, body(): pl.pallas_call(functools.partial(strain_kernel, links), out_shape=[tile(1...  1 us
    add x1, other arithmetic, body(): return (forward_next[None], adjoint_next[None], gradient + other)  0.8 us
  transfers between devices with their start and end apart: 7, of which 1 were waited for; matrix products, arithmetic and copies ran while one was open for 0% of the time, Pallas kernels for 21%

profile of v2, /device:TPU:1, one launch (start us, length us, event | category | flops | bytes accessed | tf_op | source)
XLA Modules:
  0.0 25.8 jit_solution(12865581519820846158)
XLA Ops:
  0.6 0.0 copy-start.1
  0.6 0.0 copy-start
  0.7 0.0 copy-start.3
  0.7 0.0 copy-start.2
  0.7 1.7 %pack.1 = (f32[2,5,16,128]{3,2,1,0:T(8,128)S(1)}, f32[2,5,16,128]{3,2,1,0:T(8,128)S(1)}, f32[2,5,16,128]{3,2,1,0:T(8,128)S(1)}) custom-call(f32[9,16,16,128]{3,2,1,0:T(8,128)} %bitcast.4, f32[9,16,16,128]{3,2,1,0:T(8,128)} %bitcast.6), custom_call_target="tpu_custom_call" | custom-call | bytes 163840 | tf_op jit(solution)/shard_map/pack/pallas_call | solution.py:529
  2.4 0.7 %collective-permute-start = (f32[2,5,16,128]{3,2,1,0:T(8,128)S(1)}, f32[2,5,16,128]{3,2,1,0:T(8,128)S(1)}, u32[]{:S(2)}, u32[]{:S(2)}) collective-permute-start(f32[2,5,16,128]{3,2,1,0:T(8,128)S(1)} %get-tuple-element.23), channel_id=1, source_target_pairs={{1,2},{3,4},{5,6},{2,1},{4,3},{6,5},{9,10},{11,12},{13,14},{10,9},... | collective-permute-start | bytes 245768 | tf_op jit(solution)/shard_map/ppermute | solution.py:36
  3.1 2.1 %collective-permute-start.1 = (f32[2,5,16,128]{3,2,1,0:T(8,128)S(1)}, f32[2,5,16,128]{3,2,1,0:T(8,128)S(1)}, u32[]{:S(2)}, u32[]{:S(2)}) collective-permute-start(f32[2,5,16,128]{3,2,1,0:T(8,128)S(1)} %get-tuple-element.24), channel_id=1, source_target_pairs={{0,8},{8,0},{1,9},{9,1},{2,10},{10,2},{3,11},{11,3},{4,12},{12,4},... | collective-permute-start | bytes 245768 | tf_op jit(solution)/shard_map/ppermute | solution.py:36
  5.2 3.7 %collective-permute-start.2 = (f32[2,5,16,128]{3,2,1,0:T(8,128)S(1)}, f32[2,5,16,128]{3,2,1,0:T(8,128)S(1)}, u32[]{:S(2)}, u32[]{:S(2)}) collective-permute-start(f32[2,5,16,128]{3,2,1,0:T(8,128)S(1)} %get-tuple-element.25), channel_id=1, source_target_pairs={{0,1},{2,3},{4,5},{6,7},{1,0},{3,2},{5,4},{7,6},{8,9},{10,11},{12,... | collective-permute-start | bytes 245768 | tf_op jit(solution)/shard_map/ppermute | solution.py:36
  10.2 0.0 copy-done.1
  10.2 0.0 copy-done
  10.2 0.0 copy-done.3
  10.3 0.0 copy-done.2
  10.3 2.5 %velocity.1 = (f32[12,20,32,128]{3,2,1,0:T(8,128)S(1)}, f32[6,20,32,128]{3,2,1,0:T(8,128)S(1)}, f32[3,16,16,128]{3,2,1,0:T(8,128)S(1)}, f32[2,2,3,16,128]{4,3,2,...) custom-call(f32[16,16,128]{2,1,0:T(8,128)} %lame.1, ...), custom_call_target="tpu_custom_call" | custom-call | flops 6553600 | bytes 2359296 | tf_op jit(solution)/shard_map/velocity/pallas_call | solution.py:544
  12.8 0.0 collective-permute-done.refs_0_
  12.8 0.0 collective-permute-done.1.refs_1_
  12.8 0.0 collective-permute-done.2.refs_2_
  12.8 0.3 %boundary.1 = (f32[6,20,32,128]{3,2,1,0:T(8,128)S(1)}, f32[2,5,16,128]{3,2,1,0:T(8,128)S(1)}, f32[2,5,16,128]{3,2,1,0:T(8,128)S(1)}, f32[2,5,16,128]{3,2,1,0:T(8,128)S(1)}) custom-call(f32[2,5,16,128]{3,2,1,0:T(8,128)S(1)} %collective-permute-done.refs_0_, f32[2,5,16,128]{3,2,1,0:T(8,128)S(1)} %collective-permute-done.1.refs_1_, ...), custom_call_target="tpu_custom_call", output_to_operand_aliasing={{0}: (5, {})} | custom-call | flops 32768 | bytes 163840 | tf_op jit(solution)/shard_map/boundary/pallas_call | solution.py:578
  13.1 0.7 %collective-permute-start.3 = (f32[2,5,16,128]{3,2,1,0:T(8,128)S(1)}, f32[2,5,16,128]{3,2,1,0:T(8,128)S(1)}, u32[]{:S(2)}, u32[]{:S(2)}) collective-permute-start(f32[2,5,16,128]{3,2,1,0:T(8,128)S(1)} %get-tuple-element.30), channel_id=1, source_target_pairs={{1,2},{3,4},{5,6},{2,1},{4,3},{6,5},{9,10},{11,12},{13,14},{10,9},... | collective-permute-start | bytes 245768 | tf_op jit(solution)/shard_map/ppermute | solution.py:36
  13.8 0.3 %collective-permute-start.4 = (f32[2,5,16,128]{3,2,1,0:T(8,128)S(1)}, f32[2,5,16,128]{3,2,1,0:T(8,128)S(1)}, u32[]{:S(2)}, u32[]{:S(2)}) collective-permute-start(f32[2,5,16,128]{3,2,1,0:T(8,128)S(1)} %get-tuple-element.31), channel_id=1, source_target_pairs={{0,8},{8,0},{1,9},{9,1},{2,10},{10,2},{3,11},{11,3},{4,12},{12,4},... | collective-permute-start | bytes 245768 | tf_op jit(solution)/shard_map/ppermute | solution.py:36
  14.1 3.8 %collective-permute-start.5 = (f32[2,5,16,128]{3,2,1,0:T(8,128)S(1)}, f32[2,5,16,128]{3,2,1,0:T(8,128)S(1)}, u32[]{:S(2)}, u32[]{:S(2)}) collective-permute-start(f32[2,5,16,128]{3,2,1,0:T(8,128)S(1)} %get-tuple-element.32), channel_id=1, source_target_pairs={{0,1},{2,3},{4,5},{6,7},{1,0},{3,2},{5,4},{7,6},{8,9},{10,11},{12,... | collective-permute-start | bytes 245768 | tf_op jit(solution)/shard_map/ppermute | solution.py:36
  17.9 1.0 %strain.1 = (f32[12,16,16,128]{3,2,1,0:T(8,128)S(1)}, f32[3,16,16,128]{3,2,1,0:T(8,128)S(1)}) custom-call(f32[2,5,16,128]{3,2,1,0:T(8,128)S(1)} %collective-permute-done.refs_0_, f32[2,5,16,128]{3,2,1,0:T(8,128)S(1)} %collective-permute-done.1.refs_1_, f32[2,5,16,128]{3,2,1,0:T(8,128)S(1)} %collective-permute-done.2.refs_2_, ...), custom_call_target="tpu_custom_call" | custom-call | flops 6553600 | bytes 2359296 | tf_op jit(solution)/shard_map/strain/pallas_call | solution.py:590
  18.9 0.0 collective-permute-done.3.refs_0_
  18.9 0.0 collective-permute-done.4.refs_1_
  18.9 1.2 %collective-permute-done.5.refs_2_ = f32[2,5,16,128]{3,2,1,0:T(8,128)S(1)} collective-permute-done((f32[2,5,16,128]{3,2,1,0:T(8,128)S(1)}, f32[2,5,16,128]{3,2,1,0:T(8,128)S(1)}, u32[]{:S(2)}, u32[]{:S(2)}) %collective-permute-start.5) | collective-permute-done | bytes 81952 | tf_op jit(solution)/shard_map/ppermute | solution.py:36
  20.1 0.3 %gradient.1 = (f32[12,16,16,128]{3,2,1,0:T(8,128)S(1)}, f32[3,16,16,128]{3,2,1,0:T(8,128)S(1)}) custom-call(f32[2,5,16,128]{3,2,1,0:T(8,128)S(1)} %collective-permute-done.3.refs_0_, f32[2,5,16,128]{3,2,1,0:T(8,128)S(1)} %collective-permute-done.4.refs_1_, ...), custom_call_target="tpu_custom_call", output_to_operand_aliasing={{0}: (6, {}), {1}: (7, {})} | custom-call | flops 983040 | bytes 262144 | tf_op jit(solution)/shard_map/gradient/pallas_call | solution.py:601
  20.5 2.6 %collective-permute-start.6 = (f32[3,16,16,128]{3,2,1,0:T(8,128)S(1)}, f32[3,16,16,128]{3,2,1,0:T(8,128)S(1)}, u32[]{:S(2)}, u32[]{:S(2)}) collective-permute-start(f32[3,16,16,128]{3,2,1,0:T(8,128)S(1)} %get-tuple-element.42), channel_id=1, source_target_pairs={{0,16},{16,0},{1,17},{17,1},{2,18},{18,2},{3,19},{19,3},{4,20},{20... | collective-permute-start | bytes 1179656 | tf_op jit(solution)/shard_map/ppermute | solution.py:611
  23.0 2.0 %outputs.1 = (f32[9,16,16,128]{3,2,1,0:T(8,128)}, f32[9,16,16,128]{3,2,1,0:T(8,128)}) custom-call(f32[6,20,32,128]{3,2,1,0:T(8,128)S(1)} %get-tuple-element.29.refs_5_.velocity, f32[12,16,16,128]{3,2,1,0:T(8,128)S(1)} %get-tuple-element.39.strain, f32[12,20,32,128]{3,2,1,0:T(8,128)S(1)} %get-tuple-element.33.refs_3_.stress, ...), custom_call_target="tpu_custom_call" | custom-call | flops 1966080 | bytes 2359296 | tf_op jit(solution)/shard_map/outputs/pallas_call | solution.py:615
  25.0 0.0 collective-permute-done.6
  25.0 0.8 %add.3 = f32[3,16,16,128]{3,2,1,0:T(8,128)} add(f32[3,16,16,128]{3,2,1,0:T(8,128)S(1)} %get-tuple-element.42, f32[3,16,16,128]{3,2,1,0:T(8,128)S(1)} %collective-permute-done.6) | non-fusion elementwise | flops 98304 | bytes 1179648 | tf_op jit(solution)/shard_map/add | solution.py:625
Async XLA Ops:
  0.6 9.6 %copy-start.1 = (f32[1,9,16,16,128]{4,3,2,1,0:T(8,128)S(1)}, f32[1,9,16,16,128]{4,3,2,1,0:T(8,128)}, u32[]{:S(2)}) copy-start(f32[1,9,16,16,128]{4,3,2,1,0:T(8,128)} %param.10) | copy-start | bytes 3538948
  0.6 9.6 %copy-start = (f32[1,9,16,16,128]{4,3,2,1,0:T(8,128)S(1)}, f32[1,9,16,16,128]{4,3,2,1,0:T(8,128)}, u32[]{:S(2)}) copy-start(f32[1,9,16,16,128]{4,3,2,1,0:T(8,128)} %param.9) | copy-start | bytes 3538948
  0.7 9.6 %copy-start.3 = (f32[1,256]{1,0:T(1,128)S(1)}, f32[1,256]{1,0:T(1,128)}, u32[]{:S(2)}) copy-start(f32[1,256]{1,0:T(1,128)} %residual_amp.1) | copy-start | bytes 3076
  0.7 9.6 %copy-start.2 = (s32[1,256]{1,0:T(1,128)S(1)}, s32[1,256]{1,0:T(1,128)}, u32[]{:S(2)}) copy-start(s32[1,256]{1,0:T(1,128)} %receiver_cell.1) | copy-start | bytes 3076
  2.4 10.4 %collective-permute-start = (f32[2,5,16,128]{3,2,1,0:T(8,128)S(1)}, f32[2,5,16,128]{3,2,1,0:T(8,128)S(1)}, u32[]{:S(2)}, u32[]{:S(2)}) collective-permute-start(f32[2,5,16,128]{3,2,1,0:T(8,128)S(1)} %get-tuple-element.23), channel_id=1, source_target_pairs={{1,2},{3,4},{5,6},{2,1},{4,3},{6,5},{9,10},{11,12},{13,14},{10,9},... | collective-permute-start | bytes 245768 | tf_op jit(solution)/shard_map/ppermute | solution.py:36
  3.1 9.7 %collective-permute-start.1 = (f32[2,5,16,128]{3,2,1,0:T(8,128)S(1)}, f32[2,5,16,128]{3,2,1,0:T(8,128)S(1)}, u32[]{:S(2)}, u32[]{:S(2)}) collective-permute-start(f32[2,5,16,128]{3,2,1,0:T(8,128)S(1)} %get-tuple-element.24), channel_id=1, source_target_pairs={{0,8},{8,0},{1,9},{9,1},{2,10},{10,2},{3,11},{11,3},{4,12},{12,4},... | collective-permute-start | bytes 245768 | tf_op jit(solution)/shard_map/ppermute | solution.py:36
  5.2 7.6 %collective-permute-start.2 = (f32[2,5,16,128]{3,2,1,0:T(8,128)S(1)}, f32[2,5,16,128]{3,2,1,0:T(8,128)S(1)}, u32[]{:S(2)}, u32[]{:S(2)}) collective-permute-start(f32[2,5,16,128]{3,2,1,0:T(8,128)S(1)} %get-tuple-element.25), channel_id=1, source_target_pairs={{0,1},{2,3},{4,5},{6,7},{1,0},{3,2},{5,4},{7,6},{8,9},{10,11},{12,... | collective-permute-start | bytes 245768 | tf_op jit(solution)/shard_map/ppermute | solution.py:36
  13.1 5.8 %collective-permute-start.3 = (f32[2,5,16,128]{3,2,1,0:T(8,128)S(1)}, f32[2,5,16,128]{3,2,1,0:T(8,128)S(1)}, u32[]{:S(2)}, u32[]{:S(2)}) collective-permute-start(f32[2,5,16,128]{3,2,1,0:T(8,128)S(1)} %get-tuple-element.30), channel_id=1, source_target_pairs={{1,2},{3,4},{5,6},{2,1},{4,3},{6,5},{9,10},{11,12},{13,14},{10,9},... | collective-permute-start | bytes 245768 | tf_op jit(solution)/shard_map/ppermute | solution.py:36
  13.8 5.1 %collective-permute-start.4 = (f32[2,5,16,128]{3,2,1,0:T(8,128)S(1)}, f32[2,5,16,128]{3,2,1,0:T(8,128)S(1)}, u32[]{:S(2)}, u32[]{:S(2)}) collective-permute-start(f32[2,5,16,128]{3,2,1,0:T(8,128)S(1)} %get-tuple-element.31), channel_id=1, source_target_pairs={{0,8},{8,0},{1,9},{9,1},{2,10},{10,2},{3,11},{11,3},{4,12},{12,4},... | collective-permute-start | bytes 245768 | tf_op jit(solution)/shard_map/ppermute | solution.py:36
  14.1 6.1 %collective-permute-start.5 = (f32[2,5,16,128]{3,2,1,0:T(8,128)S(1)}, f32[2,5,16,128]{3,2,1,0:T(8,128)S(1)}, u32[]{:S(2)}, u32[]{:S(2)}) collective-permute-start(f32[2,5,16,128]{3,2,1,0:T(8,128)S(1)} %get-tuple-element.32), channel_id=1, source_target_pairs={{0,1},{2,3},{4,5},{6,7},{1,0},{3,2},{5,4},{7,6},{8,9},{10,11},{12,... | collective-permute-start | bytes 245768 | tf_op jit(solution)/shard_map/ppermute | solution.py:36
  20.5 4.6 %collective-permute-start.6 = (f32[3,16,16,128]{3,2,1,0:T(8,128)S(1)}, f32[3,16,16,128]{3,2,1,0:T(8,128)S(1)}, u32[]{:S(2)}, u32[]{:S(2)}) collective-permute-start(f32[3,16,16,128]{3,2,1,0:T(8,128)S(1)} %get-tuple-element.42), channel_id=1, source_target_pairs={{0,16},{16,0},{1,17},{17,1},{2,18},{18,2},{3,19},{19,3},{4,20},{20... | collective-permute-start | bytes 1179656 | tf_op jit(solution)/shard_map/ppermute | solution.py:611

commit v3 on v2

--- a/solution.py
+++ b/solution.py
@@ -46,63 +46,88 @@
     return (partner >= 0) & (partner < lax.axis_size(axis))
 
 
-def pack_kernel(links, *refs):
-    fields = refs[:2]
-    sends = refs[2 : 2 + len(links)]
-    edge, sems = refs[2 + len(links) :]
-    _, tile_x, tile_y, _ = fields[0].shape
-    copies = []
-
-    def copy(source, target):
-        started = pltpu.make_async_copy(source, target, sems.at[len(copies)])
-        started.start()
-        copies.append(started)
-
-    for wave in range(2):
-        for slot, part in enumerate(STRESS_ALONG[1]):
-            for side, row in enumerate((0, tile_y - 8)):
-                copy(fields[wave].at[3 + part, :, pl.ds(row, 8), :], edge.at[wave, slot, side])
+def send_faces(field, count, links, sends, plans):
     for (axis, dim, first), send in zip(links, sends):
-        if dim == 1:
-            continue
         lower = is_lower(axis, first)
-        normal, one, two = (3 + part for part in STRESS_ALONG[0])
-        last = tile_x - 1
-        for wave in range(2):
-            for slot, (upper_part, upper_layer, lower_part, lower_layer) in enumerate((
-                (normal, 0, normal, last),
-                (normal, 1, one, last - 1),
-                (one, 0, one, last),
-                (two, 0, two, last - 1),
-                (two, 1, two, last),
-            )):
-                part = jnp.where(lower, lower_part, upper_part)
-                layer = jnp.where(lower, lower_layer, upper_layer)
-                copy(fields[wave].at[part, layer], send.at[wave, slot])
-    for started in copies:
-        started.wait()
-    rows = edge.reshape(2, 3, 2, tile_x * 8, edge.shape[-1])
-
-    def row_of(wave, part, row):
-        side, at = (0, row) if row < 8 else (1, row - (tile_y - 8))
-        return rows[wave, part, side, pl.ds(at, tile_x, stride=8), :]
-
-    last = tile_y - 1
-    for (axis, dim, first), send in zip(links, sends):
-        if dim == 0:
-            continue
-        lower = is_lower(axis, first)
-        for wave in range(2):
-            for slot, (upper_part, upper_row, lower_part, lower_row) in enumerate((
-                (0, 0, 0, last),
-                (0, 1, 1, last - 1),
-                (1, 0, 1, last),
-                (2, 0, 2, last - 1),
-                (2, 1, 2, last),
-            )):
-                send[wave, slot] = jnp.where(
-                    lower, row_of(wave, lower_part, lower_row), row_of(wave, upper_part, upper_row)
-                )
+        upper_plan, lower_plan = plans[dim]
+
+        def put(plan):
+            for wave in range(2):
+                for slot, (part, index) in enumerate(plan):
+                    send[wave, slot] = face(field, count * wave + part, dim, index, True)[...]
+
+        pl.when(lower)(functools.partial(put, lower_plan))
+        pl.when(jnp.logical_not(lower))(functools.partial(put, upper_plan))
+
+
+def stress_plan(dim):
+    n, a, b = STRESS_ALONG[dim]
+    return (
+        ((n, 0), (n, 1), (a, 0), (b, 0), (b, 0)),
+        ((n, -1), (a, -2), (a, -1), (b, -2), (b, -1)),
+    )
+
+
+def velocity_plan(dim):
+    n, a, b = VELOCITY_ALONG[dim]
+    return (
+        ((n, 0), (a, 0), (a, 1), (b, 0), (b, 1)),
+        ((n, -2), (n, -1), (a, -1), (b, -1), (b, -1)),
+    )
+
+
+def pack_kernel(links, width_y, *refs):
+    fields, (receiver_cell, residual_amp) = refs[:2], refs[2:4]
+    sends = refs[4 : 4 + len(links)]
+    stress, velocity, added, cells_now, amps_now, sems = refs[4 + len(links) :]
+    _, tile_x, tile_y, depth = fields[0].shape
+    small = [
+        pltpu.make_async_copy(receiver_cell, cells_now, sems.at[0]),
+        pltpu.make_async_copy(residual_amp, amps_now, sems.at[1]),
+    ]
+    large = [
+        pltpu.make_async_copy(
+            fields[wave].at[3 + part],
+            stress.at[6 * wave + part, pl.ds(LAYERS, tile_x), pl.ds(ROWS, tile_y), :],
+            sems.at[2 + 6 * wave + part],
+        )
+        for wave in range(2)
+        for part in range(6)
+    ]
+    for copy in small + large:
+        copy.start()
+    clear_rim(stress, tile_x, tile_y)
+    clear_rim(velocity, tile_x, tile_y)
+    columns = column_ids(tile_x, tile_y, width_y, depth)
+    for copy in small:
+        copy.wait()
+    where = cells_now[...]
+    receivers = where.shape[-1]
+    column = lax.div(where, depth)
+    depth_of = where - column * depth
+    column_hot = jnp.concatenate(
+        [
+            (columns == column[:, begin : begin + depth]).astype(jnp.bfloat16)
+            for begin in range(0, receivers, depth)
+        ],
+        axis=1,
+    )
+    level = lax.broadcasted_iota(jnp.int32, (depth, receivers), 0)
+    rest = jnp.where(level == depth_of, amps_now[...], 0.0)
+    total = jnp.zeros(columns.shape, jnp.float32)
+    for _ in range(3):
+        part = rest.astype(jnp.bfloat16)
+        rest = rest - part.astype(jnp.float32)
+        total = total + lax.dot_general(
+            column_hot,
+            part,
+            (((1,), (1,)), ((), ())),
+            preferred_element_type=jnp.float32,
+        )
+    added[...] = total
+    for copy in large:
+        copy.wait()
+    send_faces(stress, 6, links, sends, [stress_plan(dim) for dim in range(2)])
 
 
 def column_ids(tile_x, tile_y, width_y, lanes):
@@ -175,99 +200,41 @@
             )
 
 
-def velocity_kernel(
-    width_y,
-    lame,
-    shear,
-    density,
-    source_cell,
-    source_amp,
-    receiver_cell,
-    residual_amp,
-    forward,
-    adjoint,
-    stress,
-    velocity,
-    accel,
-    rim_added,
-    buoyancy,
-    scaled_lame,
-    scaled_shear,
-    added,
-    lame_now,
-    shear_now,
-    density_now,
-    sems,
-):
-    _, tile_x, tile_y, depth = forward.shape
-    receivers = receiver_cell.shape[-1]
+def velocity_kernel(width_y, *refs):
+    forward, adjoint, lame, shear, density, source_cell, source_amp, received, _, _ = refs[:10]
+    stress, velocity, accel, rim_added, buoyancy, scaled_lame, scaled_shear = refs[10:17]
+    gained, lame_now, shear_now, density_now, sems = refs[17:]
+    tile_x, tile_y, depth = density.shape
     cells = tile_x * tile_y
+    middle = pl.ds(ROWS, tile_y)
     copies = [
         pltpu.make_async_copy(source, target, sems.at[at])
         for at, (source, target) in enumerate((
             (density, density_now),
             (lame, lame_now),
             (shear, shear_now),
+            (forward.at[pl.ds(0, 3)], velocity.at[pl.ds(0, 3), pl.ds(LAYERS, tile_x), middle, :]),
+            (adjoint.at[pl.ds(0, 3)], velocity.at[pl.ds(3, 3), pl.ds(LAYERS, tile_x), middle, :]),
         ))
     ]
     for copy in copies:
         copy.start()
-    where = receiver_cell[...]
-    column = lax.div(where, depth)
-    depth_of = where - column * depth
     columns = column_ids(tile_x, tile_y, width_y, depth)
-    column_hot = jnp.concatenate(
-        [
-            (columns == column[:, begin : begin + depth]).astype(jnp.bfloat16)
-            for begin in range(0, receivers, depth)
-        ],
-        axis=1,
-    )
-    level = lax.broadcasted_iota(jnp.int32, (depth, receivers), 0)
-    rest = jnp.where(level == depth_of, residual_amp[...], 0.0)
-    total = jnp.zeros(columns.shape, jnp.float32)
-    for _ in range(3):
-        part = rest.astype(jnp.bfloat16)
-        rest = rest - part.astype(jnp.float32)
-        total = total + lax.dot_general(
-            column_hot,
-            part,
-            (((1,), (1,)), ((), ())),
-            preferred_element_type=jnp.float32,
-        )
-    added[1] = total
     lane = lax.broadcasted_iota(jnp.int32, columns.shape, 1)
-    added[0] = jnp.where(columns * depth + lane == source_cell[0], source_amp[0], 0.0)
-    for copy in copies:
-        copy.wait()
-    for wave in range(2):
+    sourced = jnp.where(columns * depth + lane == source_cell[0], source_amp[0], 0.0)
+    for wave, added in enumerate((sourced, received[...])):
         for layer in range(3):
-            rim_added[wave, 0, layer] = added[wave, pl.ds(cells + layer * tile_y, tile_y), :]
-            rim_added[wave, 1, layer] = added[
-                wave, pl.ds(cells + 3 * tile_y + layer * tile_x, tile_x), :
-            ]
-    clear_rim(stress, tile_x, tile_y)
-    clear_rim(velocity, tile_x, tile_y)
-    middle = pl.ds(ROWS, tile_y)
-
-    def fill(x, carry):
-        for wave, fields in enumerate((forward, adjoint)):
-            extra = added[wave, pl.ds(pl.multiple_of(x * tile_y, 8), tile_y), :]
-            for part in range(6):
-                value = fields[3 + part, x]
-                stress[6 * wave + part, x + LAYERS, middle, :] = (
-                    value + extra if part < 3 else value
-                )
-        buoyancy[x] = 1.0 / density_now[x]
-        scaled_lame[x] = time_step * lame_now[x]
-        scaled_shear[x] = time_step * shear_now[x]
-        return carry
-
-    lax.fori_loop(0, tile_x, fill, 0, unroll=4)
+            begin = cells + layer * tile_y
+            rim_added[wave, 0, layer] = added[begin : begin + tile_y]
+            begin = cells + 3 * tile_y + layer * tile_x
+            rim_added[wave, 1, layer] = added[begin : begin + tile_x]
+        for x in range(tile_x):
+            extra = added[x * tile_y : (x + 1) * tile_y]
+            for part in range(3):
+                stress[6 * wave + part, x + LAYERS, middle, :] += extra
 
     def layer(x, carry):
-        light = buoyancy[x]
-        for wave, fields in enumerate((forward, adjoint)):
+        for wave in range(2):
             xx, yy, zz, xy, xz, yz = range(6 * wave, 6 * wave + 6)
             values = (
                 along_x(stress, xx, x, tile_y, True)
@@ -281,15 +248,26 @@
                 + along_z(stress, zz, x, tile_y, True),
             )
             for part, value in enumerate(values):
-                value = light * value
-                if wave == 0:
-                    accel[part, x] = value
-                velocity[3 * wave + part, x + LAYERS, middle, :] = (
-                    fields[part, x] + time_step * value
-                )
+                gained[3 * wave + part, x] = value
         return carry
 
     lax.fori_loop(0, tile_x, layer, 0, unroll=4)
+    for copy in copies:
+        copy.wait()
+
+    def finish(x, carry):
+        light = 1.0 / density_now[x]
+        buoyancy[x] = light
+        scaled_lame[x] = time_step * lame_now[x]
+        scaled_shear[x] = time_step * shear_now[x]
+        for part in range(6):
+            value = light * gained[part, x]
+            if part < 3:
+                accel[part, x] = value
+            velocity[part, x + LAYERS, middle, :] += time_step * value
+        return carry
+
+    lax.fori_loop(0, tile_x, finish, 0, unroll=4)
 
 
 def stress_halo_terms(links, received, rim_added, waves, add):
@@ -378,30 +356,27 @@
         target[...] += time_step * light_face(buoyancy, dim, index) * term
 
     stress_halo_terms(links, received, rim_added, (0, 1), add)
-    for (axis, dim, first), send in zip(links, sends):
-        lower = is_lower(axis, first)
-        n, a, b = VELOCITY_ALONG[dim]
-
-        def put(plan):
-            for wave in range(2):
-                for slot, (part, index) in enumerate(plan):
-                    send[wave, slot] = face(velocity, 3 * wave + part, dim, index, True)[...]
-
-        @pl.when(lower)
-        def up():
-            put(((n, -2), (n, -1), (a, -1), (b, -1), (b, -1)))
-
-        @pl.when(jnp.logical_not(lower))
-        def down():
-            put(((n, 0), (a, 0), (a, 1), (b, 0), (b, 1)))
+    send_faces(velocity, 3, links, sends, [velocity_plan(dim) for dim in range(2)])
 
 
 def strain_kernel(links, *refs):
     count = len(links)
     received = refs[:count]
-    rim_added, buoyancy, velocity, accel, strain, gradient, accel_now = refs[count:]
+    rim_added, buoyancy, velocity, accel, strain, gradient = refs[count : count + 6]
+    outputs, (accel_now, sems) = refs[count + 6 : count + 8], refs[count + 8 :]
     tile_x, tile_y, _ = buoyancy.shape
     middle = pl.ds(ROWS, tile_y)
+    copies = [
+        pltpu.make_async_copy(
+            velocity.at[3 * wave + part, pl.ds(LAYERS, tile_x), middle, :],
+            outputs[wave].at[part],
+            sems.at[3 * wave + part],
+        )
+        for wave in range(2)
+        for part in range(3)
+    ]
+    for copy in copies:
+        copy.start()
     accel_now[...] = accel[...]
 
     def add(wave, part, dim, index, term):
@@ -430,6 +405,8 @@
         return carry
 
     lax.fori_loop(0, tile_x, layer, 0, unroll=4)
+    for copy in copies:
+        copy.wait()
 
 
 def new_stress(strain, stress, scaled_lame, scaled_shear, wave, x, tile_y):
@@ -470,17 +447,37 @@
     lax.fori_loop(0, tile_x, layer, 0, unroll=4)
 
 
-def output_kernel(velocity, strain, stress, scaled_lame, scaled_shear, forward, adjoint):
-    layers, tile_y = forward.shape[1:3]
-    begin = pl.program_id(0) * layers
-    for at in range(layers):
-        x = begin + at
-        for wave, out in enumerate((forward, adjoint)):
-            for part in range(3):
-                out[part, at] = velocity[3 * wave + part, x + LAYERS, pl.ds(ROWS, tile_y), :]
-            _, values = new_stress(strain, stress, scaled_lame, scaled_shear, wave, x, tile_y)
-            for part in range(6):
-                out[3 + part, at] = values[part]
+def output_kernel(chunk, strain, stress, scaled_lame, scaled_shear, *refs):
+    outputs, (values_now, sems) = refs[2:4], refs[4:]
+    tile_x, tile_y, _ = scaled_lame.shape
+    copies = []
+    for begin in range(0, tile_x, chunk):
+        for wave in range(2):
+            for x in range(begin, begin + chunk):
+                _, values = new_stress(strain, stress, scaled_lame, scaled_shear, wave, x, tile_y)
+                for part in range(6):
+                    values_now[6 * wave + part, x] = values[part]
+            layers = pl.ds(begin, chunk)
+            copy = pltpu.make_async_copy(
+                values_now.at[pl.ds(6 * wave, 6), layers],
+                outputs[wave].at[pl.ds(3, 6), layers],
+                sems.at[len(copies)],
+            )
+            copy.start()
+            copies.append(copy)
+    for copy in copies:
+        copy.wait()
+
+
+def sum_kernel(mine, other, total, total_now, sems):
+    copies = []
+    for part in range(mine.shape[0]):
+        total_now[part] = mine[part] + other[part]
+        copy = pltpu.make_async_copy(total_now.at[part], total.at[part], sems.at[part])
+        copy.start()
+        copies.append(copy)
+    for copy in copies:
+        copy.wait()
 
 
 def in_hbm(value):
@@ -526,19 +523,23 @@
         return [swap(send, axis, first) for (axis, _, first), send in zip(links, sends)]
 
     send_shapes = [buffers(dim) for _, dim, _ in links]
-    sends = pl.pallas_call(
-        functools.partial(pack_kernel, links),
-        out_shape=send_shapes,
-        in_specs=[hbm] * 2,
-        out_specs=[vmem] * len(links),
+    count = len(links)
+    receivers = receiver_cell.shape[-1]
+    *sends, stress, velocity, added = pl.pallas_call(
+        functools.partial(pack_kernel, links, width_y),
+        out_shape=send_shapes
+        + [padded(12), padded(6), pltpu.VMEM((tile_x * tile_y + rims, depth), jnp.float32)],
+        in_specs=[hbm] * 4,
+        out_specs=[vmem] * (count + 3),
         scratch_shapes=[
-            pltpu.VMEM((2, 3, 2, tile_x, 8, depth), jnp.float32),
-            pltpu.SemaphoreType.DMA((12 + 10 * len(links),)),
+            pltpu.VMEM((1, receivers), jnp.int32),
+            pltpu.VMEM((1, receivers), jnp.float32),
+            pltpu.SemaphoreType.DMA((14,)),
         ],
         compiler_params=params,
-        cost_estimate=cost(0, 10 * 2 * tile_x * depth * 4),
+        cost_estimate=cost(6 * 400 * 256 * 128, 12 * 4 * cells),
         name="pack",
-    )(in_hbm(forward), in_hbm(adjoint))
+    )(*(in_hbm(x) for x in (forward, adjoint, receiver_cell, residual_amp)))
     halos = exchange(sends)
 
     stress, velocity, accel, rim_added, buoyancy, scaled_lame, scaled_shear = pl.pallas_call(
@@ -552,29 +553,22 @@
             tile(),
             tile(),
         ],
-        in_specs=[hbm] * 3 + [smem] * 2 + [vmem] * 4,
+        in_specs=[hbm] * 5 + [smem] * 2 + [vmem] * 3,
         out_specs=[vmem] * 7,
-        scratch_shapes=[
-            pltpu.VMEM((2, tile_x * tile_y + rims, depth), jnp.float32),
-            tile(),
-            tile(),
-            tile(),
-            pltpu.SemaphoreType.DMA((3,)),
-        ],
+        input_output_aliases={8: 0, 9: 1},
+        scratch_shapes=[tile(6), tile(), tile(), tile(), pltpu.SemaphoreType.DMA((5,))],
         compiler_params=params,
-        cost_estimate=cost(200 * cells, 18 * 4 * cells),
+        cost_estimate=cost(200 * cells, 9 * 4 * cells),
         name="velocity",
     )(
-        *(in_hbm(x) for x in (lame_lambda, shear_modulus, density)),
+        *(in_hbm(x) for x in (forward, adjoint, lame_lambda, shear_modulus, density)),
         source_cell,
         source_amp,
-        receiver_cell,
-        residual_amp,
-        forward,
-        adjoint,
+        added,
+        stress,
+        velocity,
     )
 
-    count = len(links)
     velocity, *sends = pl.pallas_call(
         functools.partial(boundary_kernel, links),
         out_shape=[padded(6)] + send_shapes,
@@ -587,12 +581,13 @@
     )(*halos, rim_added, buoyancy, velocity)
     velocity_halos = exchange(sends)
 
-    strain, gradient = pl.pallas_call(
+    out_shape = jax.ShapeDtypeStruct(forward.shape, jnp.float32)
+    strain, gradient, forward_next, adjoint_next = pl.pallas_call(
         functools.partial(strain_kernel, links),
-        out_shape=[tile(12), tile(3)],
+        out_shape=[tile(12), tile(3), out_shape, out_shape],
         in_specs=[vmem] * (count + 4),
-        out_specs=[vmem] * 2,
-        scratch_shapes=[tile(3)],
+        out_specs=[vmem] * 2 + [hbm] * 2,
+        scratch_shapes=[tile(3), pltpu.SemaphoreType.DMA((6,))],
         compiler_params=params,
         cost_estimate=cost(200 * cells, 18 * 4 * cells),
         name="strain",
@@ -610,19 +605,29 @@
     )(*velocity_halos, stress, scaled_lame, scaled_shear, strain, gradient)
     other = lax.ppermute(gradient, "shot", [(0, 1), (1, 0)])
 
-    step = 4 if tile_x % 4 == 0 else 1
-    out_block = pl.BlockSpec((9, step, tile_y, depth), lambda i: (0, i, 0, 0))
+    chunk = 4 if tile_x % 4 == 0 else 1
     forward_next, adjoint_next = pl.pallas_call(
-        output_kernel,
-        grid=(tile_x // step,),
-        out_shape=[jax.ShapeDtypeStruct(forward.shape, jnp.float32)] * 2,
-        in_specs=[vmem] * 5,
-        out_specs=[out_block] * 2,
+        functools.partial(output_kernel, chunk),
+        out_shape=[out_shape, out_shape],
+        in_specs=[vmem] * 4 + [hbm] * 2,
+        out_specs=[hbm] * 2,
+        input_output_aliases={4: 0, 5: 1},
+        scratch_shapes=[tile(12), pltpu.SemaphoreType.DMA((2 * tile_x // chunk,))],
         compiler_params=params,
         cost_estimate=cost(60 * cells, 18 * 4 * cells),
         name="outputs",
-    )(velocity, strain, stress, scaled_lame, scaled_shear)
-    return forward_next[None], adjoint_next[None], gradient + other
+    )(strain, stress, scaled_lame, scaled_shear, forward_next, adjoint_next)
+    total = pl.pallas_call(
+        sum_kernel,
+        out_shape=jax.ShapeDtypeStruct((3, tile_x, tile_y, depth), jnp.float32),
+        in_specs=[vmem] * 2,
+        out_specs=hbm,
+        scratch_shapes=[tile(3), pltpu.SemaphoreType.DMA((3,))],
+        compiler_params=params,
+        cost_estimate=cost(3 * cells, 9 * 4 * cells),
+        name="sum",
+    )(gradient, other)
+    return forward_next[None], adjoint_next[None], total
 
 
 def solution(mesh):

time: 26 us -> 25 us (0.962)
  the two profiles are of different devices: /device:TPU:1 before, /device:TPU:0 now
where the time goes in v3:
time: 25 us; the launch traced here: 24.8 us
  starting transfers between devices  14 us (56%)
  Pallas kernels  6.91 us (28%)
  between operations  2.04 us (8%)
  waiting for transfers between devices  1.81 us (7%)
    ppermute x6, starting transfers between devices, swap(): return lax.ppermute(value, axis, pairs + [(j, i) for i, j in pairs])  13.9 us
    pallas_call x1, Pallas kernels, body(): pl.pallas_call(functools.partial(pack_kernel, links, width_y), out_shape=...  1.79 us
    pallas_call x1, Pallas kernels, body(): pl.pallas_call(functools.partial(velocity_kernel, width_y), out_shape=[pa...  1.51 us
    ppermute x6, waiting for transfers between devices, swap(): return lax.ppermute(value, axis, pairs + [(j, i) for i, j in pairs])  1.34 us
    pallas_call x1, Pallas kernels, body(): pl.pallas_call(functools.partial(output_kernel, chunk), out_shape=[out_sh...  1.23 us
    pallas_call x1, Pallas kernels, body(): pl.pallas_call(functools.partial(strain_kernel, links), out_shape=[tile(1...  1.06 us
    pallas_call x1, Pallas kernels, body(): pl.pallas_call(sum_kernel, out_shape=jax.ShapeDtypeStruct((3, tile_x, til...  0.78 us
  transfers between devices with their start and end apart: 7, of which 2 were waited for; matrix products, arithmetic and copies ran while one was open for 0% of the time, Pallas kernels for 15%

profile of v3, /device:TPU:0, one launch (start us, length us, event | category | flops | bytes accessed | tf_op | source)
XLA Modules:
  0.0 24.8 jit_solution(444890187538248111)
XLA Ops:
  0.6 1.8 %pack.1 = (f32[2,5,16,128]{3,2,1,0:T(8,128)S(1)}, f32[2,5,16,128]{3,2,1,0:T(8,128)S(1)}, f32[2,5,16,128]{3,2,1,0:T(8,128)S(1)}, f32[12,20,32,128]{3,2,1,0:T(8,12...) custom-call(f32[9,16,16,128]{3,2,1,0:T(8,128)} %bitcast.4, f32[9,16,16,128]{3,2,1,0:T(8,128)} %bitcast.6, ...), custom_call_target="tpu_custom_call" | custom-call | flops 78643200 | bytes 1572864 | tf_op jit(solution)/shard_map/pack/pallas_call | solution.py:528
  2.4 0.7 %collective-permute-start = (f32[2,5,16,128]{3,2,1,0:T(8,128)S(1)}, f32[2,5,16,128]{3,2,1,0:T(8,128)S(1)}, u32[]{:S(2)}, u32[]{:S(2)}) collective-permute-start(f32[2,5,16,128]{3,2,1,0:T(8,128)S(1)} %get-tuple-element.28), channel_id=1, source_target_pairs={{1,2},{3,4},{5,6},{2,1},{4,3},{6,5},{9,10},{11,12},{13,14},{10,9},... | collective-permute-start | bytes 245768 | tf_op jit(solution)/shard_map/ppermute | solution.py:36
  3.1 3.0 %collective-permute-start.1 = (f32[2,5,16,128]{3,2,1,0:T(8,128)S(1)}, f32[2,5,16,128]{3,2,1,0:T(8,128)S(1)}, u32[]{:S(2)}, u32[]{:S(2)}) collective-permute-start(f32[2,5,16,128]{3,2,1,0:T(8,128)S(1)} %get-tuple-element.29), channel_id=1, source_target_pairs={{0,8},{8,0},{1,9},{9,1},{2,10},{10,2},{3,11},{11,3},{4,12},{12,4},... | collective-permute-start | bytes 245768 | tf_op jit(solution)/shard_map/ppermute | solution.py:36
  6.1 4.3 %collective-permute-start.2 = (f32[2,5,16,128]{3,2,1,0:T(8,128)S(1)}, f32[2,5,16,128]{3,2,1,0:T(8,128)S(1)}, u32[]{:S(2)}, u32[]{:S(2)}) collective-permute-start(f32[2,5,16,128]{3,2,1,0:T(8,128)S(1)} %get-tuple-element.30), channel_id=1, source_target_pairs={{0,1},{2,3},{4,5},{6,7},{1,0},{3,2},{5,4},{7,6},{8,9},{10,11},{12,... | collective-permute-start | bytes 245768 | tf_op jit(solution)/shard_map/ppermute | solution.py:36
  11.7 1.5 %velocity.1 = (f32[12,20,32,128]{3,2,1,0:T(8,128)S(1)}, f32[6,20,32,128]{3,2,1,0:T(8,128)S(1)}, f32[3,16,16,128]{3,2,1,0:T(8,128)S(1)}, f32[2,2,3,16,128]{4,3,2,...) custom-call(f32[9,16,16,128]{3,2,1,0:T(8,128)} %bitcast.5, ...), custom_call_target="tpu_custom_call", output_to_operand_aliasing={{0}: (8, {}), {1}: (9, {})} | custom-call | flops 6553600 | bytes 1179648 | tf_op jit(solution)/shard_map/velocity/pallas_call | solution.py:545
  13.2 0.0 collective-permute-done.refs_0_
  13.2 0.0 collective-permute-done.1.refs_1_
  13.3 0.0 collective-permute-done.2.refs_2_
  13.3 0.3 %boundary.1 = (f32[6,20,32,128]{3,2,1,0:T(8,128)S(1)}, f32[2,5,16,128]{3,2,1,0:T(8,128)S(1)}, f32[2,5,16,128]{3,2,1,0:T(8,128)S(1)}, f32[2,5,16,128]{3,2,1,0:T(8,128)S(1)}) custom-call(f32[2,5,16,128]{3,2,1,0:T(8,128)S(1)} %collective-permute-done.refs_0_, f32[2,5,16,128]{3,2,1,0:T(8,128)S(1)} %collective-permute-done.1.refs_1_, ...), custom_call_target="tpu_custom_call", output_to_operand_aliasing={{0}: (5, {})} | custom-call | flops 32768 | bytes 163840 | tf_op jit(solution)/shard_map/boundary/pallas_call | solution.py:572
  13.5 0.7 %collective-permute-start.3 = (f32[2,5,16,128]{3,2,1,0:T(8,128)S(1)}, f32[2,5,16,128]{3,2,1,0:T(8,128)S(1)}, u32[]{:S(2)}, u32[]{:S(2)}) collective-permute-start(f32[2,5,16,128]{3,2,1,0:T(8,128)S(1)} %get-tuple-element.37), channel_id=1, source_target_pairs={{1,2},{3,4},{5,6},{2,1},{4,3},{6,5},{9,10},{11,12},{13,14},{10,9},... | collective-permute-start | bytes 245768 | tf_op jit(solution)/shard_map/ppermute | solution.py:36
  14.2 0.6 %collective-permute-start.4 = (f32[2,5,16,128]{3,2,1,0:T(8,128)S(1)}, f32[2,5,16,128]{3,2,1,0:T(8,128)S(1)}, u32[]{:S(2)}, u32[]{:S(2)}) collective-permute-start(f32[2,5,16,128]{3,2,1,0:T(8,128)S(1)} %get-tuple-element.38), channel_id=1, source_target_pairs={{0,8},{8,0},{1,9},{9,1},{2,10},{10,2},{3,11},{11,3},{4,12},{12,4},... | collective-permute-start | bytes 245768 | tf_op jit(solution)/shard_map/ppermute | solution.py:36
  14.8 4.7 %collective-permute-start.5 = (f32[2,5,16,128]{3,2,1,0:T(8,128)S(1)}, f32[2,5,16,128]{3,2,1,0:T(8,128)S(1)}, u32[]{:S(2)}, u32[]{:S(2)}) collective-permute-start(f32[2,5,16,128]{3,2,1,0:T(8,128)S(1)} %get-tuple-element.39), channel_id=1, source_target_pairs={{0,1},{2,3},{4,5},{6,7},{1,0},{3,2},{5,4},{7,6},{8,9},{10,11},{12,... | collective-permute-start | bytes 245768 | tf_op jit(solution)/shard_map/ppermute | solution.py:36
  19.5 1.1 %strain.1 = (f32[12,16,16,128]{3,2,1,0:T(8,128)S(1)}, f32[3,16,16,128]{3,2,1,0:T(8,128)S(1)}, f32[9,16,16,128]{3,2,1,0:T(8,128)}, f32[9,16,16,128]{3,2,1,0:T(8,128)}) custom-call(f32[2,5,16,128]{3,2,1,0:T(8,128)S(1)} %collective-permute-done.refs_0_, f32[2,5,16,128]{3,2,1,0:T(8,128)S(1)} %collective-permute-done.1.refs_1_, ...), custom_call_target="tpu_custom_call" | custom-call | flops 6553600 | bytes 2359296 | tf_op jit(solution)/shard_map/strain/pallas_call | solution.py:585
  20.6 0.0 collective-permute-done.3.refs_0_
  20.6 0.0 collective-permute-done.4.refs_1_
  20.6 1.3 %collective-permute-done.5.refs_2_ = f32[2,5,16,128]{3,2,1,0:T(8,128)S(1)} collective-permute-done((f32[2,5,16,128]{3,2,1,0:T(8,128)S(1)}, f32[2,5,16,128]{3,2,1,0:T(8,128)S(1)}, u32[]{:S(2)}, u32[]{:S(2)}) %collective-permute-start.5) | collective-permute-done | bytes 81952 | tf_op jit(solution)/shard_map/ppermute | solution.py:36
  21.9 0.3 %gradient.1 = (f32[12,16,16,128]{3,2,1,0:T(8,128)S(1)}, f32[3,16,16,128]{3,2,1,0:T(8,128)S(1)}) custom-call(f32[2,5,16,128]{3,2,1,0:T(8,128)S(1)} %collective-permute-done.3.refs_0_, f32[2,5,16,128]{3,2,1,0:T(8,128)S(1)} %collective-permute-done.4.refs_1_, ...), custom_call_target="tpu_custom_call", output_to_operand_aliasing={{0}: (6, {}), {1}: (7, {})} | custom-call | flops 983040 | bytes 262144 | tf_op jit(solution)/shard_map/gradient/pallas_call | solution.py:596
  22.2 0.1 collective-permute-start.6
  22.3 1.2 %outputs.1 = (f32[9,16,16,128]{3,2,1,0:T(8,128)}, f32[9,16,16,128]{3,2,1,0:T(8,128)}) custom-call(f32[12,16,16,128]{3,2,1,0:T(8,128)S(1)} %get-tuple-element.47.strain, f32[12,20,32,128]{3,2,1,0:T(8,128)S(1)} %get-tuple-element.40.refs_3_.stress, ...), custom_call_target="tpu_custom_call", output_to_operand_aliasing={{0}: (4, {}), {1}: (5, {})} | custom-call | flops 1966080 | bytes 2359296 | tf_op jit(solution)/shard_map/outputs/pallas_call | solution.py:609
  23.5 0.5 %collective-permute-done.6.other = f32[3,16,16,128]{3,2,1,0:T(8,128)S(1)} collective-permute-done((f32[3,16,16,128]{3,2,1,0:T(8,128)S(1)}, f32[3,16,16,128]{3,2,1,0:T(8,128)S(1)}, u32[]{:S(2)}, u32[]{:S(2)}) %collective-permute-start.6) | collective-permute-done | bytes 393248 | tf_op jit(solution)/shard_map/ppermute | solution.py:606
  24.0 0.8 %sum.1 = f32[3,16,16,128]{3,2,1,0:T(8,128)} custom-call(f32[3,16,16,128]{3,2,1,0:T(8,128)S(1)} %get-tuple-element.52.mine, f32[3,16,16,128]{3,2,1,0:T(8,128)S(1)} %collective-permute-done.6.other), custom_call_target="tpu_custom_call" | custom-call | flops 98304 | bytes 1179648 | tf_op jit(solution)/shard_map/sum/pallas_call | solution.py:620
Async XLA Ops:
  2.4 10.8 %collective-permute-start = (f32[2,5,16,128]{3,2,1,0:T(8,128)S(1)}, f32[2,5,16,128]{3,2,1,0:T(8,128)S(1)}, u32[]{:S(2)}, u32[]{:S(2)}) collective-permute-start(f32[2,5,16,128]{3,2,1,0:T(8,128)S(1)} %get-tuple-element.28), channel_id=1, source_target_pairs={{1,2},{3,4},{5,6},{2,1},{4,3},{6,5},{9,10},{11,12},{13,14},{10,9},... | collective-permute-start | bytes 245768 | tf_op jit(solution)/shard_map/ppermute | solution.py:36
  3.1 10.1 %collective-permute-start.1 = (f32[2,5,16,128]{3,2,1,0:T(8,128)S(1)}, f32[2,5,16,128]{3,2,1,0:T(8,128)S(1)}, u32[]{:S(2)}, u32[]{:S(2)}) collective-permute-start(f32[2,5,16,128]{3,2,1,0:T(8,128)S(1)} %get-tuple-element.29), channel_id=1, source_target_pairs={{0,8},{8,0},{1,9},{9,1},{2,10},{10,2},{3,11},{11,3},{4,12},{12,4},... | collective-permute-start | bytes 245768 | tf_op jit(solution)/shard_map/ppermute | solution.py:36
  6.1 7.1 %collective-permute-start.2 = (f32[2,5,16,128]{3,2,1,0:T(8,128)S(1)}, f32[2,5,16,128]{3,2,1,0:T(8,128)S(1)}, u32[]{:S(2)}, u32[]{:S(2)}) collective-permute-start(f32[2,5,16,128]{3,2,1,0:T(8,128)S(1)} %get-tuple-element.30), channel_id=1, source_target_pairs={{0,1},{2,3},{4,5},{6,7},{1,0},{3,2},{5,4},{7,6},{8,9},{10,11},{12,... | collective-permute-start | bytes 245768 | tf_op jit(solution)/shard_map/ppermute | solution.py:36
  13.5 7.0 %collective-permute-start.3 = (f32[2,5,16,128]{3,2,1,0:T(8,128)S(1)}, f32[2,5,16,128]{3,2,1,0:T(8,128)S(1)}, u32[]{:S(2)}, u32[]{:S(2)}) collective-permute-start(f32[2,5,16,128]{3,2,1,0:T(8,128)S(1)} %get-tuple-element.37), channel_id=1, source_target_pairs={{1,2},{3,4},{5,6},{2,1},{4,3},{6,5},{9,10},{11,12},{13,14},{10,9},... | collective-permute-start | bytes 245768 | tf_op jit(solution)/shard_map/ppermute | solution.py:36
  14.2 6.4 %collective-permute-start.4 = (f32[2,5,16,128]{3,2,1,0:T(8,128)S(1)}, f32[2,5,16,128]{3,2,1,0:T(8,128)S(1)}, u32[]{:S(2)}, u32[]{:S(2)}) collective-permute-start(f32[2,5,16,128]{3,2,1,0:T(8,128)S(1)} %get-tuple-element.38), channel_id=1, source_target_pairs={{0,8},{8,0},{1,9},{9,1},{2,10},{10,2},{3,11},{11,3},{4,12},{12,4},... | collective-permute-start | bytes 245768 | tf_op jit(solution)/shard_map/ppermute | solution.py:36
  14.8 7.1 %collective-permute-start.5 = (f32[2,5,16,128]{3,2,1,0:T(8,128)S(1)}, f32[2,5,16,128]{3,2,1,0:T(8,128)S(1)}, u32[]{:S(2)}, u32[]{:S(2)}) collective-permute-start(f32[2,5,16,128]{3,2,1,0:T(8,128)S(1)} %get-tuple-element.39), channel_id=1, source_target_pairs={{0,1},{2,3},{4,5},{6,7},{1,0},{3,2},{5,4},{7,6},{8,9},{10,11},{12,... | collective-permute-start | bytes 245768 | tf_op jit(solution)/shard_map/ppermute | solution.py:36
  22.2 1.8 %collective-permute-start.6 = (f32[3,16,16,128]{3,2,1,0:T(8,128)S(1)}, f32[3,16,16,128]{3,2,1,0:T(8,128)S(1)}, u32[]{:S(2)}, u32[]{:S(2)}) collective-permute-start(f32[3,16,16,128]{3,2,1,0:T(8,128)S(1)} %get-tuple-element.52.mine), channel_id=1, source_target_pairs={{0,16},{16,0},{1,17},{17,1},{2,18},{18,2},{3,19},{19,3},{4,20},{20... | collective-permute-start | bytes 1179656 | tf_op jit(solution)/shard_map/ppermute | solution.py:606

commit v4 on v3

--- a/solution.py
+++ b/solution.py
@@ -76,58 +76,22 @@
     )
 
 
-def pack_kernel(links, width_y, *refs):
-    fields, (receiver_cell, residual_amp) = refs[:2], refs[2:4]
-    sends = refs[4 : 4 + len(links)]
-    stress, velocity, added, cells_now, amps_now, sems = refs[4 + len(links) :]
-    _, tile_x, tile_y, depth = fields[0].shape
-    small = [
-        pltpu.make_async_copy(receiver_cell, cells_now, sems.at[0]),
-        pltpu.make_async_copy(residual_amp, amps_now, sems.at[1]),
-    ]
-    large = [
-        pltpu.make_async_copy(
-            fields[wave].at[3 + part],
-            stress.at[6 * wave + part, pl.ds(LAYERS, tile_x), pl.ds(ROWS, tile_y), :],
-            sems.at[2 + 6 * wave + part],
-        )
-        for wave in range(2)
-        for part in range(6)
-    ]
-    for copy in small + large:
-        copy.start()
-    clear_rim(stress, tile_x, tile_y)
-    clear_rim(velocity, tile_x, tile_y)
-    columns = column_ids(tile_x, tile_y, width_y, depth)
-    for copy in small:
+def pack_kernel(links, forward, adjoint, *refs):
+    sends, sems = refs[: len(links)], refs[-1]
+    tile = forward.shape[1:3]
+    copies = []
+    for (axis, dim, first), send in zip(links, sends):
+        lower = is_lower(axis, first)
+        for slot, ((up_part, up_at), (low_part, low_at)) in enumerate(zip(*stress_plan(dim))):
+            part = 3 + jnp.where(lower, low_part, up_part)
+            at = jnp.where(lower, low_at % tile[dim], up_at % tile[dim])
+            for wave, fields in enumerate((forward, adjoint)):
+                source = fields.at[part, at] if dim == 0 else fields.at[part, :, at, :]
+                copy = pltpu.make_async_copy(source, send.at[wave, slot], sems.at[len(copies)])
+                copy.start()
+                copies.append(copy)
+    for copy in copies:
         copy.wait()
-    where = cells_now[...]
-    receivers = where.shape[-1]
-    column = lax.div(where, depth)
-    depth_of = where - column * depth
-    column_hot = jnp.concatenate(
-        [
-            (columns == column[:, begin : begin + depth]).astype(jnp.bfloat16)
-            for begin in range(0, receivers, depth)
-        ],
-        axis=1,
-    )
-    level = lax.broadcasted_iota(jnp.int32, (depth, receivers), 0)
-    rest = jnp.where(level == depth_of, amps_now[...], 0.0)
-    total = jnp.zeros(columns.shape, jnp.float32)
-    for _ in range(3):
-        part = rest.astype(jnp.bfloat16)
-        rest = rest - part.astype(jnp.float32)
-        total = total + lax.dot_general(
-            column_hot,
-            part,
-            (((1,), (1,)), ((), ())),
-            preferred_element_type=jnp.float32,
-        )
-    added[...] = total
-    for copy in large:
-        copy.wait()
-    send_faces(stress, 6, links, sends, [stress_plan(dim) for dim in range(2)])
 
 
 def column_ids(tile_x, tile_y, width_y, lanes):
@@ -189,52 +153,118 @@
     return differ(at(0), at(1), at(2), at(-1)) if upward else differ(at(-1), at(0), at(1), at(-2))
 
 
-def clear_rim(ref, tile_x, tile_y):
-    parts, layers, rows, depth = ref.shape
-    for part in range(parts):
-        for layer in (*range(LAYERS), *range(LAYERS + tile_x, layers)):
-            ref[part, layer] = jnp.zeros((rows, depth), jnp.float32)
-        for row in (0, ROWS + tile_y):
-            ref[part, pl.ds(LAYERS, tile_x), pl.ds(row, ROWS), :] = jnp.zeros(
+def clear_rim(ref, parts_x, parts_y):
+    _, layers, rows, depth = ref.shape
+    tile_x, tile_y = layers - 2 * LAYERS, rows - 2 * ROWS
+    for part in parts_x:
+        for begin in (0, LAYERS + tile_x):
+            ref[part, pl.ds(begin, LAYERS), pl.ds(ROWS, tile_y), :] = jnp.zeros(
+                (LAYERS, tile_y, depth), jnp.float32
+            )
+    for part in parts_y:
+        for begin in (0, ROWS + tile_y):
+            ref[part, pl.ds(LAYERS, tile_x), pl.ds(begin, ROWS), :] = jnp.zeros(
                 (tile_x, ROWS, depth), jnp.float32
             )
 
 
-def velocity_kernel(width_y, *refs):
-    forward, adjoint, lame, shear, density, source_cell, source_amp, received, _, _ = refs[:10]
-    stress, velocity, accel, rim_added, buoyancy, scaled_lame, scaled_shear = refs[10:17]
-    gained, lame_now, shear_now, density_now, sems = refs[17:]
+def receiver_sum(cells, amps, columns):
+    depth, receivers = columns.shape[-1], cells.shape[-1]
+    column = lax.div(cells, depth)
+    level = cells - column * depth
+    column_hot = jnp.concatenate(
+        [
+            (columns == column[:, begin : begin + depth]).astype(jnp.bfloat16)
+            for begin in range(0, receivers, depth)
+        ],
+        axis=1,
+    )
+    levels = lax.broadcasted_iota(jnp.int32, (depth, receivers), 0)
+    rest = jnp.where(levels == level, amps, 0.0)
+    total = jnp.zeros(columns.shape, jnp.float32)
+    for _ in range(3):
+        part = rest.astype(jnp.bfloat16)
+        rest = rest - part.astype(jnp.float32)
+        total = total + lax.dot_general(
+            column_hot,
+            part,
+            (((1,), (1,)), ((), ())),
+            preferred_element_type=jnp.float32,
+        )
+    return total
+
+
+def velocity_kernel(
+    width_y,
+    lame,
+    shear,
+    density,
+    source_cell,
+    source_amp,
+    receiver_cell,
+    residual_amp,
+    forward,
+    adjoint,
+    stress,
+    velocity,
+    accel,
+    rim_added,
+    buoyancy,
+    scaled_lame,
+    scaled_shear,
+    added,
+    lame_now,
+    shear_now,
+    density_now,
+    sems,
+):
     tile_x, tile_y, depth = density.shape
-    cells = tile_x * tile_y
-    middle = pl.ds(ROWS, tile_y)
     copies = [
         pltpu.make_async_copy(source, target, sems.at[at])
         for at, (source, target) in enumerate((
             (density, density_now),
             (lame, lame_now),
             (shear, shear_now),
-            (forward.at[pl.ds(0, 3)], velocity.at[pl.ds(0, 3), pl.ds(LAYERS, tile_x), middle, :]),
-            (adjoint.at[pl.ds(0, 3)], velocity.at[pl.ds(3, 3), pl.ds(LAYERS, tile_x), middle, :]),
         ))
     ]
     for copy in copies:
         copy.start()
+    cells = tile_x * tile_y
+    middle = pl.ds(ROWS, tile_y)
     columns = column_ids(tile_x, tile_y, width_y, depth)
     lane = lax.broadcasted_iota(jnp.int32, columns.shape, 1)
-    sourced = jnp.where(columns * depth + lane == source_cell[0], source_amp[0], 0.0)
-    for wave, added in enumerate((sourced, received[...])):
+    added[0] = jnp.where(columns * depth + lane == source_cell[0], source_amp[0], 0.0)
+    added[1] = receiver_sum(receiver_cell[...], residual_amp[...], columns)
+    for wave in range(2):
+        clear_rim(
+            stress, *([6 * wave + part for part in STRESS_ALONG[dim]] for dim in range(2))
+        )
         for layer in range(3):
-            begin = cells + layer * tile_y
-            rim_added[wave, 0, layer] = added[begin : begin + tile_y]
+            rim_added[wave, 0, layer] = added[wave, pl.ds(cells + layer * tile_y, tile_y), :]
             begin = cells + 3 * tile_y + layer * tile_x
-            rim_added[wave, 1, layer] = added[begin : begin + tile_x]
-        for x in range(tile_x):
-            extra = added[x * tile_y : (x + 1) * tile_y]
-            for part in range(3):
-                stress[6 * wave + part, x + LAYERS, middle, :] += extra
+            rim_added[wave, 1, layer] = added[wave, pl.ds(begin, tile_x), :]
+
+    for copy in copies:
+        copy.wait()
+
+    def fill(x, carry):
+        for wave, fields in enumerate((forward, adjoint)):
+            extra = added[wave, pl.ds(pl.multiple_of(x * tile_y, 8), tile_y), :]
+            for part in range(6):
+                value = fields[3 + part, x]
+                stress[6 * wave + part, x + LAYERS, middle, :] = (
+                    value + extra if part < 3 else value
+                )
+        buoyancy[x] = 1.0 / density_now[x]
+        scaled_lame[x] = time_step * lame_now[x]
+        scaled_shear[x] = time_step * shear_now[x]
+        return carry
+
+    lax.fori_loop(0, tile_x, fill, 0, unroll=4)
 
     def layer(x, carry):
-        for wave in range(2):
+        light = buoyancy[x]
+        for wave, fields in enumerate((forward, adjoint)):
             xx, yy, zz, xy, xz, yz = range(6 * wave, 6 * wave + 6)
             values = (
                 along_x(stress, xx, x, tile_y, True)
@@ -248,26 +278,15 @@
                 + along_z(stress, zz, x, tile_y, True),
             )
             for part, value in enumerate(values):
-                gained[3 * wave + part, x] = value
+                value = light * value
+                if wave == 0:
+                    accel[part, x] = value
+                velocity[3 * wave + part, x + LAYERS, middle, :] = (
+                    fields[part, x] + time_step * value
+                )
         return carry
 
     lax.fori_loop(0, tile_x, layer, 0, unroll=4)
-    for copy in copies:
-        copy.wait()
-
-    def finish(x, carry):
-        light = 1.0 / density_now[x]
-        buoyancy[x] = light
-        scaled_lame[x] = time_step * lame_now[x]
-        scaled_shear[x] = time_step * shear_now[x]
-        for part in range(6):
-            value = light * gained[part, x]
-            if part < 3:
-                accel[part, x] = value
-            velocity[part, x + LAYERS, middle, :] += time_step * value
-        return carry
-
-    lax.fori_loop(0, tile_x, finish, 0, unroll=4)
 
 
 def stress_halo_terms(links, received, rim_added, waves, add):
@@ -362,8 +381,8 @@
 def strain_kernel(links, *refs):
     count = len(links)
     received = refs[:count]
-    rim_added, buoyancy, velocity, accel, strain, gradient = refs[count : count + 6]
-    outputs, (accel_now, sems) = refs[count + 6 : count + 8], refs[count + 8 :]
+    rim_added, buoyancy, _, accel, strain, gradient, velocity = refs[count : count + 7]
+    outputs, (accel_now, sems) = refs[count + 7 : count + 9], refs[count + 9 :]
     tile_x, tile_y, _ = buoyancy.shape
     middle = pl.ds(ROWS, tile_y)
     copies = [
@@ -377,6 +396,7 @@
     ]
     for copy in copies:
         copy.start()
+    clear_rim(velocity, range(6), range(6))
     accel_now[...] = accel[...]
 
     def add(wave, part, dim, index, term):
@@ -506,7 +526,6 @@
     width_y = tile_y * sizes["ty"]
     links = links_of(sizes)
     cells = tile_x * tile_y * depth
-    rims = 3 * tile_x + 3 * tile_y
 
     def buffers(dim):
         return pltpu.VMEM((2, SLOTS, tile_y if dim == 0 else tile_x, depth), jnp.float32)
@@ -524,22 +543,16 @@
 
     send_shapes = [buffers(dim) for _, dim, _ in links]
     count = len(links)
-    receivers = receiver_cell.shape[-1]
-    *sends, stress, velocity, added = pl.pallas_call(
-        functools.partial(pack_kernel, links, width_y),
-        out_shape=send_shapes
-        + [padded(12), padded(6), pltpu.VMEM((tile_x * tile_y + rims, depth), jnp.float32)],
-        in_specs=[hbm] * 4,
-        out_specs=[vmem] * (count + 3),
-        scratch_shapes=[
-            pltpu.VMEM((1, receivers), jnp.int32),
-            pltpu.VMEM((1, receivers), jnp.float32),
-            pltpu.SemaphoreType.DMA((14,)),
-        ],
+    sends = pl.pallas_call(
+        functools.partial(pack_kernel, links),
+        out_shape=send_shapes,
+        in_specs=[hbm] * 2,
+        out_specs=[vmem] * count,
+        scratch_shapes=[pltpu.SemaphoreType.DMA((2 * SLOTS * count,))],
         compiler_params=params,
-        cost_estimate=cost(6 * 400 * 256 * 128, 12 * 4 * cells),
+        cost_estimate=cost(0, 2 * SLOTS * count * tile_x * depth * 4),
         name="pack",
-    )(*(in_hbm(x) for x in (forward, adjoint, receiver_cell, residual_amp)))
+    )(in_hbm(forward), in_hbm(adjoint))
     halos = exchange(sends)
 
     stress, velocity, accel, rim_added, buoyancy, scaled_lame, scaled_shear = pl.pallas_call(
@@ -553,20 +566,26 @@
             tile(),
             tile(),
         ],
-        in_specs=[hbm] * 5 + [smem] * 2 + [vmem] * 3,
+        in_specs=[hbm] * 3 + [smem] * 2 + [vmem] * 4,
         out_specs=[vmem] * 7,
-        input_output_aliases={8: 0, 9: 1},
-        scratch_shapes=[tile(6), tile(), tile(), tile(), pltpu.SemaphoreType.DMA((5,))],
+        scratch_shapes=[
+            pltpu.VMEM((2, tile_x * tile_y + 3 * (tile_x + tile_y), depth), jnp.float32),
+            tile(),
+            tile(),
+            tile(),
+            pltpu.SemaphoreType.DMA((3,)),
+        ],
         compiler_params=params,
-        cost_estimate=cost(200 * cells, 9 * 4 * cells),
+        cost_estimate=cost(200 * cells, 18 * 4 * cells),
         name="velocity",
     )(
-        *(in_hbm(x) for x in (forward, adjoint, lame_lambda, shear_modulus, density)),
+        *(in_hbm(x) for x in (lame_lambda, shear_modulus, density)),
         source_cell,
         source_amp,
-        added,
-        stress,
-        velocity,
+        receiver_cell,
+        residual_amp,
+        forward,
+        adjoint,
     )
 
     velocity, *sends = pl.pallas_call(
@@ -582,11 +601,12 @@
     velocity_halos = exchange(sends)
 
     out_shape = jax.ShapeDtypeStruct(forward.shape, jnp.float32)
-    strain, gradient, forward_next, adjoint_next = pl.pallas_call(
+    strain, gradient, _, forward_next, adjoint_next = pl.pallas_call(
         functools.partial(strain_kernel, links),
-        out_shape=[tile(12), tile(3), out_shape, out_shape],
+        out_shape=[tile(12), tile(3), padded(6), out_shape, out_shape],
         in_specs=[vmem] * (count + 4),
-        out_specs=[vmem] * 2 + [hbm] * 2,
+        out_specs=[vmem] * 3 + [hbm] * 2,
+        input_output_aliases={count + 2: 2},
         scratch_shapes=[tile(3), pltpu.SemaphoreType.DMA((6,))],
         compiler_params=params,
         cost_estimate=cost(200 * cells, 18 * 4 * cells),

time: 25 us -> 24.9 us (level)
  Pallas kernels: 6.91 us -> 7.23 us
  starting transfers between devices: 14 us -> 13.7 us
    pallas_call x1, Pallas kernels: 1.51 us -> 2.21 us  [body(): pl.pallas_call(functools.partial(velocity_kernel, width_y), out_shape=[pa...]
    pallas_call x1, Pallas kernels: 1.79 us -> 1.26 us  [body(): pl.pallas_call(functools.partial(pack_kernel, links), out_shape=send_shap...]
    ppermute x6, starting transfers between devices: 13.9 us -> 13.6 us  [swap(): return lax.ppermute(value, axis, pairs + [(j, i) for i, j in pairs])]
  transfers between devices with their start and end apart: 7 -> 7, of which waited for: 2 -> 2; matrix products, arithmetic and copies ran while one was open for 0% -> 0% of each run, Pallas kernels for 15% -> 19%
where the time goes in v4:
time: 24.9 us; the launch traced here: 24.7 us
  starting transfers between devices  13.7 us (55%)
  Pallas kernels  7.23 us (29%)
  between operations  2.1 us (8%)
  waiting for transfers between devices  1.7 us (7%)
    ppermute x6, starting transfers between devices, swap(): return lax.ppermute(value, axis, pairs + [(j, i) for i, j in pairs])  13.6 us
    pallas_call x1, Pallas kernels, body(): pl.pallas_call(functools.partial(velocity_kernel, width_y), out_shape=[pa...  2.21 us
    pallas_call x1, Pallas kernels, body(): pl.pallas_call(functools.partial(pack_kernel, links), out_shape=send_shap...  1.26 us
    pallas_call x1, Pallas kernels, body(): pl.pallas_call(functools.partial(output_kernel, chunk), out_shape=[out_sh...  1.24 us
    ppermute x6, waiting for transfers between devices, swap(): return lax.ppermute(value, axis, pairs + [(j, i) for i, j in pairs])  1.24 us
    pallas_call x1, Pallas kernels, body(): pl.pallas_call(functools.partial(strain_kernel, links), out_shape=[tile(1...  1.16 us
    pallas_call x1, Pallas kernels, body(): pl.pallas_call(sum_kernel, out_shape=jax.ShapeDtypeStruct((3, tile_x, til...  0.78 us
  transfers between devices with their start and end apart: 7, of which 2 were waited for; matrix products, arithmetic and copies ran while one was open for 0% of the time, Pallas kernels for 19%

profile of v4, /device:TPU:0, one launch (start us, length us, event | category | flops | bytes accessed | tf_op | source)
XLA Modules:
  0.0 24.7 jit_solution(7242063122625645793)
XLA Ops:
  0.6 0.0 copy-start.1
  0.6 0.0 copy-start
  0.7 0.0 copy-start.3
  0.7 0.0 copy-start.2
  0.7 1.3 %pack.1 = (f32[2,5,16,128]{3,2,1,0:T(8,128)S(1)}, f32[2,5,16,128]{3,2,1,0:T(8,128)S(1)}, f32[2,5,16,128]{3,2,1,0:T(8,128)S(1)}) custom-call(f32[9,16,16,128]{3,2,1,0:T(8,128)} %bitcast.4, f32[9,16,16,128]{3,2,1,0:T(8,128)} %bitcast.6), custom_call_target="tpu_custom_call" | custom-call | bytes 245760 | tf_op jit(solution)/shard_map/pack/pallas_call | solution.py:546
  1.9 0.7 %collective-permute-start = (f32[2,5,16,128]{3,2,1,0:T(8,128)S(1)}, f32[2,5,16,128]{3,2,1,0:T(8,128)S(1)}, u32[]{:S(2)}, u32[]{:S(2)}) collective-permute-start(f32[2,5,16,128]{3,2,1,0:T(8,128)S(1)} %get-tuple-element.25), channel_id=1, source_target_pairs={{1,2},{3,4},{5,6},{2,1},{4,3},{6,5},{9,10},{11,12},{13,14},{10,9},... | collective-permute-start | bytes 245768 | tf_op jit(solution)/shard_map/ppermute | solution.py:36
  2.6 3.0 %collective-permute-start.1 = (f32[2,5,16,128]{3,2,1,0:T(8,128)S(1)}, f32[2,5,16,128]{3,2,1,0:T(8,128)S(1)}, u32[]{:S(2)}, u32[]{:S(2)}) collective-permute-start(f32[2,5,16,128]{3,2,1,0:T(8,128)S(1)} %get-tuple-element.26), channel_id=1, source_target_pairs={{0,8},{8,0},{1,9},{9,1},{2,10},{10,2},{3,11},{11,3},{4,12},{12,4},... | collective-permute-start | bytes 245768 | tf_op jit(solution)/shard_map/ppermute | solution.py:36
  5.6 4.3 %collective-permute-start.2 = (f32[2,5,16,128]{3,2,1,0:T(8,128)S(1)}, f32[2,5,16,128]{3,2,1,0:T(8,128)S(1)}, u32[]{:S(2)}, u32[]{:S(2)}) collective-permute-start(f32[2,5,16,128]{3,2,1,0:T(8,128)S(1)} %get-tuple-element.27), channel_id=1, source_target_pairs={{0,1},{2,3},{4,5},{6,7},{1,0},{3,2},{5,4},{7,6},{8,9},{10,11},{12,... | collective-permute-start | bytes 245768 | tf_op jit(solution)/shard_map/ppermute | solution.py:36
  11.2 0.0 copy-done.1
  11.2 0.0 copy-done
  11.2 0.0 copy-done.3
  11.3 0.0 copy-done.2
  11.3 2.2 %velocity.1 = (f32[12,20,32,128]{3,2,1,0:T(8,128)S(1)}, f32[6,20,32,128]{3,2,1,0:T(8,128)S(1)}, f32[3,16,16,128]{3,2,1,0:T(8,128)S(1)}, f32[2,2,3,16,128]{4,3,2,...) custom-call(f32[16,16,128]{2,1,0:T(8,128)} %lame.1, ...), custom_call_target="tpu_custom_call" | custom-call | flops 6553600 | bytes 2359296 | tf_op jit(solution)/shard_map/velocity/pallas_call | solution.py:558
  13.5 0.0 collective-permute-done.refs_0_
  13.5 0.0 collective-permute-done.1.refs_1_
  13.5 0.0 collective-permute-done.2.refs_2_
  13.5 0.3 %boundary.1 = (f32[6,20,32,128]{3,2,1,0:T(8,128)S(1)}, f32[2,5,16,128]{3,2,1,0:T(8,128)S(1)}, f32[2,5,16,128]{3,2,1,0:T(8,128)S(1)}, f32[2,5,16,128]{3,2,1,0:T(8,128)S(1)}) custom-call(f32[2,5,16,128]{3,2,1,0:T(8,128)S(1)} %collective-permute-done.refs_0_, f32[2,5,16,128]{3,2,1,0:T(8,128)S(1)} %collective-permute-done.1.refs_1_, ...), custom_call_target="tpu_custom_call", output_to_operand_aliasing={{0}: (5, {})} | custom-call | flops 32768 | bytes 163840 | tf_op jit(solution)/shard_map/boundary/pallas_call | solution.py:591
  13.8 0.7 %collective-permute-start.3 = (f32[2,5,16,128]{3,2,1,0:T(8,128)S(1)}, f32[2,5,16,128]{3,2,1,0:T(8,128)S(1)}, u32[]{:S(2)}, u32[]{:S(2)}) collective-permute-start(f32[2,5,16,128]{3,2,1,0:T(8,128)S(1)} %get-tuple-element.31), channel_id=1, source_target_pairs={{1,2},{3,4},{5,6},{2,1},{4,3},{6,5},{9,10},{11,12},{13,14},{10,9},... | collective-permute-start | bytes 245768 | tf_op jit(solution)/shard_map/ppermute | solution.py:36
  14.5 0.6 %collective-permute-start.4 = (f32[2,5,16,128]{3,2,1,0:T(8,128)S(1)}, f32[2,5,16,128]{3,2,1,0:T(8,128)S(1)}, u32[]{:S(2)}, u32[]{:S(2)}) collective-permute-start(f32[2,5,16,128]{3,2,1,0:T(8,128)S(1)} %get-tuple-element.32), channel_id=1, source_target_pairs={{0,8},{8,0},{1,9},{9,1},{2,10},{10,2},{3,11},{11,3},{4,12},{12,4},... | collective-permute-start | bytes 245768 | tf_op jit(solution)/shard_map/ppermute | solution.py:36
  15.0 4.4 %collective-permute-start.5 = (f32[2,5,16,128]{3,2,1,0:T(8,128)S(1)}, f32[2,5,16,128]{3,2,1,0:T(8,128)S(1)}, u32[]{:S(2)}, u32[]{:S(2)}) collective-permute-start(f32[2,5,16,128]{3,2,1,0:T(8,128)S(1)} %get-tuple-element.33), channel_id=1, source_target_pairs={{0,1},{2,3},{4,5},{6,7},{1,0},{3,2},{5,4},{7,6},{8,9},{10,11},{12,... | collective-permute-start | bytes 245768 | tf_op jit(solution)/shard_map/ppermute | solution.py:36
  19.4 1.2 %strain.1 = (f32[12,16,16,128]{3,2,1,0:T(8,128)S(1)}, f32[3,16,16,128]{3,2,1,0:T(8,128)S(1)}, f32[6,20,32,128]{3,2,1,0:T(8,128)S(1)}, f32[9,16,16,128]{3,2,1,0:T(8,128)}, f32[9,16,16,128]{3,2,1,0:T(8,128)}) custom-call(f32[2,5,16,128]{3,2,1,0:T(8,128)S(1)} %collective-permute-done.refs_0_, ...), custom_call_target="tpu_custom_call", output_to_operand_aliasing={{2}: (5, {})} | custom-call | flops 6553600 | bytes 2359296 | tf_op jit(solution)/shard_map/strain/pallas_call | solution.py:604
  20.6 0.0 collective-permute-done.3.refs_0_
  20.6 0.0 collective-permute-done.4.refs_1_
  20.6 1.2 %collective-permute-done.5.refs_2_ = f32[2,5,16,128]{3,2,1,0:T(8,128)S(1)} collective-permute-done((f32[2,5,16,128]{3,2,1,0:T(8,128)S(1)}, f32[2,5,16,128]{3,2,1,0:T(8,128)S(1)}, u32[]{:S(2)}, u32[]{:S(2)}) %collective-permute-start.5) | collective-permute-done | bytes 81952 | tf_op jit(solution)/shard_map/ppermute | solution.py:36
  21.8 0.3 %gradient.1 = (f32[12,16,16,128]{3,2,1,0:T(8,128)S(1)}, f32[3,16,16,128]{3,2,1,0:T(8,128)S(1)}) custom-call(f32[2,5,16,128]{3,2,1,0:T(8,128)S(1)} %collective-permute-done.3.refs_0_, f32[2,5,16,128]{3,2,1,0:T(8,128)S(1)} %collective-permute-done.4.refs_1_, ...), custom_call_target="tpu_custom_call", output_to_operand_aliasing={{0}: (6, {}), {1}: (7, {})} | custom-call | flops 983040 | bytes 262144 | tf_op jit(solution)/shard_map/gradient/pallas_call | solution.py:616
  22.2 0.1 collective-permute-start.6
  22.2 1.2 %outputs.1 = (f32[9,16,16,128]{3,2,1,0:T(8,128)}, f32[9,16,16,128]{3,2,1,0:T(8,128)}) custom-call(f32[12,16,16,128]{3,2,1,0:T(8,128)S(1)} %get-tuple-element.41.strain, f32[12,20,32,128]{3,2,1,0:T(8,128)S(1)} %get-tuple-element.34.refs_3_.stress, ...), custom_call_target="tpu_custom_call", output_to_operand_aliasing={{0}: (4, {}), {1}: (5, {})} | custom-call | flops 1966080 | bytes 2359296 | tf_op jit(solution)/shard_map/outputs/pallas_call | solution.py:629
  23.5 0.5 %collective-permute-done.6.other = f32[3,16,16,128]{3,2,1,0:T(8,128)S(1)} collective-permute-done((f32[3,16,16,128]{3,2,1,0:T(8,128)S(1)}, f32[3,16,16,128]{3,2,1,0:T(8,128)S(1)}, u32[]{:S(2)}, u32[]{:S(2)}) %collective-permute-start.6) | collective-permute-done | bytes 393248 | tf_op jit(solution)/shard_map/ppermute | solution.py:626
  23.9 0.8 %sum.1 = f32[3,16,16,128]{3,2,1,0:T(8,128)} custom-call(f32[3,16,16,128]{3,2,1,0:T(8,128)S(1)} %get-tuple-element.46.mine, f32[3,16,16,128]{3,2,1,0:T(8,128)S(1)} %collective-permute-done.6.other), custom_call_target="tpu_custom_call" | custom-call | flops 98304 | bytes 1179648 | tf_op jit(solution)/shard_map/sum/pallas_call | solution.py:640
Async XLA Ops:
  0.6 10.6 %copy-start.1 = (f32[1,9,16,16,128]{4,3,2,1,0:T(8,128)S(1)}, f32[1,9,16,16,128]{4,3,2,1,0:T(8,128)}, u32[]{:S(2)}) copy-start(f32[1,9,16,16,128]{4,3,2,1,0:T(8,128)} %param.10) | copy-start | bytes 3538948
  0.6 10.6 %copy-start = (f32[1,9,16,16,128]{4,3,2,1,0:T(8,128)S(1)}, f32[1,9,16,16,128]{4,3,2,1,0:T(8,128)}, u32[]{:S(2)}) copy-start(f32[1,9,16,16,128]{4,3,2,1,0:T(8,128)} %param.9) | copy-start | bytes 3538948
  0.7 10.6 %copy-start.3 = (f32[1,256]{1,0:T(1,128)S(1)}, f32[1,256]{1,0:T(1,128)}, u32[]{:S(2)}) copy-start(f32[1,256]{1,0:T(1,128)} %residual_amp.1) | copy-start | bytes 3076
  0.7 10.6 %copy-start.2 = (s32[1,256]{1,0:T(1,128)S(1)}, s32[1,256]{1,0:T(1,128)}, u32[]{:S(2)}) copy-start(s32[1,256]{1,0:T(1,128)} %receiver_cell.1) | copy-start | bytes 3076
  1.9 11.5 %collective-permute-start = (f32[2,5,16,128]{3,2,1,0:T(8,128)S(1)}, f32[2,5,16,128]{3,2,1,0:T(8,128)S(1)}, u32[]{:S(2)}, u32[]{:S(2)}) collective-permute-start(f32[2,5,16,128]{3,2,1,0:T(8,128)S(1)} %get-tuple-element.25), channel_id=1, source_target_pairs={{1,2},{3,4},{5,6},{2,1},{4,3},{6,5},{9,10},{11,12},{13,14},{10,9},... | collective-permute-start | bytes 245768 | tf_op jit(solution)/shard_map/ppermute | solution.py:36
  2.6 10.9 %collective-permute-start.1 = (f32[2,5,16,128]{3,2,1,0:T(8,128)S(1)}, f32[2,5,16,128]{3,2,1,0:T(8,128)S(1)}, u32[]{:S(2)}, u32[]{:S(2)}) collective-permute-start(f32[2,5,16,128]{3,2,1,0:T(8,128)S(1)} %get-tuple-element.26), channel_id=1, source_target_pairs={{0,8},{8,0},{1,9},{9,1},{2,10},{10,2},{3,11},{11,3},{4,12},{12,4},... | collective-permute-start | bytes 245768 | tf_op jit(solution)/shard_map/ppermute | solution.py:36
  5.6 7.9 %collective-permute-start.2 = (f32[2,5,16,128]{3,2,1,0:T(8,128)S(1)}, f32[2,5,16,128]{3,2,1,0:T(8,128)S(1)}, u32[]{:S(2)}, u32[]{:S(2)}) collective-permute-start(f32[2,5,16,128]{3,2,1,0:T(8,128)S(1)} %get-tuple-element.27), channel_id=1, source_target_pairs={{0,1},{2,3},{4,5},{6,7},{1,0},{3,2},{5,4},{7,6},{8,9},{10,11},{12,... | collective-permute-start | bytes 245768 | tf_op jit(solution)/shard_map/ppermute | solution.py:36
  13.8 6.8 %collective-permute-start.3 = (f32[2,5,16,128]{3,2,1,0:T(8,128)S(1)}, f32[2,5,16,128]{3,2,1,0:T(8,128)S(1)}, u32[]{:S(2)}, u32[]{:S(2)}) collective-permute-start(f32[2,5,16,128]{3,2,1,0:T(8,128)S(1)} %get-tuple-element.31), channel_id=1, source_target_pairs={{1,2},{3,4},{5,6},{2,1},{4,3},{6,5},{9,10},{11,12},{13,14},{10,9},... | collective-permute-start | bytes 245768 | tf_op jit(solution)/shard_map/ppermute | solution.py:36
  14.5 6.1 %collective-permute-start.4 = (f32[2,5,16,128]{3,2,1,0:T(8,128)S(1)}, f32[2,5,16,128]{3,2,1,0:T(8,128)S(1)}, u32[]{:S(2)}, u32[]{:S(2)}) collective-permute-start(f32[2,5,16,128]{3,2,1,0:T(8,128)S(1)} %get-tuple-element.32), channel_id=1, source_target_pairs={{0,8},{8,0},{1,9},{9,1},{2,10},{10,2},{3,11},{11,3},{4,12},{12,4},... | collective-permute-start | bytes 245768 | tf_op jit(solution)/shard_map/ppermute | solution.py:36
  15.0 6.8 %collective-permute-start.5 = (f32[2,5,16,128]{3,2,1,0:T(8,128)S(1)}, f32[2,5,16,128]{3,2,1,0:T(8,128)S(1)}, u32[]{:S(2)}, u32[]{:S(2)}) collective-permute-start(f32[2,5,16,128]{3,2,1,0:T(8,128)S(1)} %get-tuple-element.33), channel_id=1, source_target_pairs={{0,1},{2,3},{4,5},{6,7},{1,0},{3,2},{5,4},{7,6},{8,9},{10,11},{12,... | collective-permute-start | bytes 245768 | tf_op jit(solution)/shard_map/ppermute | solution.py:36
  22.2 1.8 %collective-permute-start.6 = (f32[3,16,16,128]{3,2,1,0:T(8,128)S(1)}, f32[3,16,16,128]{3,2,1,0:T(8,128)S(1)}, u32[]{:S(2)}, u32[]{:S(2)}) collective-permute-start(f32[3,16,16,128]{3,2,1,0:T(8,128)S(1)} %get-tuple-element.46.mine), channel_id=1, source_target_pairs={{0,16},{16,0},{1,17},{17,1},{2,18},{18,2},{3,19},{19,3},{4,20},{20... | collective-permute-start | bytes 1179656 | tf_op jit(solution)/shard_map/ppermute | solution.py:626

commit v5 on v4

--- a/solution.py
+++ b/solution.py
@@ -27,8 +27,11 @@
 
 
 def links_of(sizes):
-    order = (("ty", 1, 1), ("tx", 0, 1), ("tx", 0, 0), ("ty", 1, 0))
-    return [(name, dim, first) for name, dim, first in order if first + 1 < sizes[name]]
+    far_y, near_y, *along = ("ty", 1, 1), ("ty", 1, 0), ("tx", 0, 1), ("tx", 0, 0)
+    return [
+        [link for link in order if link[2] + 1 < sizes[link[0]]]
+        for order in ((far_y, near_y, *along), (far_y, *along, near_y))
+    ]
 
 
 def swap(value, axis, first):
@@ -76,10 +79,15 @@
     )
 
 
-def pack_kernel(links, forward, adjoint, *refs):
-    sends, sems = refs[: len(links)], refs[-1]
+def pack_kernel(links, width_y, forward, adjoint, receiver_cell, residual_amp, *refs):
+    sends, (added, stress, cells_now, amps_now, sems) = refs[: len(links)], refs[len(links) :]
     tile = forward.shape[1:3]
-    copies = []
+    copies = [
+        pltpu.make_async_copy(receiver_cell, cells_now, sems.at[0]),
+        pltpu.make_async_copy(residual_amp, amps_now, sems.at[1]),
+    ]
+    for copy in copies:
+        copy.start()
     for (axis, dim, first), send in zip(links, sends):
         lower = is_lower(axis, first)
         for slot, ((up_part, up_at), (low_part, low_at)) in enumerate(zip(*stress_plan(dim))):
@@ -90,7 +98,15 @@
                 copy = pltpu.make_async_copy(source, send.at[wave, slot], sems.at[len(copies)])
                 copy.start()
                 copies.append(copy)
-    for copy in copies:
+    for wave in range(2):
+        clear_rim(
+            stress, *([6 * wave + part for part in STRESS_ALONG[dim]] for dim in range(2))
+        )
+    columns = column_ids(*tile, width_y, forward.shape[-1])
+    for copy in copies[:2]:
+        copy.wait()
+    added[...] = receiver_sum(cells_now[...], amps_now[...], columns)
+    for copy in copies[2:]:
         copy.wait()
 
 
@@ -201,10 +217,10 @@
     density,
     source_cell,
     source_amp,
-    receiver_cell,
-    residual_amp,
+    received,
     forward,
     adjoint,
+    _,
     stress,
     velocity,
     accel,
@@ -212,7 +228,7 @@
     buoyancy,
     scaled_lame,
     scaled_shear,
-    added,
+    sourced,
     lame_now,
     shear_now,
     density_now,
@@ -233,23 +249,18 @@
     middle = pl.ds(ROWS, tile_y)
     columns = column_ids(tile_x, tile_y, width_y, depth)
     lane = lax.broadcasted_iota(jnp.int32, columns.shape, 1)
-    added[0] = jnp.where(columns * depth + lane == source_cell[0], source_amp[0], 0.0)
-    added[1] = receiver_sum(receiver_cell[...], residual_amp[...], columns)
-    for wave in range(2):
-        clear_rim(
-            stress, *([6 * wave + part for part in STRESS_ALONG[dim]] for dim in range(2))
-        )
+    sourced[...] = jnp.where(columns * depth + lane == source_cell[0], source_amp[0], 0.0)
+    for wave, added in enumerate((sourced, received)):
         for layer in range(3):
-            rim_added[wave, 0, layer] = added[wave, pl.ds(cells + layer * tile_y, tile_y), :]
+            rim_added[wave, 0, layer] = added[pl.ds(cells + layer * tile_y, tile_y), :]
             begin = cells + 3 * tile_y + layer * tile_x
-            rim_added[wave, 1, layer] = added[wave, pl.ds(begin, tile_x), :]
-
+            rim_added[wave, 1, layer] = added[pl.ds(begin, tile_x), :]
     for copy in copies:
         copy.wait()
 
     def fill(x, carry):
-        for wave, fields in enumerate((forward, adjoint)):
-            extra = added[wave, pl.ds(pl.multiple_of(x * tile_y, 8), tile_y), :]
+        for wave, (fields, added) in enumerate(((forward, sourced), (adjoint, received))):
+            extra = added[pl.ds(pl.multiple_of(x * tile_y, 8), tile_y), :]
             for part in range(6):
                 value = fields[3 + part, x]
                 stress[6 * wave + part, x + LAYERS, middle, :] = (
@@ -363,7 +374,7 @@
     return buoyancy.reshape(layers * rows, depth)[pl.ds(index % rows, layers, stride=rows), :]
 
 
-def boundary_kernel(links, *refs):
+def boundary_kernel(links, later_links, *refs):
     count = len(links)
     received = refs[:count]
     rim_added, buoyancy, _ = refs[count : count + 3]
@@ -375,7 +386,7 @@
         target[...] += time_step * light_face(buoyancy, dim, index) * term
 
     stress_halo_terms(links, received, rim_added, (0, 1), add)
-    send_faces(velocity, 3, links, sends, [velocity_plan(dim) for dim in range(2)])
+    send_faces(velocity, 3, later_links, sends, [velocity_plan(dim) for dim in range(2)])
 
 
 def strain_kernel(links, *refs):
@@ -524,7 +535,7 @@
     adjoint = adjoint_fields.reshape(adjoint_fields.shape[1:])
     sizes = {name: lax.axis_size(name) for name in ("tx", "ty")}
     width_y = tile_y * sizes["ty"]
-    links = links_of(sizes)
+    links, later_links = links_of(sizes)
     cells = tile_x * tile_y * depth
 
     def buffers(dim):
@@ -538,22 +549,28 @@
             (parts, tile_x + 2 * LAYERS, tile_y + 2 * ROWS, depth), jnp.float32
         )
 
-    def exchange(sends):
+    def exchange(links, sends):
         return [swap(send, axis, first) for (axis, _, first), send in zip(links, sends)]
 
     send_shapes = [buffers(dim) for _, dim, _ in links]
     count = len(links)
-    sends = pl.pallas_call(
-        functools.partial(pack_kernel, links),
-        out_shape=send_shapes,
-        in_specs=[hbm] * 2,
-        out_specs=[vmem] * count,
-        scratch_shapes=[pltpu.SemaphoreType.DMA((2 * SLOTS * count,))],
+    receivers = receiver_cell.shape[-1]
+    rows = tile_x * tile_y + 3 * (tile_x + tile_y)
+    *sends, added, stress = pl.pallas_call(
+        functools.partial(pack_kernel, links, width_y),
+        out_shape=send_shapes + [pltpu.VMEM((rows, depth), jnp.float32), padded(12)],
+        in_specs=[hbm] * 4,
+        out_specs=[vmem] * (count + 2),
+        scratch_shapes=[
+            pltpu.VMEM((1, receivers), jnp.int32),
+            pltpu.VMEM((1, receivers), jnp.float32),
+            pltpu.SemaphoreType.DMA((2 + 2 * SLOTS * count,)),
+        ],
         compiler_params=params,
-        cost_estimate=cost(0, 2 * SLOTS * count * tile_x * depth * 4),
+        cost_estimate=cost(6 * rows * receivers * depth, 2 * SLOTS * count * tile_x * depth * 4),
         name="pack",
-    )(in_hbm(forward), in_hbm(adjoint))
-    halos = exchange(sends)
+    )(*(in_hbm(x) for x in (forward, adjoint, receiver_cell, residual_amp)))
+    halos = exchange(links, sends)
 
     stress, velocity, accel, rim_added, buoyancy, scaled_lame, scaled_shear = pl.pallas_call(
         functools.partial(velocity_kernel, width_y),
@@ -568,8 +585,9 @@
         ],
         in_specs=[hbm] * 3 + [smem] * 2 + [vmem] * 4,
         out_specs=[vmem] * 7,
+        input_output_aliases={8: 0},
         scratch_shapes=[
-            pltpu.VMEM((2, tile_x * tile_y + 3 * (tile_x + tile_y), depth), jnp.float32),
+            pltpu.VMEM((rows, depth), jnp.float32),
             tile(),
             tile(),
             tile(),
@@ -582,15 +600,15 @@
         *(in_hbm(x) for x in (lame_lambda, shear_modulus, density)),
         source_cell,
         source_amp,
-        receiver_cell,
-        residual_amp,
+        added,
         forward,
         adjoint,
+        stress,
     )
 
     velocity, *sends = pl.pallas_call(
-        functools.partial(boundary_kernel, links),
-        out_shape=[padded(6)] + send_shapes,
+        functools.partial(boundary_kernel, links, later_links),
+        out_shape=[padded(6)] + [buffers(dim) for _, dim, _ in later_links],
         in_specs=[vmem] * (count + 3),
         out_specs=[vmem] * (count + 1),
         input_output_aliases={count + 2: 0},
@@ -598,7 +616,7 @@
         cost_estimate=cost(cells, 10 * 2 * tile_x * depth * 4),
         name="boundary",
     )(*halos, rim_added, buoyancy, velocity)
-    velocity_halos = exchange(sends)
+    velocity_halos = exchange(later_links, sends)
 
     out_shape = jax.ShapeDtypeStruct(forward.shape, jnp.float32)
     strain, gradient, _, forward_next, adjoint_next = pl.pallas_call(
@@ -614,7 +632,7 @@
     )(*halos, rim_added, buoyancy, velocity, accel)
 
     strain, gradient = pl.pallas_call(
-        functools.partial(gradient_kernel, links),
+        functools.partial(gradient_kernel, later_links),
         out_shape=[tile(12), tile(3)],
         in_specs=[vmem] * (count + 5),
         out_specs=[vmem] * 2,

time: 24.9 us -> 25.4 us (1.020)
  starting transfers between devices: 13.7 us -> 14.1 us
    ppermute x6, starting transfers between devices: 13.6 us -> 14 us  [swap(): return lax.ppermute(value, axis, pairs + [(j, i) for i, j in pairs])]
  transfers between devices with their start and end apart: 7 -> 7, of which waited for: 2 -> 2; matrix products, arithmetic and copies ran while one was open for 0% -> 0% of each run, Pallas kernels for 19% -> 18%
where the time goes in v5:
time: 25.4 us; the launch traced here: 25.2 us
  starting transfers between devices  14.1 us (56%)
  Pallas kernels  7.37 us (29%)
  between operations  2.07 us (8%)
  waiting for transfers between devices  1.71 us (7%)
    ppermute x6, starting transfers between devices, swap(): return lax.ppermute(value, axis, pairs + [(j, i) for i, j in pairs])  14 us
    pallas_call x1, Pallas kernels, body(): pl.pallas_call(functools.partial(velocity_kernel, width_y), out_shape=[pa...  2.15 us
    pallas_call x1, Pallas kernels, body(): pl.pallas_call(functools.partial(pack_kernel, links, width_y), out_shape=...  1.51 us
    ppermute x6, waiting for transfers between devices, swap(): return lax.ppermute(value, axis, pairs + [(j, i) for i, j in pairs])  1.24 us
    pallas_call x1, Pallas kernels, body(): pl.pallas_call(functools.partial(output_kernel, chunk), out_shape=[out_sh...  1.23 us
    pallas_call x1, Pallas kernels, body(): pl.pallas_call(functools.partial(strain_kernel, links), out_shape=[tile(1...  1.16 us
    pallas_call x1, Pallas kernels, body(): pl.pallas_call(sum_kernel, out_shape=jax.ShapeDtypeStruct((3, tile_x, til...  0.78 us
  transfers between devices with their start and end apart: 7, of which 2 were waited for; matrix products, arithmetic and copies ran while one was open for 0% of the time, Pallas kernels for 18%

profile of v5, /device:TPU:0, one launch (start us, length us, event | category | flops | bytes accessed | tf_op | source)
XLA Modules:
  0.0 25.2 jit_solution(10383980166849946104)
XLA Ops:
  0.6 0.0 copy-start.1
  0.6 0.0 copy-start
  0.7 1.5 %pack.1 = (f32[2,5,16,128]{3,2,1,0:T(8,128)S(1)}, f32[2,5,16,128]{3,2,1,0:T(8,128)S(1)}, f32[2,5,16,128]{3,2,1,0:T(8,128)S(1)}, f32[352,128]{1,0:T(8,128)S(1)}, f32[12,20,32,128]{3,2,1,0:T(8,128)S(1)}) custom-call(f32[9,16,16,128]{3,2,1,0:T(8,128)} %bitcast.4, f32[9,16,16,128]{3,2,1,0:T(8,128)} %bitcast.6, s32[1,256]{1,0:T(1,128)} %receiver_cell.1, ...), custom_call_target="tpu_custom_call" | custom-call | flops 69206016 | bytes 245760 | tf_op jit(solution)/shard_map/pack/pallas_call | solution.py:559
  2.2 0.7 %collective-permute-start = (f32[2,5,16,128]{3,2,1,0:T(8,128)S(1)}, f32[2,5,16,128]{3,2,1,0:T(8,128)S(1)}, u32[]{:S(2)}, u32[]{:S(2)}) collective-permute-start(f32[2,5,16,128]{3,2,1,0:T(8,128)S(1)} %get-tuple-element.27), channel_id=1, source_target_pairs={{1,2},{3,4},{5,6},{2,1},{4,3},{6,5},{9,10},{11,12},{13,14},{10,9},... | collective-permute-start | bytes 245768 | tf_op jit(solution)/shard_map/ppermute | solution.py:39
  2.8 5.8 %collective-permute-start.1 = (f32[2,5,16,128]{3,2,1,0:T(8,128)S(1)}, f32[2,5,16,128]{3,2,1,0:T(8,128)S(1)}, u32[]{:S(2)}, u32[]{:S(2)}) collective-permute-start(f32[2,5,16,128]{3,2,1,0:T(8,128)S(1)} %get-tuple-element.28), channel_id=1, source_target_pairs={{0,1},{2,3},{4,5},{6,7},{1,0},{3,2},{5,4},{7,6},{8,9},{10,11},{12,... | collective-permute-start | bytes 245768 | tf_op jit(solution)/shard_map/ppermute | solution.py:39
  8.6 1.5 %collective-permute-start.2 = (f32[2,5,16,128]{3,2,1,0:T(8,128)S(1)}, f32[2,5,16,128]{3,2,1,0:T(8,128)S(1)}, u32[]{:S(2)}, u32[]{:S(2)}) collective-permute-start(f32[2,5,16,128]{3,2,1,0:T(8,128)S(1)} %get-tuple-element.29), channel_id=1, source_target_pairs={{0,8},{8,0},{1,9},{9,1},{2,10},{10,2},{3,11},{11,3},{4,12},{12,4},... | collective-permute-start | bytes 245768 | tf_op jit(solution)/shard_map/ppermute | solution.py:39
  11.5 0.0 copy-done.1
  11.5 0.0 copy-done
  11.5 2.1 %velocity.1 = (f32[12,20,32,128]{3,2,1,0:T(8,128)S(1)}, f32[6,20,32,128]{3,2,1,0:T(8,128)S(1)}, f32[3,16,16,128]{3,2,1,0:T(8,128)S(1)}, f32[2,2,3,16,128]{4,3,2,...) custom-call(f32[16,16,128]{2,1,0:T(8,128)} %lame.1, ...), custom_call_target="tpu_custom_call", output_to_operand_aliasing={{0}: (8, {})} | custom-call | flops 6553600 | bytes 2359296 | tf_op jit(solution)/shard_map/velocity/pallas_call | solution.py:575
  13.6 0.0 collective-permute-done.refs_0_
  13.6 0.0 collective-permute-done.1.refs_1_
  13.6 0.0 collective-permute-done.2.refs_2_
  13.7 0.3 %boundary.1 = (f32[6,20,32,128]{3,2,1,0:T(8,128)S(1)}, f32[2,5,16,128]{3,2,1,0:T(8,128)S(1)}, f32[2,5,16,128]{3,2,1,0:T(8,128)S(1)}, f32[2,5,16,128]{3,2,1,0:T(8,128)S(1)}) custom-call(f32[2,5,16,128]{3,2,1,0:T(8,128)S(1)} %collective-permute-done.refs_0_, f32[2,5,16,128]{3,2,1,0:T(8,128)S(1)} %collective-permute-done.1.refs_1_, ...), custom_call_target="tpu_custom_call", output_to_operand_aliasing={{0}: (5, {})} | custom-call | flops 32768 | bytes 163840 | tf_op jit(solution)/shard_map/boundary/pallas_call | solution.py:609
  13.9 0.7 %collective-permute-start.3 = (f32[2,5,16,128]{3,2,1,0:T(8,128)S(1)}, f32[2,5,16,128]{3,2,1,0:T(8,128)S(1)}, u32[]{:S(2)}, u32[]{:S(2)}) collective-permute-start(f32[2,5,16,128]{3,2,1,0:T(8,128)S(1)} %get-tuple-element.35), channel_id=1, source_target_pairs={{1,2},{3,4},{5,6},{2,1},{4,3},{6,5},{9,10},{11,12},{13,14},{10,9},... | collective-permute-start | bytes 245768 | tf_op jit(solution)/shard_map/ppermute | solution.py:39
  14.6 1.0 %collective-permute-start.4 = (f32[2,5,16,128]{3,2,1,0:T(8,128)S(1)}, f32[2,5,16,128]{3,2,1,0:T(8,128)S(1)}, u32[]{:S(2)}, u32[]{:S(2)}) collective-permute-start(f32[2,5,16,128]{3,2,1,0:T(8,128)S(1)} %get-tuple-element.36), channel_id=1, source_target_pairs={{0,8},{8,0},{1,9},{9,1},{2,10},{10,2},{3,11},{11,3},{4,12},{12,4},... | collective-permute-start | bytes 245768 | tf_op jit(solution)/shard_map/ppermute | solution.py:39
  15.6 4.4 %collective-permute-start.5 = (f32[2,5,16,128]{3,2,1,0:T(8,128)S(1)}, f32[2,5,16,128]{3,2,1,0:T(8,128)S(1)}, u32[]{:S(2)}, u32[]{:S(2)}) collective-permute-start(f32[2,5,16,128]{3,2,1,0:T(8,128)S(1)} %get-tuple-element.37), channel_id=1, source_target_pairs={{0,1},{2,3},{4,5},{6,7},{1,0},{3,2},{5,4},{7,6},{8,9},{10,11},{12,... | collective-permute-start | bytes 245768 | tf_op jit(solution)/shard_map/ppermute | solution.py:39
  20.0 1.2 %strain.1 = (f32[12,16,16,128]{3,2,1,0:T(8,128)S(1)}, f32[3,16,16,128]{3,2,1,0:T(8,128)S(1)}, f32[6,20,32,128]{3,2,1,0:T(8,128)S(1)}, f32[9,16,16,128]{3,2,1,0:T(8,128)}, f32[9,16,16,128]{3,2,1,0:T(8,128)}) custom-call(f32[2,5,16,128]{3,2,1,0:T(8,128)S(1)} %collective-permute-done.refs_0_, ...), custom_call_target="tpu_custom_call", output_to_operand_aliasing={{2}: (5, {})} | custom-call | flops 6553600 | bytes 2359296 | tf_op jit(solution)/shard_map/strain/pallas_call | solution.py:622
  21.1 0.0 collective-permute-done.3.refs_0_
  21.2 0.0 collective-permute-done.4.refs_1_
  21.2 1.2 %collective-permute-done.5.refs_2_ = f32[2,5,16,128]{3,2,1,0:T(8,128)S(1)} collective-permute-done((f32[2,5,16,128]{3,2,1,0:T(8,128)S(1)}, f32[2,5,16,128]{3,2,1,0:T(8,128)S(1)}, u32[]{:S(2)}, u32[]{:S(2)}) %collective-permute-start.5) | collective-permute-done | bytes 81952 | tf_op jit(solution)/shard_map/ppermute | solution.py:39
  22.4 0.3 %gradient.1 = (f32[12,16,16,128]{3,2,1,0:T(8,128)S(1)}, f32[3,16,16,128]{3,2,1,0:T(8,128)S(1)}) custom-call(f32[2,5,16,128]{3,2,1,0:T(8,128)S(1)} %collective-permute-done.3.refs_0_, f32[2,5,16,128]{3,2,1,0:T(8,128)S(1)} %collective-permute-done.4.refs_1_, ...), custom_call_target="tpu_custom_call", output_to_operand_aliasing={{0}: (6, {}), {1}: (7, {})} | custom-call | flops 983040 | bytes 262144 | tf_op jit(solution)/shard_map/gradient/pallas_call | solution.py:634
  22.7 0.1 collective-permute-start.6
  22.8 1.2 %outputs.1 = (f32[9,16,16,128]{3,2,1,0:T(8,128)}, f32[9,16,16,128]{3,2,1,0:T(8,128)}) custom-call(f32[12,16,16,128]{3,2,1,0:T(8,128)S(1)} %get-tuple-element.45.strain, f32[12,20,32,128]{3,2,1,0:T(8,128)S(1)} %get-tuple-element.38.refs_3_.stress, ...), custom_call_target="tpu_custom_call", output_to_operand_aliasing={{0}: (4, {}), {1}: (5, {})} | custom-call | flops 1966080 | bytes 2359296 | tf_op jit(solution)/shard_map/outputs/pallas_call | solution.py:647
  24.0 0.5 %collective-permute-done.6.other = f32[3,16,16,128]{3,2,1,0:T(8,128)S(1)} collective-permute-done((f32[3,16,16,128]{3,2,1,0:T(8,128)S(1)}, f32[3,16,16,128]{3,2,1,0:T(8,128)S(1)}, u32[]{:S(2)}, u32[]{:S(2)}) %collective-permute-start.6) | collective-permute-done | bytes 393248 | tf_op jit(solution)/shard_map/ppermute | solution.py:644
  24.5 0.8 %sum.1 = f32[3,16,16,128]{3,2,1,0:T(8,128)} custom-call(f32[3,16,16,128]{3,2,1,0:T(8,128)S(1)} %get-tuple-element.50.mine, f32[3,16,16,128]{3,2,1,0:T(8,128)S(1)} %collective-permute-done.6.other), custom_call_target="tpu_custom_call" | custom-call | flops 98304 | bytes 1179648 | tf_op jit(solution)/shard_map/sum/pallas_call | solution.py:658
Async XLA Ops:
  0.6 10.8 %copy-start.1 = (f32[1,9,16,16,128]{4,3,2,1,0:T(8,128)S(1)}, f32[1,9,16,16,128]{4,3,2,1,0:T(8,128)}, u32[]{:S(2)}) copy-start(f32[1,9,16,16,128]{4,3,2,1,0:T(8,128)} %param.10) | copy-start | bytes 3538948
  0.6 10.8 %copy-start = (f32[1,9,16,16,128]{4,3,2,1,0:T(8,128)S(1)}, f32[1,9,16,16,128]{4,3,2,1,0:T(8,128)}, u32[]{:S(2)}) copy-start(f32[1,9,16,16,128]{4,3,2,1,0:T(8,128)} %param.9) | copy-start | bytes 3538948
  2.2 11.5 %collective-permute-start = (f32[2,5,16,128]{3,2,1,0:T(8,128)S(1)}, f32[2,5,16,128]{3,2,1,0:T(8,128)S(1)}, u32[]{:S(2)}, u32[]{:S(2)}) collective-permute-start(f32[2,5,16,128]{3,2,1,0:T(8,128)S(1)} %get-tuple-element.27), channel_id=1, source_target_pairs={{1,2},{3,4},{5,6},{2,1},{4,3},{6,5},{9,10},{11,12},{13,14},{10,9},... | collective-permute-start | bytes 245768 | tf_op jit(solution)/shard_map/ppermute | solution.py:39
  2.8 10.8 %collective-permute-start.1 = (f32[2,5,16,128]{3,2,1,0:T(8,128)S(1)}, f32[2,5,16,128]{3,2,1,0:T(8,128)S(1)}, u32[]{:S(2)}, u32[]{:S(2)}) collective-permute-start(f32[2,5,16,128]{3,2,1,0:T(8,128)S(1)} %get-tuple-element.28), channel_id=1, source_target_pairs={{0,1},{2,3},{4,5},{6,7},{1,0},{3,2},{5,4},{7,6},{8,9},{10,11},{12,... | collective-permute-start | bytes 245768 | tf_op jit(solution)/shard_map/ppermute | solution.py:39
  8.6 5.0 %collective-permute-start.2 = (f32[2,5,16,128]{3,2,1,0:T(8,128)S(1)}, f32[2,5,16,128]{3,2,1,0:T(8,128)S(1)}, u32[]{:S(2)}, u32[]{:S(2)}) collective-permute-start(f32[2,5,16,128]{3,2,1,0:T(8,128)S(1)} %get-tuple-element.29), channel_id=1, source_target_pairs={{0,8},{8,0},{1,9},{9,1},{2,10},{10,2},{3,11},{11,3},{4,12},{12,4},... | collective-permute-start | bytes 245768 | tf_op jit(solution)/shard_map/ppermute | solution.py:39
  13.9 7.2 %collective-permute-start.3 = (f32[2,5,16,128]{3,2,1,0:T(8,128)S(1)}, f32[2,5,16,128]{3,2,1,0:T(8,128)S(1)}, u32[]{:S(2)}, u32[]{:S(2)}) collective-permute-start(f32[2,5,16,128]{3,2,1,0:T(8,128)S(1)} %get-tuple-element.35), channel_id=1, source_target_pairs={{1,2},{3,4},{5,6},{2,1},{4,3},{6,5},{9,10},{11,12},{13,14},{10,9},... | collective-permute-start | bytes 245768 | tf_op jit(solution)/shard_map/ppermute | solution.py:39
  14.6 6.5 %collective-permute-start.4 = (f32[2,5,16,128]{3,2,1,0:T(8,128)S(1)}, f32[2,5,16,128]{3,2,1,0:T(8,128)S(1)}, u32[]{:S(2)}, u32[]{:S(2)}) collective-permute-start(f32[2,5,16,128]{3,2,1,0:T(8,128)S(1)} %get-tuple-element.36), channel_id=1, source_target_pairs={{0,8},{8,0},{1,9},{9,1},{2,10},{10,2},{3,11},{11,3},{4,12},{12,4},... | collective-permute-start | bytes 245768 | tf_op jit(solution)/shard_map/ppermute | solution.py:39
  15.6 6.8 %collective-permute-start.5 = (f32[2,5,16,128]{3,2,1,0:T(8,128)S(1)}, f32[2,5,16,128]{3,2,1,0:T(8,128)S(1)}, u32[]{:S(2)}, u32[]{:S(2)}) collective-permute-start(f32[2,5,16,128]{3,2,1,0:T(8,128)S(1)} %get-tuple-element.37), channel_id=1, source_target_pairs={{0,1},{2,3},{4,5},{6,7},{1,0},{3,2},{5,4},{7,6},{8,9},{10,11},{12,... | collective-permute-start | bytes 245768 | tf_op jit(solution)/shard_map/ppermute | solution.py:39
  22.7 1.8 %collective-permute-start.6 = (f32[3,16,16,128]{3,2,1,0:T(8,128)S(1)}, f32[3,16,16,128]{3,2,1,0:T(8,128)S(1)}, u32[]{:S(2)}, u32[]{:S(2)}) collective-permute-start(f32[3,16,16,128]{3,2,1,0:T(8,128)S(1)} %get-tuple-element.50.mine), channel_id=1, source_target_pairs={{0,16},{16,0},{1,17},{17,1},{2,18},{18,2},{3,19},{19,3},{4,20},{20... | collective-permute-start | bytes 1179656 | tf_op jit(solution)/shard_map/ppermute | solution.py:644

commit v6 on v5

--- a/solution.py
+++ b/solution.py
@@ -30,7 +30,7 @@
     far_y, near_y, *along = ("ty", 1, 1), ("ty", 1, 0), ("tx", 0, 1), ("tx", 0, 0)
     return [
         [link for link in order if link[2] + 1 < sizes[link[0]]]
-        for order in ((far_y, near_y, *along), (far_y, *along, near_y))
+        for order in ((far_y, *along, near_y), (far_y, *along, near_y))
     ]
 
 
@@ -229,6 +229,7 @@
     scaled_lame,
     scaled_shear,
     sourced,
+    gained,
     lame_now,
     shear_now,
     density_now,
@@ -255,8 +256,6 @@
             rim_added[wave, 0, layer] = added[pl.ds(cells + layer * tile_y, tile_y), :]
             begin = cells + 3 * tile_y + layer * tile_x
             rim_added[wave, 1, layer] = added[pl.ds(begin, tile_x), :]
-    for copy in copies:
-        copy.wait()
 
     def fill(x, carry):
         for wave, (fields, added) in enumerate(((forward, sourced), (adjoint, received))):
@@ -266,16 +265,12 @@
                 stress[6 * wave + part, x + LAYERS, middle, :] = (
                     value + extra if part < 3 else value
                 )
-        buoyancy[x] = 1.0 / density_now[x]
-        scaled_lame[x] = time_step * lame_now[x]
-        scaled_shear[x] = time_step * shear_now[x]
         return carry
 
     lax.fori_loop(0, tile_x, fill, 0, unroll=4)
 
     def layer(x, carry):
-        light = buoyancy[x]
-        for wave, fields in enumerate((forward, adjoint)):
+        for wave in range(2):
             xx, yy, zz, xy, xz, yz = range(6 * wave, 6 * wave + 6)
             values = (
                 along_x(stress, xx, x, tile_y, True)
@@ -289,7 +284,21 @@
                 + along_z(stress, zz, x, tile_y, True),
             )
             for part, value in enumerate(values):
-                value = light * value
+                gained[3 * wave + part, x] = value
+        return carry
+
+    lax.fori_loop(0, tile_x, layer, 0, unroll=4)
+    for copy in copies:
+        copy.wait()
+
+    def finish(x, carry):
+        light = 1.0 / density_now[x]
+        buoyancy[x] = light
+        scaled_lame[x] = time_step * lame_now[x]
+        scaled_shear[x] = time_step * shear_now[x]
+        for wave, fields in enumerate((forward, adjoint)):
+            for part in range(3):
+                value = light * gained[3 * wave + part, x]
                 if wave == 0:
                     accel[part, x] = value
                 velocity[3 * wave + part, x + LAYERS, middle, :] = (
@@ -297,7 +306,7 @@
                 )
         return carry
 
-    lax.fori_loop(0, tile_x, layer, 0, unroll=4)
+    lax.fori_loop(0, tile_x, finish, 0, unroll=4)
 
 
 def stress_halo_terms(links, received, rim_added, waves, add):
@@ -588,6 +597,7 @@
         input_output_aliases={8: 0},
         scratch_shapes=[
             pltpu.VMEM((rows, depth), jnp.float32),
+            tile(6),
             tile(),
             tile(),
             tile(),

time: 25.4 us -> 24.7 us (0.972)
  Pallas kernels: 7.37 us -> 6.49 us
    pallas_call x1, Pallas kernels: 2.15 us -> 1.28 us  [body(): pl.pallas_call(functools.partial(velocity_kernel, width_y), out_shape=[pa...]
  transfers between devices with their start and end apart: 7 -> 7, of which waited for: 2 -> 2; matrix products, arithmetic and copies ran while one was open for 0% -> 0% of each run, Pallas kernels for 18% -> 15%
where the time goes in v6:
time: 24.7 us; the launch traced here: 24.5 us
  starting transfers between devices  14.2 us (57%)
  Pallas kernels  6.49 us (26%)
  between operations  2.07 us (8%)
  waiting for transfers between devices  1.71 us (7%)
    ppermute x6, starting transfers between devices, swap(): return lax.ppermute(value, axis, pairs + [(j, i) for i, j in pairs])  14.2 us
    pallas_call x1, Pallas kernels, body(): pl.pallas_call(functools.partial(pack_kernel, links, width_y), out_shape=...  1.5 us
    pallas_call x1, Pallas kernels, body(): pl.pallas_call(functools.partial(velocity_kernel, width_y), out_shape=[pa...  1.28 us
    ppermute x6, waiting for transfers between devices, swap(): return lax.ppermute(value, axis, pairs + [(j, i) for i, j in pairs])  1.24 us
    pallas_call x1, Pallas kernels, body(): pl.pallas_call(functools.partial(output_kernel, chunk), out_shape=[out_sh...  1.23 us
    pallas_call x1, Pallas kernels, body(): pl.pallas_call(functools.partial(strain_kernel, links), out_shape=[tile(1...  1.16 us
    pallas_call x1, Pallas kernels, body(): pl.pallas_call(sum_kernel, out_shape=jax.ShapeDtypeStruct((3, tile_x, til...  0.78 us
  transfers between devices with their start and end apart: 7, of which 2 were waited for; matrix products, arithmetic and copies ran while one was open for 0% of the time, Pallas kernels for 15%

profile of v6, /device:TPU:0, one launch (start us, length us, event | category | flops | bytes accessed | tf_op | source)
XLA Modules:
  0.0 24.5 jit_solution(8539837054188621295)
XLA Ops:
  0.6 0.0 copy-start.1
  0.6 0.0 copy-start
  0.7 1.5 %pack.1 = (f32[2,5,16,128]{3,2,1,0:T(8,128)S(1)}, f32[2,5,16,128]{3,2,1,0:T(8,128)S(1)}, f32[2,5,16,128]{3,2,1,0:T(8,128)S(1)}, f32[352,128]{1,0:T(8,128)S(1)}, f32[12,20,32,128]{3,2,1,0:T(8,128)S(1)}) custom-call(f32[9,16,16,128]{3,2,1,0:T(8,128)} %bitcast.4, f32[9,16,16,128]{3,2,1,0:T(8,128)} %bitcast.6, s32[1,256]{1,0:T(1,128)} %receiver_cell.1, ...), custom_call_target="tpu_custom_call" | custom-call | flops 69206016 | bytes 245760 | tf_op jit(solution)/shard_map/pack/pallas_call | solution.py:568
  2.2 0.7 %collective-permute-start = (f32[2,5,16,128]{3,2,1,0:T(8,128)S(1)}, f32[2,5,16,128]{3,2,1,0:T(8,128)S(1)}, u32[]{:S(2)}, u32[]{:S(2)}) collective-permute-start(f32[2,5,16,128]{3,2,1,0:T(8,128)S(1)} %get-tuple-element.27), channel_id=1, source_target_pairs={{1,2},{3,4},{5,6},{2,1},{4,3},{6,5},{9,10},{11,12},{13,14},{10,9},... | collective-permute-start | bytes 245768 | tf_op jit(solution)/shard_map/ppermute | solution.py:39
  2.8 3.0 %collective-permute-start.1 = (f32[2,5,16,128]{3,2,1,0:T(8,128)S(1)}, f32[2,5,16,128]{3,2,1,0:T(8,128)S(1)}, u32[]{:S(2)}, u32[]{:S(2)}) collective-permute-start(f32[2,5,16,128]{3,2,1,0:T(8,128)S(1)} %get-tuple-element.28), channel_id=1, source_target_pairs={{0,8},{8,0},{1,9},{9,1},{2,10},{10,2},{3,11},{11,3},{4,12},{12,4},... | collective-permute-start | bytes 245768 | tf_op jit(solution)/shard_map/ppermute | solution.py:39
  5.9 4.3 %collective-permute-start.2 = (f32[2,5,16,128]{3,2,1,0:T(8,128)S(1)}, f32[2,5,16,128]{3,2,1,0:T(8,128)S(1)}, u32[]{:S(2)}, u32[]{:S(2)}) collective-permute-start(f32[2,5,16,128]{3,2,1,0:T(8,128)S(1)} %get-tuple-element.29), channel_id=1, source_target_pairs={{0,1},{2,3},{4,5},{6,7},{1,0},{3,2},{5,4},{7,6},{8,9},{10,11},{12,... | collective-permute-start | bytes 245768 | tf_op jit(solution)/shard_map/ppermute | solution.py:39
  11.5 0.0 copy-done.1
  11.5 0.0 copy-done
  11.5 1.3 %velocity.1 = (f32[12,20,32,128]{3,2,1,0:T(8,128)S(1)}, f32[6,20,32,128]{3,2,1,0:T(8,128)S(1)}, f32[3,16,16,128]{3,2,1,0:T(8,128)S(1)}, f32[2,2,3,16,128]{4,3,2,...) custom-call(f32[16,16,128]{2,1,0:T(8,128)} %lame.1, ...), custom_call_target="tpu_custom_call", output_to_operand_aliasing={{0}: (8, {})} | custom-call | flops 6553600 | bytes 2359296 | tf_op jit(solution)/shard_map/velocity/pallas_call | solution.py:584
  12.8 0.0 collective-permute-done.refs_0_
  12.8 0.0 collective-permute-done.1.refs_1_
  12.8 0.0 collective-permute-done.2.refs_2_
  12.8 0.3 %boundary.1 = (f32[6,20,32,128]{3,2,1,0:T(8,128)S(1)}, f32[2,5,16,128]{3,2,1,0:T(8,128)S(1)}, f32[2,5,16,128]{3,2,1,0:T(8,128)S(1)}, f32[2,5,16,128]{3,2,1,0:T(8,128)S(1)}) custom-call(f32[2,5,16,128]{3,2,1,0:T(8,128)S(1)} %collective-permute-done.refs_0_, f32[2,5,16,128]{3,2,1,0:T(8,128)S(1)} %collective-permute-done.1.refs_1_, ...), custom_call_target="tpu_custom_call", output_to_operand_aliasing={{0}: (5, {})} | custom-call | flops 32768 | bytes 163840 | tf_op jit(solution)/shard_map/boundary/pallas_call | solution.py:619
  13.1 0.7 %collective-permute-start.3 = (f32[2,5,16,128]{3,2,1,0:T(8,128)S(1)}, f32[2,5,16,128]{3,2,1,0:T(8,128)S(1)}, u32[]{:S(2)}, u32[]{:S(2)}) collective-permute-start(f32[2,5,16,128]{3,2,1,0:T(8,128)S(1)} %get-tuple-element.35), channel_id=1, source_target_pairs={{1,2},{3,4},{5,6},{2,1},{4,3},{6,5},{9,10},{11,12},{13,14},{10,9},... | collective-permute-start | bytes 245768 | tf_op jit(solution)/shard_map/ppermute | solution.py:39
  13.7 0.6 %collective-permute-start.4 = (f32[2,5,16,128]{3,2,1,0:T(8,128)S(1)}, f32[2,5,16,128]{3,2,1,0:T(8,128)S(1)}, u32[]{:S(2)}, u32[]{:S(2)}) collective-permute-start(f32[2,5,16,128]{3,2,1,0:T(8,128)S(1)} %get-tuple-element.36), channel_id=1, source_target_pairs={{0,8},{8,0},{1,9},{9,1},{2,10},{10,2},{3,11},{11,3},{4,12},{12,4},... | collective-permute-start | bytes 245768 | tf_op jit(solution)/shard_map/ppermute | solution.py:39
  14.3 4.9 %collective-permute-start.5 = (f32[2,5,16,128]{3,2,1,0:T(8,128)S(1)}, f32[2,5,16,128]{3,2,1,0:T(8,128)S(1)}, u32[]{:S(2)}, u32[]{:S(2)}) collective-permute-start(f32[2,5,16,128]{3,2,1,0:T(8,128)S(1)} %get-tuple-element.37), channel_id=1, source_target_pairs={{0,1},{2,3},{4,5},{6,7},{1,0},{3,2},{5,4},{7,6},{8,9},{10,11},{12,... | collective-permute-start | bytes 245768 | tf_op jit(solution)/shard_map/ppermute | solution.py:39
  19.2 1.2 %strain.1 = (f32[12,16,16,128]{3,2,1,0:T(8,128)S(1)}, f32[3,16,16,128]{3,2,1,0:T(8,128)S(1)}, f32[6,20,32,128]{3,2,1,0:T(8,128)S(1)}, f32[9,16,16,128]{3,2,1,0:T(8,128)}, f32[9,16,16,128]{3,2,1,0:T(8,128)}) custom-call(f32[2,5,16,128]{3,2,1,0:T(8,128)S(1)} %collective-permute-done.refs_0_, ...), custom_call_target="tpu_custom_call", output_to_operand_aliasing={{2}: (5, {})} | custom-call | flops 6553600 | bytes 2359296 | tf_op jit(solution)/shard_map/strain/pallas_call | solution.py:632
  20.4 0.0 collective-permute-done.3.refs_0_
  20.4 0.0 collective-permute-done.4.refs_1_
  20.4 1.2 %collective-permute-done.5.refs_2_ = f32[2,5,16,128]{3,2,1,0:T(8,128)S(1)} collective-permute-done((f32[2,5,16,128]{3,2,1,0:T(8,128)S(1)}, f32[2,5,16,128]{3,2,1,0:T(8,128)S(1)}, u32[]{:S(2)}, u32[]{:S(2)}) %collective-permute-start.5) | collective-permute-done | bytes 81952 | tf_op jit(solution)/shard_map/ppermute | solution.py:39
  21.7 0.3 %gradient.1 = (f32[12,16,16,128]{3,2,1,0:T(8,128)S(1)}, f32[3,16,16,128]{3,2,1,0:T(8,128)S(1)}) custom-call(f32[2,5,16,128]{3,2,1,0:T(8,128)S(1)} %collective-permute-done.3.refs_0_, f32[2,5,16,128]{3,2,1,0:T(8,128)S(1)} %collective-permute-done.4.refs_1_, ...), custom_call_target="tpu_custom_call", output_to_operand_aliasing={{0}: (6, {}), {1}: (7, {})} | custom-call | flops 983040 | bytes 262144 | tf_op jit(solution)/shard_map/gradient/pallas_call | solution.py:644
  21.9 0.1 collective-permute-start.6
  22.0 1.2 %outputs.1 = (f32[9,16,16,128]{3,2,1,0:T(8,128)}, f32[9,16,16,128]{3,2,1,0:T(8,128)}) custom-call(f32[12,16,16,128]{3,2,1,0:T(8,128)S(1)} %get-tuple-element.45.strain, f32[12,20,32,128]{3,2,1,0:T(8,128)S(1)} %get-tuple-element.38.refs_3_.stress, ...), custom_call_target="tpu_custom_call", output_to_operand_aliasing={{0}: (4, {}), {1}: (5, {})} | custom-call | flops 1966080 | bytes 2359296 | tf_op jit(solution)/shard_map/outputs/pallas_call | solution.py:657
  23.3 0.5 %collective-permute-done.6.other = f32[3,16,16,128]{3,2,1,0:T(8,128)S(1)} collective-permute-done((f32[3,16,16,128]{3,2,1,0:T(8,128)S(1)}, f32[3,16,16,128]{3,2,1,0:T(8,128)S(1)}, u32[]{:S(2)}, u32[]{:S(2)}) %collective-permute-start.6) | collective-permute-done | bytes 393248 | tf_op jit(solution)/shard_map/ppermute | solution.py:654
  23.7 0.8 %sum.1 = f32[3,16,16,128]{3,2,1,0:T(8,128)} custom-call(f32[3,16,16,128]{3,2,1,0:T(8,128)S(1)} %get-tuple-element.50.mine, f32[3,16,16,128]{3,2,1,0:T(8,128)S(1)} %collective-permute-done.6.other), custom_call_target="tpu_custom_call" | custom-call | flops 98304 | bytes 1179648 | tf_op jit(solution)/shard_map/sum/pallas_call | solution.py:668
Async XLA Ops:
  0.6 10.8 %copy-start.1 = (f32[1,9,16,16,128]{4,3,2,1,0:T(8,128)S(1)}, f32[1,9,16,16,128]{4,3,2,1,0:T(8,128)}, u32[]{:S(2)}) copy-start(f32[1,9,16,16,128]{4,3,2,1,0:T(8,128)} %param.10) | copy-start | bytes 3538948
  0.6 10.8 %copy-start = (f32[1,9,16,16,128]{4,3,2,1,0:T(8,128)S(1)}, f32[1,9,16,16,128]{4,3,2,1,0:T(8,128)}, u32[]{:S(2)}) copy-start(f32[1,9,16,16,128]{4,3,2,1,0:T(8,128)} %param.9) | copy-start | bytes 3538948
  2.2 10.6 %collective-permute-start = (f32[2,5,16,128]{3,2,1,0:T(8,128)S(1)}, f32[2,5,16,128]{3,2,1,0:T(8,128)S(1)}, u32[]{:S(2)}, u32[]{:S(2)}) collective-permute-start(f32[2,5,16,128]{3,2,1,0:T(8,128)S(1)} %get-tuple-element.27), channel_id=1, source_target_pairs={{1,2},{3,4},{5,6},{2,1},{4,3},{6,5},{9,10},{11,12},{13,14},{10,9},... | collective-permute-start | bytes 245768 | tf_op jit(solution)/shard_map/ppermute | solution.py:39
  2.8 9.9 %collective-permute-start.1 = (f32[2,5,16,128]{3,2,1,0:T(8,128)S(1)}, f32[2,5,16,128]{3,2,1,0:T(8,128)S(1)}, u32[]{:S(2)}, u32[]{:S(2)}) collective-permute-start(f32[2,5,16,128]{3,2,1,0:T(8,128)S(1)} %get-tuple-element.28), channel_id=1, source_target_pairs={{0,8},{8,0},{1,9},{9,1},{2,10},{10,2},{3,11},{11,3},{4,12},{12,4},... | collective-permute-start | bytes 245768 | tf_op jit(solution)/shard_map/ppermute | solution.py:39
  5.9 6.9 %collective-permute-start.2 = (f32[2,5,16,128]{3,2,1,0:T(8,128)S(1)}, f32[2,5,16,128]{3,2,1,0:T(8,128)S(1)}, u32[]{:S(2)}, u32[]{:S(2)}) collective-permute-start(f32[2,5,16,128]{3,2,1,0:T(8,128)S(1)} %get-tuple-element.29), channel_id=1, source_target_pairs={{0,1},{2,3},{4,5},{6,7},{1,0},{3,2},{5,4},{7,6},{8,9},{10,11},{12,... | collective-permute-start | bytes 245768 | tf_op jit(solution)/shard_map/ppermute | solution.py:39
  13.1 7.4 %collective-permute-start.3 = (f32[2,5,16,128]{3,2,1,0:T(8,128)S(1)}, f32[2,5,16,128]{3,2,1,0:T(8,128)S(1)}, u32[]{:S(2)}, u32[]{:S(2)}) collective-permute-start(f32[2,5,16,128]{3,2,1,0:T(8,128)S(1)} %get-tuple-element.35), channel_id=1, source_target_pairs={{1,2},{3,4},{5,6},{2,1},{4,3},{6,5},{9,10},{11,12},{13,14},{10,9},... | collective-permute-start | bytes 245768 | tf_op jit(solution)/shard_map/ppermute | solution.py:39
  13.7 6.7 %collective-permute-start.4 = (f32[2,5,16,128]{3,2,1,0:T(8,128)S(1)}, f32[2,5,16,128]{3,2,1,0:T(8,128)S(1)}, u32[]{:S(2)}, u32[]{:S(2)}) collective-permute-start(f32[2,5,16,128]{3,2,1,0:T(8,128)S(1)} %get-tuple-element.36), channel_id=1, source_target_pairs={{0,8},{8,0},{1,9},{9,1},{2,10},{10,2},{3,11},{11,3},{4,12},{12,4},... | collective-permute-start | bytes 245768 | tf_op jit(solution)/shard_map/ppermute | solution.py:39
  14.3 7.3 %collective-permute-start.5 = (f32[2,5,16,128]{3,2,1,0:T(8,128)S(1)}, f32[2,5,16,128]{3,2,1,0:T(8,128)S(1)}, u32[]{:S(2)}, u32[]{:S(2)}) collective-permute-start(f32[2,5,16,128]{3,2,1,0:T(8,128)S(1)} %get-tuple-element.37), channel_id=1, source_target_pairs={{0,1},{2,3},{4,5},{6,7},{1,0},{3,2},{5,4},{7,6},{8,9},{10,11},{12,... | collective-permute-start | bytes 245768 | tf_op jit(solution)/shard_map/ppermute | solution.py:39
  21.9 1.8 %collective-permute-start.6 = (f32[3,16,16,128]{3,2,1,0:T(8,128)S(1)}, f32[3,16,16,128]{3,2,1,0:T(8,128)S(1)}, u32[]{:S(2)}, u32[]{:S(2)}) collective-permute-start(f32[3,16,16,128]{3,2,1,0:T(8,128)S(1)} %get-tuple-element.50.mine), channel_id=1, source_target_pairs={{0,16},{16,0},{1,17},{17,1},{2,18},{18,2},{3,19},{19,3},{4,20},{20... | collective-permute-start | bytes 1179656 | tf_op jit(solution)/shard_map/ppermute | solution.py:654

commit v7 on v6

--- a/solution.py
+++ b/solution.py
@@ -79,15 +79,10 @@
     )
 
 
-def pack_kernel(links, width_y, forward, adjoint, receiver_cell, residual_amp, *refs):
-    sends, (added, stress, cells_now, amps_now, sems) = refs[: len(links)], refs[len(links) :]
+def early_pack_kernel(links, forward, adjoint, *refs):
+    sends, sems = refs[: len(links)], refs[-1]
     tile = forward.shape[1:3]
-    copies = [
-        pltpu.make_async_copy(receiver_cell, cells_now, sems.at[0]),
-        pltpu.make_async_copy(residual_amp, amps_now, sems.at[1]),
-    ]
-    for copy in copies:
-        copy.start()
+    copies = []
     for (axis, dim, first), send in zip(links, sends):
         lower = is_lower(axis, first)
         for slot, ((up_part, up_at), (low_part, low_at)) in enumerate(zip(*stress_plan(dim))):
@@ -98,16 +93,22 @@
                 copy = pltpu.make_async_copy(source, send.at[wave, slot], sems.at[len(copies)])
                 copy.start()
                 copies.append(copy)
-    for wave in range(2):
-        clear_rim(
-            stress, *([6 * wave + part for part in STRESS_ALONG[dim]] for dim in range(2))
-        )
-    columns = column_ids(*tile, width_y, forward.shape[-1])
-    for copy in copies[:2]:
+    for copy in copies:
         copy.wait()
-    added[...] = receiver_sum(cells_now[...], amps_now[...], columns)
-    for copy in copies[2:]:
-        copy.wait()
+
+
+def pack_kernel(links, forward, adjoint, *sends):
+    for (axis, dim, first), send in zip(links, sends):
+        lower = is_lower(axis, first)
+
+        def put(plan):
+            for wave, fields in enumerate((forward, adjoint)):
+                for slot, (part, index) in enumerate(plan):
+                    send[wave, slot] = face(fields, 3 + part, dim, index, False)[...]
+
+        upper_plan, lower_plan = stress_plan(dim)
+        pl.when(lower)(functools.partial(put, lower_plan))
+        pl.when(jnp.logical_not(lower))(functools.partial(put, upper_plan))
 
 
 def column_ids(tile_x, tile_y, width_y, lanes):
@@ -217,10 +218,10 @@
     density,
     source_cell,
     source_amp,
-    received,
+    receiver_cell,
+    residual_amp,
     forward,
     adjoint,
-    _,
     stress,
     velocity,
     accel,
@@ -229,6 +230,7 @@
     scaled_lame,
     scaled_shear,
     sourced,
+    received,
     gained,
     lame_now,
     shear_now,
@@ -251,7 +253,11 @@
     columns = column_ids(tile_x, tile_y, width_y, depth)
     lane = lax.broadcasted_iota(jnp.int32, columns.shape, 1)
     sourced[...] = jnp.where(columns * depth + lane == source_cell[0], source_amp[0], 0.0)
+    received[...] = receiver_sum(receiver_cell[...], residual_amp[...], columns)
     for wave, added in enumerate((sourced, received)):
+        clear_rim(
+            stress, *([6 * wave + part for part in STRESS_ALONG[dim]] for dim in range(2))
+        )
         for layer in range(3):
             rim_added[wave, 0, layer] = added[pl.ds(cells + layer * tile_y, tile_y), :]
             begin = cells + 3 * tile_y + layer * tile_x
@@ -563,23 +569,29 @@
 
     send_shapes = [buffers(dim) for _, dim, _ in links]
     count = len(links)
-    receivers = receiver_cell.shape[-1]
     rows = tile_x * tile_y + 3 * (tile_x + tile_y)
-    *sends, added, stress = pl.pallas_call(
-        functools.partial(pack_kernel, links, width_y),
-        out_shape=send_shapes + [pltpu.VMEM((rows, depth), jnp.float32), padded(12)],
-        in_specs=[hbm] * 4,
-        out_specs=[vmem] * (count + 2),
-        scratch_shapes=[
-            pltpu.VMEM((1, receivers), jnp.int32),
-            pltpu.VMEM((1, receivers), jnp.float32),
-            pltpu.SemaphoreType.DMA((2 + 2 * SLOTS * count,)),
-        ],
+    sends = pl.pallas_call(
+        functools.partial(early_pack_kernel, links[:1]),
+        out_shape=send_shapes[:1],
+        in_specs=[hbm] * 2,
+        out_specs=[vmem],
+        scratch_shapes=[pltpu.SemaphoreType.DMA((2 * SLOTS,))],
         compiler_params=params,
-        cost_estimate=cost(6 * rows * receivers * depth, 2 * SLOTS * count * tile_x * depth * 4),
-        name="pack",
-    )(*(in_hbm(x) for x in (forward, adjoint, receiver_cell, residual_amp)))
-    halos = exchange(links, sends)
+        cost_estimate=cost(0, 2 * 2 * SLOTS * tile_x * depth * 4),
+        name="early_pack",
+    )(in_hbm(forward), in_hbm(adjoint))
+    halos = exchange(links[:1], sends)
+    if count > 1:
+        sends = pl.pallas_call(
+            functools.partial(pack_kernel, links[1:]),
+            out_shape=send_shapes[1:],
+            in_specs=[vmem] * 2,
+            out_specs=[vmem] * (count - 1),
+            compiler_params=params,
+            cost_estimate=cost(0, 2 * 2 * SLOTS * (count - 1) * tile_x * depth * 4),
+            name="pack",
+        )(forward, adjoint)
+        halos += exchange(links[1:], sends)
 
     stress, velocity, accel, rim_added, buoyancy, scaled_lame, scaled_shear = pl.pallas_call(
         functools.partial(velocity_kernel, width_y),
@@ -594,8 +606,8 @@
         ],
         in_specs=[hbm] * 3 + [smem] * 2 + [vmem] * 4,
         out_specs=[vmem] * 7,
-        input_output_aliases={8: 0},
         scratch_shapes=[
+            pltpu.VMEM((rows, depth), jnp.float32),
             pltpu.VMEM((rows, depth), jnp.float32),
             tile(6),
             tile(),
@@ -610,10 +622,10 @@
         *(in_hbm(x) for x in (lame_lambda, shear_modulus, density)),
         source_cell,
         source_amp,
-        added,
+        receiver_cell,
+        residual_amp,
         forward,
         adjoint,
-        stress,
     )
 
     velocity, *sends = pl.pallas_call(

time: 24.7 us -> 24.3 us (0.984)
  starting transfers between devices: 14.2 us -> 13.8 us
    ppermute x6, starting transfers between devices: 14.2 us -> 13.7 us  [swap(): return lax.ppermute(value, axis, pairs + [(j, i) for i, j in pairs])]
    pallas_call x1 -> x2, Pallas kernels: 1.5 us -> 1.12 us  [the longest x1 1.06 us: body(): pl.pallas_call(functools.partial(early_pack_kernel, links[:1]), out_shape...]
    pallas_call x1, Pallas kernels: 1.28 us -> 1.59 us  [body(): pl.pallas_call(functools.partial(velocity_kernel, width_y), out_shape=[pa...]
  transfers between devices with their start and end apart: 7 -> 7, of which waited for: 2 -> 2; matrix products, arithmetic and copies ran while one was open for 0% -> 0% of each run, Pallas kernels for 15% -> 17%
where the time goes in v7:
time: 24.3 us; the launch traced here: 24.1 us
  starting transfers between devices  13.8 us (57%)
  Pallas kernels  6.48 us (27%)
  between operations  2.11 us (9%)
  waiting for transfers between devices  1.7 us (7%)
    ppermute x6, starting transfers between devices, swap(): return lax.ppermute(value, axis, pairs + [(j, i) for i, j in pairs])  13.7 us
    pallas_call x1, Pallas kernels, body(): pl.pallas_call(functools.partial(velocity_kernel, width_y), out_shape=[pa...  1.59 us
    pallas_call x1, Pallas kernels, body(): pl.pallas_call(functools.partial(output_kernel, chunk), out_shape=[out_sh...  1.24 us
    ppermute x6, waiting for transfers between devices, swap(): return lax.ppermute(value, axis, pairs + [(j, i) for i, j in pairs])  1.24 us
    pallas_call x1, Pallas kernels, body(): pl.pallas_call(functools.partial(strain_kernel, links), out_shape=[tile(1...  1.16 us
    pallas_call x1, Pallas kernels, body(): pl.pallas_call(functools.partial(early_pack_kernel, links[:1]), out_shape...  1.06 us
    pallas_call x1, Pallas kernels, body(): pl.pallas_call(sum_kernel, out_shape=jax.ShapeDtypeStruct((3, tile_x, til...  0.78 us
  transfers between devices with their start and end apart: 7, of which 2 were waited for; matrix products, arithmetic and copies ran while one was open for 0% of the time, Pallas kernels for 17%

profile of v7, /device:TPU:0, one launch (start us, length us, event | category | flops | bytes accessed | tf_op | source)
XLA Modules:
  0.0 24.1 jit_solution(8286454435543967489)
XLA Ops:
  0.6 0.0 copy-start.1
  0.6 0.0 copy-start
  0.6 1.1 %early_pack.1 = f32[2,5,16,128]{3,2,1,0:T(8,128)S(1)} custom-call(f32[9,16,16,128]{3,2,1,0:T(8,128)} %bitcast.4, f32[9,16,16,128]{3,2,1,0:T(8,128)} %bitcast.7), custom_call_target="tpu_custom_call" | custom-call | bytes 163840 | tf_op jit(solution)/shard_map/early_pack/pallas_call | solution.py:573
  1.7 0.0 copy-start.2
  1.7 0.0 copy-start.3
  1.7 0.7 %collective-permute-start = (f32[2,5,16,128]{3,2,1,0:T(8,128)S(1)}, f32[2,5,16,128]{3,2,1,0:T(8,128)S(1)}, u32[]{:S(2)}, u32[]{:S(2)}) collective-permute-start(f32[2,5,16,128]{3,2,1,0:T(8,128)S(1)} %early_pack.1), channel_id=1, source_target_pairs={{1,2},{3,4},{5,6},{2,1},{4,3},{6,5},{9,10},{11,12},{13,14},{10,9},... | collective-permute-start | bytes 245768 | tf_op jit(solution)/shard_map/ppermute | solution.py:39
  2.4 0.0 copy-done.1
  2.4 0.0 copy-done
  2.4 0.1 pack.1
  2.5 3.0 %collective-permute-start.1 = (f32[2,5,16,128]{3,2,1,0:T(8,128)S(1)}, f32[2,5,16,128]{3,2,1,0:T(8,128)S(1)}, u32[]{:S(2)}, u32[]{:S(2)}) collective-permute-start(f32[2,5,16,128]{3,2,1,0:T(8,128)S(1)} %get-tuple-element.24), channel_id=1, source_target_pairs={{0,8},{8,0},{1,9},{9,1},{2,10},{10,2},{3,11},{11,3},{4,12},{12,4},... | collective-permute-start | bytes 245768 | tf_op jit(solution)/shard_map/ppermute | solution.py:39
  5.5 4.3 %collective-permute-start.2 = (f32[2,5,16,128]{3,2,1,0:T(8,128)S(1)}, f32[2,5,16,128]{3,2,1,0:T(8,128)S(1)}, u32[]{:S(2)}, u32[]{:S(2)}) collective-permute-start(f32[2,5,16,128]{3,2,1,0:T(8,128)S(1)} %get-tuple-element.25), channel_id=1, source_target_pairs={{0,1},{2,3},{4,5},{6,7},{1,0},{3,2},{5,4},{7,6},{8,9},{10,11},{12,... | collective-permute-start | bytes 245768 | tf_op jit(solution)/shard_map/ppermute | solution.py:39
  11.1 0.0 copy-done.2
  11.1 0.0 copy-done.3
  11.1 1.6 %velocity.1 = (f32[12,20,32,128]{3,2,1,0:T(8,128)S(1)}, f32[6,20,32,128]{3,2,1,0:T(8,128)S(1)}, f32[3,16,16,128]{3,2,1,0:T(8,128)S(1)}, f32[2,2,3,16,128]{4,3,2,...) custom-call(f32[16,16,128]{2,1,0:T(8,128)} %lame.1, ...), custom_call_target="tpu_custom_call" | custom-call | flops 6553600 | bytes 2359296 | tf_op jit(solution)/shard_map/velocity/pallas_call | solution.py:596
  12.7 0.0 collective-permute-done.refs_0_
  12.7 0.0 collective-permute-done.1.refs_1_
  12.8 0.0 collective-permute-done.2.refs_2_
  12.8 0.3 %boundary.1 = (f32[6,20,32,128]{3,2,1,0:T(8,128)S(1)}, f32[2,5,16,128]{3,2,1,0:T(8,128)S(1)}, f32[2,5,16,128]{3,2,1,0:T(8,128)S(1)}, f32[2,5,16,128]{3,2,1,0:T(8,128)S(1)}) custom-call(f32[2,5,16,128]{3,2,1,0:T(8,128)S(1)} %collective-permute-done.refs_0_, f32[2,5,16,128]{3,2,1,0:T(8,128)S(1)} %collective-permute-done.1.refs_1_, ...), custom_call_target="tpu_custom_call", output_to_operand_aliasing={{0}: (5, {})} | custom-call | flops 32768 | bytes 163840 | tf_op jit(solution)/shard_map/boundary/pallas_call | solution.py:631
  13.1 0.7 %collective-permute-start.3 = (f32[2,5,16,128]{3,2,1,0:T(8,128)S(1)}, f32[2,5,16,128]{3,2,1,0:T(8,128)S(1)}, u32[]{:S(2)}, u32[]{:S(2)}) collective-permute-start(f32[2,5,16,128]{3,2,1,0:T(8,128)S(1)} %get-tuple-element.29), channel_id=1, source_target_pairs={{1,2},{3,4},{5,6},{2,1},{4,3},{6,5},{9,10},{11,12},{13,14},{10,9},... | collective-permute-start | bytes 245768 | tf_op jit(solution)/shard_map/ppermute | solution.py:39
  13.7 0.6 %collective-permute-start.4 = (f32[2,5,16,128]{3,2,1,0:T(8,128)S(1)}, f32[2,5,16,128]{3,2,1,0:T(8,128)S(1)}, u32[]{:S(2)}, u32[]{:S(2)}) collective-permute-start(f32[2,5,16,128]{3,2,1,0:T(8,128)S(1)} %get-tuple-element.30), channel_id=1, source_target_pairs={{0,8},{8,0},{1,9},{9,1},{2,10},{10,2},{3,11},{11,3},{4,12},{12,4},... | collective-permute-start | bytes 245768 | tf_op jit(solution)/shard_map/ppermute | solution.py:39
  14.3 4.5 %collective-permute-start.5 = (f32[2,5,16,128]{3,2,1,0:T(8,128)S(1)}, f32[2,5,16,128]{3,2,1,0:T(8,128)S(1)}, u32[]{:S(2)}, u32[]{:S(2)}) collective-permute-start(f32[2,5,16,128]{3,2,1,0:T(8,128)S(1)} %get-tuple-element.31), channel_id=1, source_target_pairs={{0,1},{2,3},{4,5},{6,7},{1,0},{3,2},{5,4},{7,6},{8,9},{10,11},{12,... | collective-permute-start | bytes 245768 | tf_op jit(solution)/shard_map/ppermute | solution.py:39
  18.8 1.2 %strain.1 = (f32[12,16,16,128]{3,2,1,0:T(8,128)S(1)}, f32[3,16,16,128]{3,2,1,0:T(8,128)S(1)}, f32[6,20,32,128]{3,2,1,0:T(8,128)S(1)}, f32[9,16,16,128]{3,2,1,0:T(8,128)}, f32[9,16,16,128]{3,2,1,0:T(8,128)}) custom-call(f32[2,5,16,128]{3,2,1,0:T(8,128)S(1)} %collective-permute-done.refs_0_, ...), custom_call_target="tpu_custom_call", output_to_operand_aliasing={{2}: (5, {})} | custom-call | flops 6553600 | bytes 2359296 | tf_op jit(solution)/shard_map/strain/pallas_call | solution.py:644
  20.0 0.0 collective-permute-done.3.refs_0_
  20.0 0.0 collective-permute-done.4.refs_1_
  20.0 1.2 %collective-permute-done.5.refs_2_ = f32[2,5,16,128]{3,2,1,0:T(8,128)S(1)} collective-permute-done((f32[2,5,16,128]{3,2,1,0:T(8,128)S(1)}, f32[2,5,16,128]{3,2,1,0:T(8,128)S(1)}, u32[]{:S(2)}, u32[]{:S(2)}) %collective-permute-start.5) | collective-permute-done | bytes 81952 | tf_op jit(solution)/shard_map/ppermute | solution.py:39
  21.2 0.3 %gradient.1 = (f32[12,16,16,128]{3,2,1,0:T(8,128)S(1)}, f32[3,16,16,128]{3,2,1,0:T(8,128)S(1)}) custom-call(f32[2,5,16,128]{3,2,1,0:T(8,128)S(1)} %collective-permute-done.3.refs_0_, f32[2,5,16,128]{3,2,1,0:T(8,128)S(1)} %collective-permute-done.4.refs_1_, ...), custom_call_target="tpu_custom_call", output_to_operand_aliasing={{0}: (6, {}), {1}: (7, {})} | custom-call | flops 983040 | bytes 262144 | tf_op jit(solution)/shard_map/gradient/pallas_call | solution.py:656
  21.5 0.1 collective-permute-start.6
  21.6 1.2 %outputs.1 = (f32[9,16,16,128]{3,2,1,0:T(8,128)}, f32[9,16,16,128]{3,2,1,0:T(8,128)}) custom-call(f32[12,16,16,128]{3,2,1,0:T(8,128)S(1)} %get-tuple-element.39.strain, f32[12,20,32,128]{3,2,1,0:T(8,128)S(1)} %get-tuple-element.32.refs_3_.stress, ...), custom_call_target="tpu_custom_call", output_to_operand_aliasing={{0}: (4, {}), {1}: (5, {})} | custom-call | flops 1966080 | bytes 2359296 | tf_op jit(solution)/shard_map/outputs/pallas_call | solution.py:669
  22.9 0.5 %collective-permute-done.6.other = f32[3,16,16,128]{3,2,1,0:T(8,128)S(1)} collective-permute-done((f32[3,16,16,128]{3,2,1,0:T(8,128)S(1)}, f32[3,16,16,128]{3,2,1,0:T(8,128)S(1)}, u32[]{:S(2)}, u32[]{:S(2)}) %collective-permute-start.6) | collective-permute-done | bytes 393248 | tf_op jit(solution)/shard_map/ppermute | solution.py:666
  23.3 0.8 %sum.1 = f32[3,16,16,128]{3,2,1,0:T(8,128)} custom-call(f32[3,16,16,128]{3,2,1,0:T(8,128)S(1)} %get-tuple-element.44.mine, f32[3,16,16,128]{3,2,1,0:T(8,128)S(1)} %collective-permute-done.6.other), custom_call_target="tpu_custom_call" | custom-call | flops 98304 | bytes 1179648 | tf_op jit(solution)/shard_map/sum/pallas_call | solution.py:680
Async XLA Ops:
  0.6 1.8 %copy-start.1 = (f32[1,9,16,16,128]{4,3,2,1,0:T(8,128)S(1)}, f32[1,9,16,16,128]{4,3,2,1,0:T(8,128)}, u32[]{:S(2)}) copy-start(f32[1,9,16,16,128]{4,3,2,1,0:T(8,128)} %param.10) | copy-start | bytes 3538948
  0.6 1.8 %copy-start = (f32[1,9,16,16,128]{4,3,2,1,0:T(8,128)S(1)}, f32[1,9,16,16,128]{4,3,2,1,0:T(8,128)}, u32[]{:S(2)}) copy-start(f32[1,9,16,16,128]{4,3,2,1,0:T(8,128)} %param.9) | copy-start | bytes 3538948
  1.7 9.4 %copy-start.2 = (s32[1,256]{1,0:T(1,128)S(1)}, s32[1,256]{1,0:T(1,128)}, u32[]{:S(2)}) copy-start(s32[1,256]{1,0:T(1,128)} %receiver_cell.1) | copy-start | bytes 3076
  1.7 9.4 %copy-start.3 = (f32[1,256]{1,0:T(1,128)S(1)}, f32[1,256]{1,0:T(1,128)}, u32[]{:S(2)}) copy-start(f32[1,256]{1,0:T(1,128)} %residual_amp.1) | copy-start | bytes 3076
  1.7 11.0 %collective-permute-start = (f32[2,5,16,128]{3,2,1,0:T(8,128)S(1)}, f32[2,5,16,128]{3,2,1,0:T(8,128)S(1)}, u32[]{:S(2)}, u32[]{:S(2)}) collective-permute-start(f32[2,5,16,128]{3,2,1,0:T(8,128)S(1)} %early_pack.1), channel_id=1, source_target_pairs={{1,2},{3,4},{5,6},{2,1},{4,3},{6,5},{9,10},{11,12},{13,14},{10,9},... | collective-permute-start | bytes 245768 | tf_op jit(solution)/shard_map/ppermute | solution.py:39
  2.5 10.2 %collective-permute-start.1 = (f32[2,5,16,128]{3,2,1,0:T(8,128)S(1)}, f32[2,5,16,128]{3,2,1,0:T(8,128)S(1)}, u32[]{:S(2)}, u32[]{:S(2)}) collective-permute-start(f32[2,5,16,128]{3,2,1,0:T(8,128)S(1)} %get-tuple-element.24), channel_id=1, source_target_pairs={{0,8},{8,0},{1,9},{9,1},{2,10},{10,2},{3,11},{11,3},{4,12},{12,4},... | collective-permute-start | bytes 245768 | tf_op jit(solution)/shard_map/ppermute | solution.py:39
  5.5 7.2 %collective-permute-start.2 = (f32[2,5,16,128]{3,2,1,0:T(8,128)S(1)}, f32[2,5,16,128]{3,2,1,0:T(8,128)S(1)}, u32[]{:S(2)}, u32[]{:S(2)}) collective-permute-start(f32[2,5,16,128]{3,2,1,0:T(8,128)S(1)} %get-tuple-element.25), channel_id=1, source_target_pairs={{0,1},{2,3},{4,5},{6,7},{1,0},{3,2},{5,4},{7,6},{8,9},{10,11},{12,... | collective-permute-start | bytes 245768 | tf_op jit(solution)/shard_map/ppermute | solution.py:39
  13.1 6.9 %collective-permute-start.3 = (f32[2,5,16,128]{3,2,1,0:T(8,128)S(1)}, f32[2,5,16,128]{3,2,1,0:T(8,128)S(1)}, u32[]{:S(2)}, u32[]{:S(2)}) collective-permute-start(f32[2,5,16,128]{3,2,1,0:T(8,128)S(1)} %get-tuple-element.29), channel_id=1, source_target_pairs={{1,2},{3,4},{5,6},{2,1},{4,3},{6,5},{9,10},{11,12},{13,14},{10,9},... | collective-permute-start | bytes 245768 | tf_op jit(solution)/shard_map/ppermute | solution.py:39
  13.7 6.3 %collective-permute-start.4 = (f32[2,5,16,128]{3,2,1,0:T(8,128)S(1)}, f32[2,5,16,128]{3,2,1,0:T(8,128)S(1)}, u32[]{:S(2)}, u32[]{:S(2)}) collective-permute-start(f32[2,5,16,128]{3,2,1,0:T(8,128)S(1)} %get-tuple-element.30), channel_id=1, source_target_pairs={{0,8},{8,0},{1,9},{9,1},{2,10},{10,2},{3,11},{11,3},{4,12},{12,4},... | collective-permute-start | bytes 245768 | tf_op jit(solution)/shard_map/ppermute | solution.py:39
  14.3 6.9 %collective-permute-start.5 = (f32[2,5,16,128]{3,2,1,0:T(8,128)S(1)}, f32[2,5,16,128]{3,2,1,0:T(8,128)S(1)}, u32[]{:S(2)}, u32[]{:S(2)}) collective-permute-start(f32[2,5,16,128]{3,2,1,0:T(8,128)S(1)} %get-tuple-element.31), channel_id=1, source_target_pairs={{0,1},{2,3},{4,5},{6,7},{1,0},{3,2},{5,4},{7,6},{8,9},{10,11},{12,... | collective-permute-start | bytes 245768 | tf_op jit(solution)/shard_map/ppermute | solution.py:39
  21.5 1.8 %collective-permute-start.6 = (f32[3,16,16,128]{3,2,1,0:T(8,128)S(1)}, f32[3,16,16,128]{3,2,1,0:T(8,128)S(1)}, u32[]{:S(2)}, u32[]{:S(2)}) collective-permute-start(f32[3,16,16,128]{3,2,1,0:T(8,128)S(1)} %get-tuple-element.44.mine), channel_id=1, source_target_pairs={{0,16},{16,0},{1,17},{17,1},{2,18},{18,2},{3,19},{19,3},{4,20},{20... | collective-permute-start | bytes 1179656 | tf_op jit(solution)/shard_map/ppermute | solution.py:666

commit v8 on v7

--- a/solution.py
+++ b/solution.py
@@ -27,11 +27,9 @@
 
 
 def links_of(sizes):
-    far_y, near_y, *along = ("ty", 1, 1), ("ty", 1, 0), ("tx", 0, 1), ("tx", 0, 0)
-    return [
-        [link for link in order if link[2] + 1 < sizes[link[0]]]
-        for order in ((far_y, *along, near_y), (far_y, *along, near_y))
-    ]
+    along_x = (("tx", 0, 1), ("tx", 0, 0))
+    along_y = (("ty", 1, 1), ("ty", 1, 0))
+    return [[link for link in order if link[2] + 1 < sizes[link[0]]] for order in (along_x, along_y)]
 
 
 def swap(value, axis, first):
@@ -49,66 +47,86 @@
     return (partner >= 0) & (partner < lax.axis_size(axis))
 
 
-def send_faces(field, count, links, sends, plans):
-    for (axis, dim, first), send in zip(links, sends):
-        lower = is_lower(axis, first)
-        upper_plan, lower_plan = plans[dim]
-
-        def put(plan):
-            for wave in range(2):
-                for slot, (part, index) in enumerate(plan):
-                    send[wave, slot] = face(field, count * wave + part, dim, index, True)[...]
-
-        pl.when(lower)(functools.partial(put, lower_plan))
-        pl.when(jnp.logical_not(lower))(functools.partial(put, upper_plan))
+def by_role(link, act, upper, lower):
+    lower_here = is_lower(link[0], link[2])
+    pl.when(lower_here)(lambda: act(lower, True))
+    pl.when(jnp.logical_not(lower_here))(lambda: act(upper, False))
+
+
+SPARE = SLOTS - 1
 
 
 def stress_plan(dim):
     n, a, b = STRESS_ALONG[dim]
-    return (
-        ((n, 0), (n, 1), (a, 0), (b, 0), (b, 0)),
-        ((n, -1), (a, -2), (a, -1), (b, -2), (b, -1)),
-    )
+    return ((n, 0), (n, 1), (a, 0), (b, 0)), ((n, -1), (a, -2), (a, -1), (b, -2), (b, -1))
 
 
 def velocity_plan(dim):
     n, a, b = VELOCITY_ALONG[dim]
-    return (
-        ((n, 0), (a, 0), (a, 1), (b, 0), (b, 1)),
-        ((n, -2), (n, -1), (a, -1), (b, -1), (b, -1)),
-    )
-
-
-def early_pack_kernel(links, forward, adjoint, *refs):
-    sends, sems = refs[: len(links)], refs[-1]
-    tile = forward.shape[1:3]
-    copies = []
-    for (axis, dim, first), send in zip(links, sends):
-        lower = is_lower(axis, first)
-        for slot, ((up_part, up_at), (low_part, low_at)) in enumerate(zip(*stress_plan(dim))):
-            part = 3 + jnp.where(lower, low_part, up_part)
-            at = jnp.where(lower, low_at % tile[dim], up_at % tile[dim])
-            for wave, fields in enumerate((forward, adjoint)):
-                source = fields.at[part, at] if dim == 0 else fields.at[part, :, at, :]
-                copy = pltpu.make_async_copy(source, send.at[wave, slot], sems.at[len(copies)])
-                copy.start()
-                copies.append(copy)
-    for copy in copies:
+    return ((n, 0), (a, 0), (a, 1), (b, 0), (b, 1)), ((n, -2), (n, -1), (a, -1), (b, -1))
+
+
+def early_pack_kernel(links, forward, adjoint, density, *refs):
+    sends, (density_now, sems) = refs[: len(links)], refs[len(links) :]
+    tile_x = forward.shape[1]
+    whole = pltpu.make_async_copy(density, density_now, sems.at[0])
+    whole.start()
+    waits = []
+    for at, (link, send) in enumerate(zip(links, sends)):
+
+        def sources(plan, lower, wave):
+            fields = (forward, adjoint)[wave]
+            found = [fields.at[3 + part, index % tile_x] for part, index in plan]
+            return found if lower else found + [density.at[wave]]
+
+        def start(plan, lower):
+            for wave in range(2):
+                for slot, source in enumerate(sources(plan, lower, wave)):
+                    pltpu.make_async_copy(
+                        source, send.at[wave, slot], sems.at[1 + (2 * at + wave) * SLOTS + slot]
+                    ).start()
+
+        by_role(link, start, *stress_plan(link[1]))
+        for wave in range(2):
+            for slot in range(SLOTS):
+                waits.append(
+                    pltpu.make_async_copy(
+                        density.at[0],
+                        send.at[wave, slot],
+                        sems.at[1 + (2 * at + wave) * SLOTS + slot],
+                    )
+                )
+    for copy in waits:
         copy.wait()
-
-
-def pack_kernel(links, forward, adjoint, *sends):
-    for (axis, dim, first), send in zip(links, sends):
-        lower = is_lower(axis, first)
-
-        def put(plan):
+    whole.wait()
+
+
+def pack_kernel(links, forward, adjoint, density, *sends):
+    for link, send in zip(links, sends):
+        dim = link[1]
+
+        def put(plan, lower):
             for wave, fields in enumerate((forward, adjoint)):
                 for slot, (part, index) in enumerate(plan):
                     send[wave, slot] = face(fields, 3 + part, dim, index, False)[...]
-
-        upper_plan, lower_plan = stress_plan(dim)
-        pl.when(lower)(functools.partial(put, lower_plan))
-        pl.when(jnp.logical_not(lower))(functools.partial(put, upper_plan))
+                if not lower:
+                    send[wave, SPARE] = light_face(density, dim, wave)
+
+        by_role(link, put, *stress_plan(dim))
+
+
+def send_velocities(links, velocity, buoyancy, sends):
+    for link, send in zip(links, sends):
+        dim = link[1]
+
+        def put(plan, lower):
+            for wave in range(2):
+                for slot, (part, index) in enumerate(plan):
+                    send[wave, slot] = face(velocity, 3 * wave + part, dim, index, True)[...]
+                if lower:
+                    send[wave, SPARE] = light_face(buoyancy, dim, -1 - wave)
+
+        by_role(link, put, *velocity_plan(dim))
 
 
 def column_ids(tile_x, tile_y, width_y, lanes):
@@ -215,13 +233,11 @@
     width_y,
     lame,
     shear,
-    density,
-    source_cell,
-    source_amp,
     receiver_cell,
     residual_amp,
     forward,
     adjoint,
+    density,
     stress,
     velocity,
     accel,
@@ -229,47 +245,38 @@
     buoyancy,
     scaled_lame,
     scaled_shear,
-    sourced,
     received,
     gained,
     lame_now,
     shear_now,
-    density_now,
     sems,
 ):
     tile_x, tile_y, depth = density.shape
     copies = [
-        pltpu.make_async_copy(source, target, sems.at[at])
-        for at, (source, target) in enumerate((
-            (density, density_now),
-            (lame, lame_now),
-            (shear, shear_now),
-        ))
+        pltpu.make_async_copy(lame, lame_now, sems.at[0]),
+        pltpu.make_async_copy(shear, shear_now, sems.at[1]),
     ]
     for copy in copies:
         copy.start()
     cells = tile_x * tile_y
     middle = pl.ds(ROWS, tile_y)
     columns = column_ids(tile_x, tile_y, width_y, depth)
-    lane = lax.broadcasted_iota(jnp.int32, columns.shape, 1)
-    sourced[...] = jnp.where(columns * depth + lane == source_cell[0], source_amp[0], 0.0)
     received[...] = receiver_sum(receiver_cell[...], residual_amp[...], columns)
-    for wave, added in enumerate((sourced, received)):
+    for layer in range(3):
+        rim_added[0, layer] = received[pl.ds(cells + layer * tile_y, tile_y), :]
+        rim_added[1, layer] = received[pl.ds(cells + 3 * tile_y + layer * tile_x, tile_x), :]
+    for wave in range(2):
         clear_rim(
             stress, *([6 * wave + part for part in STRESS_ALONG[dim]] for dim in range(2))
         )
-        for layer in range(3):
-            rim_added[wave, 0, layer] = added[pl.ds(cells + layer * tile_y, tile_y), :]
-            begin = cells + 3 * tile_y + layer * tile_x
-            rim_added[wave, 1, layer] = added[pl.ds(begin, tile_x), :]
 
     def fill(x, carry):
-        for wave, (fields, added) in enumerate(((forward, sourced), (adjoint, received))):
-            extra = added[pl.ds(pl.multiple_of(x * tile_y, 8), tile_y), :]
+        extra = received[pl.ds(pl.multiple_of(x * tile_y, 8), tile_y), :]
+        for wave, fields in enumerate((forward, adjoint)):
             for part in range(6):
                 value = fields[3 + part, x]
                 stress[6 * wave + part, x + LAYERS, middle, :] = (
-                    value + extra if part < 3 else value
+                    value + extra if wave == 1 and part < 3 else value
                 )
         return carry
 
@@ -298,7 +305,7 @@
         copy.wait()
 
     def finish(x, carry):
-        light = 1.0 / density_now[x]
+        light = 1.0 / density[x]
         buoyancy[x] = light
         scaled_lame[x] = time_step * lame_now[x]
         scaled_shear[x] = time_step * shear_now[x]
@@ -316,55 +323,116 @@
 
 
 def stress_halo_terms(links, received, rim_added, waves, add):
-    for (axis, dim, first), halo in zip(links, received):
+    for link, halo in zip(links, received):
+        dim = link[1]
         part_n, part_a, part_b = ACCEL_OF[dim]
-        lower = is_lower(axis, first)
-        real = has_peer(axis, first)
-
-        @pl.when(real & lower)
+
+        def normal(wave, slot, layer):
+            value = halo[wave, slot]
+            return value + rim_added[dim, layer] if wave == 1 else value
+
         def after():
             for wave in waves:
-                n0 = halo[wave, 0] + rim_added[wave, dim, 1]
-                n1 = halo[wave, 1] + rim_added[wave, dim, 2]
+                n0, n1 = normal(wave, 0, 1), normal(wave, 1, 2)
                 add(wave, part_n, dim, -1, near * n0 + far * n1)
                 add(wave, part_n, dim, -2, far * n0)
                 add(wave, part_a, dim, -1, far * halo[wave, 2])
                 add(wave, part_b, dim, -1, far * halo[wave, 3])
 
-        @pl.when(real & jnp.logical_not(lower))
         def before():
             for wave in waves:
-                n0 = halo[wave, 0] + rim_added[wave, dim, 0]
-                add(wave, part_n, dim, 0, -far * n0)
+                add(wave, part_n, dim, 0, -far * normal(wave, 0, 0))
                 for part, slot in ((part_a, 1), (part_b, 3)):
                     outer, inner = halo[wave, slot], halo[wave, slot + 1]
                     add(wave, part, dim, 0, -near * inner - far * outer)
                     add(wave, part, dim, 1, -far * inner)
 
-
-def velocity_halo_terms(links, received, add):
-    for (axis, dim, first), halo in zip(links, received):
+        real = has_peer(link[0], link[2])
+        lower = is_lower(link[0], link[2])
+        pl.when(real & lower)(after)
+        pl.when(real & jnp.logical_not(lower))(before)
+
+
+def source_gain(cell, part, x, y, z, width_y):
+    depth = z.shape[-1]
+    column = lax.div(cell, depth)
+    source_x = lax.div(column, width_y)
+    away = [source_x - x, column - source_x * width_y - y, cell - column * depth - z]
+    along = away.pop(part)
+    gain = jnp.where(along == 0, -near, 0.0)
+    for offset, value in ((1, near), (2, far), (-1, -far)):
+        gain = jnp.where(along == offset, value, gain)
+    return jnp.where((away[0] == 0) & (away[1] == 0), gain, 0.0)
+
+
+def start_of(tile_x, tile_y):
+    return lax.axis_index("tx") * tile_x, lax.axis_index("ty") * tile_y
+
+
+def velocity_halo_terms(links, received, stresses, stress, source, width_y, add):
+    cell, amp = source
+    layers, rows, depth = stress.shape[1:]
+    tile = layers - 2 * LAYERS, rows - 2 * ROWS
+    starts = start_of(*tile)
+    for link, halo, stress_halo in zip(links, received, stresses):
+        dim = link[1]
         part_n, part_a, part_b = STRAIN_OF[dim]
-        lower = is_lower(axis, first)
-        real = has_peer(axis, first)
-
-        @pl.when(real & lower)
+        shape = halo.shape[2:]
+        cross = starts[1 - dim] + lax.broadcasted_iota(jnp.int32, shape, 0)
+        level = lax.broadcasted_iota(jnp.int32, shape, 1)
+
+        def own(wave, part, index):
+            return face(stress, 6 * wave + STRESS_ALONG[dim][part], dim, index, True)[...]
+
+        def whole(wave, slot, part, layer, light, terms):
+            value = halo[wave, slot]
+            if dim == 1:
+                value += time_step * light * terms()
+            if wave == 0:
+                here = jnp.full(shape, starts[dim] + layer, jnp.int32)
+                x, y = (here, cross) if dim == 0 else (cross, here)
+                gain = source_gain(cell, VELOCITY_ALONG[dim][part], x, y, level, width_y)
+                value += time_step * amp * light * gain
+            return value
+
         def after():
+            count = tile[dim]
+            lights = [1.0 / stress_halo[layer, SPARE] for layer in range(2)]
             for wave in range(2):
-                add(wave, part_n, dim, -1, far * halo[wave, 0])
-                for part, slot in ((part_a, 1), (part_b, 3)):
-                    inner, outer = halo[wave, slot], halo[wave, slot + 1]
+                n = whole(wave, 0, 0, count, lights[0], lambda: -far * own(wave, 0, -1))
+                add(wave, part_n, dim, -1, far * n)
+                for part, name, slot in ((part_a, 1, 1), (part_b, 2, 3)):
+                    inner = whole(
+                        wave, slot, name, count, lights[0],
+                        lambda: -near * own(wave, name, -1) - far * own(wave, name, -2),
+                    )
+                    outer = whole(
+                        wave, slot + 1, name, count + 1, lights[1],
+                        lambda: -far * own(wave, name, -1),
+                    )
                     add(wave, part, dim, -1, near * inner + far * outer)
                     add(wave, part, dim, -2, far * inner)
 
-        @pl.when(real & jnp.logical_not(lower))
         def before():
+            lights = [halo[layer, SPARE] for layer in range(2)]
             for wave in range(2):
-                outer, inner = halo[wave, 0], halo[wave, 1]
+                outer = whole(wave, 0, 0, -2, lights[1], lambda: far * own(wave, 0, 0))
+                inner = whole(
+                    wave, 1, 0, -1, lights[0],
+                    lambda: near * own(wave, 0, 0) + far * own(wave, 0, 1),
+                )
                 add(wave, part_n, dim, 0, -near * inner - far * outer)
                 add(wave, part_n, dim, 1, -far * inner)
-                add(wave, part_a, dim, 0, -far * halo[wave, 2])
-                add(wave, part_b, dim, 0, -far * halo[wave, 3])
+                for part, name, slot in ((part_a, 1, 2), (part_b, 2, 3)):
+                    value = whole(
+                        wave, slot, name, -1, lights[0], lambda: far * own(wave, name, 0)
+                    )
+                    add(wave, part, dim, 0, -far * value)
+
+        real = has_peer(link[0], link[2])
+        lower = is_lower(link[0], link[2])
+        pl.when(real & lower)(after)
+        pl.when(real & jnp.logical_not(lower))(before)
 
 
 def face(ref, part, dim, index, padded):
@@ -389,11 +457,10 @@
     return buoyancy.reshape(layers * rows, depth)[pl.ds(index % rows, layers, stride=rows), :]
 
 
-def boundary_kernel(links, later_links, *refs):
+def boundary_kernel(links, send_links, *refs):
     count = len(links)
     received = refs[:count]
-    rim_added, buoyancy, _ = refs[count : count + 3]
-    velocity = refs[count + 3]
+    rim_added, buoyancy, _, velocity = refs[count : count + 4]
     sends = refs[count + 4 :]
 
     def add(wave, part, dim, index, term):
@@ -401,16 +468,42 @@
         target[...] += time_step * light_face(buoyancy, dim, index) * term
 
     stress_halo_terms(links, received, rim_added, (0, 1), add)
-    send_faces(velocity, 3, later_links, sends, [velocity_plan(dim) for dim in range(2)])
-
-
-def strain_kernel(links, *refs):
+    send_velocities(send_links, velocity, buoyancy, sends)
+
+
+def strain_kernel(links, width_y, *refs):
     count = len(links)
     received = refs[:count]
-    rim_added, buoyancy, _, accel, strain, gradient, velocity = refs[count : count + 7]
-    outputs, (accel_now, sems) = refs[count + 7 : count + 9], refs[count + 9 :]
-    tile_x, tile_y, _ = buoyancy.shape
+    source_cell, source_amp, rim_added, buoyancy, accel = refs[count : count + 5]
+    strain, gradient, velocity = refs[count + 6 : count + 9]
+    outputs, (accel_now, sems) = refs[count + 9 : count + 11], refs[count + 11 :]
+    tile_x, tile_y, depth = buoyancy.shape
     middle = pl.ds(ROWS, tile_y)
+    clear_rim(velocity, range(6), range(6))
+    accel_now[...] = accel[...]
+
+    def add(wave, part, dim, index, term):
+        target = face(accel_now, part, dim, index, False)
+        target[...] += light_face(buoyancy, dim, index) * term
+
+    stress_halo_terms(links, received, rim_added, (0,), add)
+    x_start, y_start = start_of(tile_x, tile_y)
+    cell, amp = source_cell[0], source_amp[0]
+    source_x = lax.div(cell, width_y * depth)
+    y = y_start + lax.broadcasted_iota(jnp.int32, (tile_y, depth), 0)
+    level = lax.broadcasted_iota(jnp.int32, (tile_y, depth), 1)
+    for offset in (-2, -1, 0, 1):
+        x = source_x + offset - x_start
+
+        @pl.when((x >= 0) & (x < tile_x))
+        def add_source():
+            here = jnp.full((tile_y, depth), source_x + offset, jnp.int32)
+            for part in range(3):
+                gain = source_gain(cell, part, here, y, level, width_y)
+                value = amp * buoyancy[x] * gain
+                accel_now[part, x] += value
+                velocity[part, x + LAYERS, middle, :] += time_step * value
+
     copies = [
         pltpu.make_async_copy(
             velocity.at[3 * wave + part, pl.ds(LAYERS, tile_x), middle, :],
@@ -422,15 +515,6 @@
     ]
     for copy in copies:
         copy.start()
-    clear_rim(velocity, range(6), range(6))
-    accel_now[...] = accel[...]
-
-    def add(wave, part, dim, index, term):
-        target = face(accel_now, part, dim, index, False)
-        target[...] += light_face(buoyancy, dim, index) * term
-
-    stress_halo_terms(links, received, rim_added, (0,), add)
-
     def layer(x, carry):
         for wave in range(2):
             vx, vy, vz = range(3 * wave, 3 * wave + 3)
@@ -469,17 +553,19 @@
     return strains, values
 
 
-def gradient_kernel(links, *refs):
+def gradient_kernel(links, width_y, *refs):
     count = len(links)
-    received = refs[:count]
-    stress, scaled_lame, scaled_shear, _, _, strain, gradient = refs[count:]
+    received, stresses = refs[:count], refs[count : 2 * count]
+    source_cell, source_amp, stress, scaled_lame, scaled_shear = refs[2 * count : 2 * count + 5]
+    strain, gradient = refs[2 * count + 7 :]
     tile_x, tile_y, _ = scaled_lame.shape
 
     def add(wave, part, dim, index, term):
         target = face(strain, 6 * wave + part, dim, index, False)
         target[...] += term
 
-    velocity_halo_terms(links, received, add)
+    source = source_cell[0], source_amp[0]
+    velocity_halo_terms(links, received, stresses, stress, source, width_y, add)
 
     def layer(x, carry):
         strains = [strain[part, x] for part in range(6)]
@@ -493,14 +579,24 @@
     lax.fori_loop(0, tile_x, layer, 0, unroll=4)
 
 
-def output_kernel(chunk, strain, stress, scaled_lame, scaled_shear, *refs):
+def output_kernel(
+    chunk, width_y, source_cell, source_amp, strain, stress, scaled_lame, scaled_shear, *refs
+):
     outputs, (values_now, sems) = refs[2:4], refs[4:]
-    tile_x, tile_y, _ = scaled_lame.shape
+    tile_x, tile_y, depth = scaled_lame.shape
+    x_start, y_start = start_of(tile_x, tile_y)
+    y = y_start + lax.broadcasted_iota(jnp.int32, (tile_y, depth), 0)
+    level = lax.broadcasted_iota(jnp.int32, (tile_y, depth), 1)
+    in_layer = y * depth + level - source_cell[0]
     copies = []
     for begin in range(0, tile_x, chunk):
         for wave in range(2):
             for x in range(begin, begin + chunk):
                 _, values = new_stress(strain, stress, scaled_lame, scaled_shear, wave, x, tile_y)
+                if wave == 0:
+                    first = (x_start + x) * (width_y * depth)
+                    added = jnp.where(in_layer == -first, source_amp[0], 0.0)
+                    values[:3] = [value + added for value in values[:3]]
                 for part in range(6):
                     values_now[6 * wave + part, x] = values[part]
             layers = pl.ds(begin, chunk)
@@ -550,7 +646,7 @@
     adjoint = adjoint_fields.reshape(adjoint_fields.shape[1:])
     sizes = {name: lax.axis_size(name) for name in ("tx", "ty")}
     width_y = tile_y * sizes["ty"]
-    links, later_links = links_of(sizes)
+    links_x, links_y = links_of(sizes)
     cells = tile_x * tile_y * depth
 
     def buffers(dim):
@@ -567,31 +663,37 @@
     def exchange(links, sends):
         return [swap(send, axis, first) for (axis, _, first), send in zip(links, sends)]
 
-    send_shapes = [buffers(dim) for _, dim, _ in links]
-    count = len(links)
+    def shapes(links):
+        return [buffers(dim) for _, dim, _ in links]
+
+    links = links_x + links_y
+    count, count_x, count_y = len(links), len(links_x), len(links_y)
     rows = tile_x * tile_y + 3 * (tile_x + tile_y)
-    sends = pl.pallas_call(
-        functools.partial(early_pack_kernel, links[:1]),
-        out_shape=send_shapes[:1],
-        in_specs=[hbm] * 2,
-        out_specs=[vmem],
-        scratch_shapes=[pltpu.SemaphoreType.DMA((2 * SLOTS,))],
+    source = source_cell, source_amp
+
+    *sends, density_now = pl.pallas_call(
+        functools.partial(early_pack_kernel, links_x),
+        out_shape=shapes(links_x) + [tile()],
+        in_specs=[hbm] * 3,
+        out_specs=[vmem] * (count_x + 1),
+        scratch_shapes=[pltpu.SemaphoreType.DMA((1 + 2 * SLOTS * count_x,))],
         compiler_params=params,
-        cost_estimate=cost(0, 2 * 2 * SLOTS * tile_x * depth * 4),
+        cost_estimate=cost(0, 4 * cells),
         name="early_pack",
-    )(in_hbm(forward), in_hbm(adjoint))
-    halos = exchange(links[:1], sends)
-    if count > 1:
+    )(*(in_hbm(x) for x in (forward, adjoint, density)))
+    halos_x = exchange(links_x, sends)
+    halos_y = []
+    if links_y:
         sends = pl.pallas_call(
-            functools.partial(pack_kernel, links[1:]),
-            out_shape=send_shapes[1:],
-            in_specs=[vmem] * 2,
-            out_specs=[vmem] * (count - 1),
+            functools.partial(pack_kernel, links_y),
+            out_shape=shapes(links_y),
+            in_specs=[vmem] * 3,
+            out_specs=[vmem] * count_y,
             compiler_params=params,
-            cost_estimate=cost(0, 2 * 2 * SLOTS * (count - 1) * tile_x * depth * 4),
+            cost_estimate=cost(0, 2 * 2 * SLOTS * count_y * tile_x * depth * 4),
             name="pack",
-        )(forward, adjoint)
-        halos += exchange(links[1:], sends)
+        )(forward, adjoint, density_now)
+        halos_y = exchange(links_y, sends)
 
     stress, velocity, accel, rim_added, buoyancy, scaled_lame, scaled_shear = pl.pallas_call(
         functools.partial(velocity_kernel, width_y),
@@ -599,84 +701,88 @@
             padded(12),
             padded(6),
             tile(3),
-            pltpu.VMEM((2, 2, 3, max(tile_x, tile_y), depth), jnp.float32),
+            pltpu.VMEM((2, 3, max(tile_x, tile_y), depth), jnp.float32),
             tile(),
             tile(),
             tile(),
         ],
-        in_specs=[hbm] * 3 + [smem] * 2 + [vmem] * 4,
+        in_specs=[hbm] * 2 + [vmem] * 5,
         out_specs=[vmem] * 7,
         scratch_shapes=[
-            pltpu.VMEM((rows, depth), jnp.float32),
             pltpu.VMEM((rows, depth), jnp.float32),
             tile(6),
             tile(),
             tile(),
-            tile(),
-            pltpu.SemaphoreType.DMA((3,)),
+            pltpu.SemaphoreType.DMA((2,)),
         ],
         compiler_params=params,
         cost_estimate=cost(200 * cells, 18 * 4 * cells),
         name="velocity",
     )(
-        *(in_hbm(x) for x in (lame_lambda, shear_modulus, density)),
-        source_cell,
-        source_amp,
+        in_hbm(lame_lambda),
+        in_hbm(shear_modulus),
         receiver_cell,
         residual_amp,
         forward,
         adjoint,
+        density_now,
     )
 
-    velocity, *sends = pl.pallas_call(
-        functools.partial(boundary_kernel, links, later_links),
-        out_shape=[padded(6)] + [buffers(dim) for _, dim, _ in later_links],
-        in_specs=[vmem] * (count + 3),
-        out_specs=[vmem] * (count + 1),
-        input_output_aliases={count + 2: 0},
-        compiler_params=params,
-        cost_estimate=cost(cells, 10 * 2 * tile_x * depth * 4),
-        name="boundary",
-    )(*halos, rim_added, buoyancy, velocity)
-    velocity_halos = exchange(later_links, sends)
+    def boundary(links, send_links, halos, velocity, name):
+        velocity, *sends = pl.pallas_call(
+            functools.partial(boundary_kernel, links, send_links),
+            out_shape=[padded(6)] + shapes(send_links),
+            in_specs=[vmem] * (len(links) + 3),
+            out_specs=[vmem] * (1 + len(send_links)),
+            input_output_aliases={len(links) + 2: 0},
+            compiler_params=params,
+            cost_estimate=cost(cells, 10 * 2 * tile_x * depth * 4),
+            name=name,
+        )(*halos, rim_added, buoyancy, velocity)
+        return velocity, exchange(send_links, sends)
+
+    velocity, velocity_halos_y = boundary(links_x, links_y, halos_x, velocity, "boundary_x")
+    velocity, velocity_halos_x = boundary(links_y, links_x, halos_y, velocity, "boundary_y")
+    halos = halos_x + halos_y
+    velocity_halos = velocity_halos_x + velocity_halos_y
 
     out_shape = jax.ShapeDtypeStruct(forward.shape, jnp.float32)
     strain, gradient, _, forward_next, adjoint_next = pl.pallas_call(
-        functools.partial(strain_kernel, links),
+        functools.partial(strain_kernel, links, width_y),
         out_shape=[tile(12), tile(3), padded(6), out_shape, out_shape],
-        in_specs=[vmem] * (count + 4),
+        in_specs=[vmem] * count + [smem] * 2 + [vmem] * 4,
         out_specs=[vmem] * 3 + [hbm] * 2,
-        input_output_aliases={count + 2: 2},
+        input_output_aliases={count + 5: 2},
         scratch_shapes=[tile(3), pltpu.SemaphoreType.DMA((6,))],
         compiler_params=params,
         cost_estimate=cost(200 * cells, 18 * 4 * cells),
         name="strain",
-    )(*halos, rim_added, buoyancy, velocity, accel)
+    )(*halos, *source, rim_added, buoyancy, accel, velocity)
 
     strain, gradient = pl.pallas_call(
-        functools.partial(gradient_kernel, later_links),
+        functools.partial(gradient_kernel, links, width_y),
         out_shape=[tile(12), tile(3)],
-        in_specs=[vmem] * (count + 5),
+        in_specs=[vmem] * (2 * count) + [smem] * 2 + [vmem] * 5,
         out_specs=[vmem] * 2,
-        input_output_aliases={count + 3: 0, count + 4: 1},
+        input_output_aliases={2 * count + 5: 0, 2 * count + 6: 1},
         compiler_params=params,
         cost_estimate=cost(30 * cells, 2 * 4 * cells),
         name="gradient",
-    )(*velocity_halos, stress, scaled_lame, scaled_shear, strain, gradient)
+    )(*velocity_halos, *halos, *source, stress, scaled_lame, scaled_shear, strain, gradient)
     other = lax.ppermute(gradient, "shot", [(0, 1), (1, 0)])
 
     chunk = 4 if tile_x % 4 == 0 else 1
     forward_next, adjoint_next = pl.pallas_call(
-        functools.partial(output_kernel, chunk),
+        functools.partial(output_kernel, chunk, width_y),
         out_shape=[out_shape, out_shape],
-        in_specs=[vmem] * 4 + [hbm] * 2,
+        in_specs=[smem] * 2 + [vmem] * 4 + [hbm] * 2,
         out_specs=[hbm] * 2,
-        input_output_aliases={4: 0, 5: 1},
+        input_output_aliases={6: 0, 7: 1},
         scratch_shapes=[tile(12), pltpu.SemaphoreType.DMA((2 * tile_x // chunk,))],
         compiler_params=params,
         cost_estimate=cost(60 * cells, 18 * 4 * cells),
         name="outputs",
-    )(strain, stress, scaled_lame, scaled_shear, forward_next, adjoint_next)
+    )(*source, strain, stress, scaled_lame, scaled_shear, forward_next, adjoint_next)
     total = pl.pallas_call(
         sum_kernel,
         out_shape=jax.ShapeDtypeStruct((3, tile_x, tile_y, depth), jnp.float32),

time: 24.3 us -> 25.3 us (1.041)
  the two profiles are of different devices: /device:TPU:0 before, /device:TPU:9 now
where the time goes in v8:
time: 25.3 us; the launch traced here: 24.8 us
  starting transfers between devices  12.4 us (49%)
  Pallas kernels  6.89 us (27%)
  waiting for transfers between devices  3.45 us (14%)
  between operations  2.07 us (8%)
    ppermute x6, starting transfers between devices, swap(): return lax.ppermute(value, axis, pairs + [(j, i) for i, j in pairs])  11.2 us
    ppermute x6, waiting for transfers between devices, swap(): return lax.ppermute(value, axis, pairs + [(j, i) for i, j in pairs])  3.34 us
    pallas_call x1, Pallas kernels, body(): pl.pallas_call(functools.partial(velocity_kernel, width_y), out_shape=[pa...  1.58 us
    pallas_call x1, Pallas kernels, body(): pl.pallas_call(functools.partial(output_kernel, chunk, width_y), out_shap...  1.23 us
    pallas_call x1, Pallas kernels, body(): pl.pallas_call(functools.partial(strain_kernel, links, width_y), out_shap...  1.23 us
    ppermute x1, starting transfers between devices, body(): other = lax.ppermute(gradient, 'shot', [(0, 1), (1, 0)])  1.19 us
    pallas_call x1, Pallas kernels, body(): pl.pallas_call(functools.partial(early_pack_kernel, links_x), out_shape=s...  1.15 us
    pallas_call x1, Pallas kernels, body(): pl.pallas_call(sum_kernel, out_shape=jax.ShapeDtypeStruct((3, tile_x, til...  0.78 us
  transfers between devices with their start and end apart: 7, of which 3 were waited for; matrix products, arithmetic and copies ran while one was open for 0% of the time, Pallas kernels for 17%

profile of v8, /device:TPU:9, one launch (start us, length us, event | category | flops | bytes accessed | tf_op | source)
XLA Modules:
  0.0 24.8 jit_solution(18267906214921030840)
XLA Ops:
  0.6 0.0 copy-start.1
  0.6 0.0 copy-start
  0.7 1.2 %early_pack.1 = (f32[2,5,16,128]{3,2,1,0:T(8,128)S(1)}, f32[16,16,128]{2,1,0:T(8,128)S(1)}) custom-call(f32[9,16,16,128]{3,2,1,0:T(8,128)} %bitcast.4, f32[9,16,16,128]{3,2,1,0:T(8,128)} %bitcast.7, f32[16,16,128]{2,1,0:T(8,128)} %density.1), custom_call_target="tpu_custom_call" | custom-call | bytes 131072 | tf_op jit(solution)/shard_map/early_pack/pallas_call | solution.py:674
  1.8 0.0 copy-start.2
  1.8 0.0 copy-start.3
  1.8 1.3 %collective-permute-start.2 = (f32[2,5,16,128]{3,2,1,0:T(8,128)S(1)}, f32[2,5,16,128]{3,2,1,0:T(8,128)S(1)}, u32[]{:S(2)}, u32[]{:S(2)}) collective-permute-start(f32[2,5,16,128]{3,2,1,0:T(8,128)S(1)} %get-tuple-element.32), channel_id=1, source_target_pairs={{0,8},{8,0},{1,9},{9,1},{2,10},{10,2},{3,11},{11,3},{4,12},{12,4},... | collective-permute-start | bytes 245768 | tf_op jit(solution)/shard_map/ppermute | solution.py:37
  3.1 0.0 copy-done.1
  3.1 0.0 copy-done
  3.1 0.1 pack.1
  3.2 3.0 %collective-permute-start = (f32[2,5,16,128]{3,2,1,0:T(8,128)S(1)}, f32[2,5,16,128]{3,2,1,0:T(8,128)S(1)}, u32[]{:S(2)}, u32[]{:S(2)}) collective-permute-start(f32[2,5,16,128]{3,2,1,0:T(8,128)S(1)} %get-tuple-element.28), channel_id=1, source_target_pairs={{1,2},{3,4},{5,6},{2,1},{4,3},{6,5},{9,10},{11,12},{13,14},{10,9},... | collective-permute-start | bytes 245768 | tf_op jit(solution)/shard_map/ppermute | solution.py:37
  6.2 1.4 %collective-permute-start.1 = (f32[2,5,16,128]{3,2,1,0:T(8,128)S(1)}, f32[2,5,16,128]{3,2,1,0:T(8,128)S(1)}, u32[]{:S(2)}, u32[]{:S(2)}) collective-permute-start(f32[2,5,16,128]{3,2,1,0:T(8,128)S(1)} %get-tuple-element.29), channel_id=1, source_target_pairs={{0,1},{2,3},{4,5},{6,7},{1,0},{3,2},{5,4},{7,6},{8,9},{10,11},{12,... | collective-permute-start | bytes 245768 | tf_op jit(solution)/shard_map/ppermute | solution.py:37
  7.7 0.0 copy-done.2
  7.7 0.0 copy-done.3
  7.7 1.6 %velocity.1 = (f32[12,20,32,128]{3,2,1,0:T(8,128)S(1)}, f32[6,20,32,128]{3,2,1,0:T(8,128)S(1)}, f32[3,16,16,128]{3,2,1,0:T(8,128)S(1)}, f32[2,3,16,128]{3,2,1,0:...) custom-call(f32[16,16,128]{2,1,0:T(8,128)} %lame.1, ...), custom_call_target="tpu_custom_call" | custom-call | flops 6553600 | bytes 2359296 | tf_op jit(solution)/shard_map/velocity/pallas_call | solution.py:698
  9.3 0.0 collective-permute-done.2.refs_0_.refs_3_
  9.3 0.2 boundary_x.1
  9.4 0.0 collective-permute-done.refs_0_.refs_1_.refs_4_
  9.5 2.1 %collective-permute-done.1.refs_1_.refs_2_.refs_5_ = f32[2,5,16,128]{3,2,1,0:T(8,128)S(1)} collective-permute-done((f32[2,5,16,128]{3,2,1,0:T(8,128)S(1)}, f32[2,5,16,128]{3,2,1,0:T(8,128)S(1)}, u32[]{:S(2)}, u32[]{:S(2)}) %collective-permute-start.1) | collective-permute-done | bytes 81952 | tf_op jit(solution)/shard_map/ppermute | solution.py:37
  11.5 0.2 boundary_y.1
  11.8 1.0 %collective-permute-start.3 = (f32[2,5,16,128]{3,2,1,0:T(8,128)S(1)}, f32[2,5,16,128]{3,2,1,0:T(8,128)S(1)}, u32[]{:S(2)}, u32[]{:S(2)}) collective-permute-start(f32[2,5,16,128]{3,2,1,0:T(8,128)S(1)} %get-tuple-element.35), channel_id=1, source_target_pairs={{0,8},{8,0},{1,9},{9,1},{2,10},{10,2},{3,11},{11,3},{4,12},{12,4},... | collective-permute-start | bytes 245768 | tf_op jit(solution)/shard_map/ppermute | solution.py:37
  12.7 3.0 %collective-permute-start.4 = (f32[2,5,16,128]{3,2,1,0:T(8,128)S(1)}, f32[2,5,16,128]{3,2,1,0:T(8,128)S(1)}, u32[]{:S(2)}, u32[]{:S(2)}) collective-permute-start(f32[2,5,16,128]{3,2,1,0:T(8,128)S(1)} %get-tuple-element.36), channel_id=1, source_target_pairs={{1,2},{3,4},{5,6},{2,1},{4,3},{6,5},{9,10},{11,12},{13,14},{10,9},... | collective-permute-start | bytes 245768 | tf_op jit(solution)/shard_map/ppermute | solution.py:37
  15.7 1.4 %collective-permute-start.5 = (f32[2,5,16,128]{3,2,1,0:T(8,128)S(1)}, f32[2,5,16,128]{3,2,1,0:T(8,128)S(1)}, u32[]{:S(2)}, u32[]{:S(2)}) collective-permute-start(f32[2,5,16,128]{3,2,1,0:T(8,128)S(1)} %get-tuple-element.37), channel_id=1, source_target_pairs={{0,1},{2,3},{4,5},{6,7},{1,0},{3,2},{5,4},{7,6},{8,9},{10,11},{12,... | collective-permute-start | bytes 245768 | tf_op jit(solution)/shard_map/ppermute | solution.py:37
  18.5 1.2 %strain.1 = (f32[12,16,16,128]{3,2,1,0:T(8,128)S(1)}, f32[3,16,16,128]{3,2,1,0:T(8,128)S(1)}, f32[6,20,32,128]{3,2,1,0:T(8,128)S(1)}, f32[9,16,16,128]{3,2,1,0:T(8,128)}, f32[9,16,16,128]{3,2,1,0:T(8,128)}) custom-call(f32[2,5,16,128]{3,2,1,0:T(8,128)S(1)} %collective-permute-done.2.refs_0_.refs_3_, ...), custom_call_target="tpu_custom_call", output_to_operand_aliasing={{2}: (8, {})} | custom-call | flops 6553600 | bytes 2359296 | tf_op jit(solution)/shard_map/strain/pallas_call | solution.py:750
  19.7 0.0 collective-permute-done.3.refs_0_
  19.7 0.0 collective-permute-done.4.refs_1_
  19.7 1.3 %collective-permute-done.5.refs_2_ = f32[2,5,16,128]{3,2,1,0:T(8,128)S(1)} collective-permute-done((f32[2,5,16,128]{3,2,1,0:T(8,128)S(1)}, f32[2,5,16,128]{3,2,1,0:T(8,128)S(1)}, u32[]{:S(2)}, u32[]{:S(2)}) %collective-permute-start.5) | collective-permute-done | bytes 81952 | tf_op jit(solution)/shard_map/ppermute | solution.py:37
  21.0 0.5 %gradient.1 = (f32[12,16,16,128]{3,2,1,0:T(8,128)S(1)}, f32[3,16,16,128]{3,2,1,0:T(8,128)S(1)}) custom-call(f32[2,5,16,128]{3,2,1,0:T(8,128)S(1)} %collective-permute-done.3.refs_0_, f32[2,5,16,128]{3,2,1,0:T(8,128)S(1)} %collective-permute-done.4.refs_1_, ...), custom_call_target="tpu_custom_call", output_to_operand_aliasing={{0}: (11, {}), {1}: (12, {})} | custom-call | flops 983040 | bytes 262144 | tf_op jit(solution)/shard_map/gradient/pallas_call | solution.py:762
  21.5 1.2 %collective-permute-start.6 = (f32[3,16,16,128]{3,2,1,0:T(8,128)S(1)}, f32[3,16,16,128]{3,2,1,0:T(8,128)S(1)}, u32[]{:S(2)}, u32[]{:S(2)}) collective-permute-start(f32[3,16,16,128]{3,2,1,0:T(8,128)S(1)} %get-tuple-element.50.mine), channel_id=1, source_target_pairs={{0,16},{16,0},{1,17},{17,1},{2,18},{18,2},{3,19},{19,3},{4,20},{20... | collective-permute-start | bytes 1179656 | tf_op jit(solution)/shard_map/ppermute | solution.py:772
  22.7 1.2 %outputs.1 = (f32[9,16,16,128]{3,2,1,0:T(8,128)}, f32[9,16,16,128]{3,2,1,0:T(8,128)}) custom-call(s32[1]{0:T(128)S(6)} %copy.26.refs_3_.refs_6_.source_cell, f32[1]{0:T(128)S(6)} %copy.27.refs_4_.refs_7_.source_amp, f32[12,16,16,128]{3,2,1,0:T(8,128)S(1)} %get-tuple-element.45.strain, ...), custom_call_target="tpu_custom_call", output_to_operand_aliasing={{0}: (6, {}), {1}: (7, {})} | custom-call | flops 1966080 | bytes 2359296 | tf_op jit(solution)/shard_map/outputs/pallas_call | solution.py:775
  23.9 0.1 collective-permute-done.6.other
  24.0 0.8 %sum.1 = f32[3,16,16,128]{3,2,1,0:T(8,128)} custom-call(f32[3,16,16,128]{3,2,1,0:T(8,128)S(1)} %get-tuple-element.50.mine, f32[3,16,16,128]{3,2,1,0:T(8,128)S(1)} %collective-permute-done.6.other), custom_call_target="tpu_custom_call" | custom-call | flops 98304 | bytes 1179648 | tf_op jit(solution)/shard_map/sum/pallas_call | solution.py:786
Async XLA Ops:
  0.6 2.5 %copy-start.1 = (f32[1,9,16,16,128]{4,3,2,1,0:T(8,128)S(1)}, f32[1,9,16,16,128]{4,3,2,1,0:T(8,128)}, u32[]{:S(2)}) copy-start(f32[1,9,16,16,128]{4,3,2,1,0:T(8,128)} %param.10) | copy-start | bytes 3538948
  0.6 2.5 %copy-start = (f32[1,9,16,16,128]{4,3,2,1,0:T(8,128)S(1)}, f32[1,9,16,16,128]{4,3,2,1,0:T(8,128)}, u32[]{:S(2)}) copy-start(f32[1,9,16,16,128]{4,3,2,1,0:T(8,128)} %param.9) | copy-start | bytes 3538948
  1.8 5.9 %copy-start.2 = (s32[1,256]{1,0:T(1,128)S(1)}, s32[1,256]{1,0:T(1,128)}, u32[]{:S(2)}) copy-start(s32[1,256]{1,0:T(1,128)} %receiver_cell.1) | copy-start | bytes 3076
  1.8 5.9 %copy-start.3 = (f32[1,256]{1,0:T(1,128)S(1)}, f32[1,256]{1,0:T(1,128)}, u32[]{:S(2)}) copy-start(f32[1,256]{1,0:T(1,128)} %residual_amp.1) | copy-start | bytes 3076
  1.8 7.4 %collective-permute-start.2 = (f32[2,5,16,128]{3,2,1,0:T(8,128)S(1)}, f32[2,5,16,128]{3,2,1,0:T(8,128)S(1)}, u32[]{:S(2)}, u32[]{:S(2)}) collective-permute-start(f32[2,5,16,128]{3,2,1,0:T(8,128)S(1)} %get-tuple-element.32), channel_id=1, source_target_pairs={{0,8},{8,0},{1,9},{9,1},{2,10},{10,2},{3,11},{11,3},{4,12},{12,4},... | collective-permute-start | bytes 245768 | tf_op jit(solution)/shard_map/ppermute | solution.py:37
  3.2 6.2 %collective-permute-start = (f32[2,5,16,128]{3,2,1,0:T(8,128)S(1)}, f32[2,5,16,128]{3,2,1,0:T(8,128)S(1)}, u32[]{:S(2)}, u32[]{:S(2)}) collective-permute-start(f32[2,5,16,128]{3,2,1,0:T(8,128)S(1)} %get-tuple-element.28), channel_id=1, source_target_pairs={{1,2},{3,4},{5,6},{2,1},{4,3},{6,5},{9,10},{11,12},{13,14},{10,9},... | collective-permute-start | bytes 245768 | tf_op jit(solution)/shard_map/ppermute | solution.py:37
  6.2 5.3 %collective-permute-start.1 = (f32[2,5,16,128]{3,2,1,0:T(8,128)S(1)}, f32[2,5,16,128]{3,2,1,0:T(8,128)S(1)}, u32[]{:S(2)}, u32[]{:S(2)}) collective-permute-start(f32[2,5,16,128]{3,2,1,0:T(8,128)S(1)} %get-tuple-element.29), channel_id=1, source_target_pairs={{0,1},{2,3},{4,5},{6,7},{1,0},{3,2},{5,4},{7,6},{8,9},{10,11},{12,... | collective-permute-start | bytes 245768 | tf_op jit(solution)/shard_map/ppermute | solution.py:37
  11.8 8.0 %collective-permute-start.3 = (f32[2,5,16,128]{3,2,1,0:T(8,128)S(1)}, f32[2,5,16,128]{3,2,1,0:T(8,128)S(1)}, u32[]{:S(2)}, u32[]{:S(2)}) collective-permute-start(f32[2,5,16,128]{3,2,1,0:T(8,128)S(1)} %get-tuple-element.35), channel_id=1, source_target_pairs={{0,8},{8,0},{1,9},{9,1},{2,10},{10,2},{3,11},{11,3},{4,12},{12,4},... | collective-permute-start | bytes 245768 | tf_op jit(solution)/shard_map/ppermute | solution.py:37
  12.7 7.0 %collective-permute-start.4 = (f32[2,5,16,128]{3,2,1,0:T(8,128)S(1)}, f32[2,5,16,128]{3,2,1,0:T(8,128)S(1)}, u32[]{:S(2)}, u32[]{:S(2)}) collective-permute-start(f32[2,5,16,128]{3,2,1,0:T(8,128)S(1)} %get-tuple-element.36), channel_id=1, source_target_pairs={{1,2},{3,4},{5,6},{2,1},{4,3},{6,5},{9,10},{11,12},{13,14},{10,9},... | collective-permute-start | bytes 245768 | tf_op jit(solution)/shard_map/ppermute | solution.py:37
  15.7 5.3 %collective-permute-start.5 = (f32[2,5,16,128]{3,2,1,0:T(8,128)S(1)}, f32[2,5,16,128]{3,2,1,0:T(8,128)S(1)}, u32[]{:S(2)}, u32[]{:S(2)}) collective-permute-start(f32[2,5,16,128]{3,2,1,0:T(8,128)S(1)} %get-tuple-element.37), channel_id=1, source_target_pairs={{0,1},{2,3},{4,5},{6,7},{1,0},{3,2},{5,4},{7,6},{8,9},{10,11},{12,... | collective-permute-start | bytes 245768 | tf_op jit(solution)/shard_map/ppermute | solution.py:37
  21.5 2.5 %collective-permute-start.6 = (f32[3,16,16,128]{3,2,1,0:T(8,128)S(1)}, f32[3,16,16,128]{3,2,1,0:T(8,128)S(1)}, u32[]{:S(2)}, u32[]{:S(2)}) collective-permute-start(f32[3,16,16,128]{3,2,1,0:T(8,128)S(1)} %get-tuple-element.50.mine), channel_id=1, source_target_pairs={{0,16},{16,0},{1,17},{17,1},{2,18},{18,2},{3,19},{19,3},{4,20},{20... | collective-permute-start | bytes 1179656 | tf_op jit(solution)/shard_map/ppermute | solution.py:772

commit v9 on v8

--- a/solution.py
+++ b/solution.py
@@ -666,7 +666,7 @@
     def shapes(links):
         return [buffers(dim) for _, dim, _ in links]
 
-    links = links_x + links_y
+    links = links_y + links_x
     count, count_x, count_y = len(links), len(links_x), len(links_y)
     rows = tile_x * tile_y + 3 * (tile_x + tile_y)
     source = source_cell, source_amp
@@ -743,8 +743,8 @@
 
     velocity, velocity_halos_y = boundary(links_x, links_y, halos_x, velocity, "boundary_x")
     velocity, velocity_halos_x = boundary(links_y, links_x, halos_y, velocity, "boundary_y")
-    halos = halos_x + halos_y
-    velocity_halos = velocity_halos_x + velocity_halos_y
+    halos = halos_y + halos_x
+    velocity_halos = velocity_halos_y + velocity_halos_x
 
     out_shape = jax.ShapeDtypeStruct(forward.shape, jnp.float32)
     strain, gradient, _, forward_next, adjoint_next = pl.pallas_call(

time: 25.3 us -> 24.6 us (0.972)
  the two profiles are of different devices: /device:TPU:9 before, /device:TPU:0 now
where the time goes in v9:
time: 24.6 us; the launch traced here: 24.3 us
  starting transfers between devices  13.7 us (56%)
  Pallas kernels  6.67 us (27%)
  between operations  2.07 us (8%)
  waiting for transfers between devices  1.87 us (8%)
    ppermute x6, starting transfers between devices, swap(): return lax.ppermute(value, axis, pairs + [(j, i) for i, j in pairs])  13.6 us
    pallas_call x1, Pallas kernels, body(): pl.pallas_call(functools.partial(velocity_kernel, width_y), out_shape=[pa...  1.58 us
    ppermute x6, waiting for transfers between devices, swap(): return lax.ppermute(value, axis, pairs + [(j, i) for i, j in pairs])  1.41 us
    pallas_call x1, Pallas kernels, body(): pl.pallas_call(functools.partial(output_kernel, chunk, width_y), out_shap...  1.24 us
    pallas_call x1, Pallas kernels, body(): pl.pallas_call(functools.partial(strain_kernel, links, width_y), out_shap...  1.2 us
    pallas_call x1, Pallas kernels, body(): pl.pallas_call(functools.partial(early_pack_kernel, links_x), out_shape=s...  1.15 us
    pallas_call x1, Pallas kernels, body(): pl.pallas_call(sum_kernel, out_shape=jax.ShapeDtypeStruct((3, tile_x, til...  0.78 us
  transfers between devices with their start and end apart: 7, of which 2 were waited for; matrix products, arithmetic and copies ran while one was open for 0% of the time, Pallas kernels for 18%

profile of v9, /device:TPU:0, one launch (start us, length us, event | category | flops | bytes accessed | tf_op | source)
XLA Modules:
  0.0 24.3 jit_solution(5145314532800363131)
XLA Ops:
  0.6 0.0 copy-start.1
  0.6 0.0 copy-start
  0.7 1.2 %early_pack.1 = (f32[2,5,16,128]{3,2,1,0:T(8,128)S(1)}, f32[16,16,128]{2,1,0:T(8,128)S(1)}) custom-call(f32[9,16,16,128]{3,2,1,0:T(8,128)} %bitcast.4, f32[9,16,16,128]{3,2,1,0:T(8,128)} %bitcast.7, f32[16,16,128]{2,1,0:T(8,128)} %density.1), custom_call_target="tpu_custom_call" | custom-call | bytes 131072 | tf_op jit(solution)/shard_map/early_pack/pallas_call | solution.py:674
  1.8 0.0 copy-start.2
  1.8 0.0 copy-start.3
  1.8 3.0 %collective-permute-start = (f32[2,5,16,128]{3,2,1,0:T(8,128)S(1)}, f32[2,5,16,128]{3,2,1,0:T(8,128)S(1)}, u32[]{:S(2)}, u32[]{:S(2)}) collective-permute-start(f32[2,5,16,128]{3,2,1,0:T(8,128)S(1)} %get-tuple-element.27), channel_id=1, source_target_pairs={{0,8},{8,0},{1,9},{9,1},{2,10},{10,2},{3,11},{11,3},{4,12},{12,4},... | collective-permute-start | bytes 245768 | tf_op jit(solution)/shard_map/ppermute | solution.py:37
  4.9 0.0 copy-done.1
  4.9 0.0 copy-done
  4.9 0.1 pack.1
  4.9 0.7 %collective-permute-start.3 = (f32[2,5,16,128]{3,2,1,0:T(8,128)S(1)}, f32[2,5,16,128]{3,2,1,0:T(8,128)S(1)}, u32[]{:S(2)}, u32[]{:S(2)}) collective-permute-start(f32[2,5,16,128]{3,2,1,0:T(8,128)S(1)} %get-tuple-element.34), channel_id=1, source_target_pairs={{1,2},{3,4},{5,6},{2,1},{4,3},{6,5},{9,10},{11,12},{13,14},{10,9},... | collective-permute-start | bytes 245768 | tf_op jit(solution)/shard_map/ppermute | solution.py:37
  5.6 4.3 %collective-permute-start.4 = (f32[2,5,16,128]{3,2,1,0:T(8,128)S(1)}, f32[2,5,16,128]{3,2,1,0:T(8,128)S(1)}, u32[]{:S(2)}, u32[]{:S(2)}) collective-permute-start(f32[2,5,16,128]{3,2,1,0:T(8,128)S(1)} %get-tuple-element.35), channel_id=1, source_target_pairs={{0,1},{2,3},{4,5},{6,7},{1,0},{3,2},{5,4},{7,6},{8,9},{10,11},{12,... | collective-permute-start | bytes 245768 | tf_op jit(solution)/shard_map/ppermute | solution.py:37
  10.0 0.0 copy-done.2
  10.0 0.0 copy-done.3
  10.0 1.6 %velocity.1 = (f32[12,20,32,128]{3,2,1,0:T(8,128)S(1)}, f32[6,20,32,128]{3,2,1,0:T(8,128)S(1)}, f32[3,16,16,128]{3,2,1,0:T(8,128)S(1)}, f32[2,3,16,128]{3,2,1,0:...) custom-call(f32[16,16,128]{2,1,0:T(8,128)} %lame.1, ...), custom_call_target="tpu_custom_call" | custom-call | flops 6553600 | bytes 2359296 | tf_op jit(solution)/shard_map/velocity/pallas_call | solution.py:698
  11.6 0.0 collective-permute-done.refs_0_.refs_2_.refs_5_
  11.6 0.2 boundary_x.1
  11.7 0.7 %collective-permute-start.1 = (f32[2,5,16,128]{3,2,1,0:T(8,128)S(1)}, f32[2,5,16,128]{3,2,1,0:T(8,128)S(1)}, u32[]{:S(2)}, u32[]{:S(2)}) collective-permute-start(f32[2,5,16,128]{3,2,1,0:T(8,128)S(1)} %get-tuple-element.32), channel_id=1, source_target_pairs={{1,2},{3,4},{5,6},{2,1},{4,3},{6,5},{9,10},{11,12},{13,14},{10,9},... | collective-permute-start | bytes 245768 | tf_op jit(solution)/shard_map/ppermute | solution.py:37
  12.4 4.3 %collective-permute-start.2 = (f32[2,5,16,128]{3,2,1,0:T(8,128)S(1)}, f32[2,5,16,128]{3,2,1,0:T(8,128)S(1)}, u32[]{:S(2)}, u32[]{:S(2)}) collective-permute-start(f32[2,5,16,128]{3,2,1,0:T(8,128)S(1)} %get-tuple-element.33), channel_id=1, source_target_pairs={{0,1},{2,3},{4,5},{6,7},{1,0},{3,2},{5,4},{7,6},{8,9},{10,11},{12,... | collective-permute-start | bytes 245768 | tf_op jit(solution)/shard_map/ppermute | solution.py:37
  16.8 0.0 collective-permute-done.3.refs_0_.refs_3_
  16.8 0.0 collective-permute-done.4.refs_1_.refs_4_
  16.8 0.1 boundary_y.1
  16.9 0.6 %collective-permute-start.5 = (f32[2,5,16,128]{3,2,1,0:T(8,128)S(1)}, f32[2,5,16,128]{3,2,1,0:T(8,128)S(1)}, u32[]{:S(2)}, u32[]{:S(2)}) collective-permute-start(f32[2,5,16,128]{3,2,1,0:T(8,128)S(1)} %get-tuple-element.37), channel_id=1, source_target_pairs={{0,8},{8,0},{1,9},{9,1},{2,10},{10,2},{3,11},{11,3},{4,12},{12,4},... | collective-permute-start | bytes 245768 | tf_op jit(solution)/shard_map/ppermute | solution.py:37
  18.8 1.2 %strain.1 = (f32[12,16,16,128]{3,2,1,0:T(8,128)S(1)}, f32[3,16,16,128]{3,2,1,0:T(8,128)S(1)}, f32[6,20,32,128]{3,2,1,0:T(8,128)S(1)}, f32[9,16,16,128]{3,2,1,0:T(8,128)}, f32[9,16,16,128]{3,2,1,0:T(8,128)}) custom-call(f32[2,5,16,128]{3,2,1,0:T(8,128)S(1)} %collective-permute-done.3.refs_0_.refs_3_, ...), custom_call_target="tpu_custom_call", output_to_operand_aliasing={{2}: (8, {})} | custom-call | flops 6553600 | bytes 2359296 | tf_op jit(solution)/shard_map/strain/pallas_call | solution.py:750
  20.0 0.0 collective-permute-done.1.refs_0_
  20.0 0.0 collective-permute-done.2.refs_1_
  20.0 1.4 %collective-permute-done.5.refs_2_ = f32[2,5,16,128]{3,2,1,0:T(8,128)S(1)} collective-permute-done((f32[2,5,16,128]{3,2,1,0:T(8,128)S(1)}, f32[2,5,16,128]{3,2,1,0:T(8,128)S(1)}, u32[]{:S(2)}, u32[]{:S(2)}) %collective-permute-start.5) | collective-permute-done | bytes 81952 | tf_op jit(solution)/shard_map/ppermute | solution.py:37
  21.4 0.4 %gradient.1 = (f32[12,16,16,128]{3,2,1,0:T(8,128)S(1)}, f32[3,16,16,128]{3,2,1,0:T(8,128)S(1)}) custom-call(f32[2,5,16,128]{3,2,1,0:T(8,128)S(1)} %collective-permute-done.1.refs_0_, f32[2,5,16,128]{3,2,1,0:T(8,128)S(1)} %collective-permute-done.2.refs_1_, ...), custom_call_target="tpu_custom_call", output_to_operand_aliasing={{0}: (11, {}), {1}: (12, {})} | custom-call | flops 983040 | bytes 262144 | tf_op jit(solution)/shard_map/gradient/pallas_call | solution.py:762
  21.8 0.1 collective-permute-start.6
  21.8 1.2 %outputs.1 = (f32[9,16,16,128]{3,2,1,0:T(8,128)}, f32[9,16,16,128]{3,2,1,0:T(8,128)}) custom-call(s32[1]{0:T(128)S(6)} %copy.26.refs_3_.refs_6_.source_cell, f32[1]{0:T(128)S(6)} %copy.27.refs_4_.refs_7_.source_amp, f32[12,16,16,128]{3,2,1,0:T(8,128)S(1)} %get-tuple-element.45.strain, ...), custom_call_target="tpu_custom_call", output_to_operand_aliasing={{0}: (6, {}), {1}: (7, {})} | custom-call | flops 1966080 | bytes 2359296 | tf_op jit(solution)/shard_map/outputs/pallas_call | solution.py:775
  23.1 0.5 %collective-permute-done.6.other = f32[3,16,16,128]{3,2,1,0:T(8,128)S(1)} collective-permute-done((f32[3,16,16,128]{3,2,1,0:T(8,128)S(1)}, f32[3,16,16,128]{3,2,1,0:T(8,128)S(1)}, u32[]{:S(2)}, u32[]{:S(2)}) %collective-permute-start.6) | collective-permute-done | bytes 393248 | tf_op jit(solution)/shard_map/ppermute | solution.py:772
  23.6 0.8 %sum.1 = f32[3,16,16,128]{3,2,1,0:T(8,128)} custom-call(f32[3,16,16,128]{3,2,1,0:T(8,128)S(1)} %get-tuple-element.50.mine, f32[3,16,16,128]{3,2,1,0:T(8,128)S(1)} %collective-permute-done.6.other), custom_call_target="tpu_custom_call" | custom-call | flops 98304 | bytes 1179648 | tf_op jit(solution)/shard_map/sum/pallas_call | solution.py:786
Async XLA Ops:
  0.6 4.2 %copy-start.1 = (f32[1,9,16,16,128]{4,3,2,1,0:T(8,128)S(1)}, f32[1,9,16,16,128]{4,3,2,1,0:T(8,128)}, u32[]{:S(2)}) copy-start(f32[1,9,16,16,128]{4,3,2,1,0:T(8,128)} %param.10) | copy-start | bytes 3538948
  0.6 4.2 %copy-start = (f32[1,9,16,16,128]{4,3,2,1,0:T(8,128)S(1)}, f32[1,9,16,16,128]{4,3,2,1,0:T(8,128)}, u32[]{:S(2)}) copy-start(f32[1,9,16,16,128]{4,3,2,1,0:T(8,128)} %param.9) | copy-start | bytes 3538948
  1.8 8.2 %copy-start.2 = (s32[1,256]{1,0:T(1,128)S(1)}, s32[1,256]{1,0:T(1,128)}, u32[]{:S(2)}) copy-start(s32[1,256]{1,0:T(1,128)} %receiver_cell.1) | copy-start | bytes 3076
  1.8 8.1 %copy-start.3 = (f32[1,256]{1,0:T(1,128)S(1)}, f32[1,256]{1,0:T(1,128)}, u32[]{:S(2)}) copy-start(f32[1,256]{1,0:T(1,128)} %residual_amp.1) | copy-start | bytes 3076
  1.8 9.7 %collective-permute-start = (f32[2,5,16,128]{3,2,1,0:T(8,128)S(1)}, f32[2,5,16,128]{3,2,1,0:T(8,128)S(1)}, u32[]{:S(2)}, u32[]{:S(2)}) collective-permute-start(f32[2,5,16,128]{3,2,1,0:T(8,128)S(1)} %get-tuple-element.27), channel_id=1, source_target_pairs={{0,8},{8,0},{1,9},{9,1},{2,10},{10,2},{3,11},{11,3},{4,12},{12,4},... | collective-permute-start | bytes 245768 | tf_op jit(solution)/shard_map/ppermute | solution.py:37
  4.9 11.8 %collective-permute-start.3 = (f32[2,5,16,128]{3,2,1,0:T(8,128)S(1)}, f32[2,5,16,128]{3,2,1,0:T(8,128)S(1)}, u32[]{:S(2)}, u32[]{:S(2)}) collective-permute-start(f32[2,5,16,128]{3,2,1,0:T(8,128)S(1)} %get-tuple-element.34), channel_id=1, source_target_pairs={{1,2},{3,4},{5,6},{2,1},{4,3},{6,5},{9,10},{11,12},{13,14},{10,9},... | collective-permute-start | bytes 245768 | tf_op jit(solution)/shard_map/ppermute | solution.py:37
  5.6 11.1 %collective-permute-start.4 = (f32[2,5,16,128]{3,2,1,0:T(8,128)S(1)}, f32[2,5,16,128]{3,2,1,0:T(8,128)S(1)}, u32[]{:S(2)}, u32[]{:S(2)}) collective-permute-start(f32[2,5,16,128]{3,2,1,0:T(8,128)S(1)} %get-tuple-element.35), channel_id=1, source_target_pairs={{0,1},{2,3},{4,5},{6,7},{1,0},{3,2},{5,4},{7,6},{8,9},{10,11},{12,... | collective-permute-start | bytes 245768 | tf_op jit(solution)/shard_map/ppermute | solution.py:37
  11.7 8.2 %collective-permute-start.1 = (f32[2,5,16,128]{3,2,1,0:T(8,128)S(1)}, f32[2,5,16,128]{3,2,1,0:T(8,128)S(1)}, u32[]{:S(2)}, u32[]{:S(2)}) collective-permute-start(f32[2,5,16,128]{3,2,1,0:T(8,128)S(1)} %get-tuple-element.32), channel_id=1, source_target_pairs={{1,2},{3,4},{5,6},{2,1},{4,3},{6,5},{9,10},{11,12},{13,14},{10,9},... | collective-permute-start | bytes 245768 | tf_op jit(solution)/shard_map/ppermute | solution.py:37
  12.4 7.6 %collective-permute-start.2 = (f32[2,5,16,128]{3,2,1,0:T(8,128)S(1)}, f32[2,5,16,128]{3,2,1,0:T(8,128)S(1)}, u32[]{:S(2)}, u32[]{:S(2)}) collective-permute-start(f32[2,5,16,128]{3,2,1,0:T(8,128)S(1)} %get-tuple-element.33), channel_id=1, source_target_pairs={{0,1},{2,3},{4,5},{6,7},{1,0},{3,2},{5,4},{7,6},{8,9},{10,11},{12,... | collective-permute-start | bytes 245768 | tf_op jit(solution)/shard_map/ppermute | solution.py:37
  16.9 4.5 %collective-permute-start.5 = (f32[2,5,16,128]{3,2,1,0:T(8,128)S(1)}, f32[2,5,16,128]{3,2,1,0:T(8,128)S(1)}, u32[]{:S(2)}, u32[]{:S(2)}) collective-permute-start(f32[2,5,16,128]{3,2,1,0:T(8,128)S(1)} %get-tuple-element.37), channel_id=1, source_target_pairs={{0,8},{8,0},{1,9},{9,1},{2,10},{10,2},{3,11},{11,3},{4,12},{12,4},... | collective-permute-start | bytes 245768 | tf_op jit(solution)/shard_map/ppermute | solution.py:37
  21.8 1.8 %collective-permute-start.6 = (f32[3,16,16,128]{3,2,1,0:T(8,128)S(1)}, f32[3,16,16,128]{3,2,1,0:T(8,128)S(1)}, u32[]{:S(2)}, u32[]{:S(2)}) collective-permute-start(f32[3,16,16,128]{3,2,1,0:T(8,128)S(1)} %get-tuple-element.50.mine), channel_id=1, source_target_pairs={{0,16},{16,0},{1,17},{17,1},{2,18},{18,2},{3,19},{19,3},{4,20},{20... | collective-permute-start | bytes 1179656 | tf_op jit(solution)/shard_map/ppermute | solution.py:772

commit v10 on v9

--- a/solution.py
+++ b/solution.py
@@ -741,9 +741,12 @@
         )(*halos, rim_added, buoyancy, velocity)
         return velocity, exchange(send_links, sends)
 
-    velocity, velocity_halos_y = boundary(links_x, links_y, halos_x, velocity, "boundary_x")
+    later_y = links_y[::-1]
+    velocity, velocity_halos_y = boundary(links_x, later_y, halos_x, velocity, "boundary_x")
     velocity, velocity_halos_x = boundary(links_y, links_x, halos_y, velocity, "boundary_y")
     halos = halos_y + halos_x
+    later_links = later_y + links_x
+    later_halos = halos_y[::-1] + halos_x
     velocity_halos = velocity_halos_y + velocity_halos_x
 
     out_shape = jax.ShapeDtypeStruct(forward.shape, jnp.float32)
@@ -760,7 +763,7 @@
     )(*halos, *source, rim_added, buoyancy, accel, velocity)
 
     strain, gradient = pl.pallas_call(
-        functools.partial(gradient_kernel, links, width_y),
+        functools.partial(gradient_kernel, later_links, width_y),
         out_shape=[tile(12), tile(3)],
         in_specs=[vmem] * (2 * count) + [smem] * 2 + [vmem] * 5,
         out_specs=[vmem] * 2,
@@ -768,7 +771,7 @@
         compiler_params=params,
         cost_estimate=cost(30 * cells, 2 * 4 * cells),
         name="gradient",
-    )(*velocity_halos, *halos, *source, stress, scaled_lame, scaled_shear, strain, gradient)
+    )(*velocity_halos, *later_halos, *source, stress, scaled_lame, scaled_shear, strain, gradient)
     other = lax.ppermute(gradient, "shot", [(0, 1), (1, 0)])
 
     chunk = 4 if tile_x % 4 == 0 else 1

time: 24.6 us -> 22.5 us (0.915)
  the two profiles are of different devices: /device:TPU:0 before, /device:TPU:9 now
where the time goes in v10:
time: 22.5 us; the launch traced here: 22.3 us
  starting transfers between devices  12.9 us (57%)
  Pallas kernels  6.93 us (31%)
  between operations  2.08 us (9%)
  waiting for transfers between devices  0.32 us (1%)
    ppermute x6, starting transfers between devices, swap(): return lax.ppermute(value, axis, pairs + [(j, i) for i, j in pairs])  9.65 us
    ppermute x1, starting transfers between devices, body(): other = lax.ppermute(gradient, 'shot', [(0, 1), (1, 0)])  3.29 us
    pallas_call x1, Pallas kernels, body(): pl.pallas_call(functools.partial(velocity_kernel, width_y), out_shape=[pa...  1.58 us
    pallas_call x1, Pallas kernels, body(): pl.pallas_call(functools.partial(strain_kernel, links, width_y), out_shap...  1.25 us
    pallas_call x1, Pallas kernels, body(): pl.pallas_call(functools.partial(output_kernel, chunk, width_y), out_shap...  1.23 us
    pallas_call x1, Pallas kernels, body(): pl.pallas_call(functools.partial(early_pack_kernel, links_x), out_shape=s...  1.15 us
    pallas_call x1, Pallas kernels, body(): pl.pallas_call(sum_kernel, out_shape=jax.ShapeDtypeStruct((3, tile_x, til...  0.78 us
    pallas_call x1, Pallas kernels, body(): pl.pallas_call(functools.partial(gradient_kernel, later_links, width_y),...  0.48 us
  transfers between devices with their start and end apart: 7, of which 2 were waited for; matrix products, arithmetic and copies ran while one was open for 0% of the time, Pallas kernels for 20%

profile of v10, /device:TPU:9, one launch (start us, length us, event | category | flops | bytes accessed | tf_op | source)
XLA Modules:
  0.0 22.3 jit_solution(18148089890906378918)
XLA Ops:
  0.6 0.0 copy-start.1
  0.6 0.0 copy-start
  0.7 1.2 %early_pack.1 = (f32[2,5,16,128]{3,2,1,0:T(8,128)S(1)}, f32[16,16,128]{2,1,0:T(8,128)S(1)}) custom-call(f32[9,16,16,128]{3,2,1,0:T(8,128)} %bitcast.4, f32[9,16,16,128]{3,2,1,0:T(8,128)} %bitcast.7, f32[16,16,128]{2,1,0:T(8,128)} %density.1), custom_call_target="tpu_custom_call" | custom-call | bytes 131072 | tf_op jit(solution)/shard_map/early_pack/pallas_call | solution.py:674
  1.8 0.0 copy-start.2
  1.8 0.0 copy-start.3
  1.8 1.3 %collective-permute-start = (f32[2,5,16,128]{3,2,1,0:T(8,128)S(1)}, f32[2,5,16,128]{3,2,1,0:T(8,128)S(1)}, u32[]{:S(2)}, u32[]{:S(2)}) collective-permute-start(f32[2,5,16,128]{3,2,1,0:T(8,128)S(1)} %get-tuple-element.27), channel_id=1, source_target_pairs={{0,8},{8,0},{1,9},{9,1},{2,10},{10,2},{3,11},{11,3},{4,12},{12,4},... | collective-permute-start | bytes 245768 | tf_op jit(solution)/shard_map/ppermute | solution.py:37
  3.1 0.0 copy-done.1
  3.1 0.0 copy-done
  3.1 0.1 pack.1
  3.2 3.0 %collective-permute-start.3 = (f32[2,5,16,128]{3,2,1,0:T(8,128)S(1)}, f32[2,5,16,128]{3,2,1,0:T(8,128)S(1)}, u32[]{:S(2)}, u32[]{:S(2)}) collective-permute-start(f32[2,5,16,128]{3,2,1,0:T(8,128)S(1)} %get-tuple-element.34), channel_id=1, source_target_pairs={{1,2},{3,4},{5,6},{2,1},{4,3},{6,5},{9,10},{11,12},{13,14},{10,9},... | collective-permute-start | bytes 245768 | tf_op jit(solution)/shard_map/ppermute | solution.py:37
  6.2 1.4 %collective-permute-start.4 = (f32[2,5,16,128]{3,2,1,0:T(8,128)S(1)}, f32[2,5,16,128]{3,2,1,0:T(8,128)S(1)}, u32[]{:S(2)}, u32[]{:S(2)}) collective-permute-start(f32[2,5,16,128]{3,2,1,0:T(8,128)S(1)} %get-tuple-element.35), channel_id=1, source_target_pairs={{0,1},{2,3},{4,5},{6,7},{1,0},{3,2},{5,4},{7,6},{8,9},{10,11},{12,... | collective-permute-start | bytes 245768 | tf_op jit(solution)/shard_map/ppermute | solution.py:37
  7.7 0.0 copy-done.2
  7.7 0.0 copy-done.3
  7.7 1.6 %velocity.1 = (f32[12,20,32,128]{3,2,1,0:T(8,128)S(1)}, f32[6,20,32,128]{3,2,1,0:T(8,128)S(1)}, f32[3,16,16,128]{3,2,1,0:T(8,128)S(1)}, f32[2,3,16,128]{3,2,1,0:...) custom-call(f32[16,16,128]{2,1,0:T(8,128)} %lame.1, ...), custom_call_target="tpu_custom_call" | custom-call | flops 6553600 | bytes 2359296 | tf_op jit(solution)/shard_map/velocity/pallas_call | solution.py:698
  9.3 0.0 collective-permute-done.refs_0_.refs_2_.refs_5_
  9.3 0.2 boundary_x.1
  9.4 0.2 collective-permute-start.1
  9.6 3.2 %collective-permute-start.2 = (f32[2,5,16,128]{3,2,1,0:T(8,128)S(1)}, f32[2,5,16,128]{3,2,1,0:T(8,128)S(1)}, u32[]{:S(2)}, u32[]{:S(2)}) collective-permute-start(f32[2,5,16,128]{3,2,1,0:T(8,128)S(1)} %get-tuple-element.33), channel_id=1, source_target_pairs={{1,2},{3,4},{5,6},{2,1},{4,3},{6,5},{9,10},{11,12},{13,14},{10,9},... | collective-permute-start | bytes 245768 | tf_op jit(solution)/shard_map/ppermute | solution.py:37
  12.8 0.0 collective-permute-done.3.refs_0_.refs_4_
  12.8 0.0 collective-permute-done.4.refs_1_.refs_3_
  12.8 0.2 %boundary_y.1 = (f32[6,20,32,128]{3,2,1,0:T(8,128)S(1)}, f32[2,5,16,128]{3,2,1,0:T(8,128)S(1)}) custom-call(f32[2,5,16,128]{3,2,1,0:T(8,128)S(1)} %collective-permute-done.3.refs_0_.refs_4_, f32[2,5,16,128]{3,2,1,0:T(8,128)S(1)} %collective-permute-done.4.refs_1_.refs_3_, ...), custom_call_target="tpu_custom_call", output_to_operand_aliasing={{0}: (4, {})} | custom-call | flops 32768 | bytes 163840 | tf_op jit(solution)/shard_map/boundary_y/pallas_call | solution.py:732
  13.0 0.6 %collective-permute-start.5 = (f32[2,5,16,128]{3,2,1,0:T(8,128)S(1)}, f32[2,5,16,128]{3,2,1,0:T(8,128)S(1)}, u32[]{:S(2)}, u32[]{:S(2)}) collective-permute-start(f32[2,5,16,128]{3,2,1,0:T(8,128)S(1)} %get-tuple-element.37), channel_id=1, source_target_pairs={{0,8},{8,0},{1,9},{9,1},{2,10},{10,2},{3,11},{11,3},{4,12},{12,4},... | collective-permute-start | bytes 245768 | tf_op jit(solution)/shard_map/ppermute | solution.py:37
  14.9 1.2 %strain.1 = (f32[12,16,16,128]{3,2,1,0:T(8,128)S(1)}, f32[3,16,16,128]{3,2,1,0:T(8,128)S(1)}, f32[6,20,32,128]{3,2,1,0:T(8,128)S(1)}, f32[9,16,16,128]{3,2,1,0:T(8,128)}, f32[9,16,16,128]{3,2,1,0:T(8,128)}) custom-call(f32[2,5,16,128]{3,2,1,0:T(8,128)S(1)} %collective-permute-done.3.refs_0_.refs_4_, ...), custom_call_target="tpu_custom_call", output_to_operand_aliasing={{2}: (8, {})} | custom-call | flops 6553600 | bytes 2359296 | tf_op jit(solution)/shard_map/strain/pallas_call | solution.py:753
  16.2 0.0 collective-permute-done.1.refs_0_
  16.2 0.0 collective-permute-done.2.refs_1_
  16.2 0.2 collective-permute-done.5.refs_2_
  16.4 0.5 %gradient.1 = (f32[12,16,16,128]{3,2,1,0:T(8,128)S(1)}, f32[3,16,16,128]{3,2,1,0:T(8,128)S(1)}) custom-call(f32[2,5,16,128]{3,2,1,0:T(8,128)S(1)} %collective-permute-done.1.refs_0_, f32[2,5,16,128]{3,2,1,0:T(8,128)S(1)} %collective-permute-done.2.refs_1_, ...), custom_call_target="tpu_custom_call", output_to_operand_aliasing={{0}: (11, {}), {1}: (12, {})} | custom-call | flops 983040 | bytes 262144 | tf_op jit(solution)/shard_map/gradient/pallas_call | solution.py:765
  16.9 3.3 %collective-permute-start.6 = (f32[3,16,16,128]{3,2,1,0:T(8,128)S(1)}, f32[3,16,16,128]{3,2,1,0:T(8,128)S(1)}, u32[]{:S(2)}, u32[]{:S(2)}) collective-permute-start(f32[3,16,16,128]{3,2,1,0:T(8,128)S(1)} %get-tuple-element.50.mine), channel_id=1, source_target_pairs={{0,16},{16,0},{1,17},{17,1},{2,18},{18,2},{3,19},{19,3},{4,20},{20... | collective-permute-start | bytes 1179656 | tf_op jit(solution)/shard_map/ppermute | solution.py:775
  20.2 1.2 %outputs.1 = (f32[9,16,16,128]{3,2,1,0:T(8,128)}, f32[9,16,16,128]{3,2,1,0:T(8,128)}) custom-call(s32[1]{0:T(128)S(6)} %copy.26.refs_3_.refs_6_.source_cell, f32[1]{0:T(128)S(6)} %copy.27.refs_4_.refs_7_.source_amp, f32[12,16,16,128]{3,2,1,0:T(8,128)S(1)} %get-tuple-element.45.strain, ...), custom_call_target="tpu_custom_call", output_to_operand_aliasing={{0}: (6, {}), {1}: (7, {})} | custom-call | flops 1966080 | bytes 2359296 | tf_op jit(solution)/shard_map/outputs/pallas_call | solution.py:778
  21.4 0.1 collective-permute-done.6.other
  21.5 0.8 %sum.1 = f32[3,16,16,128]{3,2,1,0:T(8,128)} custom-call(f32[3,16,16,128]{3,2,1,0:T(8,128)S(1)} %get-tuple-element.50.mine, f32[3,16,16,128]{3,2,1,0:T(8,128)S(1)} %collective-permute-done.6.other), custom_call_target="tpu_custom_call" | custom-call | flops 98304 | bytes 1179648 | tf_op jit(solution)/shard_map/sum/pallas_call | solution.py:789
Async XLA Ops:
  0.6 2.5 %copy-start.1 = (f32[1,9,16,16,128]{4,3,2,1,0:T(8,128)S(1)}, f32[1,9,16,16,128]{4,3,2,1,0:T(8,128)}, u32[]{:S(2)}) copy-start(f32[1,9,16,16,128]{4,3,2,1,0:T(8,128)} %param.10) | copy-start | bytes 3538948
  0.6 2.5 %copy-start = (f32[1,9,16,16,128]{4,3,2,1,0:T(8,128)S(1)}, f32[1,9,16,16,128]{4,3,2,1,0:T(8,128)}, u32[]{:S(2)}) copy-start(f32[1,9,16,16,128]{4,3,2,1,0:T(8,128)} %param.9) | copy-start | bytes 3538948
  1.8 5.9 %copy-start.2 = (s32[1,256]{1,0:T(1,128)S(1)}, s32[1,256]{1,0:T(1,128)}, u32[]{:S(2)}) copy-start(s32[1,256]{1,0:T(1,128)} %receiver_cell.1) | copy-start | bytes 3076
  1.8 5.9 %copy-start.3 = (f32[1,256]{1,0:T(1,128)S(1)}, f32[1,256]{1,0:T(1,128)}, u32[]{:S(2)}) copy-start(f32[1,256]{1,0:T(1,128)} %residual_amp.1) | copy-start | bytes 3076
  1.8 7.4 %collective-permute-start = (f32[2,5,16,128]{3,2,1,0:T(8,128)S(1)}, f32[2,5,16,128]{3,2,1,0:T(8,128)S(1)}, u32[]{:S(2)}, u32[]{:S(2)}) collective-permute-start(f32[2,5,16,128]{3,2,1,0:T(8,128)S(1)} %get-tuple-element.27), channel_id=1, source_target_pairs={{0,8},{8,0},{1,9},{9,1},{2,10},{10,2},{3,11},{11,3},{4,12},{12,4},... | collective-permute-start | bytes 245768 | tf_op jit(solution)/shard_map/ppermute | solution.py:37
  3.2 9.6 %collective-permute-start.3 = (f32[2,5,16,128]{3,2,1,0:T(8,128)S(1)}, f32[2,5,16,128]{3,2,1,0:T(8,128)S(1)}, u32[]{:S(2)}, u32[]{:S(2)}) collective-permute-start(f32[2,5,16,128]{3,2,1,0:T(8,128)S(1)} %get-tuple-element.34), channel_id=1, source_target_pairs={{1,2},{3,4},{5,6},{2,1},{4,3},{6,5},{9,10},{11,12},{13,14},{10,9},... | collective-permute-start | bytes 245768 | tf_op jit(solution)/shard_map/ppermute | solution.py:37
  6.2 6.5 %collective-permute-start.4 = (f32[2,5,16,128]{3,2,1,0:T(8,128)S(1)}, f32[2,5,16,128]{3,2,1,0:T(8,128)S(1)}, u32[]{:S(2)}, u32[]{:S(2)}) collective-permute-start(f32[2,5,16,128]{3,2,1,0:T(8,128)S(1)} %get-tuple-element.35), channel_id=1, source_target_pairs={{0,1},{2,3},{4,5},{6,7},{1,0},{3,2},{5,4},{7,6},{8,9},{10,11},{12,... | collective-permute-start | bytes 245768 | tf_op jit(solution)/shard_map/ppermute | solution.py:37
  9.4 6.7 %collective-permute-start.1 = (f32[2,5,16,128]{3,2,1,0:T(8,128)S(1)}, f32[2,5,16,128]{3,2,1,0:T(8,128)S(1)}, u32[]{:S(2)}, u32[]{:S(2)}) collective-permute-start(f32[2,5,16,128]{3,2,1,0:T(8,128)S(1)} %get-tuple-element.32), channel_id=1, source_target_pairs={{0,1},{2,3},{4,5},{6,7},{1,0},{3,2},{5,4},{7,6},{8,9},{10,11},{12,... | collective-permute-start | bytes 245768 | tf_op jit(solution)/shard_map/ppermute | solution.py:37
  9.6 6.6 %collective-permute-start.2 = (f32[2,5,16,128]{3,2,1,0:T(8,128)S(1)}, f32[2,5,16,128]{3,2,1,0:T(8,128)S(1)}, u32[]{:S(2)}, u32[]{:S(2)}) collective-permute-start(f32[2,5,16,128]{3,2,1,0:T(8,128)S(1)} %get-tuple-element.33), channel_id=1, source_target_pairs={{1,2},{3,4},{5,6},{2,1},{4,3},{6,5},{9,10},{11,12},{13,14},{10,9},... | collective-permute-start | bytes 245768 | tf_op jit(solution)/shard_map/ppermute | solution.py:37
  13.0 3.4 %collective-permute-start.5 = (f32[2,5,16,128]{3,2,1,0:T(8,128)S(1)}, f32[2,5,16,128]{3,2,1,0:T(8,128)S(1)}, u32[]{:S(2)}, u32[]{:S(2)}) collective-permute-start(f32[2,5,16,128]{3,2,1,0:T(8,128)S(1)} %get-tuple-element.37), channel_id=1, source_target_pairs={{0,8},{8,0},{1,9},{9,1},{2,10},{10,2},{3,11},{11,3},{4,12},{12,4},... | collective-permute-start | bytes 245768 | tf_op jit(solution)/shard_map/ppermute | solution.py:37
  16.9 4.6 %collective-permute-start.6 = (f32[3,16,16,128]{3,2,1,0:T(8,128)S(1)}, f32[3,16,16,128]{3,2,1,0:T(8,128)S(1)}, u32[]{:S(2)}, u32[]{:S(2)}) collective-permute-start(f32[3,16,16,128]{3,2,1,0:T(8,128)S(1)} %get-tuple-element.50.mine), channel_id=1, source_target_pairs={{0,16},{16,0},{1,17},{17,1},{2,18},{18,2},{3,19},{19,3},{4,20},{20... | collective-permute-start | bytes 1179656 | tf_op jit(solution)/shard_map/ppermute | solution.py:775

commit v11 on v10

--- a/solution.py
+++ b/solution.py
@@ -369,65 +369,90 @@
     return lax.axis_index("tx") * tile_x, lax.axis_index("ty") * tile_y
 
 
-def velocity_halo_terms(links, received, stresses, stress, source, width_y, add):
+def missing_terms(links, stress, source, width_y, missing):
     cell, amp = source
     layers, rows, depth = stress.shape[1:]
     tile = layers - 2 * LAYERS, rows - 2 * ROWS
     starts = start_of(*tile)
-    for link, halo, stress_halo in zip(links, received, stresses):
+    for link, out in zip(links, missing):
+        dim = link[1]
+        shape = out.shape[2:]
+        cross = starts[1 - dim] + lax.broadcasted_iota(jnp.int32, shape, 0)
+        level = lax.broadcasted_iota(jnp.int32, shape, 1)
+
+        def own(wave, part, index):
+            return face(stress, 6 * wave + STRESS_ALONG[dim][part], dim, index, True)[...]
+
+        def put(slots):
+            for wave in range(2):
+                for slot, (part, layer, terms) in enumerate(slots):
+                    value = terms(wave) if dim == 1 else jnp.zeros(shape, jnp.float32)
+                    if wave == 0:
+                        here = jnp.full(shape, starts[dim] + layer, jnp.int32)
+                        x, y = (here, cross) if dim == 0 else (cross, here)
+                        value += amp * source_gain(
+                            cell, VELOCITY_ALONG[dim][part], x, y, level, width_y
+                        )
+                    out[wave, slot] = value
+
+        def after():
+            count = tile[dim]
+            slots = [(0, count, lambda wave: -far * own(wave, 0, -1))]
+            for part in (1, 2):
+                slots += [
+                    (
+                        part,
+                        count,
+                        lambda wave, part=part: -near * own(wave, part, -1)
+                        - far * own(wave, part, -2),
+                    ),
+                    (part, count + 1, lambda wave, part=part: -far * own(wave, part, -1)),
+                ]
+            put(slots)
+
+        def before():
+            put([
+                (0, -2, lambda wave: far * own(wave, 0, 0)),
+                (0, -1, lambda wave: near * own(wave, 0, 0) + far * own(wave, 0, 1)),
+                (1, -1, lambda wave: far * own(wave, 1, 0)),
+                (2, -1, lambda wave: far * own(wave, 2, 0)),
+            ])
+
+        lower = is_lower(link[0], link[2])
+        pl.when(lower)(after)
+        pl.when(jnp.logical_not(lower))(before)
+
+
+def velocity_halo_terms(links, received, stresses, missing, add):
+    for link, halo, stress_halo, lack in zip(links, received, stresses, missing):
         dim = link[1]
         part_n, part_a, part_b = STRAIN_OF[dim]
-        shape = halo.shape[2:]
-        cross = starts[1 - dim] + lax.broadcasted_iota(jnp.int32, shape, 0)
-        level = lax.broadcasted_iota(jnp.int32, shape, 1)
-
-        def own(wave, part, index):
-            return face(stress, 6 * wave + STRESS_ALONG[dim][part], dim, index, True)[...]
-
-        def whole(wave, slot, part, layer, light, terms):
-            value = halo[wave, slot]
-            if dim == 1:
-                value += time_step * light * terms()
-            if wave == 0:
-                here = jnp.full(shape, starts[dim] + layer, jnp.int32)
-                x, y = (here, cross) if dim == 0 else (cross, here)
-                gain = source_gain(cell, VELOCITY_ALONG[dim][part], x, y, level, width_y)
-                value += time_step * amp * light * gain
-            return value
 
         def after():
-            count = tile[dim]
-            lights = [1.0 / stress_halo[layer, SPARE] for layer in range(2)]
+            lights = [time_step / stress_halo[layer, SPARE] for layer in range(2)]
             for wave in range(2):
-                n = whole(wave, 0, 0, count, lights[0], lambda: -far * own(wave, 0, -1))
-                add(wave, part_n, dim, -1, far * n)
-                for part, name, slot in ((part_a, 1, 1), (part_b, 2, 3)):
-                    inner = whole(
-                        wave, slot, name, count, lights[0],
-                        lambda: -near * own(wave, name, -1) - far * own(wave, name, -2),
-                    )
-                    outer = whole(
-                        wave, slot + 1, name, count + 1, lights[1],
-                        lambda: -far * own(wave, name, -1),
-                    )
+
+                def whole(slot, layer):
+                    return halo[wave, slot] + lights[layer] * lack[wave, slot]
+
+                add(wave, part_n, dim, -1, far * whole(0, 0))
+                for part, slot in ((part_a, 1), (part_b, 3)):
+                    inner, outer = whole(slot, 0), whole(slot + 1, 1)
                     add(wave, part, dim, -1, near * inner + far * outer)
                     add(wave, part, dim, -2, far * inner)
 
         def before():
-            lights = [halo[layer, SPARE] for layer in range(2)]
+            lights = [time_step * halo[layer, SPARE] for layer in range(2)]
             for wave in range(2):
-                outer = whole(wave, 0, 0, -2, lights[1], lambda: far * own(wave, 0, 0))
-                inner = whole(
-                    wave, 1, 0, -1, lights[0],
-                    lambda: near * own(wave, 0, 0) + far * own(wave, 0, 1),
-                )
+
+                def whole(slot, layer):
+                    return halo[wave, slot] + lights[layer] * lack[wave, slot]
+
+                outer, inner = whole(0, 1), whole(1, 0)
                 add(wave, part_n, dim, 0, -near * inner - far * outer)
                 add(wave, part_n, dim, 1, -far * inner)
-                for part, name, slot in ((part_a, 1, 2), (part_b, 2, 3)):
-                    value = whole(
-                        wave, slot, name, -1, lights[0], lambda: far * own(wave, name, 0)
-                    )
-                    add(wave, part, dim, 0, -far * value)
+                add(wave, part_a, dim, 0, -far * whole(2, 0))
+                add(wave, part_b, dim, 0, -far * whole(3, 0))
 
         real = has_peer(link[0], link[2])
         lower = is_lower(link[0], link[2])
@@ -475,8 +500,10 @@
     count = len(links)
     received = refs[:count]
     source_cell, source_amp, rim_added, buoyancy, accel = refs[count : count + 5]
-    strain, gradient, velocity = refs[count + 6 : count + 9]
-    outputs, (accel_now, sems) = refs[count + 9 : count + 11], refs[count + 11 :]
+    stress = refs[count + 6]
+    strain, low_part, high_part, velocity = refs[count + 7 : count + 11]
+    outputs, missing = refs[count + 11 : count + 13], refs[count + 13 : 2 * count + 13]
+    accel_now, sems = refs[2 * count + 13 :]
     tile_x, tile_y, depth = buoyancy.shape
     middle = pl.ds(ROWS, tile_y)
     clear_rim(velocity, range(6), range(6))
@@ -515,7 +542,7 @@
     ]
     for copy in copies:
         copy.start()
-    def layer(x, carry):
+    def layer(begin, half, x, carry):
         for wave in range(2):
             vx, vy, vz = range(3 * wave, 3 * wave + 3)
             values = (
@@ -531,10 +558,18 @@
         total = sum(
             accel_now[part, x] * velocity[3 + part, x + LAYERS, middle, :] for part in range(3)
         )
-        gradient[2, x] = -time_step * total
+        half[x - begin] = -time_step * total
         return carry
 
-    lax.fori_loop(0, tile_x, layer, 0, unroll=4)
+    for begin, half in ((0, low_part), (tile_x // 2, high_part)):
+        lax.fori_loop(
+            begin,
+            begin + half.shape[0],
+            functools.partial(layer, begin, half),
+            0,
+            unroll=4,
+        )
+    missing_terms(links, stress, (cell, amp), width_y, missing)
     for copy in copies:
         copy.wait()
 
@@ -553,19 +588,20 @@
     return strains, values
 
 
-def gradient_kernel(links, width_y, *refs):
+def gradient_kernel(links, *refs):
     count = len(links)
-    received, stresses = refs[:count], refs[count : 2 * count]
-    source_cell, source_amp, stress, scaled_lame, scaled_shear = refs[2 * count : 2 * count + 5]
-    strain, gradient = refs[2 * count + 7 :]
+    received, stresses, missing = (refs[at : at + count] for at in range(0, 3 * count, count))
+    stress, scaled_lame, scaled_shear, *halves, _ = refs[3 * count : 3 * count + 8]
+    strain, gradient, density_total = refs[3 * count + 8 :]
     tile_x, tile_y, _ = scaled_lame.shape
+    for at, (mine, other) in enumerate(zip(halves[:2], halves[2:])):
+        density_total[pl.ds(at * (tile_x // 2), mine.shape[0])] = mine[...] + other[...]
 
     def add(wave, part, dim, index, term):
         target = face(strain, 6 * wave + part, dim, index, False)
         target[...] += term
 
-    source = source_cell[0], source_amp[0]
-    velocity_halo_terms(links, received, stresses, stress, source, width_y, add)
+    velocity_halo_terms(links, received, stresses, missing, add)
 
     def layer(x, carry):
         strains = [strain[part, x] for part in range(6)]
@@ -580,15 +616,26 @@
 
 
 def output_kernel(
-    chunk, width_y, source_cell, source_amp, strain, stress, scaled_lame, scaled_shear, *refs
+    chunk,
+    width_y,
+    source_cell,
+    source_amp,
+    strain,
+    stress,
+    scaled_lame,
+    scaled_shear,
+    density_total,
+    *refs,
 ):
-    outputs, (values_now, sems) = refs[2:4], refs[4:]
+    outputs, total = refs[2:4], refs[4]
+    values_now, sems = refs[5:]
     tile_x, tile_y, depth = scaled_lame.shape
     x_start, y_start = start_of(tile_x, tile_y)
     y = y_start + lax.broadcasted_iota(jnp.int32, (tile_y, depth), 0)
     level = lax.broadcasted_iota(jnp.int32, (tile_y, depth), 1)
     in_layer = y * depth + level - source_cell[0]
-    copies = []
+    copies = [pltpu.make_async_copy(density_total, total.at[2], sems.at[0])]
+    copies[0].start()
     for begin in range(0, tile_x, chunk):
         for wave in range(2):
             for x in range(begin, begin + chunk):
@@ -611,7 +658,7 @@
         copy.wait()
 
 
-def sum_kernel(mine, other, total, total_now, sems):
+def sum_kernel(mine, other, _, total, total_now, sems):
     copies = []
     for part in range(mine.shape[0]):
         total_now[part] = mine[part] + other[part]
@@ -750,52 +797,80 @@
     velocity_halos = velocity_halos_y + velocity_halos_x
 
     out_shape = jax.ShapeDtypeStruct(forward.shape, jnp.float32)
-    strain, gradient, _, forward_next, adjoint_next = pl.pallas_call(
+    halves = [
+        pltpu.VMEM((size, tile_y, depth), jnp.float32) for size in (tile_x // 2, -(-tile_x // 2))
+    ]
+    strain, low_part, high_part, _, forward_next, adjoint_next, *missing = pl.pallas_call(
         functools.partial(strain_kernel, links, width_y),
-        out_shape=[tile(12), tile(3), padded(6), out_shape, out_shape],
-        in_specs=[vmem] * count + [smem] * 2 + [vmem] * 4,
-        out_specs=[vmem] * 3 + [hbm] * 2,
-        input_output_aliases={count + 5: 2},
+        out_shape=[tile(12), *halves, padded(6), out_shape, out_shape] + shapes(links),
+        in_specs=[vmem] * count + [smem] * 2 + [vmem] * 5,
+        out_specs=[vmem] * 4 + [hbm] * 2 + [vmem] * count,
+        input_output_aliases={count + 5: 3},
         scratch_shapes=[tile(3), pltpu.SemaphoreType.DMA((6,))],
         compiler_params=params,
         cost_estimate=cost(200 * cells, 18 * 4 * cells),
         name="strain",
-    )(*halos, *source, rim_added, buoyancy, accel, velocity)
-
-    strain, gradient = pl.pallas_call(
-        functools.partial(gradient_kernel, later_links, width_y),
-        out_shape=[tile(12), tile(3)],
-        in_specs=[vmem] * (2 * count) + [smem] * 2 + [vmem] * 5,
-        out_specs=[vmem] * 2,
-        input_output_aliases={2 * count + 5: 0, 2 * count + 6: 1},
+    )(*halos, *source, rim_added, buoyancy, accel, velocity, stress)
+    pair = [(0, 1), (1, 0)]
+    density_parts = low_part, high_part
+    other_parts = [lax.ppermute(part, "shot", pair) for part in density_parts]
+
+    missing = missing[:count_y][::-1] + missing[count_y:]
+    strain, gradient, density_total = pl.pallas_call(
+        functools.partial(gradient_kernel, later_links),
+        out_shape=[tile(12), tile(2), tile()],
+        in_specs=[vmem] * (3 * count + 8),
+        out_specs=[vmem] * 3,
+        input_output_aliases={3 * count + 7: 0},
         compiler_params=params,
         cost_estimate=cost(30 * cells, 2 * 4 * cells),
         name="gradient",
-    )(*velocity_halos, *later_halos, *source, stress, scaled_lame, scaled_shear, strain, gradient)
-    other = lax.ppermute(gradient, "shot", [(0, 1), (1, 0)])
+    )(
+        *velocity_halos,
+        *later_halos,
+        *missing,
+        stress,
+        scaled_lame,
+        scaled_shear,
+        *density_parts,
+        *other_parts,
+        strain,
+    )
+    other = lax.ppermute(gradient, "shot", pair)
 
     chunk = 4 if tile_x % 4 == 0 else 1
-    forward_next, adjoint_next = pl.pallas_call(
+    total_shape = jax.ShapeDtypeStruct((3, tile_x, tile_y, depth), jnp.float32)
+    forward_next, adjoint_next, total = pl.pallas_call(
         functools.partial(output_kernel, chunk, width_y),
-        out_shape=[out_shape, out_shape],
-        in_specs=[smem] * 2 + [vmem] * 4 + [hbm] * 2,
-        out_specs=[hbm] * 2,
-        input_output_aliases={6: 0, 7: 1},
-        scratch_shapes=[tile(12), pltpu.SemaphoreType.DMA((2 * tile_x // chunk,))],
+        out_shape=[out_shape, out_shape, total_shape],
+        in_specs=[smem] * 2 + [vmem] * 5 + [hbm] * 2,
+        out_specs=[hbm] * 3,
+        input_output_aliases={7: 0, 8: 1},
+        scratch_shapes=[tile(12), pltpu.SemaphoreType.DMA((1 + 2 * tile_x // chunk,))],
         compiler_params=params,
         cost_estimate=cost(60 * cells, 18 * 4 * cells),
         name="outputs",
-    )(*source, strain, stress, scaled_lame, scaled_shear, forward_next, adjoint_next)
+    )(
+        *source,
+        strain,
+        stress,
+        scaled_lame,
+        scaled_shear,
+        density_total,
+        forward_next,
+        adjoint_next,
+    )
     total = pl.pallas_call(
         sum_kernel,
-        out_shape=jax.ShapeDtypeStruct((3, tile_x, tile_y, depth), jnp.float32),
-        in_specs=[vmem] * 2,
+        out_shape=total_shape,
+        in_specs=[vmem] * 2 + [hbm],
         out_specs=hbm,
-        scratch_shapes=[tile(3), pltpu.SemaphoreType.DMA((3,))],
+        input_output_aliases={2: 0},
+        scratch_shapes=[tile(2), pltpu.SemaphoreType.DMA((2,))],
         compiler_params=params,
-        cost_estimate=cost(3 * cells, 9 * 4 * cells),
+        cost_estimate=cost(2 * cells, 6 * 4 * cells),
         name="sum",
-    )(gradient, other)
+    )(gradient, other, total)
     return forward_next[None], adjoint_next[None], total
 
 

time: 22.5 us -> 22.8 us (1.013)
  waiting for transfers between devices: 0.32 us -> 1.31 us
  starting transfers between devices: 12.9 us -> 12 us
    ppermute x1 -> x3, waiting for transfers between devices: 0.11 us -> 1.3 us  [the longest x2 1.18 us: body(): other_parts = [lax.ppermute(part, 'shot', pair) for part in density_parts]]
    ppermute x1 -> x3, starting transfers between devices: 3.29 us -> 2.38 us  [the longest x2 2.16 us: body(): other_parts = [lax.ppermute(part, 'shot', pair) for part in density_parts]]
  transfers between devices with their start and end apart: 7 -> 9, of which waited for: 2 -> 3; matrix products, arithmetic and copies ran while one was open for 0% -> 0% of each run, Pallas kernels for 20% -> 21%
where the time goes in v11:
time: 22.8 us; the launch traced here: 22.5 us
  starting transfers between devices  12 us (53%)
  Pallas kernels  7.02 us (31%)
  between operations  2.07 us (9%)
  waiting for transfers between devices  1.31 us (6%)
    ppermute x6, starting transfers between devices, swap(): return lax.ppermute(value, axis, pairs + [(j, i) for i, j in pairs])  9.65 us
    ppermute x2, starting transfers between devices, body(): other_parts = [lax.ppermute(part, 'shot', pair) for part in density_parts]  2.16 us
    pallas_call x1, Pallas kernels, body(): pl.pallas_call(functools.partial(velocity_kernel, width_y), out_shape=[pa...  1.58 us
    pallas_call x1, Pallas kernels, body(): pl.pallas_call(functools.partial(strain_kernel, links, width_y), out_shap...  1.44 us
    pallas_call x1, Pallas kernels, body(): pl.pallas_call(functools.partial(output_kernel, chunk, width_y), out_shap...  1.25 us
    ppermute x2, waiting for transfers between devices, body(): other_parts = [lax.ppermute(part, 'shot', pair) for part in density_parts]  1.18 us
    pallas_call x1, Pallas kernels, body(): pl.pallas_call(functools.partial(early_pack_kernel, links_x), out_shape=s...  1.15 us
    pallas_call x1, Pallas kernels, body(): pl.pallas_call(sum_kernel, out_shape=total_shape, in_specs=[vmem] * 2 + [...  0.73 us
  transfers between devices with their start and end apart: 9, of which 3 were waited for; matrix products, arithmetic and copies ran while one was open for 0% of the time, Pallas kernels for 21%

profile of v11, /device:TPU:9, one launch (start us, length us, event | category | flops | bytes accessed | tf_op | source)
XLA Modules:
  0.0 22.5 jit_solution(5194709999376725418)
XLA Ops:
  0.6 0.0 copy-start.1
  0.6 0.0 copy-start
  0.7 1.2 %early_pack.1 = (f32[2,5,16,128]{3,2,1,0:T(8,128)S(1)}, f32[16,16,128]{2,1,0:T(8,128)S(1)}) custom-call(f32[9,16,16,128]{3,2,1,0:T(8,128)} %bitcast.4, f32[9,16,16,128]{3,2,1,0:T(8,128)} %bitcast.7, f32[16,16,128]{2,1,0:T(8,128)} %density.1), custom_call_target="tpu_custom_call" | custom-call | bytes 131072 | tf_op jit(solution)/shard_map/early_pack/pallas_call | solution.py:721
  1.8 0.0 copy-start.2
  1.8 0.0 copy-start.3
  1.8 1.3 %collective-permute-start = (f32[2,5,16,128]{3,2,1,0:T(8,128)S(1)}, f32[2,5,16,128]{3,2,1,0:T(8,128)S(1)}, u32[]{:S(2)}, u32[]{:S(2)}) collective-permute-start(f32[2,5,16,128]{3,2,1,0:T(8,128)S(1)} %get-tuple-element.33), channel_id=1, source_target_pairs={{0,8},{8,0},{1,9},{9,1},{2,10},{10,2},{3,11},{11,3},{4,12},{12,4},... | collective-permute-start | bytes 245768 | tf_op jit(solution)/shard_map/ppermute | solution.py:37
  3.1 0.0 copy-done.1
  3.1 0.0 copy-done
  3.1 0.1 pack.1
  3.2 3.0 %collective-permute-start.3 = (f32[2,5,16,128]{3,2,1,0:T(8,128)S(1)}, f32[2,5,16,128]{3,2,1,0:T(8,128)S(1)}, u32[]{:S(2)}, u32[]{:S(2)}) collective-permute-start(f32[2,5,16,128]{3,2,1,0:T(8,128)S(1)} %get-tuple-element.40), channel_id=1, source_target_pairs={{1,2},{3,4},{5,6},{2,1},{4,3},{6,5},{9,10},{11,12},{13,14},{10,9},... | collective-permute-start | bytes 245768 | tf_op jit(solution)/shard_map/ppermute | solution.py:37
  6.2 1.4 %collective-permute-start.4 = (f32[2,5,16,128]{3,2,1,0:T(8,128)S(1)}, f32[2,5,16,128]{3,2,1,0:T(8,128)S(1)}, u32[]{:S(2)}, u32[]{:S(2)}) collective-permute-start(f32[2,5,16,128]{3,2,1,0:T(8,128)S(1)} %get-tuple-element.41), channel_id=1, source_target_pairs={{0,1},{2,3},{4,5},{6,7},{1,0},{3,2},{5,4},{7,6},{8,9},{10,11},{12,... | collective-permute-start | bytes 245768 | tf_op jit(solution)/shard_map/ppermute | solution.py:37
  7.7 0.0 copy-done.2
  7.7 0.0 copy-done.3
  7.7 1.6 %velocity.1 = (f32[12,20,32,128]{3,2,1,0:T(8,128)S(1)}, f32[6,20,32,128]{3,2,1,0:T(8,128)S(1)}, f32[3,16,16,128]{3,2,1,0:T(8,128)S(1)}, f32[2,3,16,128]{3,2,1,0:...) custom-call(f32[16,16,128]{2,1,0:T(8,128)} %lame.1, ...), custom_call_target="tpu_custom_call" | custom-call | flops 6553600 | bytes 2359296 | tf_op jit(solution)/shard_map/velocity/pallas_call | solution.py:745
  9.3 0.0 collective-permute-done.refs_0_.refs_2_.refs_5_
  9.3 0.2 boundary_x.1
  9.4 0.2 collective-permute-start.1
  9.6 3.2 %collective-permute-start.2 = (f32[2,5,16,128]{3,2,1,0:T(8,128)S(1)}, f32[2,5,16,128]{3,2,1,0:T(8,128)S(1)}, u32[]{:S(2)}, u32[]{:S(2)}) collective-permute-start(f32[2,5,16,128]{3,2,1,0:T(8,128)S(1)} %get-tuple-element.39), channel_id=1, source_target_pairs={{1,2},{3,4},{5,6},{2,1},{4,3},{6,5},{9,10},{11,12},{13,14},{10,9},... | collective-permute-start | bytes 245768 | tf_op jit(solution)/shard_map/ppermute | solution.py:37
  12.8 0.0 collective-permute-done.3.refs_0_.refs_4_
  12.8 0.0 collective-permute-done.4.refs_1_.refs_3_
  12.8 0.2 %boundary_y.1 = (f32[6,20,32,128]{3,2,1,0:T(8,128)S(1)}, f32[2,5,16,128]{3,2,1,0:T(8,128)S(1)}) custom-call(f32[2,5,16,128]{3,2,1,0:T(8,128)S(1)} %collective-permute-done.3.refs_0_.refs_4_, f32[2,5,16,128]{3,2,1,0:T(8,128)S(1)} %collective-permute-done.4.refs_1_.refs_3_, ...), custom_call_target="tpu_custom_call", output_to_operand_aliasing={{0}: (4, {})} | custom-call | flops 32768 | bytes 163840 | tf_op jit(solution)/shard_map/boundary_y/pallas_call | solution.py:779
  13.0 0.6 %collective-permute-start.5 = (f32[2,5,16,128]{3,2,1,0:T(8,128)S(1)}, f32[2,5,16,128]{3,2,1,0:T(8,128)S(1)}, u32[]{:S(2)}, u32[]{:S(2)}) collective-permute-start(f32[2,5,16,128]{3,2,1,0:T(8,128)S(1)} %get-tuple-element.43), channel_id=1, source_target_pairs={{0,8},{8,0},{1,9},{9,1},{2,10},{10,2},{3,11},{11,3},{4,12},{12,4},... | collective-permute-start | bytes 245768 | tf_op jit(solution)/shard_map/ppermute | solution.py:37
  14.9 1.4 %strain.1 = (f32[12,16,16,128]{3,2,1,0:T(8,128)S(1)}, f32[8,16,128]{2,1,0:T(8,128)S(1)}, f32[8,16,128]{2,1,0:T(8,128)S(1)}, f32[6,20,32,128]{3,2,1,0:T(8,128)S(1...) custom-call(f32[2,5,16,128]{3,2,1,0:T(8,128)S(1)} %collective-permut, ...), custom_call_target="tpu_custom_call", output_to_operand_aliasing={{3}: (8, {})} | custom-call | flops 6553600 | bytes 2359296 | tf_op jit(solution)/shard_map/strain/pallas_call | solution.py:803
  16.4 2.1 %collective-permute-start.6 = (f32[8,16,128]{2,1,0:T(8,128)S(1)}, f32[8,16,128]{2,1,0:T(8,128)S(1)}, u32[]{:S(2)}, u32[]{:S(2)}) collective-permute-start(f32[8,16,128]{2,1,0:T(8,128)S(1)} %get-tuple-element.52.refs_12_), channel_id=1, source_target_pairs={{0,16},{16,0},{1,17},{17,1},{2,18},{18,2},{3,19},{19,3},{4,20},{20... | collective-permute-start | bytes 196616 | tf_op jit(solution)/shard_map/ppermute | solution.py:816
  18.4 0.1 collective-permute-start.7
  18.5 0.8 %collective-permute-done.6.refs_14_ = f32[8,16,128]{2,1,0:T(8,128)S(1)} collective-permute-done((f32[8,16,128]{2,1,0:T(8,128)S(1)}, f32[8,16,128]{2,1,0:T(8,128)S(1)}, u32[]{:S(2)}, u32[]{:S(2)}) %collective-permute-start.6) | collective-permute-done | bytes 65568 | tf_op jit(solution)/shard_map/ppermute | solution.py:816
  19.3 0.4 %collective-permute-done.7.refs_15_ = f32[8,16,128]{2,1,0:T(8,128)S(1)} collective-permute-done((f32[8,16,128]{2,1,0:T(8,128)S(1)}, f32[8,16,128]{2,1,0:T(8,128)S(1)}, u32[]{:S(2)}, u32[]{:S(2)}) %collective-permute-start.7) | collective-permute-done | bytes 65568 | tf_op jit(solution)/shard_map/ppermute | solution.py:816
  19.7 0.0 collective-permute-done.1.refs_0_
  19.7 0.0 collective-permute-done.2.refs_1_
  19.7 0.0 collective-permute-done.5.refs_2_
  19.7 0.4 %gradient.1 = (f32[12,16,16,128]{3,2,1,0:T(8,128)S(1)}, f32[2,16,16,128]{3,2,1,0:T(8,128)S(1)}, f32[16,16,128]{2,1,0:T(8,128)S(1)}) custom-call(f32[2,5,16,128]{3,2,1,0:T(8,128)S(1)} %collective-permute-done.1.refs_0_, f32[2,5,16,128]{3,2,1,0:T(8,128)S(1)} %collective-permute-done.2.refs_1_, ...), custom_call_target="tpu_custom_call", output_to_operand_aliasing={{0}: (16, {})} | custom-call | flops 983040 | bytes 262144 | tf_op jit(solution)/shard_map/gradient/pallas_call | solution.py:819
  20.1 0.2 collective-permute-start.8
  20.3 1.2 %outputs.1 = (f32[9,16,16,128]{3,2,1,0:T(8,128)}, f32[9,16,16,128]{3,2,1,0:T(8,128)}, f32[3,16,16,128]{3,2,1,0:T(8,128)}) custom-call(s32[1]{0:T(128)S(6)} %copy.26.refs_3_.source_cell, f32[1]{0:T(128)S(6)} %copy.27.refs_4_.source_amp, f32[12,16,16,128]{3,2,1,0:T(8,128)S(1)} %get-tuple-element.55.strain, ...), custom_call_target="tpu_custom_call", output_to_operand_aliasing={{0}: (7, {}), {1}: (8, {})} | custom-call | flops 1966080 | bytes 2359296 | tf_op jit(solution)/shard_map/outputs/pallas_call | solution.py:843
  21.6 0.1 collective-permute-done.8.other
  21.7 0.7 %sum.1 = f32[3,16,16,128]{3,2,1,0:T(8,128)} custom-call(f32[2,16,16,128]{3,2,1,0:T(8,128)S(1)} %get-tuple-element.61.mine, f32[2,16,16,128]{3,2,1,0:T(8,128)S(1)} %collective-permute-done.8.other, f32[3,16,16,128]{3,2,1,0:T(8,128)} %get-tuple-element.62._), custom_call_target="tpu_custom_call", output_to_operand_aliasing={{}: (2, {})} | custom-call | flops 65536 | bytes 786432 | tf_op jit(solution)/shard_map/sum/pallas_call | solution.py:863
Async XLA Ops:
  0.6 2.5 %copy-start.1 = (f32[1,9,16,16,128]{4,3,2,1,0:T(8,128)S(1)}, f32[1,9,16,16,128]{4,3,2,1,0:T(8,128)}, u32[]{:S(2)}) copy-start(f32[1,9,16,16,128]{4,3,2,1,0:T(8,128)} %param.10) | copy-start | bytes 3538948
  0.6 2.5 %copy-start = (f32[1,9,16,16,128]{4,3,2,1,0:T(8,128)S(1)}, f32[1,9,16,16,128]{4,3,2,1,0:T(8,128)}, u32[]{:S(2)}) copy-start(f32[1,9,16,16,128]{4,3,2,1,0:T(8,128)} %param.9) | copy-start | bytes 3538948
  1.8 5.9 %copy-start.2 = (s32[1,256]{1,0:T(1,128)S(1)}, s32[1,256]{1,0:T(1,128)}, u32[]{:S(2)}) copy-start(s32[1,256]{1,0:T(1,128)} %receiver_cell.1) | copy-start | bytes 3076
  1.8 5.9 %copy-start.3 = (f32[1,256]{1,0:T(1,128)S(1)}, f32[1,256]{1,0:T(1,128)}, u32[]{:S(2)}) copy-start(f32[1,256]{1,0:T(1,128)} %residual_amp.1) | copy-start | bytes 3076
  1.8 7.4 %collective-permute-start = (f32[2,5,16,128]{3,2,1,0:T(8,128)S(1)}, f32[2,5,16,128]{3,2,1,0:T(8,128)S(1)}, u32[]{:S(2)}, u32[]{:S(2)}) collective-permute-start(f32[2,5,16,128]{3,2,1,0:T(8,128)S(1)} %get-tuple-element.33), channel_id=1, source_target_pairs={{0,8},{8,0},{1,9},{9,1},{2,10},{10,2},{3,11},{11,3},{4,12},{12,4},... | collective-permute-start | bytes 245768 | tf_op jit(solution)/shard_map/ppermute | solution.py:37
  3.2 9.6 %collective-permute-start.3 = (f32[2,5,16,128]{3,2,1,0:T(8,128)S(1)}, f32[2,5,16,128]{3,2,1,0:T(8,128)S(1)}, u32[]{:S(2)}, u32[]{:S(2)}) collective-permute-start(f32[2,5,16,128]{3,2,1,0:T(8,128)S(1)} %get-tuple-element.40), channel_id=1, source_target_pairs={{1,2},{3,4},{5,6},{2,1},{4,3},{6,5},{9,10},{11,12},{13,14},{10,9},... | collective-permute-start | bytes 245768 | tf_op jit(solution)/shard_map/ppermute | solution.py:37
  6.2 6.5 %collective-permute-start.4 = (f32[2,5,16,128]{3,2,1,0:T(8,128)S(1)}, f32[2,5,16,128]{3,2,1,0:T(8,128)S(1)}, u32[]{:S(2)}, u32[]{:S(2)}) collective-permute-start(f32[2,5,16,128]{3,2,1,0:T(8,128)S(1)} %get-tuple-element.41), channel_id=1, source_target_pairs={{0,1},{2,3},{4,5},{6,7},{1,0},{3,2},{5,4},{7,6},{8,9},{10,11},{12,... | collective-permute-start | bytes 245768 | tf_op jit(solution)/shard_map/ppermute | solution.py:37
  9.4 10.3 %collective-permute-start.1 = (f32[2,5,16,128]{3,2,1,0:T(8,128)S(1)}, f32[2,5,16,128]{3,2,1,0:T(8,128)S(1)}, u32[]{:S(2)}, u32[]{:S(2)}) collective-permute-start(f32[2,5,16,128]{3,2,1,0:T(8,128)S(1)} %get-tuple-element.38), channel_id=1, source_target_pairs={{0,1},{2,3},{4,5},{6,7},{1,0},{3,2},{5,4},{7,6},{8,9},{10,11},{12,... | collective-permute-start | bytes 245768 | tf_op jit(solution)/shard_map/ppermute | solution.py:37
  9.6 10.1 %collective-permute-start.2 = (f32[2,5,16,128]{3,2,1,0:T(8,128)S(1)}, f32[2,5,16,128]{3,2,1,0:T(8,128)S(1)}, u32[]{:S(2)}, u32[]{:S(2)}) collective-permute-start(f32[2,5,16,128]{3,2,1,0:T(8,128)S(1)} %get-tuple-element.39), channel_id=1, source_target_pairs={{1,2},{3,4},{5,6},{2,1},{4,3},{6,5},{9,10},{11,12},{13,14},{10,9},... | collective-permute-start | bytes 245768 | tf_op jit(solution)/shard_map/ppermute | solution.py:37
  13.0 6.7 %collective-permute-start.5 = (f32[2,5,16,128]{3,2,1,0:T(8,128)S(1)}, f32[2,5,16,128]{3,2,1,0:T(8,128)S(1)}, u32[]{:S(2)}, u32[]{:S(2)}) collective-permute-start(f32[2,5,16,128]{3,2,1,0:T(8,128)S(1)} %get-tuple-element.43), channel_id=1, source_target_pairs={{0,8},{8,0},{1,9},{9,1},{2,10},{10,2},{3,11},{11,3},{4,12},{12,4},... | collective-permute-start | bytes 245768 | tf_op jit(solution)/shard_map/ppermute | solution.py:37
  16.4 3.0 %collective-permute-start.6 = (f32[8,16,128]{2,1,0:T(8,128)S(1)}, f32[8,16,128]{2,1,0:T(8,128)S(1)}, u32[]{:S(2)}, u32[]{:S(2)}) collective-permute-start(f32[8,16,128]{2,1,0:T(8,128)S(1)} %get-tuple-element.52.refs_12_), channel_id=1, source_target_pairs={{0,16},{16,0},{1,17},{17,1},{2,18},{18,2},{3,19},{19,3},{4,20},{20... | collective-permute-start | bytes 196616 | tf_op jit(solution)/shard_map/ppermute | solution.py:816
  18.4 1.3 %collective-permute-start.7 = (f32[8,16,128]{2,1,0:T(8,128)S(1)}, f32[8,16,128]{2,1,0:T(8,128)S(1)}, u32[]{:S(2)}, u32[]{:S(2)}) collective-permute-start(f32[8,16,128]{2,1,0:T(8,128)S(1)} %get-tuple-element.53.refs_13_), channel_id=1, source_target_pairs={{0,16},{16,0},{1,17},{17,1},{2,18},{18,2},{3,19},{19,3},{4,20},{20... | collective-permute-start | bytes 196616 | tf_op jit(solution)/shard_map/ppermute | solution.py:816
  20.1 1.6 %collective-permute-start.8 = (f32[2,16,16,128]{3,2,1,0:T(8,128)S(1)}, f32[2,16,16,128]{3,2,1,0:T(8,128)S(1)}, u32[]{:S(2)}, u32[]{:S(2)}) collective-permute-start(f32[2,16,16,128]{3,2,1,0:T(8,128)S(1)} %get-tuple-element.61.mine), channel_id=1, source_target_pairs={{0,16},{16,0},{1,17},{17,1},{2,18},{18,2},{3,19},{19,3},{4,20},{20... | collective-permute-start | bytes 786440 | tf_op jit(solution)/shard_map/ppermute | solution.py:839

commit v12 on v10

--- a/solution.py
+++ b/solution.py
@@ -67,41 +67,50 @@
 
 
 def early_pack_kernel(links, forward, adjoint, density, *refs):
-    sends, (density_now, sems) = refs[: len(links)], refs[len(links) :]
-    tile_x = forward.shape[1]
-    whole = pltpu.make_async_copy(density, density_now, sems.at[0])
-    whole.start()
+    sends, (density_rows, sems) = refs[: len(links)], refs[len(links) :]
+    tile = forward.shape[1:3]
     waits = []
+    for row in range(2):
+        copy = pltpu.make_async_copy(
+            density.at[:, row, :], density_rows.at[row], sems.at[2 * SLOTS * len(links) + row]
+        )
+        copy.start()
+        waits.append(copy)
+
+    def layer(ref, dim, index):
+        return ref.at[index] if dim == 0 else ref.at[:, index, :]
+
     for at, (link, send) in enumerate(zip(links, sends)):
-
-        def sources(plan, lower, wave):
-            fields = (forward, adjoint)[wave]
-            found = [fields.at[3 + part, index % tile_x] for part, index in plan]
-            return found if lower else found + [density.at[wave]]
+        dim = link[1]
+
+        def semaphore(wave, slot):
+            return sems.at[(2 * at + wave) * SLOTS + slot]
 
         def start(plan, lower):
-            for wave in range(2):
-                for slot, source in enumerate(sources(plan, lower, wave)):
+            for wave, fields in enumerate((forward, adjoint)):
+                sources = [
+                    layer(fields.at[3 + part], dim, index % tile[dim]) for part, index in plan
+                ]
+                if not lower:
+                    sources.append(layer(density, dim, wave))
+                for slot, source in enumerate(sources):
                     pltpu.make_async_copy(
-                        source, send.at[wave, slot], sems.at[1 + (2 * at + wave) * SLOTS + slot]
+                        source, send.at[wave, slot], semaphore(wave, slot)
                     ).start()
 
-        by_role(link, start, *stress_plan(link[1]))
+        by_role(link, start, *stress_plan(dim))
         for wave in range(2):
             for slot in range(SLOTS):
                 waits.append(
                     pltpu.make_async_copy(
-                        density.at[0],
-                        send.at[wave, slot],
-                        sems.at[1 + (2 * at + wave) * SLOTS + slot],
+                        layer(density, dim, 0), send.at[wave, slot], semaphore(wave, slot)
                     )
                 )
     for copy in waits:
         copy.wait()
-    whole.wait()
-
-
-def pack_kernel(links, forward, adjoint, density, *sends):
+
+
+def pack_kernel(links, forward, adjoint, density_rows, *sends):
     for link, send in zip(links, sends):
         dim = link[1]
 
@@ -110,7 +119,7 @@
                 for slot, (part, index) in enumerate(plan):
                     send[wave, slot] = face(fields, 3 + part, dim, index, False)[...]
                 if not lower:
-                    send[wave, SPARE] = light_face(density, dim, wave)
+                    send[wave, SPARE] = density_rows[wave]
 
         by_role(link, put, *stress_plan(dim))
 
@@ -233,11 +242,11 @@
     width_y,
     lame,
     shear,
+    density,
     receiver_cell,
     residual_amp,
     forward,
     adjoint,
-    density,
     stress,
     velocity,
     accel,
@@ -249,12 +258,14 @@
     gained,
     lame_now,
     shear_now,
+    density_now,
     sems,
 ):
     tile_x, tile_y, depth = density.shape
     copies = [
         pltpu.make_async_copy(lame, lame_now, sems.at[0]),
         pltpu.make_async_copy(shear, shear_now, sems.at[1]),
+        pltpu.make_async_copy(density, density_now, sems.at[2]),
     ]
     for copy in copies:
         copy.start()
@@ -280,7 +291,7 @@
                 )
         return carry
 
-    lax.fori_loop(0, tile_x, fill, 0, unroll=4)
+    lax.fori_loop(0, tile_x, fill, 0, unroll=8)
 
     def layer(x, carry):
         for wave in range(2):
@@ -300,12 +311,12 @@
                 gained[3 * wave + part, x] = value
         return carry
 
-    lax.fori_loop(0, tile_x, layer, 0, unroll=4)
+    lax.fori_loop(0, tile_x, layer, 0, unroll=8)
     for copy in copies:
         copy.wait()
 
     def finish(x, carry):
-        light = 1.0 / density[x]
+        light = 1.0 / density_now[x]
         buoyancy[x] = light
         scaled_lame[x] = time_step * lame_now[x]
         scaled_shear[x] = time_step * shear_now[x]
@@ -319,7 +330,7 @@
                 )
         return carry
 
-    lax.fori_loop(0, tile_x, finish, 0, unroll=4)
+    lax.fori_loop(0, tile_x, finish, 0, unroll=8)
 
 
 def stress_halo_terms(links, received, rim_added, waves, add):
@@ -671,12 +682,12 @@
     rows = tile_x * tile_y + 3 * (tile_x + tile_y)
     source = source_cell, source_amp
 
-    *sends, density_now = pl.pallas_call(
+    *sends, density_rows = pl.pallas_call(
         functools.partial(early_pack_kernel, links_x),
-        out_shape=shapes(links_x) + [tile()],
+        out_shape=shapes(links_x) + [pltpu.VMEM((2, tile_x, depth), jnp.float32)],
         in_specs=[hbm] * 3,
         out_specs=[vmem] * (count_x + 1),
-        scratch_shapes=[pltpu.SemaphoreType.DMA((1 + 2 * SLOTS * count_x,))],
+        scratch_shapes=[pltpu.SemaphoreType.DMA((2 + 2 * SLOTS * count_x,))],
         compiler_params=params,
         cost_estimate=cost(0, 4 * cells),
         name="early_pack",
@@ -692,7 +703,7 @@
             compiler_params=params,
             cost_estimate=cost(0, 2 * 2 * SLOTS * count_y * tile_x * depth * 4),
             name="pack",
-        )(forward, adjoint, density_now)
+        )(forward, adjoint, density_rows)
         halos_y = exchange(links_y, sends)
 
     stress, velocity, accel, rim_added, buoyancy, scaled_lame, scaled_shear = pl.pallas_call(
@@ -706,26 +717,25 @@
             tile(),
             tile(),
         ],
-        in_specs=[hbm] * 2 + [vmem] * 5,
+        in_specs=[hbm] * 3 + [vmem] * 4,
         out_specs=[vmem] * 7,
         scratch_shapes=[
             pltpu.VMEM((rows, depth), jnp.float32),
             tile(6),
             tile(),
             tile(),
-            pltpu.SemaphoreType.DMA((2,)),
+            tile(),
+            pltpu.SemaphoreType.DMA((3,)),
         ],
         compiler_params=params,
         cost_estimate=cost(200 * cells, 18 * 4 * cells),
         name="velocity",
     )(
-        in_hbm(lame_lambda),
-        in_hbm(shear_modulus),
+        *(in_hbm(x) for x in (lame_lambda, shear_modulus, density)),
         receiver_cell,
         residual_amp,
         forward,
         adjoint,
-        density_now,
     )
 
     def boundary(links, send_links, halos, velocity, name):

time: 22.5 us -> 22.3 us (level)
  Pallas kernels: 6.93 us -> 6.69 us
where the time goes in v12:
time: 22.3 us; the launch traced here: 22.1 us
  starting transfers between devices  13 us (58%)
  Pallas kernels  6.69 us (30%)
  between operations  2.08 us (9%)
  waiting for transfers between devices  0.3 us (1%)
    ppermute x6, starting transfers between devices, swap(): return lax.ppermute(value, axis, pairs + [(j, i) for i, j in pairs])  9.69 us
    ppermute x1, starting transfers between devices, body(): other = lax.ppermute(gradient, 'shot', [(0, 1), (1, 0)])  3.29 us
    pallas_call x1, Pallas kernels, body(): pl.pallas_call(functools.partial(velocity_kernel, width_y), out_shape=[pa...  1.43 us
    pallas_call x1, Pallas kernels, body(): pl.pallas_call(functools.partial(output_kernel, chunk, width_y), out_shap...  1.23 us
    pallas_call x1, Pallas kernels, body(): pl.pallas_call(functools.partial(strain_kernel, links, width_y), out_shap...  1.23 us
    pallas_call x1, Pallas kernels, body(): pl.pallas_call(functools.partial(early_pack_kernel, links_x), out_shape=s...  1.07 us
    pallas_call x1, Pallas kernels, body(): pl.pallas_call(sum_kernel, out_shape=jax.ShapeDtypeStruct((3, tile_x, til...  0.78 us
    pallas_call x1, Pallas kernels, body(): pl.pallas_call(functools.partial(gradient_kernel, later_links, width_y),...  0.48 us
  transfers between devices with their start and end apart: 7, of which 2 were waited for; matrix products, arithmetic and copies ran while one was open for 0% of the time, Pallas kernels for 20%

profile of v12, /device:TPU:9, one launch (start us, length us, event | category | flops | bytes accessed | tf_op | source)
XLA Modules:
  0.0 22.1 jit_solution(10160414521425515895)
XLA Ops:
  0.6 0.0 copy-start.1
  0.6 0.0 copy-start
  0.6 1.1 %early_pack.1 = (f32[2,5,16,128]{3,2,1,0:T(8,128)S(1)}, f32[2,16,128]{2,1,0:T(8,128)S(1)}) custom-call(f32[9,16,16,128]{3,2,1,0:T(8,128)} %bitcast.4, f32[9,16,16,128]{3,2,1,0:T(8,128)} %bitcast.7, f32[16,16,128]{2,1,0:T(8,128)} %density.3), custom_call_target="tpu_custom_call" | custom-call | bytes 131072 | tf_op jit(solution)/shard_map/early_pack/pallas_call | solution.py:685
  1.7 0.0 copy-start.2
  1.7 0.0 copy-start.3
  1.8 1.3 %collective-permute-start = (f32[2,5,16,128]{3,2,1,0:T(8,128)S(1)}, f32[2,5,16,128]{3,2,1,0:T(8,128)S(1)}, u32[]{:S(2)}, u32[]{:S(2)}) collective-permute-start(f32[2,5,16,128]{3,2,1,0:T(8,128)S(1)} %get-tuple-element.27), channel_id=1, source_target_pairs={{0,8},{8,0},{1,9},{9,1},{2,10},{10,2},{3,11},{11,3},{4,12},{12,4},... | collective-permute-start | bytes 245768 | tf_op jit(solution)/shard_map/ppermute | solution.py:37
  3.1 0.0 copy-done.1
  3.1 0.0 copy-done
  3.1 0.1 pack.1
  3.1 3.0 %collective-permute-start.3 = (f32[2,5,16,128]{3,2,1,0:T(8,128)S(1)}, f32[2,5,16,128]{3,2,1,0:T(8,128)S(1)}, u32[]{:S(2)}, u32[]{:S(2)}) collective-permute-start(f32[2,5,16,128]{3,2,1,0:T(8,128)S(1)} %get-tuple-element.34), channel_id=1, source_target_pairs={{1,2},{3,4},{5,6},{2,1},{4,3},{6,5},{9,10},{11,12},{13,14},{10,9},... | collective-permute-start | bytes 245768 | tf_op jit(solution)/shard_map/ppermute | solution.py:37
  6.1 1.4 %collective-permute-start.4 = (f32[2,5,16,128]{3,2,1,0:T(8,128)S(1)}, f32[2,5,16,128]{3,2,1,0:T(8,128)S(1)}, u32[]{:S(2)}, u32[]{:S(2)}) collective-permute-start(f32[2,5,16,128]{3,2,1,0:T(8,128)S(1)} %get-tuple-element.35), channel_id=1, source_target_pairs={{0,1},{2,3},{4,5},{6,7},{1,0},{3,2},{5,4},{7,6},{8,9},{10,11},{12,... | collective-permute-start | bytes 245768 | tf_op jit(solution)/shard_map/ppermute | solution.py:37
  7.6 0.0 copy-done.2
  7.6 0.0 copy-done.3
  7.6 1.4 %velocity.1 = (f32[12,20,32,128]{3,2,1,0:T(8,128)S(1)}, f32[6,20,32,128]{3,2,1,0:T(8,128)S(1)}, f32[3,16,16,128]{3,2,1,0:T(8,128)S(1)}, f32[2,3,16,128]{3,2,1,0:...) custom-call(f32[16,16,128]{2,1,0:T(8,128)} %lame.1, ...), custom_call_target="tpu_custom_call" | custom-call | flops 6553600 | bytes 2359296 | tf_op jit(solution)/shard_map/velocity/pallas_call | solution.py:709
  9.0 0.0 collective-permute-done.refs_0_.refs_2_.refs_5_
  9.0 0.2 boundary_x.1
  9.2 0.2 collective-permute-start.1
  9.4 3.2 %collective-permute-start.2 = (f32[2,5,16,128]{3,2,1,0:T(8,128)S(1)}, f32[2,5,16,128]{3,2,1,0:T(8,128)S(1)}, u32[]{:S(2)}, u32[]{:S(2)}) collective-permute-start(f32[2,5,16,128]{3,2,1,0:T(8,128)S(1)} %get-tuple-element.32), channel_id=1, source_target_pairs={{1,2},{3,4},{5,6},{2,1},{4,3},{6,5},{9,10},{11,12},{13,14},{10,9},... | collective-permute-start | bytes 245768 | tf_op jit(solution)/shard_map/ppermute | solution.py:37
  12.5 0.0 collective-permute-done.3.refs_0_.refs_4_
  12.5 0.0 collective-permute-done.4.refs_1_.refs_3_
  12.6 0.2 %boundary_y.1 = (f32[6,20,32,128]{3,2,1,0:T(8,128)S(1)}, f32[2,5,16,128]{3,2,1,0:T(8,128)S(1)}) custom-call(f32[2,5,16,128]{3,2,1,0:T(8,128)S(1)} %collective-permute-done.3.refs_0_.refs_4_, f32[2,5,16,128]{3,2,1,0:T(8,128)S(1)} %collective-permute-done.4.refs_1_.refs_3_, ...), custom_call_target="tpu_custom_call", output_to_operand_aliasing={{0}: (4, {})} | custom-call | flops 32768 | bytes 163840 | tf_op jit(solution)/shard_map/boundary_y/pallas_call | solution.py:742
  12.8 0.6 %collective-permute-start.5 = (f32[2,5,16,128]{3,2,1,0:T(8,128)S(1)}, f32[2,5,16,128]{3,2,1,0:T(8,128)S(1)}, u32[]{:S(2)}, u32[]{:S(2)}) collective-permute-start(f32[2,5,16,128]{3,2,1,0:T(8,128)S(1)} %get-tuple-element.37), channel_id=1, source_target_pairs={{0,8},{8,0},{1,9},{9,1},{2,10},{10,2},{3,11},{11,3},{4,12},{12,4},... | collective-permute-start | bytes 245768 | tf_op jit(solution)/shard_map/ppermute | solution.py:37
  14.7 1.2 %strain.1 = (f32[12,16,16,128]{3,2,1,0:T(8,128)S(1)}, f32[3,16,16,128]{3,2,1,0:T(8,128)S(1)}, f32[6,20,32,128]{3,2,1,0:T(8,128)S(1)}, f32[9,16,16,128]{3,2,1,0:T(8,128)}, f32[9,16,16,128]{3,2,1,0:T(8,128)}) custom-call(f32[2,5,16,128]{3,2,1,0:T(8,128)S(1)} %collective-permute-done.3.refs_0_.refs_4_, ...), custom_call_target="tpu_custom_call", output_to_operand_aliasing={{2}: (8, {})} | custom-call | flops 6553600 | bytes 2359296 | tf_op jit(solution)/shard_map/strain/pallas_call | solution.py:763
  16.0 0.0 collective-permute-done.1.refs_0_
  16.0 0.0 collective-permute-done.2.refs_1_
  16.0 0.2 collective-permute-done.5.refs_2_
  16.2 0.5 %gradient.1 = (f32[12,16,16,128]{3,2,1,0:T(8,128)S(1)}, f32[3,16,16,128]{3,2,1,0:T(8,128)S(1)}) custom-call(f32[2,5,16,128]{3,2,1,0:T(8,128)S(1)} %collective-permute-done.1.refs_0_, f32[2,5,16,128]{3,2,1,0:T(8,128)S(1)} %collective-permute-done.2.refs_1_, ...), custom_call_target="tpu_custom_call", output_to_operand_aliasing={{0}: (11, {}), {1}: (12, {})} | custom-call | flops 983040 | bytes 262144 | tf_op jit(solution)/shard_map/gradient/pallas_call | solution.py:775
  16.6 3.3 %collective-permute-start.6 = (f32[3,16,16,128]{3,2,1,0:T(8,128)S(1)}, f32[3,16,16,128]{3,2,1,0:T(8,128)S(1)}, u32[]{:S(2)}, u32[]{:S(2)}) collective-permute-start(f32[3,16,16,128]{3,2,1,0:T(8,128)S(1)} %get-tuple-element.50.mine), channel_id=1, source_target_pairs={{0,16},{16,0},{1,17},{17,1},{2,18},{18,2},{3,19},{19,3},{4,20},{20... | collective-permute-start | bytes 1179656 | tf_op jit(solution)/shard_map/ppermute | solution.py:785
  19.9 1.2 %outputs.1 = (f32[9,16,16,128]{3,2,1,0:T(8,128)}, f32[9,16,16,128]{3,2,1,0:T(8,128)}) custom-call(s32[1]{0:T(128)S(6)} %copy.26.refs_3_.refs_6_.source_cell, f32[1]{0:T(128)S(6)} %copy.27.refs_4_.refs_7_.source_amp, f32[12,16,16,128]{3,2,1,0:T(8,128)S(1)} %get-tuple-element.45.strain, ...), custom_call_target="tpu_custom_call", output_to_operand_aliasing={{0}: (6, {}), {1}: (7, {})} | custom-call | flops 1966080 | bytes 2359296 | tf_op jit(solution)/shard_map/outputs/pallas_call | solution.py:788
  21.2 0.1 collective-permute-done.6.other
  21.3 0.8 %sum.1 = f32[3,16,16,128]{3,2,1,0:T(8,128)} custom-call(f32[3,16,16,128]{3,2,1,0:T(8,128)S(1)} %get-tuple-element.50.mine, f32[3,16,16,128]{3,2,1,0:T(8,128)S(1)} %collective-permute-done.6.other), custom_call_target="tpu_custom_call" | custom-call | flops 98304 | bytes 1179648 | tf_op jit(solution)/shard_map/sum/pallas_call | solution.py:799
Async XLA Ops:
  0.6 2.4 %copy-start.1 = (f32[1,9,16,16,128]{4,3,2,1,0:T(8,128)S(1)}, f32[1,9,16,16,128]{4,3,2,1,0:T(8,128)}, u32[]{:S(2)}) copy-start(f32[1,9,16,16,128]{4,3,2,1,0:T(8,128)} %param.10) | copy-start | bytes 3538948
  0.6 2.4 %copy-start = (f32[1,9,16,16,128]{4,3,2,1,0:T(8,128)S(1)}, f32[1,9,16,16,128]{4,3,2,1,0:T(8,128)}, u32[]{:S(2)}) copy-start(f32[1,9,16,16,128]{4,3,2,1,0:T(8,128)} %param.9) | copy-start | bytes 3538948
  1.7 5.9 %copy-start.2 = (s32[1,256]{1,0:T(1,128)S(1)}, s32[1,256]{1,0:T(1,128)}, u32[]{:S(2)}) copy-start(s32[1,256]{1,0:T(1,128)} %receiver_cell.1) | copy-start | bytes 3076
  1.7 5.9 %copy-start.3 = (f32[1,256]{1,0:T(1,128)S(1)}, f32[1,256]{1,0:T(1,128)}, u32[]{:S(2)}) copy-start(f32[1,256]{1,0:T(1,128)} %residual_amp.1) | copy-start | bytes 3076
  1.8 7.3 %collective-permute-start = (f32[2,5,16,128]{3,2,1,0:T(8,128)S(1)}, f32[2,5,16,128]{3,2,1,0:T(8,128)S(1)}, u32[]{:S(2)}, u32[]{:S(2)}) collective-permute-start(f32[2,5,16,128]{3,2,1,0:T(8,128)S(1)} %get-tuple-element.27), channel_id=1, source_target_pairs={{0,8},{8,0},{1,9},{9,1},{2,10},{10,2},{3,11},{11,3},{4,12},{12,4},... | collective-permute-start | bytes 245768 | tf_op jit(solution)/shard_map/ppermute | solution.py:37
  3.1 9.4 %collective-permute-start.3 = (f32[2,5,16,128]{3,2,1,0:T(8,128)S(1)}, f32[2,5,16,128]{3,2,1,0:T(8,128)S(1)}, u32[]{:S(2)}, u32[]{:S(2)}) collective-permute-start(f32[2,5,16,128]{3,2,1,0:T(8,128)S(1)} %get-tuple-element.34), channel_id=1, source_target_pairs={{1,2},{3,4},{5,6},{2,1},{4,3},{6,5},{9,10},{11,12},{13,14},{10,9},... | collective-permute-start | bytes 245768 | tf_op jit(solution)/shard_map/ppermute | solution.py:37
  6.1 6.4 %collective-permute-start.4 = (f32[2,5,16,128]{3,2,1,0:T(8,128)S(1)}, f32[2,5,16,128]{3,2,1,0:T(8,128)S(1)}, u32[]{:S(2)}, u32[]{:S(2)}) collective-permute-start(f32[2,5,16,128]{3,2,1,0:T(8,128)S(1)} %get-tuple-element.35), channel_id=1, source_target_pairs={{0,1},{2,3},{4,5},{6,7},{1,0},{3,2},{5,4},{7,6},{8,9},{10,11},{12,... | collective-permute-start | bytes 245768 | tf_op jit(solution)/shard_map/ppermute | solution.py:37
  9.2 6.7 %collective-permute-start.1 = (f32[2,5,16,128]{3,2,1,0:T(8,128)S(1)}, f32[2,5,16,128]{3,2,1,0:T(8,128)S(1)}, u32[]{:S(2)}, u32[]{:S(2)}) collective-permute-start(f32[2,5,16,128]{3,2,1,0:T(8,128)S(1)} %get-tuple-element.31), channel_id=1, source_target_pairs={{0,1},{2,3},{4,5},{6,7},{1,0},{3,2},{5,4},{7,6},{8,9},{10,11},{12,... | collective-permute-start | bytes 245768 | tf_op jit(solution)/shard_map/ppermute | solution.py:37
  9.4 6.6 %collective-permute-start.2 = (f32[2,5,16,128]{3,2,1,0:T(8,128)S(1)}, f32[2,5,16,128]{3,2,1,0:T(8,128)S(1)}, u32[]{:S(2)}, u32[]{:S(2)}) collective-permute-start(f32[2,5,16,128]{3,2,1,0:T(8,128)S(1)} %get-tuple-element.32), channel_id=1, source_target_pairs={{1,2},{3,4},{5,6},{2,1},{4,3},{6,5},{9,10},{11,12},{13,14},{10,9},... | collective-permute-start | bytes 245768 | tf_op jit(solution)/shard_map/ppermute | solution.py:37
  12.8 3.4 %collective-permute-start.5 = (f32[2,5,16,128]{3,2,1,0:T(8,128)S(1)}, f32[2,5,16,128]{3,2,1,0:T(8,128)S(1)}, u32[]{:S(2)}, u32[]{:S(2)}) collective-permute-start(f32[2,5,16,128]{3,2,1,0:T(8,128)S(1)} %get-tuple-element.37), channel_id=1, source_target_pairs={{0,8},{8,0},{1,9},{9,1},{2,10},{10,2},{3,11},{11,3},{4,12},{12,4},... | collective-permute-start | bytes 245768 | tf_op jit(solution)/shard_map/ppermute | solution.py:37
  16.6 4.6 %collective-permute-start.6 = (f32[3,16,16,128]{3,2,1,0:T(8,128)S(1)}, f32[3,16,16,128]{3,2,1,0:T(8,128)S(1)}, u32[]{:S(2)}, u32[]{:S(2)}) collective-permute-start(f32[3,16,16,128]{3,2,1,0:T(8,128)S(1)} %get-tuple-element.50.mine), channel_id=1, source_target_pairs={{0,16},{16,0},{1,17},{17,1},{2,18},{18,2},{3,19},{19,3},{4,20},{20... | collective-permute-start | bytes 1179656 | tf_op jit(solution)/shard_map/ppermute | solution.py:785

commit v13 on v12

--- a/solution.py
+++ b/solution.py
@@ -380,65 +380,90 @@
     return lax.axis_index("tx") * tile_x, lax.axis_index("ty") * tile_y
 
 
-def velocity_halo_terms(links, received, stresses, stress, source, width_y, add):
+def missing_terms(links, stress, source, width_y, missing):
     cell, amp = source
     layers, rows, depth = stress.shape[1:]
     tile = layers - 2 * LAYERS, rows - 2 * ROWS
     starts = start_of(*tile)
-    for link, halo, stress_halo in zip(links, received, stresses):
+    for link, out in zip(links, missing):
+        dim = link[1]
+        shape = out.shape[2:]
+        cross = starts[1 - dim] + lax.broadcasted_iota(jnp.int32, shape, 0)
+        level = lax.broadcasted_iota(jnp.int32, shape, 1)
+
+        def own(wave, part, index):
+            return face(stress, 6 * wave + STRESS_ALONG[dim][part], dim, index, True)[...]
+
+        def put(slots):
+            for wave in range(2):
+                for slot, (part, layer, terms) in enumerate(slots):
+                    value = terms(wave) if dim == 1 else jnp.zeros(shape, jnp.float32)
+                    if wave == 0:
+                        here = jnp.full(shape, starts[dim] + layer, jnp.int32)
+                        x, y = (here, cross) if dim == 0 else (cross, here)
+                        value += amp * source_gain(
+                            cell, VELOCITY_ALONG[dim][part], x, y, level, width_y
+                        )
+                    out[wave, slot] = value
+
+        def after():
+            count = tile[dim]
+            slots = [(0, count, lambda wave: -far * own(wave, 0, -1))]
+            for part in (1, 2):
+                slots += [
+                    (
+                        part,
+                        count,
+                        lambda wave, part=part: -near * own(wave, part, -1)
+                        - far * own(wave, part, -2),
+                    ),
+                    (part, count + 1, lambda wave, part=part: -far * own(wave, part, -1)),
+                ]
+            put(slots)
+
+        def before():
+            put([
+                (0, -2, lambda wave: far * own(wave, 0, 0)),
+                (0, -1, lambda wave: near * own(wave, 0, 0) + far * own(wave, 0, 1)),
+                (1, -1, lambda wave: far * own(wave, 1, 0)),
+                (2, -1, lambda wave: far * own(wave, 2, 0)),
+            ])
+
+        lower = is_lower(link[0], link[2])
+        pl.when(lower)(after)
+        pl.when(jnp.logical_not(lower))(before)
+
+
+def velocity_halo_terms(links, received, stresses, missing, add):
+    for link, halo, stress_halo, lack in zip(links, received, stresses, missing):
         dim = link[1]
         part_n, part_a, part_b = STRAIN_OF[dim]
-        shape = halo.shape[2:]
-        cross = starts[1 - dim] + lax.broadcasted_iota(jnp.int32, shape, 0)
-        level = lax.broadcasted_iota(jnp.int32, shape, 1)
-
-        def own(wave, part, index):
-            return face(stress, 6 * wave + STRESS_ALONG[dim][part], dim, index, True)[...]
-
-        def whole(wave, slot, part, layer, light, terms):
-            value = halo[wave, slot]
-            if dim == 1:
-                value += time_step * light * terms()
-            if wave == 0:
-                here = jnp.full(shape, starts[dim] + layer, jnp.int32)
-                x, y = (here, cross) if dim == 0 else (cross, here)
-                gain = source_gain(cell, VELOCITY_ALONG[dim][part], x, y, level, width_y)
-                value += time_step * amp * light * gain
-            return value
 
         def after():
-            count = tile[dim]
-            lights = [1.0 / stress_halo[layer, SPARE] for layer in range(2)]
+            lights = [time_step / stress_halo[layer, SPARE] for layer in range(2)]
             for wave in range(2):
-                n = whole(wave, 0, 0, count, lights[0], lambda: -far * own(wave, 0, -1))
-                add(wave, part_n, dim, -1, far * n)
-                for part, name, slot in ((part_a, 1, 1), (part_b, 2, 3)):
-                    inner = whole(
-                        wave, slot, name, count, lights[0],
-                        lambda: -near * own(wave, name, -1) - far * own(wave, name, -2),
-                    )
-                    outer = whole(
-                        wave, slot + 1, name, count + 1, lights[1],
-                        lambda: -far * own(wave, name, -1),
-                    )
+
+                def whole(slot, layer):
+                    return halo[wave, slot] + lights[layer] * lack[wave, slot]
+
+                add(wave, part_n, dim, -1, far * whole(0, 0))
+                for part, slot in ((part_a, 1), (part_b, 3)):
+                    inner, outer = whole(slot, 0), whole(slot + 1, 1)
                     add(wave, part, dim, -1, near * inner + far * outer)
                     add(wave, part, dim, -2, far * inner)
 
         def before():
-            lights = [halo[layer, SPARE] for layer in range(2)]
+            lights = [time_step * halo[layer, SPARE] for layer in range(2)]
             for wave in range(2):
-                outer = whole(wave, 0, 0, -2, lights[1], lambda: far * own(wave, 0, 0))
-                inner = whole(
-                    wave, 1, 0, -1, lights[0],
-                    lambda: near * own(wave, 0, 0) + far * own(wave, 0, 1),
-                )
+
+                def whole(slot, layer):
+                    return halo[wave, slot] + lights[layer] * lack[wave, slot]
+
+                outer, inner = whole(0, 1), whole(1, 0)
                 add(wave, part_n, dim, 0, -near * inner - far * outer)
                 add(wave, part_n, dim, 1, -far * inner)
-                for part, name, slot in ((part_a, 1, 2), (part_b, 2, 3)):
-                    value = whole(
-                        wave, slot, name, -1, lights[0], lambda: far * own(wave, name, 0)
-                    )
-                    add(wave, part, dim, 0, -far * value)
+                add(wave, part_a, dim, 0, -far * whole(2, 0))
+                add(wave, part_b, dim, 0, -far * whole(3, 0))
 
         real = has_peer(link[0], link[2])
         lower = is_lower(link[0], link[2])
@@ -486,8 +511,10 @@
     count = len(links)
     received = refs[:count]
     source_cell, source_amp, rim_added, buoyancy, accel = refs[count : count + 5]
-    strain, gradient, velocity = refs[count + 6 : count + 9]
-    outputs, (accel_now, sems) = refs[count + 9 : count + 11], refs[count + 11 :]
+    stress = refs[count + 6]
+    strain, gradient, velocity = refs[count + 7 : count + 10]
+    outputs, missing = refs[count + 10 : count + 12], refs[count + 12 : 2 * count + 12]
+    accel_now, sems = refs[2 * count + 12 :]
     tile_x, tile_y, depth = buoyancy.shape
     middle = pl.ds(ROWS, tile_y)
     clear_rim(velocity, range(6), range(6))
@@ -545,7 +572,8 @@
         gradient[2, x] = -time_step * total
         return carry
 
-    lax.fori_loop(0, tile_x, layer, 0, unroll=4)
+    lax.fori_loop(0, tile_x, layer, 0, unroll=8)
+    missing_terms(links, stress, (cell, amp), width_y, missing)
     for copy in copies:
         copy.wait()
 
@@ -564,19 +592,17 @@
     return strains, values
 
 
-def gradient_kernel(links, width_y, *refs):
+def gradient_kernel(links, *refs):
     count = len(links)
-    received, stresses = refs[:count], refs[count : 2 * count]
-    source_cell, source_amp, stress, scaled_lame, scaled_shear = refs[2 * count : 2 * count + 5]
-    strain, gradient = refs[2 * count + 7 :]
+    received, stresses, missing = (refs[at : at + count] for at in range(0, 3 * count, count))
+    stress, scaled_lame, scaled_shear, _, _, strain, gradient = refs[3 * count :]
     tile_x, tile_y, _ = scaled_lame.shape
 
     def add(wave, part, dim, index, term):
         target = face(strain, 6 * wave + part, dim, index, False)
         target[...] += term
 
-    source = source_cell[0], source_amp[0]
-    velocity_halo_terms(links, received, stresses, stress, source, width_y, add)
+    velocity_halo_terms(links, received, stresses, missing, add)
 
     def layer(x, carry):
         strains = [strain[part, x] for part in range(6)]
@@ -587,7 +613,7 @@
         gradient[1, x] = -time_step * total
         return carry
 
-    lax.fori_loop(0, tile_x, layer, 0, unroll=4)
+    lax.fori_loop(0, tile_x, layer, 0, unroll=8)
 
 
 def output_kernel(
@@ -622,13 +648,17 @@
         copy.wait()
 
 
-def sum_kernel(mine, other, total, total_now, sems):
+def sum_kernel(chunk, mine, other, total, total_now, sems):
     copies = []
     for part in range(mine.shape[0]):
-        total_now[part] = mine[part] + other[part]
-        copy = pltpu.make_async_copy(total_now.at[part], total.at[part], sems.at[part])
-        copy.start()
-        copies.append(copy)
+        for begin in range(0, mine.shape[1], chunk):
+            layers = pl.ds(begin, chunk)
+            total_now[part, layers] = mine[part, layers] + other[part, layers]
+            copy = pltpu.make_async_copy(
+                total_now.at[part, layers], total.at[part, layers], sems.at[len(copies)]
+            )
+            copy.start()
+            copies.append(copy)
     for copy in copies:
         copy.wait()
 
@@ -760,28 +790,29 @@
     velocity_halos = velocity_halos_y + velocity_halos_x
 
     out_shape = jax.ShapeDtypeStruct(forward.shape, jnp.float32)
-    strain, gradient, _, forward_next, adjoint_next = pl.pallas_call(
+    strain, gradient, _, forward_next, adjoint_next, *missing = pl.pallas_call(
         functools.partial(strain_kernel, links, width_y),
-        out_shape=[tile(12), tile(3), padded(6), out_shape, out_shape],
-        in_specs=[vmem] * count + [smem] * 2 + [vmem] * 4,
-        out_specs=[vmem] * 3 + [hbm] * 2,
+        out_shape=[tile(12), tile(3), padded(6), out_shape, out_shape] + shapes(links),
+        in_specs=[vmem] * count + [smem] * 2 + [vmem] * 5,
+        out_specs=[vmem] * 3 + [hbm] * 2 + [vmem] * count,
         input_output_aliases={count + 5: 2},
         scratch_shapes=[tile(3), pltpu.SemaphoreType.DMA((6,))],
         compiler_params=params,
         cost_estimate=cost(200 * cells, 18 * 4 * cells),
         name="strain",
-    )(*halos, *source, rim_added, buoyancy, accel, velocity)
+    )(*halos, *source, rim_added, buoyancy, accel, velocity, stress)
+    missing = missing[:count_y][::-1] + missing[count_y:]
 
     strain, gradient = pl.pallas_call(
-        functools.partial(gradient_kernel, later_links, width_y),
+        functools.partial(gradient_kernel, later_links),
         out_shape=[tile(12), tile(3)],
-        in_specs=[vmem] * (2 * count) + [smem] * 2 + [vmem] * 5,
+        in_specs=[vmem] * (3 * count + 5),
         out_specs=[vmem] * 2,
-        input_output_aliases={2 * count + 5: 0, 2 * count + 6: 1},
+        input_output_aliases={3 * count + 3: 0, 3 * count + 4: 1},
         compiler_params=params,
         cost_estimate=cost(30 * cells, 2 * 4 * cells),
         name="gradient",
-    )(*velocity_halos, *later_halos, *source, stress, scaled_lame, scaled_shear, strain, gradient)
+    )(*velocity_halos, *later_halos, *missing, stress, scaled_lame, scaled_shear, strain, gradient)
     other = lax.ppermute(gradient, "shot", [(0, 1), (1, 0)])
 
     chunk = 4 if tile_x % 4 == 0 else 1
@@ -797,11 +828,11 @@
         name="outputs",
     )(*source, strain, stress, scaled_lame, scaled_shear, forward_next, adjoint_next)
     total = pl.pallas_call(
-        sum_kernel,
+        functools.partial(sum_kernel, chunk),
         out_shape=jax.ShapeDtypeStruct((3, tile_x, tile_y, depth), jnp.float32),
         in_specs=[vmem] * 2,
         out_specs=hbm,
-        scratch_shapes=[tile(3), pltpu.SemaphoreType.DMA((3,))],
+        scratch_shapes=[tile(3), pltpu.SemaphoreType.DMA((3 * tile_x // chunk,))],
         compiler_params=params,
         cost_estimate=cost(3 * cells, 9 * 4 * cells),
         name="sum",

time: 22.3 us -> 22.3 us (level)
  no operation moved by 1% of the time
where the time goes in v13:
time: 22.3 us; the launch traced here: 22 us
  starting transfers between devices  13 us (58%)
  Pallas kernels  6.66 us (30%)
  between operations  2.08 us (9%)
  waiting for transfers between devices  0.29 us (1%)
    ppermute x6, starting transfers between devices, swap(): return lax.ppermute(value, axis, pairs + [(j, i) for i, j in pairs])  9.69 us
    ppermute x1, starting transfers between devices, body(): other = lax.ppermute(gradient, 'shot', [(0, 1), (1, 0)])  3.29 us
    pallas_call x1, Pallas kernels, body(): pl.pallas_call(functools.partial(velocity_kernel, width_y), out_shape=[pa...  1.45 us
    pallas_call x1, Pallas kernels, body(): pl.pallas_call(functools.partial(strain_kernel, links, width_y), out_shap...  1.24 us
    pallas_call x1, Pallas kernels, body(): pl.pallas_call(functools.partial(output_kernel, chunk, width_y), out_shap...  1.24 us
    pallas_call x1, Pallas kernels, body(): pl.pallas_call(functools.partial(early_pack_kernel, links_x), out_shape=s...  1.07 us
    pallas_call x1, Pallas kernels, body(): pl.pallas_call(functools.partial(sum_kernel, chunk), out_shape=jax.ShapeD...  0.84 us
  transfers between devices with their start and end apart: 7, of which 2 were waited for; matrix products, arithmetic and copies ran while one was open for 0% of the time, Pallas kernels for 20%

profile of v13, /device:TPU:9, one launch (start us, length us, event | category | flops | bytes accessed | tf_op | source)
XLA Modules:
  0.0 22.0 jit_solution(11687987288750227070)
XLA Ops:
  0.6 0.0 copy-start.1
  0.6 0.0 copy-start
  0.6 1.1 %early_pack.1 = (f32[2,5,16,128]{3,2,1,0:T(8,128)S(1)}, f32[2,16,128]{2,1,0:T(8,128)S(1)}) custom-call(f32[9,16,16,128]{3,2,1,0:T(8,128)} %bitcast.4, f32[9,16,16,128]{3,2,1,0:T(8,128)} %bitcast.7, f32[16,16,128]{2,1,0:T(8,128)} %density.3), custom_call_target="tpu_custom_call" | custom-call | bytes 131072 | tf_op jit(solution)/shard_map/early_pack/pallas_call | solution.py:715
  1.7 0.0 copy-start.2
  1.7 0.0 copy-start.3
  1.8 1.3 %collective-permute-start = (f32[2,5,16,128]{3,2,1,0:T(8,128)S(1)}, f32[2,5,16,128]{3,2,1,0:T(8,128)S(1)}, u32[]{:S(2)}, u32[]{:S(2)}) collective-permute-start(f32[2,5,16,128]{3,2,1,0:T(8,128)S(1)} %get-tuple-element.30), channel_id=1, source_target_pairs={{0,8},{8,0},{1,9},{9,1},{2,10},{10,2},{3,11},{11,3},{4,12},{12,4},... | collective-permute-start | bytes 245768 | tf_op jit(solution)/shard_map/ppermute | solution.py:37
  3.1 0.0 copy-done.1
  3.1 0.0 copy-done
  3.1 0.1 pack.1
  3.1 3.0 %collective-permute-start.3 = (f32[2,5,16,128]{3,2,1,0:T(8,128)S(1)}, f32[2,5,16,128]{3,2,1,0:T(8,128)S(1)}, u32[]{:S(2)}, u32[]{:S(2)}) collective-permute-start(f32[2,5,16,128]{3,2,1,0:T(8,128)S(1)} %get-tuple-element.37), channel_id=1, source_target_pairs={{1,2},{3,4},{5,6},{2,1},{4,3},{6,5},{9,10},{11,12},{13,14},{10,9},... | collective-permute-start | bytes 245768 | tf_op jit(solution)/shard_map/ppermute | solution.py:37
  6.1 1.4 %collective-permute-start.4 = (f32[2,5,16,128]{3,2,1,0:T(8,128)S(1)}, f32[2,5,16,128]{3,2,1,0:T(8,128)S(1)}, u32[]{:S(2)}, u32[]{:S(2)}) collective-permute-start(f32[2,5,16,128]{3,2,1,0:T(8,128)S(1)} %get-tuple-element.38), channel_id=1, source_target_pairs={{0,1},{2,3},{4,5},{6,7},{1,0},{3,2},{5,4},{7,6},{8,9},{10,11},{12,... | collective-permute-start | bytes 245768 | tf_op jit(solution)/shard_map/ppermute | solution.py:37
  7.6 0.0 copy-done.2
  7.6 0.0 copy-done.3
  7.6 1.4 %velocity.1 = (f32[12,20,32,128]{3,2,1,0:T(8,128)S(1)}, f32[6,20,32,128]{3,2,1,0:T(8,128)S(1)}, f32[3,16,16,128]{3,2,1,0:T(8,128)S(1)}, f32[2,3,16,128]{3,2,1,0:...) custom-call(f32[16,16,128]{2,1,0:T(8,128)} %lame.1, ...), custom_call_target="tpu_custom_call" | custom-call | flops 6553600 | bytes 2359296 | tf_op jit(solution)/shard_map/velocity/pallas_call | solution.py:739
  9.1 0.0 collective-permute-done.refs_0_.refs_2_.refs_5_
  9.1 0.2 boundary_x.1
  9.2 0.2 collective-permute-start.1
  9.4 3.2 %collective-permute-start.2 = (f32[2,5,16,128]{3,2,1,0:T(8,128)S(1)}, f32[2,5,16,128]{3,2,1,0:T(8,128)S(1)}, u32[]{:S(2)}, u32[]{:S(2)}) collective-permute-start(f32[2,5,16,128]{3,2,1,0:T(8,128)S(1)} %get-tuple-element.35), channel_id=1, source_target_pairs={{1,2},{3,4},{5,6},{2,1},{4,3},{6,5},{9,10},{11,12},{13,14},{10,9},... | collective-permute-start | bytes 245768 | tf_op jit(solution)/shard_map/ppermute | solution.py:37
  12.6 0.0 collective-permute-done.3.refs_0_.refs_4_
  12.6 0.0 collective-permute-done.4.refs_1_.refs_3_
  12.6 0.2 %boundary_y.1 = (f32[6,20,32,128]{3,2,1,0:T(8,128)S(1)}, f32[2,5,16,128]{3,2,1,0:T(8,128)S(1)}) custom-call(f32[2,5,16,128]{3,2,1,0:T(8,128)S(1)} %collective-permute-done.3.refs_0_.refs_4_, f32[2,5,16,128]{3,2,1,0:T(8,128)S(1)} %collective-permute-done.4.refs_1_.refs_3_, ...), custom_call_target="tpu_custom_call", output_to_operand_aliasing={{0}: (4, {})} | custom-call | flops 32768 | bytes 163840 | tf_op jit(solution)/shard_map/boundary_y/pallas_call | solution.py:772
  12.8 0.6 %collective-permute-start.5 = (f32[2,5,16,128]{3,2,1,0:T(8,128)S(1)}, f32[2,5,16,128]{3,2,1,0:T(8,128)S(1)}, u32[]{:S(2)}, u32[]{:S(2)}) collective-permute-start(f32[2,5,16,128]{3,2,1,0:T(8,128)S(1)} %get-tuple-element.40), channel_id=1, source_target_pairs={{0,8},{8,0},{1,9},{9,1},{2,10},{10,2},{3,11},{11,3},{4,12},{12,4},... | collective-permute-start | bytes 245768 | tf_op jit(solution)/shard_map/ppermute | solution.py:37
  14.7 1.2 %strain.1 = (f32[12,16,16,128]{3,2,1,0:T(8,128)S(1)}, f32[3,16,16,128]{3,2,1,0:T(8,128)S(1)}, f32[6,20,32,128]{3,2,1,0:T(8,128)S(1)}, f32[9,16,16,128]{3,2,1,0:T...) custom-call(f32[2,5,16,128]{3,2,1,0:T(8,128)S(1)} %collective-permut, ...), custom_call_target="tpu_custom_call", output_to_operand_aliasing={{2}: (8, {})} | custom-call | flops 6553600 | bytes 2359296 | tf_op jit(solution)/shard_map/strain/pallas_call | solution.py:793
  16.0 0.0 collective-permute-done.1.refs_0_
  16.0 0.0 collective-permute-done.2.refs_1_
  16.0 0.2 collective-permute-done.5.refs_2_
  16.2 0.4 %gradient.1 = (f32[12,16,16,128]{3,2,1,0:T(8,128)S(1)}, f32[3,16,16,128]{3,2,1,0:T(8,128)S(1)}) custom-call(f32[2,5,16,128]{3,2,1,0:T(8,128)S(1)} %collective-permute-done.1.refs_0_, f32[2,5,16,128]{3,2,1,0:T(8,128)S(1)} %collective-permute-done.2.refs_1_, ...), custom_call_target="tpu_custom_call", output_to_operand_aliasing={{0}: (12, {}), {1}: (13, {})} | custom-call | flops 983040 | bytes 262144 | tf_op jit(solution)/shard_map/gradient/pallas_call | solution.py:806
  16.5 3.3 %collective-permute-start.6 = (f32[3,16,16,128]{3,2,1,0:T(8,128)S(1)}, f32[3,16,16,128]{3,2,1,0:T(8,128)S(1)}, u32[]{:S(2)}, u32[]{:S(2)}) collective-permute-start(f32[3,16,16,128]{3,2,1,0:T(8,128)S(1)} %get-tuple-element.56.mine), channel_id=1, source_target_pairs={{0,16},{16,0},{1,17},{17,1},{2,18},{18,2},{3,19},{19,3},{4,20},{20... | collective-permute-start | bytes 1179656 | tf_op jit(solution)/shard_map/ppermute | solution.py:816
  19.8 1.2 %outputs.1 = (f32[9,16,16,128]{3,2,1,0:T(8,128)}, f32[9,16,16,128]{3,2,1,0:T(8,128)}) custom-call(s32[1]{0:T(128)S(6)} %copy.26.refs_3_.source_cell, f32[1]{0:T(128)S(6)} %copy.27.refs_4_.source_amp, f32[12,16,16,128]{3,2,1,0:T(8,128)S(1)} %get-tuple-element.51.strain, ...), custom_call_target="tpu_custom_call", output_to_operand_aliasing={{0}: (6, {}), {1}: (7, {})} | custom-call | flops 1966080 | bytes 2359296 | tf_op jit(solution)/shard_map/outputs/pallas_call | solution.py:819
  21.1 0.1 collective-permute-done.6.other
  21.2 0.8 %sum.1 = f32[3,16,16,128]{3,2,1,0:T(8,128)} custom-call(f32[3,16,16,128]{3,2,1,0:T(8,128)S(1)} %get-tuple-element.56.mine, f32[3,16,16,128]{3,2,1,0:T(8,128)S(1)} %collective-permute-done.6.other), custom_call_target="tpu_custom_call" | custom-call | flops 98304 | bytes 1179648 | tf_op jit(solution)/shard_map/sum/pallas_call | solution.py:830
Async XLA Ops:
  0.6 2.4 %copy-start.1 = (f32[1,9,16,16,128]{4,3,2,1,0:T(8,128)S(1)}, f32[1,9,16,16,128]{4,3,2,1,0:T(8,128)}, u32[]{:S(2)}) copy-start(f32[1,9,16,16,128]{4,3,2,1,0:T(8,128)} %param.10) | copy-start | bytes 3538948
  0.6 2.4 %copy-start = (f32[1,9,16,16,128]{4,3,2,1,0:T(8,128)S(1)}, f32[1,9,16,16,128]{4,3,2,1,0:T(8,128)}, u32[]{:S(2)}) copy-start(f32[1,9,16,16,128]{4,3,2,1,0:T(8,128)} %param.9) | copy-start | bytes 3538948
  1.7 5.9 %copy-start.2 = (s32[1,256]{1,0:T(1,128)S(1)}, s32[1,256]{1,0:T(1,128)}, u32[]{:S(2)}) copy-start(s32[1,256]{1,0:T(1,128)} %receiver_cell.1) | copy-start | bytes 3076
  1.7 5.9 %copy-start.3 = (f32[1,256]{1,0:T(1,128)S(1)}, f32[1,256]{1,0:T(1,128)}, u32[]{:S(2)}) copy-start(f32[1,256]{1,0:T(1,128)} %residual_amp.1) | copy-start | bytes 3076
  1.8 7.3 %collective-permute-start = (f32[2,5,16,128]{3,2,1,0:T(8,128)S(1)}, f32[2,5,16,128]{3,2,1,0:T(8,128)S(1)}, u32[]{:S(2)}, u32[]{:S(2)}) collective-permute-start(f32[2,5,16,128]{3,2,1,0:T(8,128)S(1)} %get-tuple-element.30), channel_id=1, source_target_pairs={{0,8},{8,0},{1,9},{9,1},{2,10},{10,2},{3,11},{11,3},{4,12},{12,4},... | collective-permute-start | bytes 245768 | tf_op jit(solution)/shard_map/ppermute | solution.py:37
  3.1 9.4 %collective-permute-start.3 = (f32[2,5,16,128]{3,2,1,0:T(8,128)S(1)}, f32[2,5,16,128]{3,2,1,0:T(8,128)S(1)}, u32[]{:S(2)}, u32[]{:S(2)}) collective-permute-start(f32[2,5,16,128]{3,2,1,0:T(8,128)S(1)} %get-tuple-element.37), channel_id=1, source_target_pairs={{1,2},{3,4},{5,6},{2,1},{4,3},{6,5},{9,10},{11,12},{13,14},{10,9},... | collective-permute-start | bytes 245768 | tf_op jit(solution)/shard_map/ppermute | solution.py:37
  6.1 6.4 %collective-permute-start.4 = (f32[2,5,16,128]{3,2,1,0:T(8,128)S(1)}, f32[2,5,16,128]{3,2,1,0:T(8,128)S(1)}, u32[]{:S(2)}, u32[]{:S(2)}) collective-permute-start(f32[2,5,16,128]{3,2,1,0:T(8,128)S(1)} %get-tuple-element.38), channel_id=1, source_target_pairs={{0,1},{2,3},{4,5},{6,7},{1,0},{3,2},{5,4},{7,6},{8,9},{10,11},{12,... | collective-permute-start | bytes 245768 | tf_op jit(solution)/shard_map/ppermute | solution.py:37
  9.2 6.8 %collective-permute-start.1 = (f32[2,5,16,128]{3,2,1,0:T(8,128)S(1)}, f32[2,5,16,128]{3,2,1,0:T(8,128)S(1)}, u32[]{:S(2)}, u32[]{:S(2)}) collective-permute-start(f32[2,5,16,128]{3,2,1,0:T(8,128)S(1)} %get-tuple-element.34), channel_id=1, source_target_pairs={{0,1},{2,3},{4,5},{6,7},{1,0},{3,2},{5,4},{7,6},{8,9},{10,11},{12,... | collective-permute-start | bytes 245768 | tf_op jit(solution)/shard_map/ppermute | solution.py:37
  9.4 6.6 %collective-permute-start.2 = (f32[2,5,16,128]{3,2,1,0:T(8,128)S(1)}, f32[2,5,16,128]{3,2,1,0:T(8,128)S(1)}, u32[]{:S(2)}, u32[]{:S(2)}) collective-permute-start(f32[2,5,16,128]{3,2,1,0:T(8,128)S(1)} %get-tuple-element.35), channel_id=1, source_target_pairs={{1,2},{3,4},{5,6},{2,1},{4,3},{6,5},{9,10},{11,12},{13,14},{10,9},... | collective-permute-start | bytes 245768 | tf_op jit(solution)/shard_map/ppermute | solution.py:37
  12.8 3.4 %collective-permute-start.5 = (f32[2,5,16,128]{3,2,1,0:T(8,128)S(1)}, f32[2,5,16,128]{3,2,1,0:T(8,128)S(1)}, u32[]{:S(2)}, u32[]{:S(2)}) collective-permute-start(f32[2,5,16,128]{3,2,1,0:T(8,128)S(1)} %get-tuple-element.40), channel_id=1, source_target_pairs={{0,8},{8,0},{1,9},{9,1},{2,10},{10,2},{3,11},{11,3},{4,12},{12,4},... | collective-permute-start | bytes 245768 | tf_op jit(solution)/shard_map/ppermute | solution.py:37
  16.5 4.6 %collective-permute-start.6 = (f32[3,16,16,128]{3,2,1,0:T(8,128)S(1)}, f32[3,16,16,128]{3,2,1,0:T(8,128)S(1)}, u32[]{:S(2)}, u32[]{:S(2)}) collective-permute-start(f32[3,16,16,128]{3,2,1,0:T(8,128)S(1)} %get-tuple-element.56.mine), channel_id=1, source_target_pairs={{0,16},{16,0},{1,17},{17,1},{2,18},{18,2},{3,19},{19,3},{4,20},{20... | collective-permute-start | bytes 1179656 | tf_op jit(solution)/shard_map/ppermute | solution.py:816

commit v14 on v13

--- a/solution.py
+++ b/solution.py
@@ -66,9 +66,20 @@
     return ((n, 0), (a, 0), (a, 1), (b, 0), (b, 1)), ((n, -2), (n, -1), (a, -1), (b, -1))
 
 
-def early_pack_kernel(links, forward, adjoint, density, *refs):
-    sends, (density_rows, sems) = refs[: len(links)], refs[len(links) :]
+def early_pack_kernel(
+    links, width_y, forward, adjoint, density, receiver_cell, residual_amp, *refs
+):
+    sends = refs[: len(links)]
+    density_rows, received, stress, cells_now, amps_now, sems = refs[len(links) :]
     tile = forward.shape[1:3]
+    small = [
+        pltpu.make_async_copy(source, target, sems.at[2 * SLOTS * len(links) + 2 + at])
+        for at, (source, target) in enumerate(
+            ((receiver_cell, cells_now), (residual_amp, amps_now))
+        )
+    ]
+    for copy in small:
+        copy.start()
     waits = []
     for row in range(2):
         copy = pltpu.make_async_copy(
@@ -106,6 +117,14 @@
                         layer(density, dim, 0), send.at[wave, slot], semaphore(wave, slot)
                     )
                 )
+    for wave in range(2):
+        clear_rim(
+            stress, *([6 * wave + part for part in STRESS_ALONG[dim]] for dim in range(2))
+        )
+    columns = column_ids(*tile, width_y, forward.shape[-1])
+    for copy in small:
+        copy.wait()
+    received[...] = receiver_sum(cells_now[...], amps_now[...], columns)
     for copy in waits:
         copy.wait()
 
@@ -239,14 +258,13 @@
 
 
 def velocity_kernel(
-    width_y,
     lame,
     shear,
     density,
-    receiver_cell,
-    residual_amp,
+    received,
     forward,
     adjoint,
+    _,
     stress,
     velocity,
     accel,
@@ -254,7 +272,6 @@
     buoyancy,
     scaled_lame,
     scaled_shear,
-    received,
     gained,
     lame_now,
     shear_now,
@@ -271,15 +288,9 @@
         copy.start()
     cells = tile_x * tile_y
     middle = pl.ds(ROWS, tile_y)
-    columns = column_ids(tile_x, tile_y, width_y, depth)
-    received[...] = receiver_sum(receiver_cell[...], residual_amp[...], columns)
     for layer in range(3):
         rim_added[0, layer] = received[pl.ds(cells + layer * tile_y, tile_y), :]
         rim_added[1, layer] = received[pl.ds(cells + 3 * tile_y + layer * tile_x, tile_x), :]
-    for wave in range(2):
-        clear_rim(
-            stress, *([6 * wave + part for part in STRESS_ALONG[dim]] for dim in range(2))
-        )
 
     def fill(x, carry):
         extra = received[pl.ds(pl.multiple_of(x * tile_y, 8), tile_y), :]
@@ -592,11 +603,12 @@
     return strains, values
 
 
-def gradient_kernel(links, *refs):
+def gradient_kernel(links, inner, *refs):
     count = len(links)
     received, stresses, missing = (refs[at : at + count] for at in range(0, 3 * count, count))
     stress, scaled_lame, scaled_shear, _, _, strain, gradient = refs[3 * count :]
     tile_x, tile_y, _ = scaled_lame.shape
+    first, last = min(2, tile_x), max(2, tile_x - 2)
 
     def add(wave, part, dim, index, term):
         target = face(strain, 6 * wave + part, dim, index, False)
@@ -613,7 +625,12 @@
         gradient[1, x] = -time_step * total
         return carry
 
-    lax.fori_loop(0, tile_x, layer, 0, unroll=8)
+    if inner:
+        if last > first:
+            lax.fori_loop(first, last, layer, 0, unroll=4)
+    else:
+        for x in (*range(first), *range(last, tile_x)):
+            layer(x, 0)
 
 
 def output_kernel(
@@ -712,16 +729,26 @@
     rows = tile_x * tile_y + 3 * (tile_x + tile_y)
     source = source_cell, source_amp
 
-    *sends, density_rows = pl.pallas_call(
-        functools.partial(early_pack_kernel, links_x),
-        out_shape=shapes(links_x) + [pltpu.VMEM((2, tile_x, depth), jnp.float32)],
-        in_specs=[hbm] * 3,
-        out_specs=[vmem] * (count_x + 1),
-        scratch_shapes=[pltpu.SemaphoreType.DMA((2 + 2 * SLOTS * count_x,))],
+    receivers = receiver_cell.shape[-1]
+    *sends, density_rows, received, stress = pl.pallas_call(
+        functools.partial(early_pack_kernel, links_x, width_y),
+        out_shape=shapes(links_x)
+        + [
+            pltpu.VMEM((2, tile_x, depth), jnp.float32),
+            pltpu.VMEM((rows, depth), jnp.float32),
+            padded(12),
+        ],
+        in_specs=[hbm] * 5,
+        out_specs=[vmem] * (count_x + 3),
+        scratch_shapes=[
+            pltpu.VMEM((1, receivers), jnp.int32),
+            pltpu.VMEM((1, receivers), jnp.float32),
+            pltpu.SemaphoreType.DMA((4 + 2 * SLOTS * count_x,)),
+        ],
         compiler_params=params,
         cost_estimate=cost(0, 4 * cells),
         name="early_pack",
-    )(*(in_hbm(x) for x in (forward, adjoint, density)))
+    )(*(in_hbm(x) for x in (forward, adjoint, density, receiver_cell, residual_amp)))
     halos_x = exchange(links_x, sends)
     halos_y = []
     if links_y:
@@ -737,7 +764,7 @@
         halos_y = exchange(links_y, sends)
 
     stress, velocity, accel, rim_added, buoyancy, scaled_lame, scaled_shear = pl.pallas_call(
-        functools.partial(velocity_kernel, width_y),
+        velocity_kernel,
         out_shape=[
             padded(12),
             padded(6),
@@ -749,8 +776,8 @@
         ],
         in_specs=[hbm] * 3 + [vmem] * 4,
         out_specs=[vmem] * 7,
+        input_output_aliases={6: 0},
         scratch_shapes=[
-            pltpu.VMEM((rows, depth), jnp.float32),
             tile(6),
             tile(),
             tile(),
@@ -762,10 +789,10 @@
         name="velocity",
     )(
         *(in_hbm(x) for x in (lame_lambda, shear_modulus, density)),
-        receiver_cell,
-        residual_amp,
+        received,
         forward,
         adjoint,
+        stress,
     )
 
     def boundary(links, send_links, halos, velocity, name):
@@ -785,9 +812,6 @@
     velocity, velocity_halos_y = boundary(links_x, later_y, halos_x, velocity, "boundary_x")
     velocity, velocity_halos_x = boundary(links_y, links_x, halos_y, velocity, "boundary_y")
     halos = halos_y + halos_x
-    later_links = later_y + links_x
-    later_halos = halos_y[::-1] + halos_x
-    velocity_halos = velocity_halos_y + velocity_halos_x
 
     out_shape = jax.ShapeDtypeStruct(forward.shape, jnp.float32)
     strain, gradient, _, forward_next, adjoint_next, *missing = pl.pallas_call(
@@ -801,18 +825,32 @@
         cost_estimate=cost(200 * cells, 18 * 4 * cells),
         name="strain",
     )(*halos, *source, rim_added, buoyancy, accel, velocity, stress)
-    missing = missing[:count_y][::-1] + missing[count_y:]
-
-    strain, gradient = pl.pallas_call(
-        functools.partial(gradient_kernel, later_links),
-        out_shape=[tile(12), tile(3)],
-        in_specs=[vmem] * (3 * count + 5),
-        out_specs=[vmem] * 2,
-        input_output_aliases={3 * count + 3: 0, 3 * count + 4: 1},
-        compiler_params=params,
-        cost_estimate=cost(30 * cells, 2 * 4 * cells),
-        name="gradient",
-    )(*velocity_halos, *later_halos, *missing, stress, scaled_lame, scaled_shear, strain, gradient)
+
+    def gradients(links, inner, received, stresses, missing, strain, gradient, name):
+        return pl.pallas_call(
+            functools.partial(gradient_kernel, links, inner),
+            out_shape=[tile(12), tile(3)],
+            in_specs=[vmem] * (3 * len(links) + 5),
+            out_specs=[vmem] * 2,
+            input_output_aliases={3 * len(links) + 3: 0, 3 * len(links) + 4: 1},
+            compiler_params=params,
+            cost_estimate=cost(30 * cells, 2 * 4 * cells),
+            name=name,
+        )(*received, *stresses, *missing, stress, scaled_lame, scaled_shear, strain, gradient)
+
+    strain, gradient = gradients(
+        later_y,
+        True,
+        velocity_halos_y,
+        halos_y[::-1],
+        missing[:count_y][::-1],
+        strain,
+        gradient,
+        "gradient_inner",
+    )
+    strain, gradient = gradients(
+        links_x, False, velocity_halos_x, halos_x, missing[count_y:], strain, gradient, "gradient"
+    )
     other = lax.ppermute(gradient, "shot", [(0, 1), (1, 0)])
 
     chunk = 4 if tile_x % 4 == 0 else 1
@@ -828,11 +866,11 @@
         name="outputs",
     )(*source, strain, stress, scaled_lame, scaled_shear, forward_next, adjoint_next)
     total = pl.pallas_call(
-        functools.partial(sum_kernel, chunk),
+        functools.partial(sum_kernel, tile_x),
         out_shape=jax.ShapeDtypeStruct((3, tile_x, tile_y, depth), jnp.float32),
         in_specs=[vmem] * 2,
         out_specs=hbm,
-        scratch_shapes=[tile(3), pltpu.SemaphoreType.DMA((3 * tile_x // chunk,))],
+        scratch_shapes=[tile(3), pltpu.SemaphoreType.DMA((3,))],
         compiler_params=params,
         cost_estimate=cost(3 * cells, 9 * 4 * cells),
         name="sum",

time: 22.3 us -> 21.8 us (0.978)
    pallas_call x4 -> x5, Pallas kernels: 3.72 us -> 3.64 us  [the longest x1 1.31 us: body(): pl.pallas_call(functools.partial(early_pack_kernel, links_x, width_y), ou...]
where the time goes in v14:
time: 21.8 us; the launch traced here: 21.6 us
  starting transfers between devices  12.8 us (59%)
  Pallas kernels  6.53 us (30%)
  between operations  2.07 us (9%)
  waiting for transfers between devices  0.25 us (1%)
    ppermute x6, starting transfers between devices, swap(): return lax.ppermute(value, axis, pairs + [(j, i) for i, j in pairs])  9.48 us
    ppermute x1, starting transfers between devices, body(): other = lax.ppermute(gradient, 'shot', [(0, 1), (1, 0)])  3.29 us
    pallas_call x1, Pallas kernels, body(): pl.pallas_call(functools.partial(early_pack_kernel, links_x, width_y), ou...  1.31 us
    pallas_call x1, Pallas kernels, body(): pl.pallas_call(functools.partial(output_kernel, chunk, width_y), out_shap...  1.23 us
    pallas_call x1, Pallas kernels, body(): pl.pallas_call(functools.partial(strain_kernel, links, width_y), out_shap...  1.21 us
    pallas_call x1, Pallas kernels, body(): pl.pallas_call(velocity_kernel, out_shape=[padded(12), padded(6), tile(3)...  1.2 us
    pallas_call x1, Pallas kernels, body(): pl.pallas_call(functools.partial(sum_kernel, tile_x), out_shape=jax.Shape...  0.78 us
  transfers between devices with their start and end apart: 7, of which 2 were waited for; matrix products, arithmetic and copies ran while one was open for 0% of the time, Pallas kernels for 20%

profile of v14, /device:TPU:9, one launch (start us, length us, event | category | flops | bytes accessed | tf_op | source)
XLA Modules:
  0.0 21.6 jit_solution(15849178273767153933)
XLA Ops:
  0.6 0.0 copy-start.1
  0.6 0.0 copy-start
  0.7 1.3 %early_pack.1 = (f32[2,5,16,128]{3,2,1,0:T(8,128)S(1)}, f32[2,16,128]{2,1,0:T(8,128)S(1)}, f32[352,128]{1,0:T(8,128)S(1)}, f32[12,20,32,128]{3,2,1,0:T(8,128)S(1)}) custom-call(f32[9,16,16,128]{3,2,1,0:T(8,128)} %bitcast.4, f32[9,16,16,128]{3,2,1,0:T(8,128)} %bitcast.7, f32[16,16,128]{2,1,0:T(8,128)} %density.3, s32[1,256]{1,0:T(1,128)} %receiver_cell.1, ...), custom_call_target="tpu_custom_call" | custom-call | bytes 131072 | tf_op jit(solution)/shard_map/early_pack/pallas_call | solution.py:733
  2.0 1.3 %collective-permute-start.2 = (f32[2,5,16,128]{3,2,1,0:T(8,128)S(1)}, f32[2,5,16,128]{3,2,1,0:T(8,128)S(1)}, u32[]{:S(2)}, u32[]{:S(2)}) collective-permute-start(f32[2,5,16,128]{3,2,1,0:T(8,128)S(1)} %get-tuple-element.41), channel_id=1, source_target_pairs={{0,8},{8,0},{1,9},{9,1},{2,10},{10,2},{3,11},{11,3},{4,12},{12,4},... | collective-permute-start | bytes 245768 | tf_op jit(solution)/shard_map/ppermute | solution.py:37
  3.3 0.0 copy-done.1
  3.3 0.0 copy-done
  3.3 0.1 pack.1
  3.4 3.0 %collective-permute-start = (f32[2,5,16,128]{3,2,1,0:T(8,128)S(1)}, f32[2,5,16,128]{3,2,1,0:T(8,128)S(1)}, u32[]{:S(2)}, u32[]{:S(2)}) collective-permute-start(f32[2,5,16,128]{3,2,1,0:T(8,128)S(1)} %get-tuple-element.35), channel_id=1, source_target_pairs={{1,2},{3,4},{5,6},{2,1},{4,3},{6,5},{9,10},{11,12},{13,14},{10,9},... | collective-permute-start | bytes 245768 | tf_op jit(solution)/shard_map/ppermute | solution.py:37
  6.4 1.4 %collective-permute-start.1 = (f32[2,5,16,128]{3,2,1,0:T(8,128)S(1)}, f32[2,5,16,128]{3,2,1,0:T(8,128)S(1)}, u32[]{:S(2)}, u32[]{:S(2)}) collective-permute-start(f32[2,5,16,128]{3,2,1,0:T(8,128)S(1)} %get-tuple-element.36), channel_id=1, source_target_pairs={{0,1},{2,3},{4,5},{6,7},{1,0},{3,2},{5,4},{7,6},{8,9},{10,11},{12,... | collective-permute-start | bytes 245768 | tf_op jit(solution)/shard_map/ppermute | solution.py:37
  7.8 1.2 %velocity.1 = (f32[12,20,32,128]{3,2,1,0:T(8,128)S(1)}, f32[6,20,32,128]{3,2,1,0:T(8,128)S(1)}, f32[3,16,16,128]{3,2,1,0:T(8,128)S(1)}, f32[2,3,16,128]{3,2,1,0:...) custom-call(f32[16,16,128]{2,1,0:T(8,128)} %lame.1, ...), custom_call_target="tpu_custom_call", output_to_operand_aliasing={{0}: (6, {})} | custom-call | flops 6553600 | bytes 2359296 | tf_op jit(solution)/shard_map/velocity/pallas_call | solution.py:766
  9.0 0.0 collective-permute-done.2.refs_0_.refs_2_.refs_1_
  9.0 0.2 boundary_x.1
  9.2 0.2 collective-permute-start.4
  9.4 3.2 %collective-permute-start.5 = (f32[2,5,16,128]{3,2,1,0:T(8,128)S(1)}, f32[2,5,16,128]{3,2,1,0:T(8,128)S(1)}, u32[]{:S(2)}, u32[]{:S(2)}) collective-permute-start(f32[2,5,16,128]{3,2,1,0:T(8,128)S(1)} %get-tuple-element.52), channel_id=1, source_target_pairs={{1,2},{3,4},{5,6},{2,1},{4,3},{6,5},{9,10},{11,12},{13,14},{10,9},... | collective-permute-start | bytes 245768 | tf_op jit(solution)/shard_map/ppermute | solution.py:37
  12.5 0.0 collective-permute-done.refs_0_.refs_3_
  12.5 0.0 collective-permute-done.1.refs_1_.refs_2_
  12.5 0.2 %boundary_y.1 = (f32[6,20,32,128]{3,2,1,0:T(8,128)S(1)}, f32[2,5,16,128]{3,2,1,0:T(8,128)S(1)}) custom-call(f32[2,5,16,128]{3,2,1,0:T(8,128)S(1)} %collective-permute-done.refs_0_.refs_3_, f32[2,5,16,128]{3,2,1,0:T(8,128)S(1)} %collective-permute-done.1.refs_1_.refs_2_, ...), custom_call_target="tpu_custom_call", output_to_operand_aliasing={{0}: (4, {})} | custom-call | flops 32768 | bytes 163840 | tf_op jit(solution)/shard_map/boundary_y/pallas_call | solution.py:799
  12.8 0.4 %collective-permute-start.3 = (f32[2,5,16,128]{3,2,1,0:T(8,128)S(1)}, f32[2,5,16,128]{3,2,1,0:T(8,128)S(1)}, u32[]{:S(2)}, u32[]{:S(2)}) collective-permute-start(f32[2,5,16,128]{3,2,1,0:T(8,128)S(1)} %get-tuple-element.44), channel_id=1, source_target_pairs={{0,8},{8,0},{1,9},{9,1},{2,10},{10,2},{3,11},{11,3},{4,12},{12,4},... | collective-permute-start | bytes 245768 | tf_op jit(solution)/shard_map/ppermute | solution.py:37
  14.5 1.2 %strain.1 = (f32[12,16,16,128]{3,2,1,0:T(8,128)S(1)}, f32[3,16,16,128]{3,2,1,0:T(8,128)S(1)}, f32[6,20,32,128]{3,2,1,0:T(8,128)S(1)}, f32[9,16,16,128]{3,2,1,0:T...) custom-call(f32[2,5,16,128]{3,2,1,0:T(8,128)S(1)} %collective-permut, ...), custom_call_target="tpu_custom_call", output_to_operand_aliasing={{2}: (8, {})} | custom-call | flops 6553600 | bytes 2359296 | tf_op jit(solution)/shard_map/strain/pallas_call | solution.py:817
  15.7 0.0 collective-permute-done.4.refs_0_
  15.7 0.0 collective-permute-done.5.refs_1_
  15.7 0.3 %gradient_inner.1 = (f32[12,16,16,128]{3,2,1,0:T(8,128)S(1)}, f32[3,16,16,128]{3,2,1,0:T(8,128)S(1)}) custom-call(f32[2,5,16,128]{3,2,1,0:T(8,128)S(1)} %collective-permute-done.4.refs_0_, f32[2,5,16,128]{3,2,1,0:T(8,128)S(1)} %collective-permute-done.5.refs_1_, ...), custom_call_target="tpu_custom_call", output_to_operand_aliasing={{0}: (9, {}), {1}: (10, {})} | custom-call | flops 983040 | bytes 262144 | tf_op jit(solution)/shard_map/gradient_inner/pallas_call | solution.py:830
  16.0 0.1 collective-permute-done.3.refs_0_
  16.1 0.1 gradient.1
  16.2 3.3 %collective-permute-start.6 = (f32[3,16,16,128]{3,2,1,0:T(8,128)S(1)}, f32[3,16,16,128]{3,2,1,0:T(8,128)S(1)}, u32[]{:S(2)}, u32[]{:S(2)}) collective-permute-start(f32[3,16,16,128]{3,2,1,0:T(8,128)S(1)} %get-tuple-element.64.mine), channel_id=1, source_target_pairs={{0,16},{16,0},{1,17},{17,1},{2,18},{18,2},{3,19},{19,3},{4,20},{20... | collective-permute-start | bytes 1179656 | tf_op jit(solution)/shard_map/ppermute | solution.py:854
  19.5 1.2 %outputs.1 = (f32[9,16,16,128]{3,2,1,0:T(8,128)}, f32[9,16,16,128]{3,2,1,0:T(8,128)}) custom-call(s32[1]{0:T(128)S(6)} %copy.32.refs_3_.source_cell, f32[1]{0:T(128)S(6)} %copy.33.refs_4_.source_amp, f32[12,16,16,128]{3,2,1,0:T(8,128)S(1)} %get-tuple-element.59.strain, ...), custom_call_target="tpu_custom_call", output_to_operand_aliasing={{0}: (6, {}), {1}: (7, {})} | custom-call | flops 1966080 | bytes 2359296 | tf_op jit(solution)/shard_map/outputs/pallas_call | solution.py:857
  20.7 0.1 collective-permute-done.6.other
  20.9 0.8 %sum.1 = f32[3,16,16,128]{3,2,1,0:T(8,128)} custom-call(f32[3,16,16,128]{3,2,1,0:T(8,128)S(1)} %get-tuple-element.64.mine, f32[3,16,16,128]{3,2,1,0:T(8,128)S(1)} %collective-permute-done.6.other), custom_call_target="tpu_custom_call" | custom-call | flops 98304 | bytes 1179648 | tf_op jit(solution)/shard_map/sum/pallas_call | solution.py:868
Async XLA Ops:
  0.6 2.7 %copy-start.1 = (f32[1,9,16,16,128]{4,3,2,1,0:T(8,128)S(1)}, f32[1,9,16,16,128]{4,3,2,1,0:T(8,128)}, u32[]{:S(2)}) copy-start(f32[1,9,16,16,128]{4,3,2,1,0:T(8,128)} %param.10) | copy-start | bytes 3538948
  0.6 2.6 %copy-start = (f32[1,9,16,16,128]{4,3,2,1,0:T(8,128)S(1)}, f32[1,9,16,16,128]{4,3,2,1,0:T(8,128)}, u32[]{:S(2)}) copy-start(f32[1,9,16,16,128]{4,3,2,1,0:T(8,128)} %param.9) | copy-start | bytes 3538948
  2.0 7.0 %collective-permute-start.2 = (f32[2,5,16,128]{3,2,1,0:T(8,128)S(1)}, f32[2,5,16,128]{3,2,1,0:T(8,128)S(1)}, u32[]{:S(2)}, u32[]{:S(2)}) collective-permute-start(f32[2,5,16,128]{3,2,1,0:T(8,128)S(1)} %get-tuple-element.41), channel_id=1, source_target_pairs={{0,8},{8,0},{1,9},{9,1},{2,10},{10,2},{3,11},{11,3},{4,12},{12,4},... | collective-permute-start | bytes 245768 | tf_op jit(solution)/shard_map/ppermute | solution.py:37
  3.4 9.2 %collective-permute-start = (f32[2,5,16,128]{3,2,1,0:T(8,128)S(1)}, f32[2,5,16,128]{3,2,1,0:T(8,128)S(1)}, u32[]{:S(2)}, u32[]{:S(2)}) collective-permute-start(f32[2,5,16,128]{3,2,1,0:T(8,128)S(1)} %get-tuple-element.35), channel_id=1, source_target_pairs={{1,2},{3,4},{5,6},{2,1},{4,3},{6,5},{9,10},{11,12},{13,14},{10,9},... | collective-permute-start | bytes 245768 | tf_op jit(solution)/shard_map/ppermute | solution.py:37
  6.4 6.2 %collective-permute-start.1 = (f32[2,5,16,128]{3,2,1,0:T(8,128)S(1)}, f32[2,5,16,128]{3,2,1,0:T(8,128)S(1)}, u32[]{:S(2)}, u32[]{:S(2)}) collective-permute-start(f32[2,5,16,128]{3,2,1,0:T(8,128)S(1)} %get-tuple-element.36), channel_id=1, source_target_pairs={{0,1},{2,3},{4,5},{6,7},{1,0},{3,2},{5,4},{7,6},{8,9},{10,11},{12,... | collective-permute-start | bytes 245768 | tf_op jit(solution)/shard_map/ppermute | solution.py:37
  9.2 6.5 %collective-permute-start.4 = (f32[2,5,16,128]{3,2,1,0:T(8,128)S(1)}, f32[2,5,16,128]{3,2,1,0:T(8,128)S(1)}, u32[]{:S(2)}, u32[]{:S(2)}) collective-permute-start(f32[2,5,16,128]{3,2,1,0:T(8,128)S(1)} %get-tuple-element.51), channel_id=1, source_target_pairs={{0,1},{2,3},{4,5},{6,7},{1,0},{3,2},{5,4},{7,6},{8,9},{10,11},{12,... | collective-permute-start | bytes 245768 | tf_op jit(solution)/shard_map/ppermute | solution.py:37
  9.4 6.4 %collective-permute-start.5 = (f32[2,5,16,128]{3,2,1,0:T(8,128)S(1)}, f32[2,5,16,128]{3,2,1,0:T(8,128)S(1)}, u32[]{:S(2)}, u32[]{:S(2)}) collective-permute-start(f32[2,5,16,128]{3,2,1,0:T(8,128)S(1)} %get-tuple-element.52), channel_id=1, source_target_pairs={{1,2},{3,4},{5,6},{2,1},{4,3},{6,5},{9,10},{11,12},{13,14},{10,9},... | collective-permute-start | bytes 245768 | tf_op jit(solution)/shard_map/ppermute | solution.py:37
  12.8 3.4 %collective-permute-start.3 = (f32[2,5,16,128]{3,2,1,0:T(8,128)S(1)}, f32[2,5,16,128]{3,2,1,0:T(8,128)S(1)}, u32[]{:S(2)}, u32[]{:S(2)}) collective-permute-start(f32[2,5,16,128]{3,2,1,0:T(8,128)S(1)} %get-tuple-element.44), channel_id=1, source_target_pairs={{0,8},{8,0},{1,9},{9,1},{2,10},{10,2},{3,11},{11,3},{4,12},{12,4},... | collective-permute-start | bytes 245768 | tf_op jit(solution)/shard_map/ppermute | solution.py:37
  16.2 4.6 %collective-permute-start.6 = (f32[3,16,16,128]{3,2,1,0:T(8,128)S(1)}, f32[3,16,16,128]{3,2,1,0:T(8,128)S(1)}, u32[]{:S(2)}, u32[]{:S(2)}) collective-permute-start(f32[3,16,16,128]{3,2,1,0:T(8,128)S(1)} %get-tuple-element.64.mine), channel_id=1, source_target_pairs={{0,16},{16,0},{1,17},{17,1},{2,18},{18,2},{3,19},{19,3},{4,20},{20... | collective-permute-start | bytes 1179656 | tf_op jit(solution)/shard_map/ppermute | solution.py:854

commit v15 on v14

--- a/solution.py
+++ b/solution.py
@@ -66,20 +66,9 @@
     return ((n, 0), (a, 0), (a, 1), (b, 0), (b, 1)), ((n, -2), (n, -1), (a, -1), (b, -1))
 
 
-def early_pack_kernel(
-    links, width_y, forward, adjoint, density, receiver_cell, residual_amp, *refs
-):
-    sends = refs[: len(links)]
-    density_rows, received, stress, cells_now, amps_now, sems = refs[len(links) :]
+def early_pack_kernel(links, forward, adjoint, density, *refs):
+    sends, (density_rows, stress, sems) = refs[: len(links)], refs[len(links) :]
     tile = forward.shape[1:3]
-    small = [
-        pltpu.make_async_copy(source, target, sems.at[2 * SLOTS * len(links) + 2 + at])
-        for at, (source, target) in enumerate(
-            ((receiver_cell, cells_now), (residual_amp, amps_now))
-        )
-    ]
-    for copy in small:
-        copy.start()
     waits = []
     for row in range(2):
         copy = pltpu.make_async_copy(
@@ -121,10 +110,6 @@
         clear_rim(
             stress, *([6 * wave + part for part in STRESS_ALONG[dim]] for dim in range(2))
         )
-    columns = column_ids(*tile, width_y, forward.shape[-1])
-    for copy in small:
-        copy.wait()
-    received[...] = receiver_sum(cells_now[...], amps_now[...], columns)
     for copy in waits:
         copy.wait()
 
@@ -258,10 +243,12 @@
 
 
 def velocity_kernel(
+    width_y,
     lame,
     shear,
     density,
-    received,
+    receiver_cell,
+    residual_amp,
     forward,
     adjoint,
     _,
@@ -272,6 +259,7 @@
     buoyancy,
     scaled_lame,
     scaled_shear,
+    received,
     gained,
     lame_now,
     shear_now,
@@ -288,6 +276,8 @@
         copy.start()
     cells = tile_x * tile_y
     middle = pl.ds(ROWS, tile_y)
+    columns = column_ids(tile_x, tile_y, width_y, depth)
+    received[...] = receiver_sum(receiver_cell[...], residual_amp[...], columns)
     for layer in range(3):
         rim_added[0, layer] = received[pl.ds(cells + layer * tile_y, tile_y), :]
         rim_added[1, layer] = received[pl.ds(cells + 3 * tile_y + layer * tile_x, tile_x), :]
@@ -322,7 +312,7 @@
                 gained[3 * wave + part, x] = value
         return carry
 
-    lax.fori_loop(0, tile_x, layer, 0, unroll=8)
+    lax.fori_loop(0, tile_x, layer, 0, unroll=True)
     for copy in copies:
         copy.wait()
 
@@ -729,26 +719,16 @@
     rows = tile_x * tile_y + 3 * (tile_x + tile_y)
     source = source_cell, source_amp
 
-    receivers = receiver_cell.shape[-1]
-    *sends, density_rows, received, stress = pl.pallas_call(
-        functools.partial(early_pack_kernel, links_x, width_y),
-        out_shape=shapes(links_x)
-        + [
-            pltpu.VMEM((2, tile_x, depth), jnp.float32),
-            pltpu.VMEM((rows, depth), jnp.float32),
-            padded(12),
-        ],
-        in_specs=[hbm] * 5,
-        out_specs=[vmem] * (count_x + 3),
-        scratch_shapes=[
-            pltpu.VMEM((1, receivers), jnp.int32),
-            pltpu.VMEM((1, receivers), jnp.float32),
-            pltpu.SemaphoreType.DMA((4 + 2 * SLOTS * count_x,)),
-        ],
+    *sends, density_rows, stress = pl.pallas_call(
+        functools.partial(early_pack_kernel, links_x),
+        out_shape=shapes(links_x) + [pltpu.VMEM((2, tile_x, depth), jnp.float32), padded(12)],
+        in_specs=[hbm] * 3,
+        out_specs=[vmem] * (count_x + 2),
+        scratch_shapes=[pltpu.SemaphoreType.DMA((2 + 2 * SLOTS * count_x,))],
         compiler_params=params,
         cost_estimate=cost(0, 4 * cells),
         name="early_pack",
-    )(*(in_hbm(x) for x in (forward, adjoint, density, receiver_cell, residual_amp)))
+    )(*(in_hbm(x) for x in (forward, adjoint, density)))
     halos_x = exchange(links_x, sends)
     halos_y = []
     if links_y:
@@ -764,7 +744,7 @@
         halos_y = exchange(links_y, sends)
 
     stress, velocity, accel, rim_added, buoyancy, scaled_lame, scaled_shear = pl.pallas_call(
-        velocity_kernel,
+        functools.partial(velocity_kernel, width_y),
         out_shape=[
             padded(12),
             padded(6),
@@ -774,10 +754,11 @@
             tile(),
             tile(),
         ],
-        in_specs=[hbm] * 3 + [vmem] * 4,
+        in_specs=[hbm] * 3 + [vmem] * 5,
         out_specs=[vmem] * 7,
-        input_output_aliases={6: 0},
+        input_output_aliases={7: 0},
         scratch_shapes=[
+            pltpu.VMEM((rows, depth), jnp.float32),
             tile(6),
             tile(),
             tile(),
@@ -789,7 +770,8 @@
         name="velocity",
     )(
         *(in_hbm(x) for x in (lame_lambda, shear_modulus, density)),
-        received,
+        receiver_cell,
+        residual_amp,
         forward,
         adjoint,
         stress,

time: 21.8 us -> 21.9 us (level)
  transfers between devices with their start and end apart: 7 -> 7, of which waited for: 2 -> 1; matrix products, arithmetic and copies ran while one was open for 0% -> 0% of each run, Pallas kernels for 20% -> 21%
where the time goes in v15:
time: 21.9 us; the launch traced here: 21.6 us
  starting transfers between devices  12.8 us (58%)
  Pallas kernels  6.59 us (30%)
  between operations  2.09 us (10%)
    ppermute x6, starting transfers between devices, swap(): return lax.ppermute(value, axis, pairs + [(j, i) for i, j in pairs])  9.61 us
    ppermute x1, starting transfers between devices, body(): other = lax.ppermute(gradient, 'shot', [(0, 1), (1, 0)])  3.22 us
    pallas_call x1, Pallas kernels, body(): pl.pallas_call(functools.partial(velocity_kernel, width_y), out_shape=[pa...  1.33 us
    pallas_call x1, Pallas kernels, body(): pl.pallas_call(functools.partial(output_kernel, chunk, width_y), out_shap...  1.24 us
    pallas_call x1, Pallas kernels, body(): pl.pallas_call(functools.partial(strain_kernel, links, width_y), out_shap...  1.22 us
    pallas_call x1, Pallas kernels, body(): pl.pallas_call(functools.partial(early_pack_kernel, links_x), out_shape=s...  1.15 us
    pallas_call x1, Pallas kernels, body(): pl.pallas_call(functools.partial(sum_kernel, tile_x), out_shape=jax.Shape...  0.78 us
  transfers between devices with their start and end apart: 7, of which 1 were waited for; matrix products, arithmetic and copies ran while one was open for 0% of the time, Pallas kernels for 21%

profile of v15, /device:TPU:9, one launch (start us, length us, event | category | flops | bytes accessed | tf_op | source)
XLA Modules:
  0.0 21.6 jit_solution(9771321126778908374)
XLA Ops:
  0.6 0.0 copy-start.1
  0.6 0.0 copy-start
  0.6 1.2 %early_pack.1 = (f32[2,5,16,128]{3,2,1,0:T(8,128)S(1)}, f32[2,16,128]{2,1,0:T(8,128)S(1)}, f32[12,20,32,128]{3,2,1,0:T(8,128)S(1)}) custom-call(f32[9,16,16,128]{3,2,1,0:T(8,128)} %bitcast.4, f32[9,16,16,128]{3,2,1,0:T(8,128)} %bitcast.7, f32[16,16,128]{2,1,0:T(8,128)} %density.3), custom_call_target="tpu_custom_call" | custom-call | bytes 131072 | tf_op jit(solution)/shard_map/early_pack/pallas_call | solution.py:722
  1.8 0.0 copy-start.2
  1.8 0.0 copy-start.3
  1.8 1.3 %collective-permute-start.2 = (f32[2,5,16,128]{3,2,1,0:T(8,128)S(1)}, f32[2,5,16,128]{3,2,1,0:T(8,128)S(1)}, u32[]{:S(2)}, u32[]{:S(2)}) collective-permute-start(f32[2,5,16,128]{3,2,1,0:T(8,128)S(1)} %get-tuple-element.39), channel_id=1, source_target_pairs={{0,8},{8,0},{1,9},{9,1},{2,10},{10,2},{3,11},{11,3},{4,12},{12,4},... | collective-permute-start | bytes 245768 | tf_op jit(solution)/shard_map/ppermute | solution.py:37
  3.1 0.0 copy-done.1
  3.1 0.0 copy-done
  3.1 0.1 pack.1
  3.2 3.0 %collective-permute-start = (f32[2,5,16,128]{3,2,1,0:T(8,128)S(1)}, f32[2,5,16,128]{3,2,1,0:T(8,128)S(1)}, u32[]{:S(2)}, u32[]{:S(2)}) collective-permute-start(f32[2,5,16,128]{3,2,1,0:T(8,128)S(1)} %get-tuple-element.34), channel_id=1, source_target_pairs={{1,2},{3,4},{5,6},{2,1},{4,3},{6,5},{9,10},{11,12},{13,14},{10,9},... | collective-permute-start | bytes 245768 | tf_op jit(solution)/shard_map/ppermute | solution.py:37
  6.2 1.4 %collective-permute-start.1 = (f32[2,5,16,128]{3,2,1,0:T(8,128)S(1)}, f32[2,5,16,128]{3,2,1,0:T(8,128)S(1)}, u32[]{:S(2)}, u32[]{:S(2)}) collective-permute-start(f32[2,5,16,128]{3,2,1,0:T(8,128)S(1)} %get-tuple-element.35), channel_id=1, source_target_pairs={{0,1},{2,3},{4,5},{6,7},{1,0},{3,2},{5,4},{7,6},{8,9},{10,11},{12,... | collective-permute-start | bytes 245768 | tf_op jit(solution)/shard_map/ppermute | solution.py:37
  7.7 0.0 copy-done.2
  7.7 0.0 copy-done.3
  7.7 1.3 %velocity.1 = (f32[12,20,32,128]{3,2,1,0:T(8,128)S(1)}, f32[6,20,32,128]{3,2,1,0:T(8,128)S(1)}, f32[3,16,16,128]{3,2,1,0:T(8,128)S(1)}, f32[2,3,16,128]{3,2,1,0:...) custom-call(f32[16,16,128]{2,1,0:T(8,128)} %lame.1, ...), custom_call_target="tpu_custom_call", output_to_operand_aliasing={{0}: (7, {})} | custom-call | flops 6553600 | bytes 2359296 | tf_op jit(solution)/shard_map/velocity/pallas_call | solution.py:746
  9.0 0.0 collective-permute-done.2.refs_0_.refs_2_.refs_1_
  9.0 0.2 boundary_x.1
  9.2 0.2 collective-permute-start.4
  9.3 3.2 %collective-permute-start.5 = (f32[2,5,16,128]{3,2,1,0:T(8,128)S(1)}, f32[2,5,16,128]{3,2,1,0:T(8,128)S(1)}, u32[]{:S(2)}, u32[]{:S(2)}) collective-permute-start(f32[2,5,16,128]{3,2,1,0:T(8,128)S(1)} %get-tuple-element.50), channel_id=1, source_target_pairs={{1,2},{3,4},{5,6},{2,1},{4,3},{6,5},{9,10},{11,12},{13,14},{10,9},... | collective-permute-start | bytes 245768 | tf_op jit(solution)/shard_map/ppermute | solution.py:37
  12.5 0.0 collective-permute-done.refs_0_.refs_3_
  12.5 0.0 collective-permute-done.1.refs_1_.refs_2_
  12.5 0.2 %boundary_y.1 = (f32[6,20,32,128]{3,2,1,0:T(8,128)S(1)}, f32[2,5,16,128]{3,2,1,0:T(8,128)S(1)}) custom-call(f32[2,5,16,128]{3,2,1,0:T(8,128)S(1)} %collective-permute-done.refs_0_.refs_3_, f32[2,5,16,128]{3,2,1,0:T(8,128)S(1)} %collective-permute-done.1.refs_1_.refs_2_, ...), custom_call_target="tpu_custom_call", output_to_operand_aliasing={{0}: (4, {})} | custom-call | flops 32768 | bytes 163840 | tf_op jit(solution)/shard_map/boundary_y/pallas_call | solution.py:781
  12.8 0.5 %collective-permute-start.3 = (f32[2,5,16,128]{3,2,1,0:T(8,128)S(1)}, f32[2,5,16,128]{3,2,1,0:T(8,128)S(1)}, u32[]{:S(2)}, u32[]{:S(2)}) collective-permute-start(f32[2,5,16,128]{3,2,1,0:T(8,128)S(1)} %get-tuple-element.42), channel_id=1, source_target_pairs={{0,8},{8,0},{1,9},{9,1},{2,10},{10,2},{3,11},{11,3},{4,12},{12,4},... | collective-permute-start | bytes 245768 | tf_op jit(solution)/shard_map/ppermute | solution.py:37
  14.6 1.2 %strain.1 = (f32[12,16,16,128]{3,2,1,0:T(8,128)S(1)}, f32[3,16,16,128]{3,2,1,0:T(8,128)S(1)}, f32[6,20,32,128]{3,2,1,0:T(8,128)S(1)}, f32[9,16,16,128]{3,2,1,0:T...) custom-call(f32[2,5,16,128]{3,2,1,0:T(8,128)S(1)} %collective-permut, ...), custom_call_target="tpu_custom_call", output_to_operand_aliasing={{2}: (8, {})} | custom-call | flops 6553600 | bytes 2359296 | tf_op jit(solution)/shard_map/strain/pallas_call | solution.py:799
  15.9 0.0 collective-permute-done.4.refs_0_
  15.9 0.0 collective-permute-done.5.refs_1_
  15.9 0.3 %gradient_inner.1 = (f32[12,16,16,128]{3,2,1,0:T(8,128)S(1)}, f32[3,16,16,128]{3,2,1,0:T(8,128)S(1)}) custom-call(f32[2,5,16,128]{3,2,1,0:T(8,128)S(1)} %collective-permute-done.4.refs_0_, f32[2,5,16,128]{3,2,1,0:T(8,128)S(1)} %collective-permute-done.5.refs_1_, ...), custom_call_target="tpu_custom_call", output_to_operand_aliasing={{0}: (9, {}), {1}: (10, {})} | custom-call | flops 983040 | bytes 262144 | tf_op jit(solution)/shard_map/gradient_inner/pallas_call | solution.py:812
  16.2 0.0 collective-permute-done.3.refs_0_
  16.2 0.1 gradient.1
  16.3 3.2 %collective-permute-start.6 = (f32[3,16,16,128]{3,2,1,0:T(8,128)S(1)}, f32[3,16,16,128]{3,2,1,0:T(8,128)S(1)}, u32[]{:S(2)}, u32[]{:S(2)}) collective-permute-start(f32[3,16,16,128]{3,2,1,0:T(8,128)S(1)} %get-tuple-element.62.mine), channel_id=1, source_target_pairs={{0,16},{16,0},{1,17},{17,1},{2,18},{18,2},{3,19},{19,3},{4,20},{20... | collective-permute-start | bytes 1179656 | tf_op jit(solution)/shard_map/ppermute | solution.py:836
  19.5 1.2 %outputs.1 = (f32[9,16,16,128]{3,2,1,0:T(8,128)}, f32[9,16,16,128]{3,2,1,0:T(8,128)}) custom-call(s32[1]{0:T(128)S(6)} %copy.32.refs_3_.source_cell, f32[1]{0:T(128)S(6)} %copy.33.refs_4_.source_amp, f32[12,16,16,128]{3,2,1,0:T(8,128)S(1)} %get-tuple-element.57.strain, ...), custom_call_target="tpu_custom_call", output_to_operand_aliasing={{0}: (6, {}), {1}: (7, {})} | custom-call | flops 1966080 | bytes 2359296 | tf_op jit(solution)/shard_map/outputs/pallas_call | solution.py:839
  20.8 0.1 collective-permute-done.6.other
  20.9 0.8 %sum.1 = f32[3,16,16,128]{3,2,1,0:T(8,128)} custom-call(f32[3,16,16,128]{3,2,1,0:T(8,128)S(1)} %get-tuple-element.62.mine, f32[3,16,16,128]{3,2,1,0:T(8,128)S(1)} %collective-permute-done.6.other), custom_call_target="tpu_custom_call" | custom-call | flops 98304 | bytes 1179648 | tf_op jit(solution)/shard_map/sum/pallas_call | solution.py:850
Async XLA Ops:
  0.6 2.5 %copy-start.1 = (f32[1,9,16,16,128]{4,3,2,1,0:T(8,128)S(1)}, f32[1,9,16,16,128]{4,3,2,1,0:T(8,128)}, u32[]{:S(2)}) copy-start(f32[1,9,16,16,128]{4,3,2,1,0:T(8,128)} %param.10) | copy-start | bytes 3538948
  0.6 2.5 %copy-start = (f32[1,9,16,16,128]{4,3,2,1,0:T(8,128)S(1)}, f32[1,9,16,16,128]{4,3,2,1,0:T(8,128)}, u32[]{:S(2)}) copy-start(f32[1,9,16,16,128]{4,3,2,1,0:T(8,128)} %param.9) | copy-start | bytes 3538948
  1.8 5.9 %copy-start.2 = (s32[1,256]{1,0:T(1,128)S(1)}, s32[1,256]{1,0:T(1,128)}, u32[]{:S(2)}) copy-start(s32[1,256]{1,0:T(1,128)} %receiver_cell.1) | copy-start | bytes 3076
  1.8 5.9 %copy-start.3 = (f32[1,256]{1,0:T(1,128)S(1)}, f32[1,256]{1,0:T(1,128)}, u32[]{:S(2)}) copy-start(f32[1,256]{1,0:T(1,128)} %residual_amp.1) | copy-start | bytes 3076
  1.8 7.2 %collective-permute-start.2 = (f32[2,5,16,128]{3,2,1,0:T(8,128)S(1)}, f32[2,5,16,128]{3,2,1,0:T(8,128)S(1)}, u32[]{:S(2)}, u32[]{:S(2)}) collective-permute-start(f32[2,5,16,128]{3,2,1,0:T(8,128)S(1)} %get-tuple-element.39), channel_id=1, source_target_pairs={{0,8},{8,0},{1,9},{9,1},{2,10},{10,2},{3,11},{11,3},{4,12},{12,4},... | collective-permute-start | bytes 245768 | tf_op jit(solution)/shard_map/ppermute | solution.py:37
  3.2 9.3 %collective-permute-start = (f32[2,5,16,128]{3,2,1,0:T(8,128)S(1)}, f32[2,5,16,128]{3,2,1,0:T(8,128)S(1)}, u32[]{:S(2)}, u32[]{:S(2)}) collective-permute-start(f32[2,5,16,128]{3,2,1,0:T(8,128)S(1)} %get-tuple-element.34), channel_id=1, source_target_pairs={{1,2},{3,4},{5,6},{2,1},{4,3},{6,5},{9,10},{11,12},{13,14},{10,9},... | collective-permute-start | bytes 245768 | tf_op jit(solution)/shard_map/ppermute | solution.py:37
  6.2 6.3 %collective-permute-start.1 = (f32[2,5,16,128]{3,2,1,0:T(8,128)S(1)}, f32[2,5,16,128]{3,2,1,0:T(8,128)S(1)}, u32[]{:S(2)}, u32[]{:S(2)}) collective-permute-start(f32[2,5,16,128]{3,2,1,0:T(8,128)S(1)} %get-tuple-element.35), channel_id=1, source_target_pairs={{0,1},{2,3},{4,5},{6,7},{1,0},{3,2},{5,4},{7,6},{8,9},{10,11},{12,... | collective-permute-start | bytes 245768 | tf_op jit(solution)/shard_map/ppermute | solution.py:37
  9.2 6.7 %collective-permute-start.4 = (f32[2,5,16,128]{3,2,1,0:T(8,128)S(1)}, f32[2,5,16,128]{3,2,1,0:T(8,128)S(1)}, u32[]{:S(2)}, u32[]{:S(2)}) collective-permute-start(f32[2,5,16,128]{3,2,1,0:T(8,128)S(1)} %get-tuple-element.49), channel_id=1, source_target_pairs={{0,1},{2,3},{4,5},{6,7},{1,0},{3,2},{5,4},{7,6},{8,9},{10,11},{12,... | collective-permute-start | bytes 245768 | tf_op jit(solution)/shard_map/ppermute | solution.py:37
  9.3 6.5 %collective-permute-start.5 = (f32[2,5,16,128]{3,2,1,0:T(8,128)S(1)}, f32[2,5,16,128]{3,2,1,0:T(8,128)S(1)}, u32[]{:S(2)}, u32[]{:S(2)}) collective-permute-start(f32[2,5,16,128]{3,2,1,0:T(8,128)S(1)} %get-tuple-element.50), channel_id=1, source_target_pairs={{1,2},{3,4},{5,6},{2,1},{4,3},{6,5},{9,10},{11,12},{13,14},{10,9},... | collective-permute-start | bytes 245768 | tf_op jit(solution)/shard_map/ppermute | solution.py:37
  12.8 3.4 %collective-permute-start.3 = (f32[2,5,16,128]{3,2,1,0:T(8,128)S(1)}, f32[2,5,16,128]{3,2,1,0:T(8,128)S(1)}, u32[]{:S(2)}, u32[]{:S(2)}) collective-permute-start(f32[2,5,16,128]{3,2,1,0:T(8,128)S(1)} %get-tuple-element.42), channel_id=1, source_target_pairs={{0,8},{8,0},{1,9},{9,1},{2,10},{10,2},{3,11},{11,3},{4,12},{12,4},... | collective-permute-start | bytes 245768 | tf_op jit(solution)/shard_map/ppermute | solution.py:37
  16.3 4.6 %collective-permute-start.6 = (f32[3,16,16,128]{3,2,1,0:T(8,128)S(1)}, f32[3,16,16,128]{3,2,1,0:T(8,128)S(1)}, u32[]{:S(2)}, u32[]{:S(2)}) collective-permute-start(f32[3,16,16,128]{3,2,1,0:T(8,128)S(1)} %get-tuple-element.62.mine), channel_id=1, source_target_pairs={{0,16},{16,0},{1,17},{17,1},{2,18},{18,2},{3,19},{19,3},{4,20},{20... | collective-permute-start | bytes 1179656 | tf_op jit(solution)/shard_map/ppermute | solution.py:836

commit v16 on v15

--- a/solution.py
+++ b/solution.py
@@ -68,44 +68,45 @@
 
 def early_pack_kernel(links, forward, adjoint, density, *refs):
     sends, (density_rows, stress, sems) = refs[: len(links)], refs[len(links) :]
-    tile = forward.shape[1:3]
+    tile_x = forward.shape[1]
     waits = []
+    for at, (link, send) in enumerate(zip(links, sends)):
+        n, a, b = (3 + part for part in STRESS_ALONG[link[1]])
+
+        def start(plan, lower):
+            for wave, fields in enumerate((forward, adjoint)):
+                first, last = pl.ds(0, 2), pl.ds(tile_x - 2, 2)
+                if lower:
+                    pieces = (
+                        (fields.at[n, pl.ds(tile_x - 1, 1)], 0, 1),
+                        (fields.at[a, last], 1, 2),
+                        (fields.at[b, last], 3, 2),
+                    )
+                else:
+                    pieces = (
+                        (fields.at[n, first], 0, 2),
+                        (fields.at[a, pl.ds(0, 1)], 2, 1),
+                        (fields.at[b, pl.ds(0, 1)], 3, 1),
+                        (density.at[pl.ds(wave, 1)], SPARE, 1),
+                    )
+                for source, slot, size in pieces:
+                    pltpu.make_async_copy(
+                        source, send.at[wave, pl.ds(slot, size)], sems.at[2 * at + wave]
+                    ).start()
+
+        by_role(link, start, *stress_plan(link[1]))
+        for wave in range(2):
+            waits.append(
+                pltpu.make_async_copy(
+                    forward.at[0, pl.ds(0, SLOTS)], send.at[wave], sems.at[2 * at + wave]
+                )
+            )
     for row in range(2):
         copy = pltpu.make_async_copy(
-            density.at[:, row, :], density_rows.at[row], sems.at[2 * SLOTS * len(links) + row]
+            density.at[:, row, :], density_rows.at[row], sems.at[2 * len(links) + row]
         )
         copy.start()
         waits.append(copy)
-
-    def layer(ref, dim, index):
-        return ref.at[index] if dim == 0 else ref.at[:, index, :]
-
-    for at, (link, send) in enumerate(zip(links, sends)):
-        dim = link[1]
-
-        def semaphore(wave, slot):
-            return sems.at[(2 * at + wave) * SLOTS + slot]
-
-        def start(plan, lower):
-            for wave, fields in enumerate((forward, adjoint)):
-                sources = [
-                    layer(fields.at[3 + part], dim, index % tile[dim]) for part, index in plan
-                ]
-                if not lower:
-                    sources.append(layer(density, dim, wave))
-                for slot, source in enumerate(sources):
-                    pltpu.make_async_copy(
-                        source, send.at[wave, slot], semaphore(wave, slot)
-                    ).start()
-
-        by_role(link, start, *stress_plan(dim))
-        for wave in range(2):
-            for slot in range(SLOTS):
-                waits.append(
-                    pltpu.make_async_copy(
-                        layer(density, dim, 0), send.at[wave, slot], semaphore(wave, slot)
-                    )
-                )
     for wave in range(2):
         clear_rim(
             stress, *([6 * wave + part for part in STRESS_ALONG[dim]] for dim in range(2))
@@ -244,8 +245,6 @@
 
 def velocity_kernel(
     width_y,
-    lame,
-    shear,
     density,
     receiver_cell,
     residual_amp,
@@ -257,23 +256,14 @@
     accel,
     rim_added,
     buoyancy,
-    scaled_lame,
-    scaled_shear,
     received,
     gained,
-    lame_now,
-    shear_now,
     density_now,
     sems,
 ):
     tile_x, tile_y, depth = density.shape
-    copies = [
-        pltpu.make_async_copy(lame, lame_now, sems.at[0]),
-        pltpu.make_async_copy(shear, shear_now, sems.at[1]),
-        pltpu.make_async_copy(density, density_now, sems.at[2]),
-    ]
-    for copy in copies:
-        copy.start()
+    copy = pltpu.make_async_copy(density, density_now, sems.at[0])
+    copy.start()
     cells = tile_x * tile_y
     middle = pl.ds(ROWS, tile_y)
     columns = column_ids(tile_x, tile_y, width_y, depth)
@@ -313,14 +303,11 @@
         return carry
 
     lax.fori_loop(0, tile_x, layer, 0, unroll=True)
-    for copy in copies:
-        copy.wait()
+    copy.wait()
 
     def finish(x, carry):
         light = 1.0 / density_now[x]
         buoyancy[x] = light
-        scaled_lame[x] = time_step * lame_now[x]
-        scaled_shear[x] = time_step * shear_now[x]
         for wave, fields in enumerate((forward, adjoint)):
             for part in range(3):
                 value = light * gained[3 * wave + part, x]
@@ -512,10 +499,16 @@
     count = len(links)
     received = refs[:count]
     source_cell, source_amp, rim_added, buoyancy, accel = refs[count : count + 5]
-    stress = refs[count + 6]
-    strain, gradient, velocity = refs[count + 7 : count + 10]
-    outputs, missing = refs[count + 10 : count + 12], refs[count + 12 : 2 * count + 12]
-    accel_now, sems = refs[2 * count + 12 :]
+    stress, lame, shear = refs[count + 6 : count + 9]
+    strain, gradient, velocity, scaled_lame, scaled_shear = refs[count + 9 : count + 14]
+    outputs, missing = refs[count + 14 : count + 16], refs[count + 16 : 2 * count + 16]
+    accel_now, lame_now, shear_now, sems = refs[2 * count + 16 :]
+    fetches = [
+        pltpu.make_async_copy(lame, lame_now, sems.at[6]),
+        pltpu.make_async_copy(shear, shear_now, sems.at[7]),
+    ]
+    for copy in fetches:
+        copy.start()
     tile_x, tile_y, depth = buoyancy.shape
     middle = pl.ds(ROWS, tile_y)
     clear_rim(velocity, range(6), range(6))
@@ -575,6 +568,10 @@
 
     lax.fori_loop(0, tile_x, layer, 0, unroll=8)
     missing_terms(links, stress, (cell, amp), width_y, missing)
+    for copy in fetches:
+        copy.wait()
+    scaled_lame[...] = time_step * lame_now[...]
+    scaled_shear[...] = time_step * shear_now[...]
     for copy in copies:
         copy.wait()
 
@@ -724,7 +721,7 @@
         out_shape=shapes(links_x) + [pltpu.VMEM((2, tile_x, depth), jnp.float32), padded(12)],
         in_specs=[hbm] * 3,
         out_specs=[vmem] * (count_x + 2),
-        scratch_shapes=[pltpu.SemaphoreType.DMA((2 + 2 * SLOTS * count_x,))],
+        scratch_shapes=[pltpu.SemaphoreType.DMA((2 + 2 * count_x,))],
         compiler_params=params,
         cost_estimate=cost(0, 4 * cells),
         name="early_pack",
@@ -743,7 +740,7 @@
         )(forward, adjoint, density_rows)
         halos_y = exchange(links_y, sends)
 
-    stress, velocity, accel, rim_added, buoyancy, scaled_lame, scaled_shear = pl.pallas_call(
+    stress, velocity, accel, rim_added, buoyancy = pl.pallas_call(
         functools.partial(velocity_kernel, width_y),
         out_shape=[
             padded(12),
@@ -751,31 +748,20 @@
             tile(3),
             pltpu.VMEM((2, 3, max(tile_x, tile_y), depth), jnp.float32),
             tile(),
-            tile(),
-            tile(),
         ],
-        in_specs=[hbm] * 3 + [vmem] * 5,
-        out_specs=[vmem] * 7,
-        input_output_aliases={7: 0},
+        in_specs=[hbm] + [vmem] * 5,
+        out_specs=[vmem] * 5,
+        input_output_aliases={5: 0},
         scratch_shapes=[
             pltpu.VMEM((rows, depth), jnp.float32),
             tile(6),
             tile(),
-            tile(),
-            tile(),
-            pltpu.SemaphoreType.DMA((3,)),
+            pltpu.SemaphoreType.DMA((1,)),
         ],
         compiler_params=params,
         cost_estimate=cost(200 * cells, 18 * 4 * cells),
         name="velocity",
-    )(
-        *(in_hbm(x) for x in (lame_lambda, shear_modulus, density)),
-        receiver_cell,
-        residual_amp,
-        forward,
-        adjoint,
-        stress,
-    )
+    )(in_hbm(density), receiver_cell, residual_amp, forward, adjoint, stress)
 
     def boundary(links, send_links, halos, velocity, name):
         velocity, *sends = pl.pallas_call(
@@ -796,17 +782,29 @@
     halos = halos_y + halos_x
 
     out_shape = jax.ShapeDtypeStruct(forward.shape, jnp.float32)
-    strain, gradient, _, forward_next, adjoint_next, *missing = pl.pallas_call(
+    strain, gradient, _, scaled_lame, scaled_shear, *rest = pl.pallas_call(
         functools.partial(strain_kernel, links, width_y),
-        out_shape=[tile(12), tile(3), padded(6), out_shape, out_shape] + shapes(links),
-        in_specs=[vmem] * count + [smem] * 2 + [vmem] * 5,
-        out_specs=[vmem] * 3 + [hbm] * 2 + [vmem] * count,
+        out_shape=[tile(12), tile(3), padded(6), tile(), tile(), out_shape, out_shape]
+        + shapes(links),
+        in_specs=[vmem] * count + [smem] * 2 + [vmem] * 5 + [hbm] * 2,
+        out_specs=[vmem] * 5 + [hbm] * 2 + [vmem] * count,
         input_output_aliases={count + 5: 2},
-        scratch_shapes=[tile(3), pltpu.SemaphoreType.DMA((6,))],
+        scratch_shapes=[tile(3), tile(), tile(), pltpu.SemaphoreType.DMA((8,))],
         compiler_params=params,
         cost_estimate=cost(200 * cells, 18 * 4 * cells),
         name="strain",
-    )(*halos, *source, rim_added, buoyancy, accel, velocity, stress)
+    )(
+        *halos,
+        *source,
+        rim_added,
+        buoyancy,
+        accel,
+        velocity,
+        stress,
+        in_hbm(lame_lambda),
+        in_hbm(shear_modulus),
+    )
+    forward_next, adjoint_next, *missing = rest
 
     def gradients(links, inner, received, stresses, missing, strain, gradient, name):
         return pl.pallas_call(

time: 21.9 us -> 21.7 us (level)
  no operation moved by 1% of the time
where the time goes in v16:
time: 21.7 us; the launch traced here: 21.5 us
  starting transfers between devices  12.8 us (59%)
  Pallas kernels  6.43 us (30%)
  between operations  2.1 us (10%)
    ppermute x6, starting transfers between devices, swap(): return lax.ppermute(value, axis, pairs + [(j, i) for i, j in pairs])  9.75 us
    ppermute x1, starting transfers between devices, body(): other = lax.ppermute(gradient, 'shot', [(0, 1), (1, 0)])  3.04 us
    pallas_call x1, Pallas kernels, body(): pl.pallas_call(functools.partial(velocity_kernel, width_y), out_shape=[pa...  1.29 us
    pallas_call x1, Pallas kernels, body(): pl.pallas_call(functools.partial(strain_kernel, links, width_y), out_shap...  1.29 us
    pallas_call x1, Pallas kernels, body(): pl.pallas_call(functools.partial(output_kernel, chunk, width_y), out_shap...  1.23 us
    pallas_call x1, Pallas kernels, body(): pl.pallas_call(functools.partial(early_pack_kernel, links_x), out_shape=s...  1 us
    pallas_call x1, Pallas kernels, body(): pl.pallas_call(functools.partial(sum_kernel, tile_x), out_shape=jax.Shape...  0.78 us
  transfers between devices with their start and end apart: 7, of which 1 were waited for; matrix products, arithmetic and copies ran while one was open for 0% of the time, Pallas kernels for 21%

profile of v16, /device:TPU:9, one launch (start us, length us, event | category | flops | bytes accessed | tf_op | source)
XLA Modules:
  0.0 21.5 jit_solution(6892386135213228640)
XLA Ops:
  0.6 0.0 copy-start.1
  0.6 0.0 copy-start
  0.6 1.0 %early_pack.1 = (f32[2,5,16,128]{3,2,1,0:T(8,128)S(1)}, f32[2,16,128]{2,1,0:T(8,128)S(1)}, f32[12,20,32,128]{3,2,1,0:T(8,128)S(1)}) custom-call(f32[9,16,16,128]{3,2,1,0:T(8,128)} %bitcast.4, f32[9,16,16,128]{3,2,1,0:T(8,128)} %bitcast.7, f32[16,16,128]{2,1,0:T(8,128)} %density.3), custom_call_target="tpu_custom_call" | custom-call | bytes 131072 | tf_op jit(solution)/shard_map/early_pack/pallas_call | solution.py:719
  1.7 0.0 copy-start.2
  1.7 0.0 copy-start.3
  1.7 1.3 %collective-permute-start.2 = (f32[2,5,16,128]{3,2,1,0:T(8,128)S(1)}, f32[2,5,16,128]{3,2,1,0:T(8,128)S(1)}, u32[]{:S(2)}, u32[]{:S(2)}) collective-permute-start(f32[2,5,16,128]{3,2,1,0:T(8,128)S(1)} %get-tuple-element.39), channel_id=1, source_target_pairs={{0,8},{8,0},{1,9},{9,1},{2,10},{10,2},{3,11},{11,3},{4,12},{12,4},... | collective-permute-start | bytes 245768 | tf_op jit(solution)/shard_map/ppermute | solution.py:37
  3.0 0.0 copy-done.1
  3.0 0.0 copy-done
  3.0 0.1 pack.1
  3.1 3.0 %collective-permute-start = (f32[2,5,16,128]{3,2,1,0:T(8,128)S(1)}, f32[2,5,16,128]{3,2,1,0:T(8,128)S(1)}, u32[]{:S(2)}, u32[]{:S(2)}) collective-permute-start(f32[2,5,16,128]{3,2,1,0:T(8,128)S(1)} %get-tuple-element.34), channel_id=1, source_target_pairs={{1,2},{3,4},{5,6},{2,1},{4,3},{6,5},{9,10},{11,12},{13,14},{10,9},... | collective-permute-start | bytes 245768 | tf_op jit(solution)/shard_map/ppermute | solution.py:37
  6.1 1.4 %collective-permute-start.1 = (f32[2,5,16,128]{3,2,1,0:T(8,128)S(1)}, f32[2,5,16,128]{3,2,1,0:T(8,128)S(1)}, u32[]{:S(2)}, u32[]{:S(2)}) collective-permute-start(f32[2,5,16,128]{3,2,1,0:T(8,128)S(1)} %get-tuple-element.35), channel_id=1, source_target_pairs={{0,1},{2,3},{4,5},{6,7},{1,0},{3,2},{5,4},{7,6},{8,9},{10,11},{12,... | collective-permute-start | bytes 245768 | tf_op jit(solution)/shard_map/ppermute | solution.py:37
  7.5 0.0 copy-done.2
  7.5 0.0 copy-done.3
  7.5 1.3 %velocity.1 = (f32[12,20,32,128]{3,2,1,0:T(8,128)S(1)}, f32[6,20,32,128]{3,2,1,0:T(8,128)S(1)}, f32[3,16,16,128]{3,2,1,0:T(8,128)S(1)}, f32[2,3,16,128]{3,2,1,0:T(8,128)S(1)}, f32[16,16,128]{2,1,0:T(8,128)S(1)}) custom-call(f32[16,16,128]{2,1,0:T(8,128)} %density.3, s32[1,256]{1,0:T(1,128)S(1)} %copy-done.2, ...), custom_call_target="tpu_custom_call", output_to_operand_aliasing={{0}: (5, {})} | custom-call | flops 6553600 | bytes 2359296 | tf_op jit(solution)/shard_map/velocity/pallas_call | solution.py:743
  8.8 0.0 collective-permute-done.2.refs_0_.refs_2_.refs_1_
  8.9 0.2 boundary_x.1
  9.0 0.2 collective-permute-start.4
  9.2 3.2 %collective-permute-start.5 = (f32[2,5,16,128]{3,2,1,0:T(8,128)S(1)}, f32[2,5,16,128]{3,2,1,0:T(8,128)S(1)}, u32[]{:S(2)}, u32[]{:S(2)}) collective-permute-start(f32[2,5,16,128]{3,2,1,0:T(8,128)S(1)} %get-tuple-element.50), channel_id=1, source_target_pairs={{1,2},{3,4},{5,6},{2,1},{4,3},{6,5},{9,10},{11,12},{13,14},{10,9},... | collective-permute-start | bytes 245768 | tf_op jit(solution)/shard_map/ppermute | solution.py:37
  12.3 0.0 collective-permute-done.refs_0_.refs_3_
  12.4 0.0 collective-permute-done.1.refs_1_.refs_2_
  12.4 0.2 %boundary_y.1 = (f32[6,20,32,128]{3,2,1,0:T(8,128)S(1)}, f32[2,5,16,128]{3,2,1,0:T(8,128)S(1)}) custom-call(f32[2,5,16,128]{3,2,1,0:T(8,128)S(1)} %collective-permute-done.refs_0_.refs_3_, f32[2,5,16,128]{3,2,1,0:T(8,128)S(1)} %collective-permute-done.1.refs_1_.refs_2_, ...), custom_call_target="tpu_custom_call", output_to_operand_aliasing={{0}: (4, {})} | custom-call | flops 32768 | bytes 163840 | tf_op jit(solution)/shard_map/boundary_y/pallas_call | solution.py:767
  12.6 0.7 %collective-permute-start.3 = (f32[2,5,16,128]{3,2,1,0:T(8,128)S(1)}, f32[2,5,16,128]{3,2,1,0:T(8,128)S(1)}, u32[]{:S(2)}, u32[]{:S(2)}) collective-permute-start(f32[2,5,16,128]{3,2,1,0:T(8,128)S(1)} %get-tuple-element.42), channel_id=1, source_target_pairs={{0,8},{8,0},{1,9},{9,1},{2,10},{10,2},{3,11},{11,3},{4,12},{12,4},... | collective-permute-start | bytes 245768 | tf_op jit(solution)/shard_map/ppermute | solution.py:37
  14.6 1.3 %strain.1 = (f32[12,16,16,128]{3,2,1,0:T(8,128)S(1)}, f32[3,16,16,128]{3,2,1,0:T(8,128)S(1)}, f32[6,20,32,128]{3,2,1,0:T(8,128)S(1)}, f32[16,16,128]{2,1,0:T(8,1...) custom-call(f32[2,5,16,128]{3,2,1,0:T(8,128)S(1)} %collective-permut, ...), custom_call_target="tpu_custom_call", output_to_operand_aliasing={{2}: (8, {})} | custom-call | flops 6553600 | bytes 2359296 | tf_op jit(solution)/shard_map/strain/pallas_call | solution.py:785
  15.9 0.0 collective-permute-done.4.refs_0_
  15.9 0.0 collective-permute-done.5.refs_1_
  15.9 0.3 %gradient_inner.1 = (f32[12,16,16,128]{3,2,1,0:T(8,128)S(1)}, f32[3,16,16,128]{3,2,1,0:T(8,128)S(1)}) custom-call(f32[2,5,16,128]{3,2,1,0:T(8,128)S(1)} %collective-permute-done.4.refs_0_, f32[2,5,16,128]{3,2,1,0:T(8,128)S(1)} %collective-permute-done.5.refs_1_, ...), custom_call_target="tpu_custom_call", output_to_operand_aliasing={{0}: (9, {}), {1}: (10, {})} | custom-call | flops 983040 | bytes 262144 | tf_op jit(solution)/shard_map/gradient_inner/pallas_call | solution.py:810
  16.2 0.0 collective-permute-done.3.refs_0_
  16.2 0.1 gradient.1
  16.3 3.0 %collective-permute-start.6 = (f32[3,16,16,128]{3,2,1,0:T(8,128)S(1)}, f32[3,16,16,128]{3,2,1,0:T(8,128)S(1)}, u32[]{:S(2)}, u32[]{:S(2)}) collective-permute-start(f32[3,16,16,128]{3,2,1,0:T(8,128)S(1)} %get-tuple-element.62.mine), channel_id=1, source_target_pairs={{0,16},{16,0},{1,17},{17,1},{2,18},{18,2},{3,19},{19,3},{4,20},{20... | collective-permute-start | bytes 1179656 | tf_op jit(solution)/shard_map/ppermute | solution.py:834
  19.3 1.2 %outputs.1 = (f32[9,16,16,128]{3,2,1,0:T(8,128)}, f32[9,16,16,128]{3,2,1,0:T(8,128)}) custom-call(s32[1]{0:T(128)S(6)} %copy.32.refs_3_.source_cell, f32[1]{0:T(128)S(6)} %copy.33.refs_4_.source_amp, f32[12,16,16,128]{3,2,1,0:T(8,128)S(1)} %get-tuple-element.57.strain, ...), custom_call_target="tpu_custom_call", output_to_operand_aliasing={{0}: (6, {}), {1}: (7, {})} | custom-call | flops 1966080 | bytes 2359296 | tf_op jit(solution)/shard_map/outputs/pallas_call | solution.py:837
  20.6 0.1 collective-permute-done.6.other
  20.7 0.8 %sum.1 = f32[3,16,16,128]{3,2,1,0:T(8,128)} custom-call(f32[3,16,16,128]{3,2,1,0:T(8,128)S(1)} %get-tuple-element.62.mine, f32[3,16,16,128]{3,2,1,0:T(8,128)S(1)} %collective-permute-done.6.other), custom_call_target="tpu_custom_call" | custom-call | flops 98304 | bytes 1179648 | tf_op jit(solution)/shard_map/sum/pallas_call | solution.py:848
Async XLA Ops:
  0.6 2.4 %copy-start.1 = (f32[1,9,16,16,128]{4,3,2,1,0:T(8,128)S(1)}, f32[1,9,16,16,128]{4,3,2,1,0:T(8,128)}, u32[]{:S(2)}) copy-start(f32[1,9,16,16,128]{4,3,2,1,0:T(8,128)} %param.10) | copy-start | bytes 3538948
  0.6 2.4 %copy-start = (f32[1,9,16,16,128]{4,3,2,1,0:T(8,128)S(1)}, f32[1,9,16,16,128]{4,3,2,1,0:T(8,128)}, u32[]{:S(2)}) copy-start(f32[1,9,16,16,128]{4,3,2,1,0:T(8,128)} %param.9) | copy-start | bytes 3538948
  1.7 5.9 %copy-start.2 = (s32[1,256]{1,0:T(1,128)S(1)}, s32[1,256]{1,0:T(1,128)}, u32[]{:S(2)}) copy-start(s32[1,256]{1,0:T(1,128)} %receiver_cell.1) | copy-start | bytes 3076
  1.7 5.9 %copy-start.3 = (f32[1,256]{1,0:T(1,128)S(1)}, f32[1,256]{1,0:T(1,128)}, u32[]{:S(2)}) copy-start(f32[1,256]{1,0:T(1,128)} %residual_amp.1) | copy-start | bytes 3076
  1.7 7.2 %collective-permute-start.2 = (f32[2,5,16,128]{3,2,1,0:T(8,128)S(1)}, f32[2,5,16,128]{3,2,1,0:T(8,128)S(1)}, u32[]{:S(2)}, u32[]{:S(2)}) collective-permute-start(f32[2,5,16,128]{3,2,1,0:T(8,128)S(1)} %get-tuple-element.39), channel_id=1, source_target_pairs={{0,8},{8,0},{1,9},{9,1},{2,10},{10,2},{3,11},{11,3},{4,12},{12,4},... | collective-permute-start | bytes 245768 | tf_op jit(solution)/shard_map/ppermute | solution.py:37
  3.1 9.3 %collective-permute-start = (f32[2,5,16,128]{3,2,1,0:T(8,128)S(1)}, f32[2,5,16,128]{3,2,1,0:T(8,128)S(1)}, u32[]{:S(2)}, u32[]{:S(2)}) collective-permute-start(f32[2,5,16,128]{3,2,1,0:T(8,128)S(1)} %get-tuple-element.34), channel_id=1, source_target_pairs={{1,2},{3,4},{5,6},{2,1},{4,3},{6,5},{9,10},{11,12},{13,14},{10,9},... | collective-permute-start | bytes 245768 | tf_op jit(solution)/shard_map/ppermute | solution.py:37
  6.1 6.3 %collective-permute-start.1 = (f32[2,5,16,128]{3,2,1,0:T(8,128)S(1)}, f32[2,5,16,128]{3,2,1,0:T(8,128)S(1)}, u32[]{:S(2)}, u32[]{:S(2)}) collective-permute-start(f32[2,5,16,128]{3,2,1,0:T(8,128)S(1)} %get-tuple-element.35), channel_id=1, source_target_pairs={{0,1},{2,3},{4,5},{6,7},{1,0},{3,2},{5,4},{7,6},{8,9},{10,11},{12,... | collective-permute-start | bytes 245768 | tf_op jit(solution)/shard_map/ppermute | solution.py:37
  9.0 6.9 %collective-permute-start.4 = (f32[2,5,16,128]{3,2,1,0:T(8,128)S(1)}, f32[2,5,16,128]{3,2,1,0:T(8,128)S(1)}, u32[]{:S(2)}, u32[]{:S(2)}) collective-permute-start(f32[2,5,16,128]{3,2,1,0:T(8,128)S(1)} %get-tuple-element.49), channel_id=1, source_target_pairs={{0,1},{2,3},{4,5},{6,7},{1,0},{3,2},{5,4},{7,6},{8,9},{10,11},{12,... | collective-permute-start | bytes 245768 | tf_op jit(solution)/shard_map/ppermute | solution.py:37
  9.2 6.7 %collective-permute-start.5 = (f32[2,5,16,128]{3,2,1,0:T(8,128)S(1)}, f32[2,5,16,128]{3,2,1,0:T(8,128)S(1)}, u32[]{:S(2)}, u32[]{:S(2)}) collective-permute-start(f32[2,5,16,128]{3,2,1,0:T(8,128)S(1)} %get-tuple-element.50), channel_id=1, source_target_pairs={{1,2},{3,4},{5,6},{2,1},{4,3},{6,5},{9,10},{11,12},{13,14},{10,9},... | collective-permute-start | bytes 245768 | tf_op jit(solution)/shard_map/ppermute | solution.py:37
  12.6 3.6 %collective-permute-start.3 = (f32[2,5,16,128]{3,2,1,0:T(8,128)S(1)}, f32[2,5,16,128]{3,2,1,0:T(8,128)S(1)}, u32[]{:S(2)}, u32[]{:S(2)}) collective-permute-start(f32[2,5,16,128]{3,2,1,0:T(8,128)S(1)} %get-tuple-element.42), channel_id=1, source_target_pairs={{0,8},{8,0},{1,9},{9,1},{2,10},{10,2},{3,11},{11,3},{4,12},{12,4},... | collective-permute-start | bytes 245768 | tf_op jit(solution)/shard_map/ppermute | solution.py:37
  16.3 4.4 %collective-permute-start.6 = (f32[3,16,16,128]{3,2,1,0:T(8,128)S(1)}, f32[3,16,16,128]{3,2,1,0:T(8,128)S(1)}, u32[]{:S(2)}, u32[]{:S(2)}) collective-permute-start(f32[3,16,16,128]{3,2,1,0:T(8,128)S(1)} %get-tuple-element.62.mine), channel_id=1, source_target_pairs={{0,16},{16,0},{1,17},{17,1},{2,18},{18,2},{3,19},{19,3},{4,20},{20... | collective-permute-start | bytes 1179656 | tf_op jit(solution)/shard_map/ppermute | solution.py:834

commit v17 on v16

--- a/solution.py
+++ b/solution.py
@@ -282,7 +282,7 @@
                 )
         return carry
 
-    lax.fori_loop(0, tile_x, fill, 0, unroll=8)
+    lax.fori_loop(0, tile_x, fill, 0, unroll=True)
 
     def layer(x, carry):
         for wave in range(2):
@@ -318,7 +318,7 @@
                 )
         return carry
 
-    lax.fori_loop(0, tile_x, finish, 0, unroll=8)
+    lax.fori_loop(0, tile_x, finish, 0, unroll=True)
 
 
 def stress_halo_terms(links, received, rim_added, waves, add):

time: 21.7 us -> 21.4 us (0.986)
  Pallas kernels: 6.43 us -> 6.16 us
    pallas_call x1, Pallas kernels: 1.29 us -> 1.06 us  [body(): pl.pallas_call(functools.partial(velocity_kernel, width_y), out_shape=[pa...]
  transfers between devices with their start and end apart: 7 -> 7, of which waited for: 1 -> 1; matrix products, arithmetic and copies ran while one was open for 0% -> 0% of each run, Pallas kernels for 21% -> 20%
where the time goes in v17:
time: 21.4 us; the launch traced here: 21.2 us
  starting transfers between devices  12.8 us (60%)
  Pallas kernels  6.16 us (29%)
  between operations  2.1 us (10%)
    ppermute x6, starting transfers between devices, swap(): return lax.ppermute(value, axis, pairs + [(j, i) for i, j in pairs])  9.75 us
    ppermute x1, starting transfers between devices, body(): other = lax.ppermute(gradient, 'shot', [(0, 1), (1, 0)])  3.07 us
    pallas_call x1, Pallas kernels, body(): pl.pallas_call(functools.partial(strain_kernel, links, width_y), out_shap...  1.26 us
    pallas_call x1, Pallas kernels, body(): pl.pallas_call(functools.partial(output_kernel, chunk, width_y), out_shap...  1.23 us
    pallas_call x1, Pallas kernels, body(): pl.pallas_call(functools.partial(velocity_kernel, width_y), out_shape=[pa...  1.06 us
    pallas_call x1, Pallas kernels, body(): pl.pallas_call(functools.partial(early_pack_kernel, links_x), out_shape=s...  1 us
    pallas_call x1, Pallas kernels, body(): pl.pallas_call(functools.partial(sum_kernel, tile_x), out_shape=jax.Shape...  0.78 us
  transfers between devices with their start and end apart: 7, of which 1 were waited for; matrix products, arithmetic and copies ran while one was open for 0% of the time, Pallas kernels for 20%

profile of v17, /device:TPU:9, one launch (start us, length us, event | category | flops | bytes accessed | tf_op | source)
XLA Modules:
  0.0 21.2 jit_solution(5856061941756897025)
XLA Ops:
  0.6 0.0 copy-start.1
  0.6 0.0 copy-start
  0.6 1.0 %early_pack.1 = (f32[2,5,16,128]{3,2,1,0:T(8,128)S(1)}, f32[2,16,128]{2,1,0:T(8,128)S(1)}, f32[12,20,32,128]{3,2,1,0:T(8,128)S(1)}) custom-call(f32[9,16,16,128]{3,2,1,0:T(8,128)} %bitcast.4, f32[9,16,16,128]{3,2,1,0:T(8,128)} %bitcast.7, f32[16,16,128]{2,1,0:T(8,128)} %density.3), custom_call_target="tpu_custom_call" | custom-call | bytes 131072 | tf_op jit(solution)/shard_map/early_pack/pallas_call | solution.py:719
  1.7 0.0 copy-start.2
  1.7 0.0 copy-start.3
  1.7 1.3 %collective-permute-start.2 = (f32[2,5,16,128]{3,2,1,0:T(8,128)S(1)}, f32[2,5,16,128]{3,2,1,0:T(8,128)S(1)}, u32[]{:S(2)}, u32[]{:S(2)}) collective-permute-start(f32[2,5,16,128]{3,2,1,0:T(8,128)S(1)} %get-tuple-element.39), channel_id=1, source_target_pairs={{0,8},{8,0},{1,9},{9,1},{2,10},{10,2},{3,11},{11,3},{4,12},{12,4},... | collective-permute-start | bytes 245768 | tf_op jit(solution)/shard_map/ppermute | solution.py:37
  3.0 0.0 copy-done.1
  3.0 0.0 copy-done
  3.0 0.1 pack.1
  3.1 3.0 %collective-permute-start = (f32[2,5,16,128]{3,2,1,0:T(8,128)S(1)}, f32[2,5,16,128]{3,2,1,0:T(8,128)S(1)}, u32[]{:S(2)}, u32[]{:S(2)}) collective-permute-start(f32[2,5,16,128]{3,2,1,0:T(8,128)S(1)} %get-tuple-element.34), channel_id=1, source_target_pairs={{1,2},{3,4},{5,6},{2,1},{4,3},{6,5},{9,10},{11,12},{13,14},{10,9},... | collective-permute-start | bytes 245768 | tf_op jit(solution)/shard_map/ppermute | solution.py:37
  6.1 1.4 %collective-permute-start.1 = (f32[2,5,16,128]{3,2,1,0:T(8,128)S(1)}, f32[2,5,16,128]{3,2,1,0:T(8,128)S(1)}, u32[]{:S(2)}, u32[]{:S(2)}) collective-permute-start(f32[2,5,16,128]{3,2,1,0:T(8,128)S(1)} %get-tuple-element.35), channel_id=1, source_target_pairs={{0,1},{2,3},{4,5},{6,7},{1,0},{3,2},{5,4},{7,6},{8,9},{10,11},{12,... | collective-permute-start | bytes 245768 | tf_op jit(solution)/shard_map/ppermute | solution.py:37
  7.5 0.0 copy-done.2
  7.5 0.0 copy-done.3
  7.5 1.1 %velocity.1 = (f32[12,20,32,128]{3,2,1,0:T(8,128)S(1)}, f32[6,20,32,128]{3,2,1,0:T(8,128)S(1)}, f32[3,16,16,128]{3,2,1,0:T(8,128)S(1)}, f32[2,3,16,128]{3,2,1,0:T(8,128)S(1)}, f32[16,16,128]{2,1,0:T(8,128)S(1)}) custom-call(f32[16,16,128]{2,1,0:T(8,128)} %density.3, s32[1,256]{1,0:T(1,128)S(1)} %copy-done.2, ...), custom_call_target="tpu_custom_call", output_to_operand_aliasing={{0}: (5, {})} | custom-call | flops 6553600 | bytes 2359296 | tf_op jit(solution)/shard_map/velocity/pallas_call | solution.py:743
  8.6 0.0 collective-permute-done.2.refs_0_.refs_2_.refs_1_
  8.6 0.2 boundary_x.1
  8.8 0.2 collective-permute-start.4
  8.9 3.2 %collective-permute-start.5 = (f32[2,5,16,128]{3,2,1,0:T(8,128)S(1)}, f32[2,5,16,128]{3,2,1,0:T(8,128)S(1)}, u32[]{:S(2)}, u32[]{:S(2)}) collective-permute-start(f32[2,5,16,128]{3,2,1,0:T(8,128)S(1)} %get-tuple-element.50), channel_id=1, source_target_pairs={{1,2},{3,4},{5,6},{2,1},{4,3},{6,5},{9,10},{11,12},{13,14},{10,9},... | collective-permute-start | bytes 245768 | tf_op jit(solution)/shard_map/ppermute | solution.py:37
  12.1 0.0 collective-permute-done.refs_0_.refs_3_
  12.1 0.0 collective-permute-done.1.refs_1_.refs_2_
  12.1 0.2 %boundary_y.1 = (f32[6,20,32,128]{3,2,1,0:T(8,128)S(1)}, f32[2,5,16,128]{3,2,1,0:T(8,128)S(1)}) custom-call(f32[2,5,16,128]{3,2,1,0:T(8,128)S(1)} %collective-permute-done.refs_0_.refs_3_, f32[2,5,16,128]{3,2,1,0:T(8,128)S(1)} %collective-permute-done.1.refs_1_.refs_2_, ...), custom_call_target="tpu_custom_call", output_to_operand_aliasing={{0}: (4, {})} | custom-call | flops 32768 | bytes 163840 | tf_op jit(solution)/shard_map/boundary_y/pallas_call | solution.py:767
  12.4 0.7 %collective-permute-start.3 = (f32[2,5,16,128]{3,2,1,0:T(8,128)S(1)}, f32[2,5,16,128]{3,2,1,0:T(8,128)S(1)}, u32[]{:S(2)}, u32[]{:S(2)}) collective-permute-start(f32[2,5,16,128]{3,2,1,0:T(8,128)S(1)} %get-tuple-element.42), channel_id=1, source_target_pairs={{0,8},{8,0},{1,9},{9,1},{2,10},{10,2},{3,11},{11,3},{4,12},{12,4},... | collective-permute-start | bytes 245768 | tf_op jit(solution)/shard_map/ppermute | solution.py:37
  14.3 1.3 %strain.1 = (f32[12,16,16,128]{3,2,1,0:T(8,128)S(1)}, f32[3,16,16,128]{3,2,1,0:T(8,128)S(1)}, f32[6,20,32,128]{3,2,1,0:T(8,128)S(1)}, f32[16,16,128]{2,1,0:T(8,1...) custom-call(f32[2,5,16,128]{3,2,1,0:T(8,128)S(1)} %collective-permut, ...), custom_call_target="tpu_custom_call", output_to_operand_aliasing={{2}: (8, {})} | custom-call | flops 6553600 | bytes 2359296 | tf_op jit(solution)/shard_map/strain/pallas_call | solution.py:785
  15.6 0.0 collective-permute-done.4.refs_0_
  15.6 0.0 collective-permute-done.5.refs_1_
  15.6 0.3 %gradient_inner.1 = (f32[12,16,16,128]{3,2,1,0:T(8,128)S(1)}, f32[3,16,16,128]{3,2,1,0:T(8,128)S(1)}) custom-call(f32[2,5,16,128]{3,2,1,0:T(8,128)S(1)} %collective-permute-done.4.refs_0_, f32[2,5,16,128]{3,2,1,0:T(8,128)S(1)} %collective-permute-done.5.refs_1_, ...), custom_call_target="tpu_custom_call", output_to_operand_aliasing={{0}: (9, {}), {1}: (10, {})} | custom-call | flops 983040 | bytes 262144 | tf_op jit(solution)/shard_map/gradient_inner/pallas_call | solution.py:810
  15.9 0.0 collective-permute-done.3.refs_0_
  15.9 0.1 gradient.1
  16.0 3.1 %collective-permute-start.6 = (f32[3,16,16,128]{3,2,1,0:T(8,128)S(1)}, f32[3,16,16,128]{3,2,1,0:T(8,128)S(1)}, u32[]{:S(2)}, u32[]{:S(2)}) collective-permute-start(f32[3,16,16,128]{3,2,1,0:T(8,128)S(1)} %get-tuple-element.62.mine), channel_id=1, source_target_pairs={{0,16},{16,0},{1,17},{17,1},{2,18},{18,2},{3,19},{19,3},{4,20},{20... | collective-permute-start | bytes 1179656 | tf_op jit(solution)/shard_map/ppermute | solution.py:834
  19.1 1.2 %outputs.1 = (f32[9,16,16,128]{3,2,1,0:T(8,128)}, f32[9,16,16,128]{3,2,1,0:T(8,128)}) custom-call(s32[1]{0:T(128)S(6)} %copy.32.refs_3_.source_cell, f32[1]{0:T(128)S(6)} %copy.33.refs_4_.source_amp, f32[12,16,16,128]{3,2,1,0:T(8,128)S(1)} %get-tuple-element.57.strain, ...), custom_call_target="tpu_custom_call", output_to_operand_aliasing={{0}: (6, {}), {1}: (7, {})} | custom-call | flops 1966080 | bytes 2359296 | tf_op jit(solution)/shard_map/outputs/pallas_call | solution.py:837
  20.3 0.1 collective-permute-done.6.other
  20.4 0.8 %sum.1 = f32[3,16,16,128]{3,2,1,0:T(8,128)} custom-call(f32[3,16,16,128]{3,2,1,0:T(8,128)S(1)} %get-tuple-element.62.mine, f32[3,16,16,128]{3,2,1,0:T(8,128)S(1)} %collective-permute-done.6.other), custom_call_target="tpu_custom_call" | custom-call | flops 98304 | bytes 1179648 | tf_op jit(solution)/shard_map/sum/pallas_call | solution.py:848
Async XLA Ops:
  0.6 2.4 %copy-start.1 = (f32[1,9,16,16,128]{4,3,2,1,0:T(8,128)S(1)}, f32[1,9,16,16,128]{4,3,2,1,0:T(8,128)}, u32[]{:S(2)}) copy-start(f32[1,9,16,16,128]{4,3,2,1,0:T(8,128)} %param.10) | copy-start | bytes 3538948
  0.6 2.4 %copy-start = (f32[1,9,16,16,128]{4,3,2,1,0:T(8,128)S(1)}, f32[1,9,16,16,128]{4,3,2,1,0:T(8,128)}, u32[]{:S(2)}) copy-start(f32[1,9,16,16,128]{4,3,2,1,0:T(8,128)} %param.9) | copy-start | bytes 3538948
  1.7 5.9 %copy-start.2 = (s32[1,256]{1,0:T(1,128)S(1)}, s32[1,256]{1,0:T(1,128)}, u32[]{:S(2)}) copy-start(s32[1,256]{1,0:T(1,128)} %receiver_cell.1) | copy-start | bytes 3076
  1.7 5.9 %copy-start.3 = (f32[1,256]{1,0:T(1,128)S(1)}, f32[1,256]{1,0:T(1,128)}, u32[]{:S(2)}) copy-start(f32[1,256]{1,0:T(1,128)} %residual_amp.1) | copy-start | bytes 3076
  1.7 6.9 %collective-permute-start.2 = (f32[2,5,16,128]{3,2,1,0:T(8,128)S(1)}, f32[2,5,16,128]{3,2,1,0:T(8,128)S(1)}, u32[]{:S(2)}, u32[]{:S(2)}) collective-permute-start(f32[2,5,16,128]{3,2,1,0:T(8,128)S(1)} %get-tuple-element.39), channel_id=1, source_target_pairs={{0,8},{8,0},{1,9},{9,1},{2,10},{10,2},{3,11},{11,3},{4,12},{12,4},... | collective-permute-start | bytes 245768 | tf_op jit(solution)/shard_map/ppermute | solution.py:37
  3.1 9.0 %collective-permute-start = (f32[2,5,16,128]{3,2,1,0:T(8,128)S(1)}, f32[2,5,16,128]{3,2,1,0:T(8,128)S(1)}, u32[]{:S(2)}, u32[]{:S(2)}) collective-permute-start(f32[2,5,16,128]{3,2,1,0:T(8,128)S(1)} %get-tuple-element.34), channel_id=1, source_target_pairs={{1,2},{3,4},{5,6},{2,1},{4,3},{6,5},{9,10},{11,12},{13,14},{10,9},... | collective-permute-start | bytes 245768 | tf_op jit(solution)/shard_map/ppermute | solution.py:37
  6.1 6.0 %collective-permute-start.1 = (f32[2,5,16,128]{3,2,1,0:T(8,128)S(1)}, f32[2,5,16,128]{3,2,1,0:T(8,128)S(1)}, u32[]{:S(2)}, u32[]{:S(2)}) collective-permute-start(f32[2,5,16,128]{3,2,1,0:T(8,128)S(1)} %get-tuple-element.35), channel_id=1, source_target_pairs={{0,1},{2,3},{4,5},{6,7},{1,0},{3,2},{5,4},{7,6},{8,9},{10,11},{12,... | collective-permute-start | bytes 245768 | tf_op jit(solution)/shard_map/ppermute | solution.py:37
  8.8 6.8 %collective-permute-start.4 = (f32[2,5,16,128]{3,2,1,0:T(8,128)S(1)}, f32[2,5,16,128]{3,2,1,0:T(8,128)S(1)}, u32[]{:S(2)}, u32[]{:S(2)}) collective-permute-start(f32[2,5,16,128]{3,2,1,0:T(8,128)S(1)} %get-tuple-element.49), channel_id=1, source_target_pairs={{0,1},{2,3},{4,5},{6,7},{1,0},{3,2},{5,4},{7,6},{8,9},{10,11},{12,... | collective-permute-start | bytes 245768 | tf_op jit(solution)/shard_map/ppermute | solution.py:37
  8.9 6.7 %collective-permute-start.5 = (f32[2,5,16,128]{3,2,1,0:T(8,128)S(1)}, f32[2,5,16,128]{3,2,1,0:T(8,128)S(1)}, u32[]{:S(2)}, u32[]{:S(2)}) collective-permute-start(f32[2,5,16,128]{3,2,1,0:T(8,128)S(1)} %get-tuple-element.50), channel_id=1, source_target_pairs={{1,2},{3,4},{5,6},{2,1},{4,3},{6,5},{9,10},{11,12},{13,14},{10,9},... | collective-permute-start | bytes 245768 | tf_op jit(solution)/shard_map/ppermute | solution.py:37
  12.4 3.5 %collective-permute-start.3 = (f32[2,5,16,128]{3,2,1,0:T(8,128)S(1)}, f32[2,5,16,128]{3,2,1,0:T(8,128)S(1)}, u32[]{:S(2)}, u32[]{:S(2)}) collective-permute-start(f32[2,5,16,128]{3,2,1,0:T(8,128)S(1)} %get-tuple-element.42), channel_id=1, source_target_pairs={{0,8},{8,0},{1,9},{9,1},{2,10},{10,2},{3,11},{11,3},{4,12},{12,4},... | collective-permute-start | bytes 245768 | tf_op jit(solution)/shard_map/ppermute | solution.py:37
  16.0 4.4 %collective-permute-start.6 = (f32[3,16,16,128]{3,2,1,0:T(8,128)S(1)}, f32[3,16,16,128]{3,2,1,0:T(8,128)S(1)}, u32[]{:S(2)}, u32[]{:S(2)}) collective-permute-start(f32[3,16,16,128]{3,2,1,0:T(8,128)S(1)} %get-tuple-element.62.mine), channel_id=1, source_target_pairs={{0,16},{16,0},{1,17},{17,1},{2,18},{18,2},{3,19},{19,3},{4,20},{20... | collective-permute-start | bytes 1179656 | tf_op jit(solution)/shard_map/ppermute | solution.py:834
